TPU v7x, 256 devices: a whole 4x4x8 slice. The times are simulated.
256 devices in a mesh: layer: 4 (over y), shower: 64 (over x, z, core).
Axes of the slice: x: 4, y: 4, z: 8, core: 2. Of those that a mesh axis runs over, the one named last changes fastest.
Arguments:
- showers: bfloat16 [32768, 6336], P('shower', 'layer'), may hold values from -6 to 6
- geometry: bfloat16 [6336, 1024], P('layer'), may hold values from -0.109375 to 0.109375
- pattern: int32 [44, 8], P('layer'), may hold values 0 or 1
- bins: int32 [256], P('shower'), may hold values from 0 to 7, as said below
- sources: int32 [256], P('shower'), may hold values from 0 to 1
Outputs:
- proof: float32 [32768], P('shower')
Inputs may be any that keep to these rules, and one draw needn't show every extreme that they name: `bins`: the blocks of one bin are consecutive; the bin of block 0 holds exactly 129 blocks, every other bin 2 or more; every pair of bin and source is held by at least one block.
All inputs are finite; a program needn't handle non-finite values. No bound on the sum of `pattern` on one device may be relied on, other than what follows from the above.
Results may differ from a plain program's by a relative error of at most 0.0046.
Values may be sent and summed in bfloat16 or wider, within the bound.
No kernel may reach another device: no remote copies, remote signals or barrier semaphores. Data moves between devices by JAX's collectives and lax.ppermute only.
A program may use at most 64 MiB of HBM per device.

v0:
```python
import math

import jax
import jax.numpy as jnp
from jax import lax
from jax.sharding import PartitionSpec as P

BLOCK_ROWS = 128
ENERGY_BINS = 8


def normalize(values):
    scale = lax.rsqrt(jnp.mean(values * values, axis=1, keepdims=True) + 1e-05)
    return (values * scale).astype(jnp.bfloat16)


def shards(showers, geometry, pattern, bins, sources):
    rows = showers.shape[0]
    cells = showers.shape[1] // pattern.shape[0]
    features = geometry.shape[1]
    feat_width = features // pattern.shape[1]
    expanded = jnp.repeat(
        jnp.repeat(pattern.astype(jnp.bfloat16), cells, axis=0), feat_width, axis=1
    )
    partial_sums = jnp.dot(showers, geometry * expanded, preferred_element_type=jnp.float32)
    quarter_rows = rows // lax.axis_size("layer")
    layer_pos = lax.axis_index("layer")
    shower_pos = lax.axis_index("shower")
    summed = lax.psum(partial_sums, "layer")
    own_feats = normalize(summed)
    quarter = lax.dynamic_slice_in_dim(own_feats, layer_pos * quarter_rows, quarter_rows, 0)
    all_bins, all_sources = (
        lax.all_gather(bins, "shower", axis=0, tiled=True),
        lax.all_gather(sources, "shower", axis=0, tiled=True),
    )
    codes = all_bins + ENERGY_BINS * all_sources
    onehot = (codes[:, None] == jnp.arange(2 * ENERGY_BINS, dtype=jnp.int32)[None, :]).astype(
        jnp.float32
    )
    counts = jnp.sum(onehot, axis=0) * BLOCK_ROWS
    signs = jnp.where(
        jnp.arange(2 * ENERGY_BINS, dtype=jnp.int32) >= ENERGY_BINS, 1.0, -1.0
    ).astype(jnp.float32)
    block_coef = jnp.sum(jnp.where(onehot > 0.5, (signs / counts)[None, :], 0.0), axis=1)
    block_bin = all_bins.astype(jnp.float32)
    block_total = all_bins.shape[0]
    block_ids = jnp.arange(block_total, dtype=jnp.int32)
    own_global = shower_pos * rows + jnp.arange(rows, dtype=jnp.int32)
    own_bin = jnp.repeat(bins, BLOCK_ROWS).astype(jnp.float32)
    inv_root = 1.0 / math.sqrt(features)

    def tile_sums(columns, col_global, valid):
        col_onehot = ((col_global // BLOCK_ROWS)[:, None] == block_ids[None, :]).astype(jnp.float32)
        col_bin = jnp.sum(col_onehot * block_bin[None, :], axis=1)
        col_coef = jnp.sum(col_onehot * block_coef[None, :], axis=1)
        products = lax.dot_general(
            own_feats, columns, (((1,), (1,)), ((), ())), preferred_element_type=jnp.float32
        )
        shifted = products * inv_root + 1.0
        kernel_vals = shifted * shifted * shifted
        matches = (
            (own_bin[:, None] == col_bin[None, :])
            & (own_global[:, None] != col_global[None, :])
            & valid[None, :]
        )
        return jnp.sum(jnp.where(matches, kernel_vals * col_coef[None, :], 0.0), axis=1)

    piece = lax.all_gather(quarter, "shower", axis=0, tiled=True)
    width = math.gcd(piece.shape[0], 2048)

    def advance(turn, totals):
        columns = lax.dynamic_slice_in_dim(piece, turn * width, width, 0)
        position = turn * width + jnp.arange(width, dtype=jnp.int32)
        col_global = (
            position // quarter_rows * rows + layer_pos * quarter_rows + position % quarter_rows
        )
        valid = jnp.ones((width,), bool)
        return totals + tile_sums(columns, col_global, valid)

    partial_proof = lax.fori_loop(
        0, piece.shape[0] // width, advance, jnp.zeros((rows,), jnp.float32)
    )
    return lax.psum(partial_proof, "layer")


def solution(mesh):
    placed = (P("shower", "layer"), P("layer", None), P("layer", None), P("shower"), P("shower"))
    return jax.shard_map(shards, mesh=mesh, in_specs=placed, out_specs=P("shower"), check_vma=False)
```

profile of v0, /device:TPU:4, one launch (start us, length us, event | category | flops | bytes accessed | tf_op | source)
XLA Modules:
  0.0 236.6 jit_solution(7438053347255921027)
XLA Ops:
  6.5 0.8 convert_element_type.25
  7.4 0.1 copy.9
  7.4 0.1 broadcast_in_dim.77
  7.5 4.5 %broadcast_in_dim.78 = bf16[1584,8,128]{2,1,0:T(8,128)(2,1)S(1)} broadcast(bf16[1584,8]{1,0:T(8,128)(2,1)S(1)} %bitcast.23), dimensions={0,1} | broadcast | bytes 3269376 | tf_op jit(solution)/shard_map/broadcast_in_dim | solution.py:22
  12.0 3.4 %fusion.30 = f32[512,1024]{0,1:T(8,128)} fusion(bf16[512,1584]{0,1:T(8,128)(2,1)S(1)} %copy-done, bf16[1584,1024]{1,0:T(8,128)(2,1)S(1)} %copy-done.2, bf16[198,8,8,128]{3,2,1,0:T(8,128)(2,1)S(1)} %bitcast.22), kind=kOutput, calls=%fused_computation.45 | convolution fusion | flops 1662566400 | bytes 10207232 | tf_op jit(solution)/shard_map/dot_general | solution.py:25
  15.6 66.8 %all-reduce.5.cloned.1.call-done = f32[512,1024]{0,1:T(8,128)} async-done(((f32[512,1024]{0,1:T(8,128)}), f32[512,1024]{0,1:T(8,128)}) %all-reduce.5.cloned.1.call-update) | async-done | bytes 2097168 | tf_op jit(solution)/shard_map/psum | solution.py:29
  82.4 2.0 multiply_reduce_fusion
  84.3 0.3 copy-done.1
  84.6 0.3 multiply_convert_fusion
  84.9 0.8 constant_dynamic-slice_fusion
  85.7 0.6 dynamic-slice
  86.9 0.2 dynamic-update-slice
  87.1 0.2 dynamic-update-slice.1
  87.4 19.2 %all-reduce.2 = (s32[256]{0:T(256)S(1)}, s32[256]{0:T(256)S(1)}) all-reduce(s32[256]{0:T(256)S(1)} %dynamic-update-slice, s32[256]{0:T(256)S(1)} %dynamic-update-slice.1), channel_id=1, replica_groups=mesh['layer'=4,'shower'=64] {'shower'}, use_global_device_ids=true, to_apply=%add | all-reduce | flops 512 | bytes 4096
  106.5 0.1 convert_reduce_fusion
  106.7 0.1 select_reduce_fusion
  106.8 1.3 copy.11
  108.1 83.4 %all-gather.2.cloned.1.call-done = bf16[8192,1024]{0,1:T(8,128)(2,1)} async-done(((bf16[128,1024]{0,1:T(8,128)(2,1)}), bf16[8192,1024]{0,1:T(8,128)(2,1)}) %all-gather.2.cloned.1.call-update) | async-done | bytes 16777232 | tf_op jit(solution)/shard_map/all_gather | solution.py:68
  191.4 27.3 %while.17 = (s32[]{:T(128)}, f32[512]{0:T(512)S(1)}, s32[]{:T(128)}, f32[256]{0:T(256)S(1)}, bf16[8192,1024]{0,1:T(8,128)(2,1)}, /*index=5*/bf16[512,1024]{1,0:T...) while((s32[]{:T(128)}, f32[512]{0:T(512)S(1)}, ...), condition=%wide.region_8.9_spmd.clone, body=%wide.region_4.8_spmd.clone.sunk | while | flops 2160665600 | bytes 5327069 | solution.py:80
  191.4 0.1 broadcast_bitcast_fusion.2
  191.5 1.1 fusion.40
  192.7 5.5 %fusion.41 = f32[512]{0:T(512)S(1)} fusion(f32[2048]{0:T(1024)S(1)} %get-tuple-element.429, s32[512]{0:T(512)S(1)} %iota_add_fusion.3, f32[512]{0:T(512)S(1)} %broadcast_bitcast_fusion.2, s32[2048]{0:T(1024)S(1)} %get-tuple-element.430, f32[2048]{0:T(1024)S(1)} %get-tuple-element.431, bf16[512,1024]{1,0:T(8,128)(2,1)} %get-tuple-element.463, ...), kind=kOutput, calls=%fused_computation.6.clone.1 | convolution fusion | flops 2157968896 | bytes 5273604 | tf_op jit(solution)/shard_map/while/body/eval_jaxpr/dot_general | solution.py:56
  198.3 0.1 broadcast_bitcast_fusion.2
  198.4 1.1 fusion.40
  199.5 5.5 %fusion.41 = f32[512]{0:T(512)S(1)} fusion(f32[2048]{0:T(1024)S(1)} %get-tuple-element.429, s32[512]{0:T(512)S(1)} %iota_add_fusion.3, f32[512]{0:T(512)S(1)} %broadcast_bitcast_fusion.2, s32[2048]{0:T(1024)S(1)} %get-tuple-element.430, f32[2048]{0:T(1024)S(1)} %get-tuple-element.431, bf16[512,1024]{1,0:T(8,128)(2,1)} %get-tuple-element.463, ...), kind=kOutput, calls=%fused_computation.6.clone.1 | convolution fusion | flops 2157968896 | bytes 5273604 | tf_op jit(solution)/shard_map/while/body/eval_jaxpr/dot_general | solution.py:56
  205.1 0.1 broadcast_bitcast_fusion.2
  205.2 1.1 fusion.40
  206.3 5.5 %fusion.41 = f32[512]{0:T(512)S(1)} fusion(f32[2048]{0:T(1024)S(1)} %get-tuple-element.429, s32[512]{0:T(512)S(1)} %iota_add_fusion.3, f32[512]{0:T(512)S(1)} %broadcast_bitcast_fusion.2, s32[2048]{0:T(1024)S(1)} %get-tuple-element.430, f32[2048]{0:T(1024)S(1)} %get-tuple-element.431, bf16[512,1024]{1,0:T(8,128)(2,1)} %get-tuple-element.463, ...), kind=kOutput, calls=%fused_computation.6.clone.1 | convolution fusion | flops 2157968896 | bytes 5273604 | tf_op jit(solution)/shard_map/while/body/eval_jaxpr/dot_general | solution.py:56
  211.9 0.1 broadcast_bitcast_fusion.2
  212.0 1.1 fusion.40
  213.2 5.5 %fusion.41 = f32[512]{0:T(512)S(1)} fusion(f32[2048]{0:T(1024)S(1)} %get-tuple-element.429, s32[512]{0:T(512)S(1)} %iota_add_fusion.3, f32[512]{0:T(512)S(1)} %broadcast_bitcast_fusion.2, s32[2048]{0:T(1024)S(1)} %get-tuple-element.430, f32[2048]{0:T(1024)S(1)} %get-tuple-element.431, bf16[512,1024]{1,0:T(8,128)(2,1)} %get-tuple-element.463, ...), kind=kOutput, calls=%fused_computation.6.clone.1 | convolution fusion | flops 2157968896 | bytes 5273604 | tf_op jit(solution)/shard_map/while/body/eval_jaxpr/dot_general | solution.py:56
  218.7 11.1 %psum.15 = f32[512]{0:T(512)} all-reduce(f32[512]{0:T(512)S(1)} %get-tuple-element.286), channel_id=1, replica_groups=mesh['layer'=4,'shower'=64] {'layer'}, use_global_device_ids=true, to_apply=%region_9.10 | all-reduce | flops 512 | bytes 4096 | tf_op jit(solution)/shard_map/psum | solution.py:83
  (34 shorter events, 0.3 us)
Async XLA Ops:
  6.5 5.5 %copy-start = (bf16[512,1584]{0,1:T(8,128)(2,1)S(1)}, bf16[512,1584]{0,1:T(8,128)(2,1)}, u32[]{:S(2)}) copy-start(bf16[512,1584]{0,1:T(8,128)(2,1)} %param.7) | copy-start | bytes 4866052
  6.5 75.8 %all-reduce.5.cloned.1.call-start = ((), (), s32[]{:S(2)}) async-start(), calls=%async_computation | async-start | bytes 4194304 | tf_op jit(solution)/shard_map/psum | solution.py:29
  7.4 4.6 %copy-start.2 = (bf16[1584,1024]{1,0:T(8,128)(2,1)S(1)}, bf16[1584,1024]{1,0:T(8,128)(2,1)}, u32[]{:S(2)}) copy-start(bf16[1584,1024]{1,0:T(8,128)(2,1)} %param.8) | copy-start | bytes 9732100
  15.5 70.2 %copy-start.3 = (s32[4]{0:T(128)S(1)}, s32[4]{0:T(128)}, u32[]{:S(2)}) copy-start(s32[4]{0:T(128)} %param.10) | copy-start | bytes 52
  15.5 70.2 %copy-start.5 = (u32[256]{0:T(256)S(1)}, u32[256]{0:T(256)}, u32[]{:S(2)}) copy-start(u32[256]{0:T(256)} %constant.205) | copy-start | bytes 3076
  15.5 71.7 %copy-start.4 = (s32[4]{0:T(128)S(1)}, s32[4]{0:T(128)}, u32[]{:S(2)}) copy-start(s32[4]{0:T(128)} %param.11) | copy-start | bytes 52
  15.5 176.0 %all-gather.2.cloned.1.call-start = ((), (), s32[]{:S(2)}) async-start(), calls=%async_computation.1 | async-start | bytes 17039360 | tf_op jit(solution)/shard_map/all_gather | solution.py:68
  82.4 2.2 copy-start.1
Sparse Core Ops, SparseCore 0:
  15.6 66.7 all-reduce.4
  85.8 105.6 all-gather.1
where the time goes:
time: 238 us; the launch traced here: 237 us
  waiting for transfers between devices  150 us (63%)
  blocking collectives  30.2 us (13%)
  matrix products  25.5 us (11%)
  between operations  14.1 us (6%)
  local copies, waits for them, and re-layouts  8.35 us (4%)
  other arithmetic  7.97 us (3%)
    all_gather x1, waiting for transfers between devices, shards(): piece = lax.all_gather(quarter, 'shower', axis=0, tiled=True)  83.4 us
    psum x1, waiting for transfers between devices, shards(): summed = lax.psum(partial_sums, 'layer')  66.8 us
    dot_general x4, matrix products, tile_sums(): lax.dot_general(own_feats, columns, (((1,), (1,)), ((), ())), preferred_e...  22.1 us
    unnamed x1, blocking collectives  19.2 us
    psum x1, blocking collectives, shards(): return lax.psum(partial_proof, 'layer')  11.1 us
  transfers between devices with their start and end apart: 2, of which 2 were waited for; matrix products, arithmetic and copies ran while one was open for 1% of the time, Pallas kernels for 0%

commit v1 on v0

v1 whole, which is shorter than its diff:
```python
import functools

import jax
import jax.numpy as jnp
from jax import lax
from jax.experimental import pallas as pl
from jax.experimental.pallas import tpu as pltpu
from jax.sharding import PartitionSpec as P

BLOCK = 128
TAG = 16
AXES = ("layer", "shower")
NY, NX, NZ, NC = 4, 4, 8, 2


def flat(y, x, z, c):
    return y * (NX * NZ * NC) + (x * NZ + z) * NC + c


def permute(value, move, keep=lambda y, x, z, c: True):
    pairs = [
        (flat(y, x, z, c), flat(*move(y, x, z, c)))
        for y in range(NY)
        for x in range(NX)
        for z in range(NZ)
        for c in range(NC)
        if keep(y, x, z, c)
    ]
    return lax.ppermute(value, AXES, pairs)


def along_y(step):
    return lambda y, x, z, c: ((y + step) % NY, x, z, c)


def swap_x(y, x, z, c):
    return (y, x ^ 1, z, c)


def raw_kernel(pattern, showers, geometry, out, masked):
    step = pl.program_id(0)
    cells = geometry.shape[0] // pattern.shape[0]
    per = geometry.shape[1] // BLOCK
    for layer in range(pattern.shape[0]):
        for part in range(per):
            rows = pl.ds(layer * cells, cells)
            cols = pl.ds(part * BLOCK, BLOCK)
            on = pattern[layer, step * per + part].astype(jnp.float32).astype(jnp.bfloat16)
            masked[rows, cols] = geometry[rows, cols] * on
    out[...] = jnp.dot(showers[...], masked[...], preferred_element_type=jnp.float32)


def raw_partial(showers, geometry, pattern):
    rows, depth = showers.shape
    feats = geometry.shape[1]
    width = 256
    return pl.pallas_call(
        raw_kernel,
        grid=(feats // width,),
        in_specs=[
            pl.BlockSpec(memory_space=pltpu.SMEM),
            pl.BlockSpec((rows, depth), lambda i: (0, 0)),
            pl.BlockSpec((depth, width), lambda i: (0, i)),
        ],
        out_specs=pl.BlockSpec((rows, width), lambda i: (0, i)),
        out_shape=jax.ShapeDtypeStruct((rows, feats), jnp.float32),
        scratch_shapes=[pltpu.VMEM((depth, width), jnp.bfloat16)],
        compiler_params=pltpu.CompilerParams(vmem_limit_bytes=40 * 2**20),
        cost_estimate=pl.CostEstimate(
            flops=2 * rows * depth * feats, bytes_accessed=8 * 2**20, transcendentals=0
        ),
        name="raw",
    )(pattern, showers, geometry)


def pair_kernel(
    place, bins, own, x1, ya, yb, xx, y2a, y2b, w2a, w2b, extra, cols, before, out, rows_at, diag_on
):
    step = pl.program_id(0)
    y, z, c = place[0], place[1], place[2]
    half = BLOCK // 2
    main = 2 * NY * BLOCK

    @pl.when(step == 0)
    def _():
        def put(side, turn, ref, start, size, shift):
            row = side * NY * BLOCK + lax.rem(y + turn, NY) * BLOCK + shift
            rows_at[pl.ds(pl.multiple_of(row, half), size), :] = ref[pl.ds(start, size), :]

        put(0, 0, own, 0, BLOCK, 0)
        put(0, 3, ya, 0, BLOCK, 0)
        put(0, 1, yb, 0, BLOCK, 0)
        put(0, 2, y2a, 0, half, 0)
        put(0, 2, y2b, 0, half, half)
        put(1, 0, x1, 0, BLOCK, 0)
        put(1, 3, xx, 0, BLOCK, 0)
        put(1, 1, xx, BLOCK, BLOCK, 0)
        put(1, 2, w2a, 0, half, 0)
        put(1, 2, w2b, 0, half, half)
        rows_at[pl.ds(main, BLOCK), :] = extra[...]
        out[...] = before[...]

    def work(with_diag):
        count = cols.shape[0] // (BLOCK + TAG)
        for part in range(count):
            block = cols[pl.ds(part * (BLOCK + TAG), BLOCK), :]
            tag = cols[pl.ds(part * (BLOCK + TAG) + BLOCK, TAG), :].astype(jnp.float32)
            code = jnp.max(tag, axis=0, keepdims=True)[:, :BLOCK] - 1.0
            source = (code >= 8.0).astype(jnp.float32)
            bin_id = code - 8.0 * source
            products = lax.dot_general(
                block, rows_at[...], (((1,), (1,)), ((), ())), preferred_element_type=jnp.float32
            )
            shifted = products + 32.0
            cubes = shifted * shifted * shifted
            if with_diag:
                lane = lax.broadcasted_iota(jnp.int32, cubes.shape, 1)
                sub = lax.broadcasted_iota(jnp.int32, cubes.shape, 0)
                same = (lane - y * BLOCK == sub) & (c == part)
                cubes = jnp.where(same, 0.0, cubes)
            sums = jnp.sum(cubes, axis=0, keepdims=True)
            for at in range(cubes.shape[1] // BLOCK):
                lanes = pl.ds(at * BLOCK, BLOCK)
                match = (bins[0:1, lanes] == bin_id).astype(jnp.float32)
                one = match * source
                zero = match - one
                total = sums[:, at * BLOCK : (at + 1) * BLOCK]
                out[0:1, lanes] += one * total
                out[1:2, lanes] += zero * total
                out[2:3, lanes] += one
                out[3:4, lanes] += zero

    if diag_on:

        @pl.when(step == z)
        def _():
            work(True)

        @pl.when(step != z)
        def _():
            work(False)
    else:
        work(False)


def pair_sums(place, bins, parts, cols, before, diag_on):
    size = cols.shape[0] // (BLOCK + TAG)
    per = min(size, NC)
    feats = cols.shape[1]
    rows = bins.shape[1]
    whole = lambda ref: pl.BlockSpec(ref.shape, lambda i: (0, 0))
    return pl.pallas_call(
        functools.partial(pair_kernel, diag_on=diag_on),
        grid=(size // per,),
        in_specs=[
            pl.BlockSpec(memory_space=pltpu.SMEM),
            whole(bins),
            *[whole(part) for part in parts],
            pl.BlockSpec((per * (BLOCK + TAG), feats), lambda i: (i, 0)),
            whole(before),
        ],
        out_specs=pl.BlockSpec((8, rows), lambda i: (0, 0)),
        out_shape=jax.ShapeDtypeStruct((8, rows), jnp.float32),
        scratch_shapes=[pltpu.VMEM((rows, feats), jnp.bfloat16)],
        compiler_params=pltpu.CompilerParams(vmem_limit_bytes=48 * 2**20),
        cost_estimate=pl.CostEstimate(
            flops=2 * rows * size * BLOCK * feats, bytes_accessed=8 * 2**20, transcendentals=0
        ),
        name="pairs",
    )(place, bins, *parts, cols, before)


def shards(showers, geometry, pattern, bins, sources):
    y = lax.axis_index("layer")
    s = lax.axis_index("shower")
    x, z, c = s // (NZ * NC), (s // NC) % NZ, s % NC
    feats = geometry.shape[1]

    partial_sums = raw_partial(showers, geometry, pattern).reshape(NY, BLOCK, feats)
    share = lambda turn: lax.dynamic_index_in_dim(partial_sums, (y + turn) % NY, 0, keepdims=False)
    raw = share(0)
    arrived = [permute(share(turn).astype(jnp.float16), along_y(turn)) for turn in (2, 1, 3)]
    for part in arrived:
        raw = raw + part.astype(jnp.float32)
    scale = lax.rsqrt(jnp.mean(raw * raw, axis=1, keepdims=True) + 1e-05)
    own = (raw * scale).astype(jnp.bfloat16)

    own_code = lax.dynamic_index_in_dim(bins + 8 * sources, y, 0, keepdims=False)
    tag = jnp.full((TAG, feats), own_code + 1, jnp.int32).astype(jnp.bfloat16)
    tagged = jnp.concatenate([own, tag], axis=0)
    lines = [[(i * NZ + j) * NC + k for j in range(NZ) for k in range(NC)] for i in range(NX)]
    cols = lax.all_gather(tagged, "shower", axis_index_groups=lines, axis=0, tiled=True)

    half = BLOCK // 2
    other_bins = permute(bins, swap_x)
    x1 = permute(own, swap_x)
    ya = permute(own, along_y(1))
    yb = permute(own, along_y(3))
    xx = permute(jnp.concatenate([ya, yb], axis=0), swap_x)
    y2a = permute(ya[:half], along_y(1))
    y2b = permute(yb[half:], along_y(3))
    w2a = permute(xx[:half], along_y(1))
    w2b = permute(xx[BLOCK + half :], along_y(3))

    y2 = jnp.concatenate([y2a, y2b], axis=0)
    w2 = jnp.concatenate([w2a, w2b], axis=0)
    near = [own, ya, y2, yb]
    far = [x1, xx[:BLOCK], w2, xx[BLOCK:]]
    odd_row = lax.select_n(y + NY * (x % 2), *near, *far)
    odd_row = permute(
        odd_row,
        lambda y, x, z, c: (y, 3 - x, z, c),
        keep=lambda y, x, z, c: x >= 2 and z == 0 and c == 0,
    )
    odd_col = permute(
        cols[: BLOCK + TAG],
        lambda y, x, z, c: (y, 1, z, c),
        keep=lambda y, x, z, c: y == 0 and x == 2,
    )

    odd_bin = jnp.where((x < 2) & (z == 0) & (c == 0), bins[:1], -2)
    row_bins = jnp.repeat(jnp.concatenate([bins, other_bins, odd_bin]), BLOCK)
    row_bins = jnp.broadcast_to(row_bins.astype(jnp.float32)[None, :], (8, row_bins.shape[0]))
    place = jnp.stack([y, z, c]).astype(jnp.int32)
    parts = (own, x1, ya, yb, xx, y2a, y2b, w2a, w2b, odd_row)
    blank = jnp.zeros((8, row_bins.shape[1]), jnp.float32)
    stats = pair_sums(place, row_bins, parts, cols, blank, True)
    main = 2 * NY * BLOCK
    col_bins = jnp.where(jnp.arange(row_bins.shape[1])[None, :] < main, row_bins, -2.0)
    stats = pair_sums(place, col_bins, parts, odd_col, stats, False)[:4]

    side = NY * BLOCK
    mine = stats[:, :side] + permute(stats[:, side:main], swap_x)
    odd_stats = stats[:, main:]
    for start in (0, 1):
        odd = permute(
            odd_stats,
            lambda y, x, z, c: (y, 2, z, c),
            keep=lambda y, x, z, c, start=start: x == start and z == 0 and c == 0,
        )
        mine = mine + jnp.pad(odd, ((0, 0), (0, side - BLOCK)))
    total = mine
    for turn in (2, 1, 3):
        total = total + permute(mine, along_y(turn))
    weight = 1.0 / (BLOCK * 32.0**3)
    return (total[0] / total[2] - total[1] / total[3]) * weight


def solution(mesh):
    placed = (P("shower", "layer"), P("layer", None), P("layer", None), P("shower"), P("shower"))
    return jax.shard_map(shards, mesh=mesh, in_specs=placed, out_specs=P("shower"), check_vma=False)
```

time: 238 us -> 123 us (0.52)
  waiting for transfers between devices: 150 us -> 43.5 us
  starting transfers between devices: 0.04 us -> 32.5 us
  blocking collectives: 30.2 us -> 0 us
  matrix products: 25.5 us -> 0 us
  Pallas kernels: 0 us -> 20.5 us
  other arithmetic: 7.97 us -> 2.37 us
    all_gather x1, waiting for transfers between devices: 83.4 us -> 10.1 us  [shards(): lax.all_gather(tagged, 'shower', axis_index_groups=lines, axis=0, tiled=T...]
    psum x1 -> x0, waiting for transfers between devices: 66.8 us -> none  [shards(): summed = lax.psum(partial_sums, 'layer')]
    ppermute x0 -> x20, waiting for transfers between devices: none -> 33.4 us  [permute(): return lax.ppermute(value, AXES, pairs)]
    ppermute x0 -> x20, starting transfers between devices: none -> 32.5 us  [permute(): return lax.ppermute(value, AXES, pairs)]
    dot_general x5 -> x0, matrix products: 25.5 us -> none  [the longest x4 22.1 us: tile_sums(): lax.dot_general(own_feats, columns, (((1,), (1,)), ((), ())), preferred_e...]
    pallas_call x0 -> x3, Pallas kernels: none -> 20.5 us  [the longest x2 16.4 us: pair_sums(): pl.pallas_call(functools.partial(pair_kernel, diag_on=diag_on), grid=(siz...]
    unnamed x1 -> x0, blocking collectives: 19.2 us -> none
    psum x1 -> x0, blocking collectives: 11.1 us -> none  [shards(): return lax.psum(partial_proof, 'layer')]
  transfers between devices with their start and end apart: 2 -> 21, of which waited for: 2 -> 10; matrix products, arithmetic and copies ran while one was open for 1% -> 2% of each run, Pallas kernels for 0% -> 12%
where the time goes in v1:
time: 123 us
  waiting for transfers between devices  43.5 us (35%)
  starting transfers between devices  32.5 us (26%)
  Pallas kernels  20.5 us (17%)
  between operations  14.3 us (12%)
  local copies, waits for them, and re-layouts  9.49 us (8%)
  other arithmetic  2.37 us (2%)
    ppermute x20, waiting for transfers between devices, permute(): return lax.ppermute(value, AXES, pairs)  33.4 us
    ppermute x20, starting transfers between devices, permute(): return lax.ppermute(value, AXES, pairs)  32.5 us
    pallas_call x2, Pallas kernels, pair_sums(): pl.pallas_call(functools.partial(pair_kernel, diag_on=diag_on), grid=(siz...  16.4 us
    all_gather x1, waiting for transfers between devices, shards(): lax.all_gather(tagged, 'shower', axis_index_groups=lines, axis=0, tiled=T...  10.1 us
    unnamed x12, local copies, waits for them, and re-layouts  7.06 us
    pallas_call x1, Pallas kernels, raw_partial(): pl.pallas_call(raw_kernel, grid=(feats // width,), in_specs=[pl.BlockSpec...  4.09 us
  transfers between devices with their start and end apart: 21, of which 10 were waited for; matrix products, arithmetic and copies ran while one was open for 2% of the time, Pallas kernels for 12%

profile of v1, /device:TPU:4, one launch (start us, length us, event | category | flops | bytes accessed | tf_op | source)
XLA Modules:
  0.0 122.7 jit_solution(11692253604894502769)
XLA Ops:
  6.5 3.6 %copy.7.showers = bf16[512,1584]{1,0:T(8,128)(2,1)} copy(bf16[512,1584]{0,1:T(8,128)(2,1)} %param.5) | data formatting | bytes 3244032 | tf_op args[0]
  10.2 1.5 %copy-done = bf16[512,1584]{1,0:T(8,128)(2,1)S(1)} copy-done((bf16[512,1584]{1,0:T(8,128)(2,1)S(1)}, bf16[512,1584]{1,0:T(8,128)(2,1)}, u32[]{:S(2)}) %copy-start) | copy-done | bytes 1622040
  11.7 1.9 %copy-done.1 = bf16[1584,1024]{1,0:T(8,128)(2,1)S(1)} copy-done((bf16[1584,1024]{1,0:T(8,128)(2,1)S(1)}, bf16[1584,1024]{1,0:T(8,128)(2,1)}, u32[]{:S(2)}) %copy-start.1) | copy-done | bytes 3244056
  13.6 4.1 %raw.1 = f32[512,1024]{1,0:T(8,128)S(1)} custom-call(s32[11,8]{1,0:T(8,128)S(1)} %copy.6.pattern, bf16[512,1584]{1,0:T(8,128)(2,1)S(1)} %copy-done, bf16[1584,1024]{1,0:T(8,128)(2,1)S(1)} %copy-done.1), custom_call_target="tpu_custom_call" | custom-call | flops 1660944384 | bytes 8388608 | tf_op jit(solution)/shard_map/raw/pallas_call | solution.py:57
  17.7 0.8 fusion.2
  18.5 3.2 %collective-permute-start.1 = (f16[128,1024]{1,0:T(8,128)(2,1)}, f16[128,1024]{1,0:T(8,128)(2,1)S(1)}, u32[]{:S(2)}, u32[]{:S(2)}) collective-permute-start(f16[128,1024]{1,0:T(8,128)(2,1)} %get-tuple-element.5), channel_id=1, source_target_pairs={{0,128},{1,129},{2,130},{3,131},{4,132},{5,133},{6,134},{7,135},{8... | collective-permute-start | bytes 786440 | tf_op jit(solution)/shard_map/ppermute | solution.py:29
  22.4 2.6 %collective-permute-start.3 = (f16[128,1024]{1,0:T(8,128)(2,1)S(1)}, f16[128,1024]{1,0:T(8,128)(2,1)S(1)}, u32[]{:S(2)}, u32[]{:S(2)}) collective-permute-start(f16[128,1024]{1,0:T(8,128)(2,1)S(1)} %get-tuple-element.6), channel_id=1, source_target_pairs={{0,192},{1,193},{2,194},{3,195},{4,196},{5,197},{6,198},{7,199},{8... | collective-permute-start | bytes 786440 | tf_op jit(solution)/shard_map/ppermute | solution.py:29
  26.2 3.3 %collective-permute-done.1 = f16[128,1024]{1,0:T(8,128)(2,1)S(1)} collective-permute-done((f16[128,1024]{1,0:T(8,128)(2,1)}, f16[128,1024]{1,0:T(8,128)(2,1)S(1)}, u32[]{:S(2)}, u32[]{:S(2)}) %collective-permute-start.1) | collective-permute-done | bytes 262176 | tf_op jit(solution)/shard_map/ppermute | solution.py:29
  29.5 4.4 %collective-permute-done.2 = f16[128,1024]{1,0:T(8,128)(2,1)S(1)} collective-permute-done((f16[128,1024]{1,0:T(8,128)(2,1)S(1)}, f16[128,1024]{1,0:T(8,128)(2,1)S(1)}, u32[]{:S(2)}, u32[]{:S(2)}) %collective-permute-start.2) | collective-permute-done | bytes 262176 | tf_op jit(solution)/shard_map/ppermute | solution.py:29
  35.4 1.4 %collective-permute-start.5 = (bf16[128,1024]{1,0:T(8,128)(2,1)S(1)}, bf16[128,1024]{1,0:T(8,128)(2,1)S(1)}, u32[]{:S(2)}, u32[]{:S(2)}) collective-permute-start(bf16[128,1024]{1,0:T(8,128)(2,1)S(1)} %multiply_convert_fusion.own), channel_id=1, source_target_pairs={{0,64},{1,65},{2,66},{3,67},{4,68},{5,69},{6,70},{7,71},{8,72},{9,... | collective-permute-start | bytes 786440 | tf_op jit(solution)/shard_map/ppermute | solution.py:29
  36.9 1.9 %collective-permute-start.6 = (bf16[128,1024]{1,0:T(8,128)(2,1)S(1)}, bf16[128,1024]{1,0:T(8,128)(2,1)S(1)}, u32[]{:S(2)}, u32[]{:S(2)}) collective-permute-start(bf16[128,1024]{1,0:T(8,128)(2,1)S(1)} %multiply_convert_fusion.own), channel_id=1, source_target_pairs={{0,192},{1,193},{2,194},{3,195},{4,196},{5,197},{6,198},{7,199},{8... | collective-permute-start | bytes 786440 | tf_op jit(solution)/shard_map/ppermute | solution.py:29
  38.8 5.9 %collective-permute-done.5.ya = bf16[128,1024]{1,0:T(8,128)(2,1)S(1)} collective-permute-done((bf16[128,1024]{1,0:T(8,128)(2,1)S(1)}, bf16[128,1024]{1,0:T(8,128)(2,1)S(1)}, u32[]{:S(2)}, u32[]{:S(2)}) %collective-permute-start.5) | collective-permute-done | bytes 262176 | tf_op jit(solution)/shard_map/ppermute | solution.py:29
  44.7 1.3 %collective-permute-start.7 = (bf16[256,1024]{1,0:T(8,128)(2,1)S(1)}, bf16[256,1024]{1,0:T(8,128)(2,1)S(1)}, u32[]{:S(2)}, u32[]{:S(2)}) collective-permute-start(bf16[256,1024]{1,0:T(8,128)(2,1)S(1)} %pad_maximum_fusion), channel_id=1, source_target_pairs={{0,16},{1,17},{2,18},{3,19},{4,20},{5,21},{6,22},{7,23},{8,24},{9,... | collective-permute-start | bytes 1572872 | tf_op jit(solution)/shard_map/ppermute | solution.py:29
  46.0 0.8 collective-permute-start
  46.9 10.5 %collective-permute-done = s32[4]{0:T(128)S(1)} collective-permute-done((s32[4]{0:T(128)S(1)}, s32[4]{0:T(128)S(1)}, u32[]{:S(2)}, u32[]{:S(2)}) %collective-permute-start) | collective-permute-done | bytes 48 | tf_op jit(solution)/shard_map/ppermute | solution.py:29
  57.5 1.2 collective-permute-start.4
  58.8 1.6 %collective-permute-start.8 = (bf16[64,1024]{1,0:T(8,128)(2,1)S(1)}, bf16[64,1024]{1,0:T(8,128)(2,1)S(1)}, u32[]{:S(2)}, u32[]{:S(2)}) collective-permute-start(bf16[64,1024]{1,0:T(8,128)(2,1)S(1)} %slice.64), channel_id=1, source_target_pairs={{0,64},{1,65},{2,66},{3,67},{4,68},{5,69},{6,70},{7,71},{8,72},{9,... | collective-permute-start | bytes 393224 | tf_op jit(solution)/shard_map/ppermute | solution.py:29
  60.4 1.8 %collective-permute-start.9 = (bf16[64,1024]{1,0:T(8,128)(2,1)S(1)}, bf16[64,1024]{1,0:T(8,128)(2,1)S(1)}, u32[]{:S(2)}, u32[]{:S(2)}) collective-permute-start(bf16[64,1024]{1,0:T(8,128)(2,1)S(1)} %slice.65), channel_id=1, source_target_pairs={{0,192},{1,193},{2,194},{3,195},{4,196},{5,197},{6,198},{7,199},{8... | collective-permute-start | bytes 393224 | tf_op jit(solution)/shard_map/ppermute | solution.py:29
  62.6 2.9 %collective-permute-start.11 = (bf16[64,1024]{1,0:T(8,128)(2,1)S(1)}, bf16[64,1024]{1,0:T(8,128)(2,1)S(1)}, u32[]{:S(2)}, u32[]{:S(2)}) collective-permute-start(bf16[64,1024]{1,0:T(8,128)(2,1)S(1)} %get-tuple-element.8), channel_id=1, source_target_pairs={{0,192},{1,193},{2,194},{3,195},{4,196},{5,197},{6,198},{7,199},{8... | collective-permute-start | bytes 393224 | tf_op jit(solution)/shard_map/ppermute | solution.py:29
  66.0 2.5 %collective-permute-done.10.w2a = bf16[64,1024]{1,0:T(8,128)(2,1)S(1)} collective-permute-done((bf16[64,1024]{1,0:T(8,128)(2,1)S(1)}, bf16[64,1024]{1,0:T(8,128)(2,1)S(1)}, u32[]{:S(2)}, u32[]{:S(2)}) %collective-permute-start.10) | collective-permute-done | bytes 131104 | tf_op jit(solution)/shard_map/ppermute | solution.py:29
  68.8 1.8 %collective-permute-start.12 = (bf16[128,1024]{1,0:T(8,128)(2,1)S(1)}, bf16[128,1024]{1,0:T(8,128)(2,1)S(1)}, u32[]{:S(2)}, u32[]{:S(2)}) collective-permute-start(bf16[128,1024]{1,0:T(8,128)(2,1)S(1)} %fusion.6), channel_id=1, source_target_pairs={{32,16},{48,0},{96,80},{112,64},{160,144},{176,128},{224,208},{240... | collective-permute-start | bytes 786440 | tf_op jit(solution)/shard_map/ppermute | solution.py:29
  70.6 10.1 %all-gather.2.cloned.1.call-done.cols = bf16[2304,1024]{1,0:T(8,128)(2,1)} async-done(((bf16[144,1024]{1,0:T(8,128)(2,1)}), bf16[2304,1024]{1,0:T(8,128)(2,1)}) %all-gather.2.cloned.1.call-update) | async-done | bytes 4718608 | tf_op jit(solution)/shard_map/all_gather | solution.py:192
  80.8 1.0 slice.70
  81.8 2.7 %collective-permute-start.13 = (bf16[144,1024]{1,0:T(8,128)(2,1)S(1)}, bf16[144,1024]{1,0:T(8,128)(2,1)S(1)}, u32[]{:S(2)}, u32[]{:S(2)}) collective-permute-start(bf16[144,1024]{1,0:T(8,128)(2,1)S(1)} %slice.70), channel_id=1, source_target_pairs={{32,16},{33,17},{34,18},{35,19},{36,20},{37,21},{38,22},{39,23},{4... | collective-permute-start | bytes 884744 | tf_op jit(solution)/shard_map/ppermute | solution.py:29
  84.4 14.7 %pairs.2.before = f32[8,1152]{1,0:T(8,128)S(1)} custom-call(s32[3]{0:T(128)S(1)} %pad_add_fusion.place, f32[8,1152]{1,0:T(8,128)S(1)} %broadcast_in_dim.31.bins, bf16[128,1024]{1,0:T(8,128)(2,1)S(1)} %multiply_convert_fusion.own, bf16[128,1024]{1,0:T(8,128)(2,1)S(1)} %collective-permute-done.4.x1, bf16[128,1024]{1,0:T(8,128)(2,1)S(1)} %collective-permute-done.5.ya, ...), custom_call_target="tpu_custom_call" | custom-call | flops 4831838208 | bytes 8388608 | tf_op jit(solution)/shard_map/pairs/pallas_call | solution.py:152
  99.2 1.6 %pairs.3 = f32[8,1152]{1,0:T(8,128)S(1)} custom-call(s32[3]{0:T(128)S(1)} %pad_add_fusion.place, f32[8,1152]{1,0:T(8,128)S(1)} %broadcast_select_fusion.bins, bf16[128,1024]{1,0:T(8,128)(2,1)S(1)} %multiply_convert_fusion.own, bf16[128,1024]{1,0:T(8,128)(2,1)S(1)} %collective-permute-done.4.x1, bf16[128,1024]{1,0:T(8,128)(2,1)S(1)} %collective-permute-done.5.ya, ...), custom_call_target="tpu_custom_call" | custom-call | flops 301989888 | bytes 8388608 | tf_op jit(solution)/shard_map/pairs/pallas_call | solution.py:152
  101.0 1.3 %collective-permute-start.15 = (f32[4,128]{1,0:T(4,128)S(1)}, f32[4,128]{1,0:T(4,128)S(1)}, u32[]{:S(2)}, u32[]{:S(2)}) collective-permute-start(f32[4,128]{1,0:T(4,128)S(1)} %slice.73), channel_id=1, source_target_pairs={{0,32},{64,96},{128,160},{192,224}} | collective-permute-start | bytes 6152 | tf_op jit(solution)/shard_map/ppermute | solution.py:29
  102.3 1.3 %collective-permute-start.16 = (f32[4,128]{1,0:T(4,128)S(1)}, f32[4,128]{1,0:T(4,128)S(1)}, u32[]{:S(2)}, u32[]{:S(2)}) collective-permute-start(f32[4,128]{1,0:T(4,128)S(1)} %slice.73), channel_id=1, source_target_pairs={{16,32},{80,96},{144,160},{208,224}} | collective-permute-start | bytes 6152 | tf_op jit(solution)/shard_map/ppermute | solution.py:29
  103.6 4.4 %collective-permute-done.15 = f32[4,128]{1,0:T(4,128)S(1)} collective-permute-done((f32[4,128]{1,0:T(4,128)S(1)}, f32[4,128]{1,0:T(4,128)S(1)}, u32[]{:S(2)}, u32[]{:S(2)}) %collective-permute-start.15) | collective-permute-done | bytes 2080 | tf_op jit(solution)/shard_map/ppermute | solution.py:29
  108.0 2.4 %collective-permute-start.17 = (f32[4,512]{1,0:T(4,128)S(1)}, f32[4,512]{1,0:T(4,128)S(1)}, u32[]{:S(2)}, u32[]{:S(2)}) collective-permute-start(f32[4,512]{1,0:T(4,128)S(1)} %fusion.9), channel_id=1, source_target_pairs={{0,128},{1,129},{2,130},{3,131},{4,132},{5,133},{6,134},{7,135},{8... | collective-permute-start | bytes 24584 | tf_op jit(solution)/shard_map/ppermute | solution.py:29
  110.9 2.7 %collective-permute-start.19 = (f32[4,512]{1,0:T(4,128)S(1)}, f32[4,512]{1,0:T(4,128)S(1)}, u32[]{:S(2)}, u32[]{:S(2)}) collective-permute-start(f32[4,512]{1,0:T(4,128)S(1)} %fusion.9), channel_id=1, source_target_pairs={{0,192},{1,193},{2,194},{3,195},{4,196},{5,197},{6,198},{7,199},{8... | collective-permute-start | bytes 24584 | tf_op jit(solution)/shard_map/ppermute | solution.py:29
  113.6 1.6 %collective-permute-done.18 = f32[4,512]{1,0:T(4,128)S(1)} collective-permute-done((f32[4,512]{1,0:T(4,128)S(1)}, f32[4,512]{1,0:T(4,128)S(1)}, u32[]{:S(2)}, u32[]{:S(2)}) %collective-permute-start.18) | collective-permute-done | bytes 8224 | tf_op jit(solution)/shard_map/ppermute | solution.py:29
  (51 shorter events, 5.6 us)
Async XLA Ops:
  6.5 3.6 %copy-start.2 = (s32[11,8]{0,1:T(8,128)S(1)}, s32[11,8]{0,1:T(8,128)}, u32[]{:S(2)}) copy-start(s32[11,8]{0,1:T(8,128)} %param.7) | copy-start | bytes 1060
  6.5 74.2 %all-gather.2.cloned.1.call-start = ((), (), s32[]{:S(2)}) async-start(), calls=%async_computation | async-start | bytes 5013504 | tf_op jit(solution)/shard_map/all_gather | solution.py:192
  10.2 1.5 %copy-start = (bf16[512,1584]{1,0:T(8,128)(2,1)S(1)}, bf16[512,1584]{1,0:T(8,128)(2,1)}, u32[]{:S(2)}) copy-start(bf16[512,1584]{1,0:T(8,128)(2,1)} %copy.7.showers) | copy-start | bytes 4866052
  11.7 1.9 %copy-start.1 = (bf16[1584,1024]{1,0:T(8,128)(2,1)S(1)}, bf16[1584,1024]{1,0:T(8,128)(2,1)}, u32[]{:S(2)}) copy-start(bf16[1584,1024]{1,0:T(8,128)(2,1)} %geometry.1) | copy-start | bytes 9732100
  17.7 7.3 %copy-start.3 = (s32[4]{0:T(128)S(1)}, s32[4]{0:T(128)}, u32[]{:S(2)}) copy-start(s32[4]{0:T(128)} %param.8) | copy-start | bytes 52
  17.7 7.3 %copy-start.4 = (s32[4]{0:T(128)S(1)}, s32[4]{0:T(128)}, u32[]{:S(2)}) copy-start(s32[4]{0:T(128)} %param.9) | copy-start | bytes 52
  18.5 11.0 %collective-permute-start.1 = (f16[128,1024]{1,0:T(8,128)(2,1)}, f16[128,1024]{1,0:T(8,128)(2,1)S(1)}, u32[]{:S(2)}, u32[]{:S(2)}) collective-permute-start(f16[128,1024]{1,0:T(8,128)(2,1)} %get-tuple-element.5), channel_id=1, source_target_pairs={{0,128},{1,129},{2,130},{3,131},{4,132},{5,133},{6,134},{7,135},{8... | collective-permute-start | bytes 786440 | tf_op jit(solution)/shard_map/ppermute | solution.py:29
  21.7 12.2 %collective-permute-start.2 = (f16[128,1024]{1,0:T(8,128)(2,1)S(1)}, f16[128,1024]{1,0:T(8,128)(2,1)S(1)}, u32[]{:S(2)}, u32[]{:S(2)}) collective-permute-start(f16[128,1024]{1,0:T(8,128)(2,1)S(1)} %get-tuple-element.7), channel_id=1, source_target_pairs={{0,64},{1,65},{2,66},{3,67},{4,68},{5,69},{6,70},{7,71},{8,72},{9,... | collective-permute-start | bytes 786440 | tf_op jit(solution)/shard_map/ppermute | solution.py:29
  22.4 11.9 %collective-permute-start.3 = (f16[128,1024]{1,0:T(8,128)(2,1)S(1)}, f16[128,1024]{1,0:T(8,128)(2,1)S(1)}, u32[]{:S(2)}, u32[]{:S(2)}) collective-permute-start(f16[128,1024]{1,0:T(8,128)(2,1)S(1)} %get-tuple-element.6), channel_id=1, source_target_pairs={{0,192},{1,193},{2,194},{3,195},{4,196},{5,197},{6,198},{7,199},{8... | collective-permute-start | bytes 786440 | tf_op jit(solution)/shard_map/ppermute | solution.py:29
  35.4 9.2 %collective-permute-start.5 = (bf16[128,1024]{1,0:T(8,128)(2,1)S(1)}, bf16[128,1024]{1,0:T(8,128)(2,1)S(1)}, u32[]{:S(2)}, u32[]{:S(2)}) collective-permute-start(bf16[128,1024]{1,0:T(8,128)(2,1)S(1)} %multiply_convert_fusion.own), channel_id=1, source_target_pairs={{0,64},{1,65},{2,66},{3,67},{4,68},{5,69},{6,70},{7,71},{8,72},{9,... | collective-permute-start | bytes 786440 | tf_op jit(solution)/shard_map/ppermute | solution.py:29
  36.9 7.8 %collective-permute-start.6 = (bf16[128,1024]{1,0:T(8,128)(2,1)S(1)}, bf16[128,1024]{1,0:T(8,128)(2,1)S(1)}, u32[]{:S(2)}, u32[]{:S(2)}) collective-permute-start(bf16[128,1024]{1,0:T(8,128)(2,1)S(1)} %multiply_convert_fusion.own), channel_id=1, source_target_pairs={{0,192},{1,193},{2,194},{3,195},{4,196},{5,197},{6,198},{7,199},{8... | collective-permute-start | bytes 786440 | tf_op jit(solution)/shard_map/ppermute | solution.py:29
  44.7 17.5 %collective-permute-start.7 = (bf16[256,1024]{1,0:T(8,128)(2,1)S(1)}, bf16[256,1024]{1,0:T(8,128)(2,1)S(1)}, u32[]{:S(2)}, u32[]{:S(2)}) collective-permute-start(bf16[256,1024]{1,0:T(8,128)(2,1)S(1)} %pad_maximum_fusion), channel_id=1, source_target_pairs={{0,16},{1,17},{2,18},{3,19},{4,20},{5,21},{6,22},{7,23},{8,24},{9,... | collective-permute-start | bytes 1572872 | tf_op jit(solution)/shard_map/ppermute | solution.py:29
  46.0 11.5 %collective-permute-start = (s32[4]{0:T(128)S(1)}, s32[4]{0:T(128)S(1)}, u32[]{:S(2)}, u32[]{:S(2)}) collective-permute-start(s32[4]{0:T(128)S(1)} %copy-done.3), channel_id=1, source_target_pairs={{0,16},{1,17},{2,18},{3,19},{4,20},{5,21},{6,22},{7,23},{8,24},{9,... | collective-permute-start | bytes 56 | tf_op jit(solution)/shard_map/ppermute | solution.py:29
  57.5 8.1 %collective-permute-start.4 = (bf16[128,1024]{1,0:T(8,128)(2,1)S(1)}, bf16[128,1024]{1,0:T(8,128)(2,1)S(1)}, u32[]{:S(2)}, u32[]{:S(2)}) collective-permute-start(bf16[128,1024]{1,0:T(8,128)(2,1)S(1)} %multiply_convert_fusion.own), channel_id=1, source_target_pairs={{0,16},{1,17},{2,18},{3,19},{4,20},{5,21},{6,22},{7,23},{8,24},{9,... | collective-permute-start | bytes 786440 | tf_op jit(solution)/shard_map/ppermute | solution.py:29
  58.8 7.2 %collective-permute-start.8 = (bf16[64,1024]{1,0:T(8,128)(2,1)S(1)}, bf16[64,1024]{1,0:T(8,128)(2,1)S(1)}, u32[]{:S(2)}, u32[]{:S(2)}) collective-permute-start(bf16[64,1024]{1,0:T(8,128)(2,1)S(1)} %slice.64), channel_id=1, source_target_pairs={{0,64},{1,65},{2,66},{3,67},{4,68},{5,69},{6,70},{7,71},{8,72},{9,... | collective-permute-start | bytes 393224 | tf_op jit(solution)/shard_map/ppermute | solution.py:29
  60.4 5.6 %collective-permute-start.9 = (bf16[64,1024]{1,0:T(8,128)(2,1)S(1)}, bf16[64,1024]{1,0:T(8,128)(2,1)S(1)}, u32[]{:S(2)}, u32[]{:S(2)}) collective-permute-start(bf16[64,1024]{1,0:T(8,128)(2,1)S(1)} %slice.65), channel_id=1, source_target_pairs={{0,192},{1,193},{2,194},{3,195},{4,196},{5,197},{6,198},{7,199},{8... | collective-permute-start | bytes 393224 | tf_op jit(solution)/shard_map/ppermute | solution.py:29
  62.2 6.3 %collective-permute-start.10 = (bf16[64,1024]{1,0:T(8,128)(2,1)S(1)}, bf16[64,1024]{1,0:T(8,128)(2,1)S(1)}, u32[]{:S(2)}, u32[]{:S(2)}) collective-permute-start(bf16[64,1024]{1,0:T(8,128)(2,1)S(1)} %get-tuple-element.9), channel_id=1, source_target_pairs={{0,64},{1,65},{2,66},{3,67},{4,68},{5,69},{6,70},{7,71},{8,72},{9,... | collective-permute-start | bytes 393224 | tf_op jit(solution)/shard_map/ppermute | solution.py:29
  62.6 5.9 %collective-permute-start.11 = (bf16[64,1024]{1,0:T(8,128)(2,1)S(1)}, bf16[64,1024]{1,0:T(8,128)(2,1)S(1)}, u32[]{:S(2)}, u32[]{:S(2)}) collective-permute-start(bf16[64,1024]{1,0:T(8,128)(2,1)S(1)} %get-tuple-element.8), channel_id=1, source_target_pairs={{0,192},{1,193},{2,194},{3,195},{4,196},{5,197},{6,198},{7,199},{8... | collective-permute-start | bytes 393224 | tf_op jit(solution)/shard_map/ppermute | solution.py:29
  68.8 15.6 %collective-permute-start.12 = (bf16[128,1024]{1,0:T(8,128)(2,1)S(1)}, bf16[128,1024]{1,0:T(8,128)(2,1)S(1)}, u32[]{:S(2)}, u32[]{:S(2)}) collective-permute-start(bf16[128,1024]{1,0:T(8,128)(2,1)S(1)} %fusion.6), channel_id=1, source_target_pairs={{32,16},{48,0},{96,80},{112,64},{160,144},{176,128},{224,208},{240... | collective-permute-start | bytes 786440 | tf_op jit(solution)/shard_map/ppermute | solution.py:29
  81.8 17.4 %collective-permute-start.13 = (bf16[144,1024]{1,0:T(8,128)(2,1)S(1)}, bf16[144,1024]{1,0:T(8,128)(2,1)S(1)}, u32[]{:S(2)}, u32[]{:S(2)}) collective-permute-start(bf16[144,1024]{1,0:T(8,128)(2,1)S(1)} %slice.70), channel_id=1, source_target_pairs={{32,16},{33,17},{34,18},{35,19},{36,20},{37,21},{38,22},{39,23},{4... | collective-permute-start | bytes 884744 | tf_op jit(solution)/shard_map/ppermute | solution.py:29
  100.9 7.1 %collective-permute-start.14 = (f32[4,512]{1,0:T(4,128)S(1)}, f32[4,512]{1,0:T(4,128)S(1)}, u32[]{:S(2)}, u32[]{:S(2)}) collective-permute-start(f32[4,512]{1,0:T(4,128)S(1)} %slice.72), channel_id=1, source_target_pairs={{0,16},{1,17},{2,18},{3,19},{4,20},{5,21},{6,22},{7,23},{8,24},{9,... | collective-permute-start | bytes 24584 | tf_op jit(solution)/shard_map/ppermute | solution.py:29
  101.0 7.0 %collective-permute-start.15 = (f32[4,128]{1,0:T(4,128)S(1)}, f32[4,128]{1,0:T(4,128)S(1)}, u32[]{:S(2)}, u32[]{:S(2)}) collective-permute-start(f32[4,128]{1,0:T(4,128)S(1)} %slice.73), channel_id=1, source_target_pairs={{0,32},{64,96},{128,160},{192,224}} | collective-permute-start | bytes 6152 | tf_op jit(solution)/shard_map/ppermute | solution.py:29
  102.3 5.7 %collective-permute-start.16 = (f32[4,128]{1,0:T(4,128)S(1)}, f32[4,128]{1,0:T(4,128)S(1)}, u32[]{:S(2)}, u32[]{:S(2)}) collective-permute-start(f32[4,128]{1,0:T(4,128)S(1)} %slice.73), channel_id=1, source_target_pairs={{16,32},{80,96},{144,160},{208,224}} | collective-permute-start | bytes 6152 | tf_op jit(solution)/shard_map/ppermute | solution.py:29
  108.0 5.6 %collective-permute-start.17 = (f32[4,512]{1,0:T(4,128)S(1)}, f32[4,512]{1,0:T(4,128)S(1)}, u32[]{:S(2)}, u32[]{:S(2)}) collective-permute-start(f32[4,512]{1,0:T(4,128)S(1)} %fusion.9), channel_id=1, source_target_pairs={{0,128},{1,129},{2,130},{3,131},{4,132},{5,133},{6,134},{7,135},{8... | collective-permute-start | bytes 24584 | tf_op jit(solution)/shard_map/ppermute | solution.py:29
  110.4 4.9 %collective-permute-start.18 = (f32[4,512]{1,0:T(4,128)S(1)}, f32[4,512]{1,0:T(4,128)S(1)}, u32[]{:S(2)}, u32[]{:S(2)}) collective-permute-start(f32[4,512]{1,0:T(4,128)S(1)} %fusion.9), channel_id=1, source_target_pairs={{0,64},{1,65},{2,66},{3,67},{4,68},{5,69},{6,70},{7,71},{8,72},{9,... | collective-permute-start | bytes 24584 | tf_op jit(solution)/shard_map/ppermute | solution.py:29
  110.9 4.3 %collective-permute-start.19 = (f32[4,512]{1,0:T(4,128)S(1)}, f32[4,512]{1,0:T(4,128)S(1)}, u32[]{:S(2)}, u32[]{:S(2)}) collective-permute-start(f32[4,512]{1,0:T(4,128)S(1)} %fusion.9), channel_id=1, source_target_pairs={{0,192},{1,193},{2,194},{3,195},{4,196},{5,197},{6,198},{7,199},{8... | collective-permute-start | bytes 24584 | tf_op jit(solution)/shard_map/ppermute | solution.py:29
Sparse Core Ops, SparseCore 0:
  35.6 45.1 all-gather.1

commit v2 on v0

v2 whole, which is shorter than its diff:
```python
import functools

import jax
import jax.numpy as jnp
from jax import lax
from jax.experimental import pallas as pl
from jax.experimental.pallas import tpu as pltpu
from jax.sharding import PartitionSpec as P

BLOCK = 128
PIECE = 32
TAG = 16
BINS = 8
CHUNK = 512
AXES = ("layer", "shower")
NY, NX, NZ, NC = 4, 4, 8, 2


def flat(y, x, z, c):
    return y * (NX * NZ * NC) + (x * NZ + z) * NC + c


def permute(value, move, keep=lambda y, x, z, c: True):
    pairs = [
        (flat(y, x, z, c), flat(*move(y, x, z, c)))
        for y in range(NY)
        for x in range(NX)
        for z in range(NZ)
        for c in range(NC)
        if keep(y, x, z, c)
    ]
    return lax.ppermute(value, AXES, pairs)


def along_y(step):
    return lambda y, x, z, c: ((y + step) % NY, x, z, c)


def along_z(step):
    return lambda y, x, z, c: (y, x, (z + step) % NZ, c)


def flip_z(bit):
    return lambda y, x, z, c: (y, x, z ^ bit, c)


def swap_x(y, x, z, c):
    return (y, x ^ 1, z, c)


def swap_core(y, x, z, c):
    return (y, x, z, 1 - c)


def same_core(y, x, z, c):
    return (y, x, (z + 1 - 2 * c) % NZ, c)


def cross_core(y, x, z, c):
    return (y, x, (z - 1 + 2 * c) % NZ, 1 - c)


def raw_kernel(pattern, showers, geometry, out, masked):
    step = pl.program_id(0)
    layers = pattern.shape[1]
    cells = geometry.shape[0] // layers
    per = geometry.shape[1] // BLOCK
    for layer in range(layers):
        for part in range(per):
            rows = pl.ds(layer * cells, cells)
            cols = pl.ds(part * BLOCK, BLOCK)
            on = pattern[step * per + part, layer].astype(jnp.float32).astype(jnp.bfloat16)
            masked[rows, cols] = geometry[rows, cols] * on
    out[...] = lax.dot_general(
        showers[...], masked[...], (((0,), (0,)), ((), ())), preferred_element_type=jnp.float32
    )


def raw_partial(showers, geometry, pattern):
    rows, depth = showers.shape
    feats = geometry.shape[1]
    width = 512
    return pl.pallas_call(
        raw_kernel,
        grid=(feats // width,),
        in_specs=[
            pl.BlockSpec(memory_space=pltpu.SMEM),
            pl.BlockSpec((depth, rows), lambda i: (0, 0)),
            pl.BlockSpec((depth, width), lambda i: (0, i)),
        ],
        out_specs=pl.BlockSpec((rows, width), lambda i: (0, i)),
        out_shape=jax.ShapeDtypeStruct((rows, feats), jnp.float32),
        scratch_shapes=[pltpu.VMEM((depth, width), jnp.bfloat16)],
        compiler_params=pltpu.CompilerParams(vmem_limit_bytes=60 * 2**20),
        cost_estimate=pl.CostEstimate(
            flops=2 * rows * depth * feats, bytes_accessed=8 * 2**20, transcendentals=0
        ),
        name="raw",
    )(pattern.T, showers.T, geometry)


def pair_kernel(*refs, row_sizes, col_sizes, diag, apart):
    n_rows, n_cols = len(row_sizes), len(col_sizes)
    col_bin, col_source, row_bins, before = refs[:4]
    rows = refs[4 : 4 + n_rows]
    cols = refs[4 + n_rows : 4 + n_rows + n_cols]
    out, rows_at, cols_at, row_sems, col_sems = refs[4 + n_rows + n_cols :]

    def copies(sources, sizes, target, sems):
        made, start = [], 0
        for at, (source, size) in enumerate(zip(sources, sizes)):
            copy = pltpu.make_async_copy(
                source.at[pl.ds(0, size), :], target.at[pl.ds(start, size), :], sems.at[at]
            )
            copy.start()
            made.append((copy, start))
            start += size
        return made, start

    col_copies, depth = copies(cols, col_sizes, cols_at, col_sems)
    row_copies, total = copies(rows, row_sizes, rows_at, row_sems)
    for copy, _ in col_copies:
        copy.wait()
    waited = 0
    for start in range(0, total, CHUNK):
        size = min(CHUNK, total - start)
        while waited < n_rows and row_copies[waited][1] < start + size:
            row_copies[waited][0].wait()
            waited += 1
        products = lax.dot_general(
            cols_at[...],
            rows_at[pl.ds(start, size), :],
            (((1,), (1,)), ((), ())),
            preferred_element_type=jnp.float32,
        )
        shifted = products + 32.0
        cubes = shifted * shifted * shifted
        lanes = pl.ds(start, size)
        bins = row_bins[0:1, lanes]
        one = jnp.zeros((8, size), jnp.float32)
        zero = jnp.zeros((8, size), jnp.float32)
        for group in range(depth // PIECE):
            if start >= 16 * BLOCK and group == apart:
                continue
            block = cubes[group * PIECE : (group + 1) * PIECE]
            if diag and start == 0 and group < BLOCK // PIECE:
                lane = lax.broadcasted_iota(jnp.int32, block.shape, 1)
                sub = lax.broadcasted_iota(jnp.int32, block.shape, 0)
                block = jnp.where(lane == sub + group * PIECE, 0.0, block)
            part = block[0:8] + block[8:16] + (block[16:24] + block[24:32])
            match = (bins == col_bin[group]).astype(jnp.float32)
            source = col_source[group]
            one += (match * source) * part
            zero += (match * (1.0 - source)) * part
        out[0:1, lanes] = before[0:1, lanes] + jnp.sum(one, axis=0, keepdims=True)
        out[1:2, lanes] = before[1:2, lanes] + jnp.sum(zero, axis=0, keepdims=True)


def pair_sums(rows, cols, codes, row_bins, before, diag, name, apart=-1):
    row_sizes = tuple(size for _, size in rows)
    col_sizes = tuple(size for _, size in cols)
    total, depth = sum(row_sizes), sum(col_sizes)
    feats = rows[0][0].shape[1]
    col_source = (codes >= BINS).astype(jnp.float32)
    col_bin = codes.astype(jnp.float32) - BINS * col_source
    vmem = pl.BlockSpec(memory_space=pltpu.VMEM)
    smem = pl.BlockSpec(memory_space=pltpu.SMEM)
    hbm = pl.BlockSpec(memory_space=pl.ANY)
    return pl.pallas_call(
        functools.partial(
            pair_kernel, row_sizes=row_sizes, col_sizes=col_sizes, diag=diag, apart=apart
        ),
        in_specs=[smem, smem, vmem, vmem] + [hbm] * (len(rows) + len(cols)),
        out_specs=vmem,
        out_shape=jax.ShapeDtypeStruct((2, total), jnp.float32),
        scratch_shapes=[
            pltpu.VMEM((total, feats), jnp.bfloat16),
            pltpu.VMEM((depth, feats), jnp.bfloat16),
            pltpu.SemaphoreType.DMA((len(rows),)),
            pltpu.SemaphoreType.DMA((len(cols),)),
        ],
        compiler_params=pltpu.CompilerParams(vmem_limit_bytes=58 * 2**20),
        cost_estimate=pl.CostEstimate(
            flops=2 * total * depth * feats,
            bytes_accessed=2 * (total + depth) * feats,
            transcendentals=0,
        ),
        name=name,
    )(col_bin, col_source, row_bins, before, *[r for r, _ in rows], *[c for c, _ in cols])


def line_codes(codes, z, c):
    other = permute(codes, swap_core)
    chip = jnp.where(c == 0, jnp.stack([codes, other]), jnp.stack([other, codes]))
    line = chip[None]
    for bit in (1, 2, 4):
        other = permute(line, flip_z(bit))
        low = (z & bit) == 0
        line = jnp.where(
            low, jnp.concatenate([line, other]), jnp.concatenate([other, line])
        )
    return line, chip


def shards(showers, geometry, pattern, bins, sources):
    y = lax.axis_index("layer")
    s = lax.axis_index("shower")
    x, z, c = s // (NZ * NC), (s // NC) % NZ, s % NC
    feats = geometry.shape[1]
    blocks = bins.shape[0]

    codes = bins + BINS * sources
    line, chip = line_codes(codes, z, c)
    chip_x = permute(chip, swap_x)

    partial_sums = raw_partial(showers, geometry, pattern).reshape(blocks, NY, PIECE, feats)

    def share(turn):
        part = lax.dynamic_index_in_dim(partial_sums, (y + turn) % NY, 1, keepdims=False)
        return part.reshape(BLOCK, feats)

    raw = share(0)
    arrived = [permute(share(turn).astype(jnp.float16), along_y(turn)) for turn in (2, 1, 3)]
    for part in arrived:
        raw = raw + part.astype(jnp.float32)
    scale = lax.rsqrt(jnp.mean(raw * raw, axis=1, keepdims=True) + 1e-05)
    own = (raw * scale).astype(jnp.bfloat16)
    own, line, chip_x = lax.optimization_barrier((own, line, chip_x))

    same, cross = [], []
    for turn in range(4):
        same.append(permute(same[-1] if same else own, same_core))
        if turn < 3:
            cross.append(permute(cross[-1], same_core) if cross else permute(own, cross_core))
        if turn == 0:
            x1 = permute(own, swap_x)
            ya = permute(own, along_y(1))
            yb = permute(own, along_y(3))

    half = BLOCK // 2
    xx = permute(jnp.concatenate([ya, yb], axis=0), swap_x)
    y2a = permute(ya[:half], along_y(1))
    y2b = permute(yb[half:], along_y(3))
    near = permute(jnp.concatenate([own, x1, ya, yb], axis=0), swap_core)
    w2a = permute(xx[:half], along_y(1))
    w2b = permute(xx[BLOCK + half :], along_y(3))
    far = permute(jnp.concatenate([xx, y2a, y2b, w2a, w2b], axis=0), swap_core)

    first_code = jnp.full((TAG, feats), codes[0] + 1, jnp.int32).astype(jnp.bfloat16)
    piece = permute(
        jnp.concatenate([own[:PIECE], first_code], axis=0),
        lambda y, x, z, c: (y, 1, z, c),
        keep=lambda y, x, z, c: x == 2 and z == 0 and c == 0,
    )
    for jump in (4, 2, 1):
        piece = piece + permute(
            piece,
            along_z(jump),
            keep=lambda y, x, z, c, jump=jump: x == 1 and c == 0 and z % (2 * jump) == 0,
        )
    heads = [own[:PIECE], yb[:PIECE], y2a[:PIECE], ya[:PIECE]]
    odd = lax.dynamic_slice_in_dim(
        jnp.concatenate(heads + heads, axis=0), (NY - y) % NY * PIECE, BLOCK, 0
    )
    at_start = lambda y, x, z, c: z == 0 and c == 0
    odd = permute(
        odd, lambda y, x, z, c: (y, 1, z, c), keep=lambda *a: a[1] == 2 and at_start(*a)
    )
    odd = odd + permute(odd, swap_x, keep=lambda *a: a[1] == 1 and at_start(*a))
    odd = odd + permute(odd, swap_core, keep=lambda *a: a[1] < 2 and at_start(*a))

    lines = jnp.concatenate([line, line], axis=0)
    run = lax.dynamic_slice_in_dim(lines, jnp.where(c == 0, z + 4, z + 1), 4, 0)
    run = jnp.where(c == 0, run[::-1], run)
    same_codes = jnp.where(c == 0, run[:, 0], run[:, 1])
    cross_codes = jnp.where(c == 0, run[:, 1], run[:, 0])
    piece_code = piece[PIECE, :1].astype(jnp.int32) - 1
    early_codes = jnp.concatenate(
        [codes, same_codes[0], cross_codes[0], same_codes[1], cross_codes[1]]
    )
    late_codes = jnp.concatenate([same_codes[2], cross_codes[2], piece_code])
    last_codes = same_codes[3]
    all_codes = jnp.concatenate([early_codes, late_codes, last_codes])

    chip_bins = jnp.where(chip >= BINS, chip - BINS, chip)
    chip_x_bins = jnp.where(chip_x >= BINS, chip_x - BINS, chip_x)
    pick = lambda both, core: jnp.repeat(jnp.where(core == 0, both[0], both[1]), PIECE)
    mine, mine_x = pick(chip_bins, c), pick(chip_x_bins, c)
    theirs, theirs_x = pick(chip_bins, 1 - c), pick(chip_x_bins, 1 - c)
    odd_bin = jnp.where((x < 2) & (z == 0), bins[:1], -2)
    row_bins = jnp.concatenate(
        [mine, mine_x, mine, mine]
        + [theirs, theirs_x, theirs, theirs]
        + [mine_x, mine_x, mine, mine_x]
        + [theirs_x, theirs_x, theirs, theirs_x]
        + [jnp.repeat(odd_bin, BLOCK)]
    ).astype(jnp.float32)
    code_source = (all_codes >= BINS).astype(jnp.float32)
    code_bin = all_codes.astype(jnp.float32) - BINS * code_source
    no_odd = jnp.where(jnp.arange(all_codes.shape[0]) == early_codes.shape[0] + 8, 0.0, 1.0)
    match = (code_bin[:, None] == row_bins[None, :]).astype(jnp.float32)
    match = jnp.where(jnp.arange(row_bins.shape[0])[None, :] >= 16 * BLOCK, match * no_odd[:, None], match)
    counts = jnp.stack(
        [jnp.sum(match * code_source[:, None], 0), jnp.sum(match * (1 - code_source[:, None]), 0)]
    )

    row_bins = row_bins[None, :]
    near_rows = [(own, BLOCK), (x1, BLOCK), (ya, BLOCK), (yb, BLOCK), (near, 4 * BLOCK)]
    far_rows = [(xx, 2 * BLOCK), (y2a, half), (y2b, half), (w2a, half), (w2b, half)]
    far_rows = far_rows + [(far, 4 * BLOCK)]
    odd_rows = [(odd, BLOCK)]
    size = lambda rows: sum(n for _, n in rows)
    blank = lambda rows: jnp.zeros((2, size(rows)), jnp.float32)
    early = [(own, BLOCK), (same[0], BLOCK), (cross[0], BLOCK), (same[1], BLOCK), (cross[1], BLOCK)]
    late = [(same[2], BLOCK), (cross[2], BLOCK), (piece, PIECE)]
    last = [(same[3], BLOCK)]
    first = size(near_rows)
    sums_near = pair_sums(
        near_rows, early, early_codes, row_bins[:, :first], blank(near_rows), True, "near"
    )
    far_odd = far_rows + odd_rows
    sums_far = pair_sums(
        far_odd, early, early_codes, row_bins[:, first:], blank(far_odd), False, "far"
    )
    sums = jnp.concatenate([sums_near, sums_far], axis=1)
    every = near_rows + far_odd
    apart = 2 * BLOCK // PIECE
    sums = pair_sums(every, late, late_codes, row_bins, sums, False, "late", apart)
    sums = pair_sums(every, last, last_codes, row_bins, sums, False, "last")

    stats = jnp.concatenate([sums, counts], axis=0).reshape(4, 17, BLOCK)
    core_mine = jnp.concatenate([stats[:, 0:4], stats[:, 8:12]], axis=1)
    core_theirs = jnp.concatenate([stats[:, 4:8], stats[:, 12:16]], axis=1)
    core_mine = core_mine + permute(core_theirs, swap_core)
    to_x = jnp.stack([core_mine[:, i] for i in (1, 4, 5, 7)], axis=1)
    keep = jnp.stack([core_mine[:, i] for i in (0, 2, 3, 6)], axis=1)
    keep = keep + permute(to_x, swap_x)
    odd_stats = stats[:, 16]
    odd_total = jnp.zeros_like(odd_stats)
    for core in (0, 1):
        for start in (0, 1):
            odd_total = odd_total + permute(
                odd_stats,
                lambda y, x, z, c: (y, 2, z, 0),
                keep=lambda y, x, z, c, k=(core, start): (c, x) == k and z == 0,
            )
    turned = jnp.stack([keep[:, 0], keep[:, 2], keep[:, 3], keep[:, 1]], axis=1)
    turned = jnp.concatenate([turned, turned], axis=1)
    ordered = lax.dynamic_slice_in_dim(turned, (NY - y) % NY, NY, 1)
    ordered = ordered.reshape(4, NY, blocks, PIECE)
    ordered = ordered.at[:, :, 0].add(odd_total.reshape(4, NY, PIECE))
    total = ordered
    for turn in (2, 1, 3):
        total = total + permute(ordered, along_y(turn))
    weight = 1.0 / (BLOCK * 32.0**3)
    proof = (total[0] / total[2] - total[1] / total[3]) * weight * (BLOCK // PIECE)
    return jnp.transpose(proof, (1, 0, 2)).reshape(-1)


def solution(mesh):
    placed = (P("shower", "layer"), P("layer", None), P("layer", None), P("shower"), P("shower"))
    return jax.shard_map(shards, mesh=mesh, in_specs=placed, out_specs=P("shower"), check_vma=False)
```

time: 238 us -> 174 us (0.73)
  waiting for transfers between devices: 150 us -> 29 us
  starting transfers between devices: 0.04 us -> 55.6 us
  local copies, waits for them, and re-layouts: 8.35 us -> 40.9 us
  blocking collectives: 30.2 us -> 0 us
  Pallas kernels: 0 us -> 29.5 us
  matrix products: 25.5 us -> 0 us
  between operations: 14.1 us -> 1.67 us
  other arithmetic: 7.97 us -> 13.8 us
    all_gather x1 -> x0, waiting for transfers between devices: 83.4 us -> none  [shards(): piece = lax.all_gather(quarter, 'shower', axis=0, tiled=True)]
    psum x1 -> x0, waiting for transfers between devices: 66.8 us -> none  [shards(): summed = lax.psum(partial_sums, 'layer')]
    ppermute x0 -> x41, starting transfers between devices: none -> 55.6 us  [permute(): return lax.ppermute(value, AXES, pairs)]
    pallas_call x0 -> x5, Pallas kernels: none -> 29.5 us  [the longest x4 24 us: pair_sums(): pl.pallas_call(functools.partial(pair_kernel, row_sizes=row_sizes, col_si...]
    ppermute x0 -> x41, waiting for transfers between devices: none -> 29 us  [permute(): return lax.ppermute(value, AXES, pairs)]
    unnamed x18 -> x99, local copies, waits for them, and re-layouts: 2.67 us -> 30.3 us
    dot_general x5 -> x0, matrix products: 25.5 us -> none  [the longest x4 22.1 us: tile_sums(): lax.dot_general(own_feats, columns, (((1,), (1,)), ((), ())), preferred_e...]
    unnamed x1 -> x0, blocking collectives: 19.2 us -> none
  transfers between devices with their start and end apart: 2 -> 41, of which waited for: 2 -> 14; matrix products, arithmetic and copies ran while one was open for 1% -> 29% of each run, Pallas kernels for 0% -> 10%
where the time goes in v2:
time: 174 us; the launch traced here: 170 us
  starting transfers between devices  55.6 us (32%)
  local copies, waits for them, and re-layouts  40.9 us (24%)
  Pallas kernels  29.5 us (17%)
  waiting for transfers between devices  29 us (17%)
  other arithmetic  13.8 us (8%)
    ppermute x41, starting transfers between devices, permute(): return lax.ppermute(value, AXES, pairs)  55.6 us
    unnamed x99, local copies, waits for them, and re-layouts  30.3 us
    ppermute x41, waiting for transfers between devices, permute(): return lax.ppermute(value, AXES, pairs)  29 us
    pallas_call x4, Pallas kernels, pair_sums(): pl.pallas_call(functools.partial(pair_kernel, row_sizes=row_sizes, col_si...  24 us
    pallas_call x1, Pallas kernels, raw_partial(): pl.pallas_call(raw_kernel, grid=(feats // width,), in_specs=[pl.BlockSpec...  5.5 us
  transfers between devices with their start and end apart: 41, of which 14 were waited for; matrix products, arithmetic and copies ran while one was open for 29% of the time, Pallas kernels for 10%

profile of v2, /device:TPU:4, one launch (start us, length us, event | category | flops | bytes accessed | tf_op | source)
XLA Modules:
  0.0 170.4 jit_solution(583375104189511613)
XLA Ops:
  0.0 5.5 %raw.1 = f32[512,1024]{1,0:T(8,128)} custom-call(s32[8,11]{1,0:T(8,128)} %bitcast.75, bf16[1584,512]{1,0:T(8,128)(2,1)} %bitcast.56, bf16[1584,1024]{1,0:T(8,128)(2,1)} %geometry.1), custom_call_target="tpu_custom_call" | custom-call | flops 1660944384 | bytes 8388608 | tf_op jit(solution)/shard_map/raw/pallas_call | solution.py:83
  5.5 1.7 %constant_dynamic-slice_fusion.2 = (f32[4,1,32,1024]{3,2,1,0:T(8,128)S(1)}, f16[4,1,32,1024]{3,2,0,1:T(8,128)(2,1)S(1)}, f16[4,1,32,1024]{3,2,0,1:T(8,128)(2,1)S(1)}, f16[4,1,32,1024]{3,2,0,1:T(8,128)(2,1)S(1)}) fusion(f32[4,4,32,1024]{3,2,1,0:T(8,128)} %bitcast.55, s32[]{:T(128)S(6)} %select_n.195, s32[]{:T(128)S(6)} %select_n.199, s32[]{:T(128)S(6)} %select_n.197, ...), kind=kLoop, calls=%fused_computation.110 | loop fusion | flops 393216 | bytes 3407888 | tf_op jit(solution)/shard_map/jit(dynamic_index_in_dim)/dynamic_slice | solution.py:219
  7.3 3.3 %collective-permute-start = (f16[128,1024]{1,0:T(8,128)(2,1)S(1)}, f16[128,1024]{1,0:T(8,128)(2,1)S(1)}, u32[]{:S(2)}, u32[]{:S(2)}) collective-permute-start(f16[128,1024]{1,0:T(8,128)(2,1)S(1)} %bitcast.59), channel_id=1, source_target_pairs={{0,128},{1,129},{2,130},{3,131},{4,132},{5,133},{6,134},{7,135},{8... | collective-permute-start | bytes 786440 | tf_op jit(solution)/shard_map/ppermute | solution.py:32
  11.2 2.6 %collective-permute-start.2 = (f16[128,1024]{1,0:T(8,128)(2,1)S(1)}, f16[128,1024]{1,0:T(8,128)(2,1)S(1)}, u32[]{:S(2)}, u32[]{:S(2)}) collective-permute-start(f16[128,1024]{1,0:T(8,128)(2,1)S(1)} %bitcast.57), channel_id=1, source_target_pairs={{0,192},{1,193},{2,194},{3,195},{4,196},{5,197},{6,198},{7,199},{8... | collective-permute-start | bytes 786440 | tf_op jit(solution)/shard_map/ppermute | solution.py:32
  15.3 2.0 %collective-permute-start.4 = (s32[1,2,4]{2,1,0:T(2,128)S(1)}, s32[1,2,4]{2,1,0:T(2,128)S(1)}, u32[]{:S(2)}, u32[]{:S(2)}) collective-permute-start(s32[1,2,4]{2,1,0:T(2,128)S(1)} %add_select_fusion.3), channel_id=1, source_target_pairs={{0,2},{1,3},{2,0},{3,1},{4,6},{5,7},{6,4},{7,5},{8,10},{9,11},{10,... | collective-permute-start | bytes 104 | tf_op jit(solution)/shard_map/ppermute | solution.py:32
  18.9 3.3 %collective-permute-start.5 = (s32[2,2,4]{2,1,0:T(2,128)S(1)}, s32[2,2,4]{2,1,0:T(2,128)S(1)}, u32[]{:S(2)}, u32[]{:S(2)}) collective-permute-start(s32[2,2,4]{2,1,0:T(2,128)S(1)} %add_select_fusion.2), channel_id=1, source_target_pairs={{0,4},{1,5},{2,6},{3,7},{4,0},{5,1},{6,2},{7,3},{8,12},{9,13},{10,... | collective-permute-start | bytes 200 | tf_op jit(solution)/shard_map/ppermute | solution.py:32
  22.3 1.5 collective-permute-done.5
  23.8 6.8 %collective-permute-start.6 = (s32[4,2,4]{2,1,0:T(2,128)S(1)}, s32[4,2,4]{2,1,0:T(2,128)S(1)}, u32[]{:S(2)}, u32[]{:S(2)}) collective-permute-start(s32[4,2,4]{2,1,0:T(2,128)S(1)} %add_select_fusion.1), channel_id=1, source_target_pairs={{0,8},{1,9},{2,10},{3,11},{4,12},{5,13},{6,14},{7,15},{8,0},{9,1},... | collective-permute-start | bytes 392 | tf_op jit(solution)/shard_map/ppermute | solution.py:32
  32.6 1.6 collective-permute-done.7
  35.4 3.2 %collective-permute-start.14 = (bf16[128,1024]{1,0:T(8,128)(2,1)S(1)}, bf16[128,1024]{1,0:T(8,128)(2,1)S(1)}, u32[]{:S(2)}, u32[]{:S(2)}) collective-permute-start(bf16[128,1024]{1,0:T(8,128)(2,1)S(1)} %multiply_convert_fusion.refs_4_.refs_9_.refs_11_), channel_id=1, source_target_pairs={{0,192},{1,193},{2,194},{3,195},{4,196},{5,197},{6,198},{7,199},{8... | collective-permute-start | bytes 786440 | tf_op jit(solution)/shard_map/ppermute | solution.py:32
  44.6 1.8 %collective-permute-start.8 = (bf16[48,1024]{1,0:T(8,128)(2,1)S(1)}, bf16[48,1024]{1,0:T(8,128)(2,1)S(1)}, u32[]{:S(2)}, u32[]{:S(2)}) collective-permute-start(bf16[48,1024]{1,0:T(8,128)(2,1)S(1)} %slice_select_fusion), channel_id=1, source_target_pairs={{32,16},{96,80},{160,144},{224,208}} | collective-permute-start | bytes 294920 | tf_op jit(solution)/shard_map/ppermute | solution.py:32
  56.7 1.3 constant_dynamic-update-slice_fusion.41
  58.0 1.3 constant_dynamic-update-slice_fusion.40
  59.3 1.3 constant_dynamic-update-slice_fusion.39
  61.9 1.3 constant_dynamic-update-slice_fusion.37
  70.5 5.4 %collective-permute-done.21.refs_5_.refs_10_ = bf16[64,1024]{1,0:T(8,128)(2,1)S(1)} collective-permute-done((bf16[64,1024]{1,0:T(8,128)(2,1)S(1)}, bf16[64,1024]{1,0:T(8,128)(2,1)S(1)}, u32[]{:S(2)}, u32[]{:S(2)}) %collective-permute-start.21) | collective-permute-done | bytes 131104 | tf_op jit(solution)/shard_map/ppermute | solution.py:32
  80.7 3.2 %collective-permute-done.20.refs_4_.refs_9_ = bf16[256,1024]{1,0:T(8,128)(2,1)S(1)} collective-permute-done((bf16[256,1024]{1,0:T(8,128)(2,1)S(1)}, bf16[256,1024]{1,0:T(8,128)(2,1)S(1)}, u32[]{:S(2)}, u32[]{:S(2)}) %collective-permute-start.20) | collective-permute-done | bytes 524320 | tf_op jit(solution)/shard_map/ppermute | solution.py:32
  85.6 3.2 %collective-permute-start.24 = (bf16[64,1024]{1,0:T(8,128)(2,1)S(1)}, bf16[64,1024]{1,0:T(8,128)(2,1)S(1)}, u32[]{:S(2)}, u32[]{:S(2)}) collective-permute-start(bf16[64,1024]{1,0:T(8,128)(2,1)S(1)} %get-tuple-element.40), channel_id=1, source_target_pairs={{0,192},{1,193},{2,194},{3,195},{4,196},{5,197},{6,198},{7,199},{8... | collective-permute-start | bytes 393224 | tf_op jit(solution)/shard_map/ppermute | solution.py:32
  91.7 10.4 %collective-permute-start.26 = (bf16[128,1024]{1,0:T(8,128)(2,1)S(1)}, bf16[128,1024]{1,0:T(8,128)(2,1)}, u32[]{:S(2)}, u32[]{:S(2)}) collective-permute-start(bf16[128,1024]{1,0:T(8,128)(2,1)S(1)} %constant_dynamic-slice_fusion.1), channel_id=1, source_target_pairs={{32,16},{96,80},{160,144},{224,208}} | collective-permute-start | bytes 786440 | tf_op jit(solution)/shard_map/ppermute | solution.py:32
  104.6 1.3 convert_element_type.115
  109.9 3.9 %collective-permute-done.18.refs_12_.refs_14_ = bf16[128,1024]{1,0:T(8,128)(2,1)} collective-permute-done((bf16[128,1024]{1,0:T(8,128)(2,1)}, bf16[128,1024]{1,0:T(8,128)(2,1)}, u32[]{:S(2)}, u32[]{:S(2)}) %collective-permute-start.18) | collective-permute-done | bytes 262176 | tf_op jit(solution)/shard_map/ppermute | solution.py:32
  117.3 4.3 %collective-permute-done.29.refs_16_ = bf16[128,1024]{1,0:T(8,128)(2,1)S(1)} collective-permute-done((bf16[128,1024]{1,0:T(8,128)(2,1)}, bf16[128,1024]{1,0:T(8,128)(2,1)S(1)}, u32[]{:S(2)}, u32[]{:S(2)}) %collective-permute-start.29) | collective-permute-done | bytes 262176 | tf_op jit(solution)/shard_map/ppermute | solution.py:32
  123.5 4.9 %near.1 = f32[2,1024]{1,0:T(2,128)} custom-call(f32[20]{0:T(128)} %fusion.21.refs_0_, f32[20]{0:T(128)} %compare_convert_fusion.2.refs_1_, f32[1,1024]{1,0:T(1,128)} %slice.232.refs_2_, f32[2,1024]{1,0:T(2,128)} %broadcast_in_dim.49.refs_3_, bf16[128,1024]{1,0:T(8,128)(2,1)} %copy-done.3, bf16[128,1024]{1,0:T(8,128)(2,1)} %copy-done.6, ...), custom_call_target="tpu_custom_call" | custom-call | flops 1342177280 | bytes 3407872 | tf_op jit(solution)/shard_map/near/pallas_call | solution.py:169
  129.4 6.5 %far.1 = f32[2,1152]{1,0:T(2,128)} custom-call(f32[20]{0:T(128)} %fusion.21.refs_0_, f32[20]{0:T(128)} %compare_convert_fusion.2.refs_1_, f32[1,1152]{1,0:T(1,128)} %slice.233.refs_2_, f32[2,1152]{1,0:T(2,128)} %broadcast_in_dim.50.refs_3_, bf16[256,1024]{1,0:T(8,128)(2,1)} %copy-done.2, bf16[64,1024]{1,0:T(8,128)(2,1)} %copy-done.7, ...), custom_call_target="tpu_custom_call" | custom-call | flops 1509949440 | bytes 3670016 | tf_op jit(solution)/shard_map/far/pallas_call | solution.py:169
  135.9 1.3 pad_maximum_fusion.2.refs_3_
  137.9 6.5 %late.1.refs_3_ = f32[2,2176]{1,0:T(2,128)} custom-call(f32[9]{0:T(128)} %fusion.20.refs_0_, f32[9]{0:T(128)} %get-tuple-element.32.refs_1_, f32[1,2176]{1,0:T(1,128)} %copy-done.15, f32[2,2176]{1,0:T(2,128)} %pad_maximum_fusion.2.refs_3_, bf16[128,1024]{1,0:T(8,128)(2,1)} %copy-done.3, bf16[128,1024]{1,0:T(8,128)(2,1)} %copy-done.6, ...), custom_call_target="tpu_custom_call" | custom-call | flops 1283457024 | bytes 5046272 | tf_op jit(solution)/shard_map/late/pallas_call | solution.py:169
  145.1 6.1 %last.1 = f32[2,2176]{1,0:T(2,128)} custom-call(f32[4]{0:T(128)} %fusion.19.refs_0_, f32[4]{0:T(128)} %compare_convert_fusion.4.refs_1_, f32[1,2176]{1,0:T(1,128)} %copy-done.15, f32[2,2176]{1,0:T(2,128)} %late.1.refs_3_, bf16[128,1024]{1,0:T(8,128)(2,1)} %copy-done.3, bf16[128,1024]{1,0:T(8,128)(2,1)} %copy-done.6, bf16[128,1024]{1,0:T(8,128)(2,1)} %copy-done, ...), custom_call_target="tpu_custom_call" | custom-call | flops 570425344 | bytes 4718592 | tf_op jit(solution)/shard_map/last/pallas_call | solution.py:169
  157.5 1.8 %collective-permute-done.34 = f32[4,128]{1,0:T(4,128)S(1)} collective-permute-done((f32[4,128]{1,0:T(4,128)S(1)}, f32[4,128]{1,0:T(4,128)S(1)}, u32[]{:S(2)}, u32[]{:S(2)}) %collective-permute-start.34) | collective-permute-done | bytes 2080 | tf_op jit(solution)/shard_map/ppermute | solution.py:32
  159.4 1.8 %collective-permute-done.36 = f32[4,128]{1,0:T(4,128)S(1)} collective-permute-done((f32[4,128]{1,0:T(4,128)S(1)}, f32[4,128]{1,0:T(4,128)S(1)}, u32[]{:S(2)}, u32[]{:S(2)}) %collective-permute-start.36) | collective-permute-done | bytes 2080 | tf_op jit(solution)/shard_map/ppermute | solution.py:32
  161.5 2.7 %collective-permute-start.40 = (f32[4,4,4,32]{3,2,1,0:T(4,128)S(1)}, f32[4,4,4,32]{3,2,1,0:T(4,128)S(1)}, u32[]{:S(2)}, u32[]{:S(2)}) collective-permute-start(f32[4,4,4,32]{3,2,1,0:T(4,128)S(1)} %scatter-add.4), channel_id=1, source_target_pairs={{0,192},{1,193},{2,194},{3,195},{4,196},{5,197},{6,198},{7,199},{8... | collective-permute-start | bytes 24584 | tf_op jit(solution)/shard_map/ppermute | solution.py:32
  164.2 2.0 %collective-permute-start.38 = (f32[4,4,4,32]{3,2,1,0:T(4,128)S(1)}, f32[4,4,4,32]{3,2,1,0:T(4,128)S(1)}, u32[]{:S(2)}, u32[]{:S(2)}) collective-permute-start(f32[4,4,4,32]{3,2,1,0:T(4,128)S(1)} %scatter-add.4), channel_id=1, source_target_pairs={{0,128},{1,129},{2,130},{3,131},{4,132},{5,133},{6,134},{7,135},{8... | collective-permute-start | bytes 24584 | tf_op jit(solution)/shard_map/ppermute | solution.py:32
  166.2 3.1 %collective-permute-done.39 = f32[4,4,4,32]{3,2,1,0:T(4,128)S(1)} collective-permute-done((f32[4,4,4,32]{3,2,1,0:T(4,128)S(1)}, f32[4,4,4,32]{3,2,1,0:T(4,128)S(1)}, u32[]{:S(2)}, u32[]{:S(2)}) %collective-permute-start.39) | collective-permute-done | bytes 8224 | tf_op jit(solution)/shard_map/ppermute | solution.py:32
  (244 shorter events, 61.7 us)
Async XLA Ops:
  7.3 25.0 %collective-permute-start = (f16[128,1024]{1,0:T(8,128)(2,1)S(1)}, f16[128,1024]{1,0:T(8,128)(2,1)S(1)}, u32[]{:S(2)}, u32[]{:S(2)}) collective-permute-start(f16[128,1024]{1,0:T(8,128)(2,1)S(1)} %bitcast.59), channel_id=1, source_target_pairs={{0,128},{1,129},{2,130},{3,131},{4,132},{5,133},{6,134},{7,135},{8... | collective-permute-start | bytes 786440 | tf_op jit(solution)/shard_map/ppermute | solution.py:32
  10.5 21.7 %collective-permute-start.1 = (f16[128,1024]{1,0:T(8,128)(2,1)S(1)}, f16[128,1024]{1,0:T(8,128)(2,1)S(1)}, u32[]{:S(2)}, u32[]{:S(2)}) collective-permute-start(f16[128,1024]{1,0:T(8,128)(2,1)S(1)} %bitcast.58), channel_id=1, source_target_pairs={{0,64},{1,65},{2,66},{3,67},{4,68},{5,69},{6,70},{7,71},{8,72},{9,... | collective-permute-start | bytes 786440 | tf_op jit(solution)/shard_map/ppermute | solution.py:32
  11.2 21.0 %collective-permute-start.2 = (f16[128,1024]{1,0:T(8,128)(2,1)S(1)}, f16[128,1024]{1,0:T(8,128)(2,1)S(1)}, u32[]{:S(2)}, u32[]{:S(2)}) collective-permute-start(f16[128,1024]{1,0:T(8,128)(2,1)S(1)} %bitcast.57), channel_id=1, source_target_pairs={{0,192},{1,193},{2,194},{3,195},{4,196},{5,197},{6,198},{7,199},{8... | collective-permute-start | bytes 786440 | tf_op jit(solution)/shard_map/ppermute | solution.py:32
  23.8 8.4 %collective-permute-start.6 = (s32[4,2,4]{2,1,0:T(2,128)S(1)}, s32[4,2,4]{2,1,0:T(2,128)S(1)}, u32[]{:S(2)}, u32[]{:S(2)}) collective-permute-start(s32[4,2,4]{2,1,0:T(2,128)S(1)} %add_select_fusion.1), channel_id=1, source_target_pairs={{0,8},{1,9},{2,10},{3,11},{4,12},{5,13},{6,14},{7,15},{8,0},{9,1},... | collective-permute-start | bytes 392 | tf_op jit(solution)/shard_map/ppermute | solution.py:32
  34.2 32.4 %collective-permute-start.12 = (bf16[128,1024]{1,0:T(8,128)(2,1)S(1)}, bf16[128,1024]{1,0:T(8,128)(2,1)S(1)}, u32[]{:S(2)}, u32[]{:S(2)}) collective-permute-start(bf16[128,1024]{1,0:T(8,128)(2,1)S(1)} %multiply_convert_fusion.refs_4_.refs_9_.refs_11_), channel_id=1, source_target_pairs={{0,16},{1,17},{2,18},{3,19},{4,20},{5,21},{6,22},{7,23},{8,24},{9,... | collective-permute-start | bytes 786440 | tf_op jit(solution)/shard_map/ppermute | solution.py:32
  35.4 31.9 %collective-permute-start.13 = (bf16[128,1024]{1,0:T(8,128)(2,1)S(1)}, bf16[128,1024]{1,0:T(8,128)(2,1)S(1)}, u32[]{:S(2)}, u32[]{:S(2)}) collective-permute-start(bf16[128,1024]{1,0:T(8,128)(2,1)S(1)} %multiply_convert_fusion.refs_4_.refs_9_.refs_11_), channel_id=1, source_target_pairs={{0,64},{1,65},{2,66},{3,67},{4,68},{5,69},{6,70},{7,71},{8,72},{9,... | collective-permute-start | bytes 786440 | tf_op jit(solution)/shard_map/ppermute | solution.py:32
  35.4 31.9 %collective-permute-start.14 = (bf16[128,1024]{1,0:T(8,128)(2,1)S(1)}, bf16[128,1024]{1,0:T(8,128)(2,1)S(1)}, u32[]{:S(2)}, u32[]{:S(2)}) collective-permute-start(bf16[128,1024]{1,0:T(8,128)(2,1)S(1)} %multiply_convert_fusion.refs_4_.refs_9_.refs_11_), channel_id=1, source_target_pairs={{0,192},{1,193},{2,194},{3,195},{4,196},{5,197},{6,198},{7,199},{8... | collective-permute-start | bytes 786440 | tf_op jit(solution)/shard_map/ppermute | solution.py:32
  41.0 61.8 %collective-permute-start.16 = (bf16[128,1024]{1,0:T(8,128)(2,1)S(1)}, bf16[128,1024]{1,0:T(8,128)(2,1)}, u32[]{:S(2)}, u32[]{:S(2)}) collective-permute-start(bf16[128,1024]{1,0:T(8,128)(2,1)S(1)} %multiply_convert_fusion.refs_4_.refs_9_.refs_11_), channel_id=1, source_target_pairs={{0,2},{1,15},{2,4},{3,1},{4,6},{5,3},{6,8},{7,5},{8,10},{9,7},{10,... | collective-permute-start | bytes 786440 | tf_op jit(solution)/shard_map/ppermute | solution.py:32
  44.6 21.2 %collective-permute-start.8 = (bf16[48,1024]{1,0:T(8,128)(2,1)S(1)}, bf16[48,1024]{1,0:T(8,128)(2,1)S(1)}, u32[]{:S(2)}, u32[]{:S(2)}) collective-permute-start(bf16[48,1024]{1,0:T(8,128)(2,1)S(1)} %slice_select_fusion), channel_id=1, source_target_pairs={{32,16},{96,80},{160,144},{224,208}} | collective-permute-start | bytes 294920 | tf_op jit(solution)/shard_map/ppermute | solution.py:32
  66.5 39.4 %collective-permute-start.17 = (bf16[128,1024]{1,0:T(8,128)(2,1)S(1)}, bf16[128,1024]{1,0:T(8,128)(2,1)}, u32[]{:S(2)}, u32[]{:S(2)}) collective-permute-start(bf16[128,1024]{1,0:T(8,128)(2,1)S(1)} %multiply_convert_fusion.refs_4_.refs_9_.refs_11_), channel_id=1, source_target_pairs={{0,15},{1,2},{2,1},{3,4},{4,3},{5,6},{6,5},{7,8},{8,7},{9,10},{10,... | collective-permute-start | bytes 786440 | tf_op jit(solution)/shard_map/ppermute | solution.py:32
  68.5 53.9 %collective-permute-start.15 = (bf16[512,1024]{1,0:T(8,128)(2,1)}, bf16[512,1024]{1,0:T(8,128)(2,1)S(1)}, u32[]{:S(2)}, u32[]{:S(2)}) collective-permute-start(bf16[512,1024]{1,0:T(8,128)(2,1)} %pad_maximum_fusion), channel_id=1, source_target_pairs={{0,1},{1,0},{2,3},{3,2},{4,5},{5,4},{6,7},{7,6},{8,9},{9,8},{10,11... | collective-permute-start | bytes 3145736 | tf_op jit(solution)/shard_map/ppermute | solution.py:32
  68.5 7.4 %collective-permute-start.21 = (bf16[64,1024]{1,0:T(8,128)(2,1)S(1)}, bf16[64,1024]{1,0:T(8,128)(2,1)S(1)}, u32[]{:S(2)}, u32[]{:S(2)}) collective-permute-start(bf16[64,1024]{1,0:T(8,128)(2,1)S(1)} %slice.234), channel_id=1, source_target_pairs={{0,64},{1,65},{2,66},{3,67},{4,68},{5,69},{6,70},{7,71},{8,72},{9,... | collective-permute-start | bytes 393224 | tf_op jit(solution)/shard_map/ppermute | solution.py:32
  69.5 14.4 %collective-permute-start.20 = (bf16[256,1024]{1,0:T(8,128)(2,1)S(1)}, bf16[256,1024]{1,0:T(8,128)(2,1)S(1)}, u32[]{:S(2)}, u32[]{:S(2)}) collective-permute-start(bf16[256,1024]{1,0:T(8,128)(2,1)S(1)} %pad_maximum_fusion.1), channel_id=1, source_target_pairs={{0,16},{1,17},{2,18},{3,19},{4,20},{5,21},{6,22},{7,23},{8,24},{9,... | collective-permute-start | bytes 1572872 | tf_op jit(solution)/shard_map/ppermute | solution.py:32
  75.9 9.7 %collective-permute-start.22 = (bf16[64,1024]{1,0:T(8,128)(2,1)S(1)}, bf16[64,1024]{1,0:T(8,128)(2,1)S(1)}, u32[]{:S(2)}, u32[]{:S(2)}) collective-permute-start(bf16[64,1024]{1,0:T(8,128)(2,1)S(1)} %slice.235), channel_id=1, source_target_pairs={{0,192},{1,193},{2,194},{3,195},{4,196},{5,197},{6,198},{7,199},{8... | collective-permute-start | bytes 393224 | tf_op jit(solution)/shard_map/ppermute | solution.py:32
  84.0 6.4 %collective-permute-start.23 = (bf16[64,1024]{1,0:T(8,128)(2,1)S(1)}, bf16[64,1024]{1,0:T(8,128)(2,1)S(1)}, u32[]{:S(2)}, u32[]{:S(2)}) collective-permute-start(bf16[64,1024]{1,0:T(8,128)(2,1)S(1)} %get-tuple-element.41), channel_id=1, source_target_pairs={{0,64},{1,65},{2,66},{3,67},{4,68},{5,69},{6,70},{7,71},{8,72},{9,... | collective-permute-start | bytes 393224 | tf_op jit(solution)/shard_map/ppermute | solution.py:32
  85.6 6.1 %collective-permute-start.24 = (bf16[64,1024]{1,0:T(8,128)(2,1)S(1)}, bf16[64,1024]{1,0:T(8,128)(2,1)S(1)}, u32[]{:S(2)}, u32[]{:S(2)}) collective-permute-start(bf16[64,1024]{1,0:T(8,128)(2,1)S(1)} %get-tuple-element.40), channel_id=1, source_target_pairs={{0,192},{1,193},{2,194},{3,195},{4,196},{5,197},{6,198},{7,199},{8... | collective-permute-start | bytes 393224 | tf_op jit(solution)/shard_map/ppermute | solution.py:32
  90.4 15.5 %collective-permute-start.11 = (bf16[48,1024]{1,0:T(8,128)(2,1)S(1)}, bf16[48,1024]{1,0:T(8,128)(2,1)S(1)}, u32[]{:S(2)}, u32[]{:S(2)}) collective-permute-start(bf16[48,1024]{1,0:T(8,128)(2,1)S(1)} %add.163), channel_id=1, source_target_pairs={{16,18},{20,22},{24,26},{28,30},{80,82},{84,86},{88,90},{92,94},{1... | collective-permute-start | bytes 294920 | tf_op jit(solution)/shard_map/ppermute | solution.py:32
  91.7 16.5 %collective-permute-start.26 = (bf16[128,1024]{1,0:T(8,128)(2,1)S(1)}, bf16[128,1024]{1,0:T(8,128)(2,1)}, u32[]{:S(2)}, u32[]{:S(2)}) collective-permute-start(bf16[128,1024]{1,0:T(8,128)(2,1)S(1)} %constant_dynamic-slice_fusion.1), channel_id=1, source_target_pairs={{32,16},{96,80},{160,144},{224,208}} | collective-permute-start | bytes 786440 | tf_op jit(solution)/shard_map/ppermute | solution.py:32
  102.8 25.6 %collective-permute-start.25 = (bf16[512,1024]{1,0:T(8,128)(2,1)}, bf16[512,1024]{1,0:T(8,128)(2,1)S(1)}, u32[]{:S(2)}, u32[]{:S(2)}) collective-permute-start(bf16[512,1024]{1,0:T(8,128)(2,1)} %constant_dynamic-update-slice_fusion.17), channel_id=1, source_target_pairs={{0,1},{1,0},{2,3},{3,2},{4,5},{5,4},{6,7},{7,6},{8,9},{9,8},{10,11... | collective-permute-start | bytes 3145736 | tf_op jit(solution)/shard_map/ppermute | solution.py:32
  105.9 7.9 %collective-permute-start.18 = (bf16[128,1024]{1,0:T(8,128)(2,1)}, bf16[128,1024]{1,0:T(8,128)(2,1)}, u32[]{:S(2)}, u32[]{:S(2)}) collective-permute-start(bf16[128,1024]{1,0:T(8,128)(2,1)} %collective-permute-done.16.refs_10_.refs_12_), channel_id=1, source_target_pairs={{0,2},{1,15},{2,4},{3,1},{4,6},{5,3},{6,8},{7,5},{8,10},{9,7},{10,... | collective-permute-start | bytes 786440 | tf_op jit(solution)/shard_map/ppermute | solution.py:32
  105.9 11.4 %collective-permute-start.19 = (bf16[128,1024]{1,0:T(8,128)(2,1)}, bf16[128,1024]{1,0:T(8,128)(2,1)}, u32[]{:S(2)}, u32[]{:S(2)}) collective-permute-start(bf16[128,1024]{1,0:T(8,128)(2,1)} %collective-permute-done.17.refs_11_.refs_13_), channel_id=1, source_target_pairs={{0,2},{1,15},{2,4},{3,1},{4,6},{5,3},{6,8},{7,5},{8,10},{9,7},{10,... | collective-permute-start | bytes 786440 | tf_op jit(solution)/shard_map/ppermute | solution.py:32
  108.2 5.6 %collective-permute-start.27 = (bf16[128,1024]{1,0:T(8,128)(2,1)}, bf16[128,1024]{1,0:T(8,128)(2,1)S(1)}, u32[]{:S(2)}, u32[]{:S(2)}) collective-permute-start(bf16[128,1024]{1,0:T(8,128)(2,1)} %collective-permute-done.26), channel_id=1, source_target_pairs={{16,0},{80,64},{144,128},{208,192}} | collective-permute-start | bytes 786440 | tf_op jit(solution)/shard_map/ppermute | solution.py:32
  113.8 7.8 %collective-permute-start.29 = (bf16[128,1024]{1,0:T(8,128)(2,1)}, bf16[128,1024]{1,0:T(8,128)(2,1)S(1)}, u32[]{:S(2)}, u32[]{:S(2)}) collective-permute-start(bf16[128,1024]{1,0:T(8,128)(2,1)} %collective-permute-done.18.refs_12_.refs_14_), channel_id=1, source_target_pairs={{0,2},{1,15},{2,4},{3,1},{4,6},{5,3},{6,8},{7,5},{8,10},{9,7},{10,... | collective-permute-start | bytes 786440 | tf_op jit(solution)/shard_map/ppermute | solution.py:32
  114.8 6.8 %collective-permute-start.28 = (bf16[128,1024]{1,0:T(8,128)(2,1)S(1)}, bf16[128,1024]{1,0:T(8,128)(2,1)S(1)}, u32[]{:S(2)}, u32[]{:S(2)}) collective-permute-start(bf16[128,1024]{1,0:T(8,128)(2,1)S(1)} %add.167), channel_id=1, source_target_pairs={{0,1},{16,17},{64,65},{80,81},{128,129},{144,145},{192,193},{208,2... | collective-permute-start | bytes 786440 | tf_op jit(solution)/shard_map/ppermute | solution.py:32
  117.3 19.9 %collective-permute-start.30 = (bf16[128,1024]{1,0:T(8,128)(2,1)}, bf16[128,1024]{1,0:T(8,128)(2,1)S(1)}, u32[]{:S(2)}, u32[]{:S(2)}) collective-permute-start(bf16[128,1024]{1,0:T(8,128)(2,1)} %collective-permute-done.19.refs_13_.refs_15_), channel_id=1, source_target_pairs={{0,2},{1,15},{2,4},{3,1},{4,6},{5,3},{6,8},{7,5},{8,10},{9,7},{10,... | collective-permute-start | bytes 786440 | tf_op jit(solution)/shard_map/ppermute | solution.py:32
  121.6 22.8 %collective-permute-start.31 = (bf16[128,1024]{1,0:T(8,128)(2,1)S(1)}, bf16[128,1024]{1,0:T(8,128)(2,1)S(1)}, u32[]{:S(2)}, u32[]{:S(2)}) collective-permute-start(bf16[128,1024]{1,0:T(8,128)(2,1)S(1)} %collective-permute-done.29.refs_16_), channel_id=1, source_target_pairs={{0,2},{1,15},{2,4},{3,1},{4,6},{5,3},{6,8},{7,5},{8,10},{9,7},{10,... | collective-permute-start | bytes 786440 | tf_op jit(solution)/shard_map/ppermute | solution.py:32
  152.0 5.3 %collective-permute-start.32 = (f32[4,8,128]{2,1,0:T(8,128)S(1)}, f32[4,8,128]{2,1,0:T(8,128)S(1)}, u32[]{:S(2)}, u32[]{:S(2)}) collective-permute-start(f32[4,8,128]{2,1,0:T(8,128)S(1)} %fusion.13), channel_id=1, source_target_pairs={{0,1},{1,0},{2,3},{3,2},{4,5},{5,4},{6,7},{7,6},{8,9},{9,8},{10,11... | collective-permute-start | bytes 49160 | tf_op jit(solution)/shard_map/ppermute | solution.py:32
  152.1 7.2 %collective-permute-start.34 = (f32[4,128]{1,0:T(4,128)S(1)}, f32[4,128]{1,0:T(4,128)S(1)}, u32[]{:S(2)}, u32[]{:S(2)}) collective-permute-start(f32[4,128]{1,0:T(4,128)S(1)} %bitcast.76), channel_id=1, source_target_pairs={{0,32},{64,96},{128,160},{192,224}} | collective-permute-start | bytes 6152 | tf_op jit(solution)/shard_map/ppermute | solution.py:32
  153.4 5.9 %collective-permute-start.35 = (f32[4,128]{1,0:T(4,128)S(1)}, f32[4,128]{1,0:T(4,128)S(1)}, u32[]{:S(2)}, u32[]{:S(2)}) collective-permute-start(f32[4,128]{1,0:T(4,128)S(1)} %bitcast.77), channel_id=1, source_target_pairs={{16,32},{80,96},{144,160},{208,224}} | collective-permute-start | bytes 6152 | tf_op jit(solution)/shard_map/ppermute | solution.py:32
  154.7 6.4 %collective-permute-start.36 = (f32[4,128]{1,0:T(4,128)S(1)}, f32[4,128]{1,0:T(4,128)S(1)}, u32[]{:S(2)}, u32[]{:S(2)}) collective-permute-start(f32[4,128]{1,0:T(4,128)S(1)} %bitcast.78), channel_id=1, source_target_pairs={{1,32},{65,96},{129,160},{193,224}} | collective-permute-start | bytes 6152 | tf_op jit(solution)/shard_map/ppermute | solution.py:32
  164.2 5.1 %collective-permute-start.39 = (f32[4,4,4,32]{3,2,1,0:T(4,128)S(1)}, f32[4,4,4,32]{3,2,1,0:T(4,128)S(1)}, u32[]{:S(2)}, u32[]{:S(2)}) collective-permute-start(f32[4,4,4,32]{3,2,1,0:T(4,128)S(1)} %scatter-add.4), channel_id=1, source_target_pairs={{0,64},{1,65},{2,66},{3,67},{4,68},{5,69},{6,70},{7,71},{8,72},{9,... | collective-permute-start | bytes 24584 | tf_op jit(solution)/shard_map/ppermute | solution.py:32
  164.2 5.5 %collective-permute-start.38 = (f32[4,4,4,32]{3,2,1,0:T(4,128)S(1)}, f32[4,4,4,32]{3,2,1,0:T(4,128)S(1)}, u32[]{:S(2)}, u32[]{:S(2)}) collective-permute-start(f32[4,4,4,32]{3,2,1,0:T(4,128)S(1)} %scatter-add.4), channel_id=1, source_target_pairs={{0,128},{1,129},{2,130},{3,131},{4,132},{5,133},{6,134},{7,135},{8... | collective-permute-start | bytes 24584 | tf_op jit(solution)/shard_map/ppermute | solution.py:32
  (37 other events, 490.0 us)

commit v3 on v0

v3 whole, which is shorter than its diff:
```python
import functools

import jax
import jax.numpy as jnp
from jax import lax
from jax.experimental import pallas as pl
from jax.experimental.pallas import tpu as pltpu
from jax.sharding import PartitionSpec as P

BLOCK = 128
PIECE = 32
TAG = 16
BINS = 8
CHUNK = 512
AXES = ("layer", "shower")
NY, NX, NZ, NC = 4, 4, 8, 2


def flat(y, x, z, c):
    return y * (NX * NZ * NC) + (x * NZ + z) * NC + c


def permute(value, move, keep=lambda y, x, z, c: True):
    pairs = [
        (flat(y, x, z, c), flat(*move(y, x, z, c)))
        for y in range(NY)
        for x in range(NX)
        for z in range(NZ)
        for c in range(NC)
        if keep(y, x, z, c)
    ]
    return lax.ppermute(value, AXES, pairs)


def along_y(step):
    return lambda y, x, z, c: ((y + step) % NY, x, z, c)


def along_z(step):
    return lambda y, x, z, c: (y, x, (z + step) % NZ, c)


def flip_z(bit):
    return lambda y, x, z, c: (y, x, z ^ bit, c)


def swap_x(y, x, z, c):
    return (y, x ^ 1, z, c)


def swap_core(y, x, z, c):
    return (y, x, z, 1 - c)


def same_core(y, x, z, c):
    return (y, x, (z + 1 - 2 * c) % NZ, c)


def cross_core(y, x, z, c):
    return (y, x, (z - 1 + 2 * c) % NZ, 1 - c)


def raw_kernel(pattern, showers, geometry, out, masked):
    step = pl.program_id(0)
    layers = pattern.shape[1]
    cells = geometry.shape[0] // layers
    per = geometry.shape[1] // BLOCK
    for layer in range(layers):
        for part in range(per):
            rows = pl.ds(layer * cells, cells)
            cols = pl.ds(part * BLOCK, BLOCK)
            on = pattern[step * per + part, layer].astype(jnp.float32).astype(jnp.bfloat16)
            masked[rows, cols] = geometry[rows, cols] * on
    out[...] = lax.dot_general(
        showers[...], masked[...], (((0,), (0,)), ((), ())), preferred_element_type=jnp.float32
    )


def raw_partial(showers, geometry, pattern):
    rows, depth = showers.shape
    feats = geometry.shape[1]
    width = 512
    return pl.pallas_call(
        raw_kernel,
        grid=(feats // width,),
        in_specs=[
            pl.BlockSpec(memory_space=pltpu.SMEM),
            pl.BlockSpec((depth, rows), lambda i: (0, 0)),
            pl.BlockSpec((depth, width), lambda i: (0, i)),
        ],
        out_specs=pl.BlockSpec((rows, width), lambda i: (0, i)),
        out_shape=jax.ShapeDtypeStruct((rows, feats), jnp.float32),
        scratch_shapes=[pltpu.VMEM((depth, width), jnp.bfloat16)],
        compiler_params=pltpu.CompilerParams(vmem_limit_bytes=60 * 2**20),
        cost_estimate=pl.CostEstimate(
            flops=2 * rows * depth * feats, bytes_accessed=8 * 2**20, transcendentals=0
        ),
        name="raw",
    )(pattern.T, showers.T, geometry)


def pair_kernel(*refs, row_cuts, tag_cuts, col_sizes, n_args, apart):
    n_cols = len(col_sizes)
    odd_here = refs[0]
    args = refs[1 : 1 + n_args]
    cols = refs[1 + n_args : 1 + n_args + n_cols]
    out, rows_at, cols_at, row_tags, col_tags, row_sems, col_sems, tag_sems = refs[1 + n_args + n_cols :]

    def start(source, first, size, target, place, sem):
        copy = pltpu.make_async_copy(
            source.at[pl.ds(first, size), :], target.at[pl.ds(place, size), :], sem
        )
        copy.start()
        return copy

    waits, depth = [], 0
    for at, (source, size) in enumerate(zip(cols, col_sizes)):
        waits.append(start(source, TAG, size, cols_at, depth, col_sems.at[at]))
        waits.append(start(source, 0, TAG, col_tags, at * TAG, tag_sems.at[at]))
        depth += size
    for at, (arg, first) in enumerate(tag_cuts):
        waits.append(start(args[arg], first, TAG, row_tags, at * TAG, tag_sems.at[n_cols + at]))
    row_copies, total = [], 0
    for at, (arg, first, size) in enumerate(row_cuts):
        row_copies.append((total, start(args[arg], first, size, rows_at, total, row_sems.at[at])))
        total += size
    for copy in waits:
        copy.wait()

    def bin_of(code):
        source = (code >= BINS).astype(jnp.float32)
        return code - BINS * source, source

    waited = 0
    for first in range(0, total, CHUNK):
        size = min(CHUNK, total - first)
        while waited < len(row_copies) and row_copies[waited][0] < first + size:
            row_copies[waited][1].wait()
            waited += 1
        odd = first >= 4 * CHUNK
        set_of = 0 if odd else first // CHUNK
        tag = row_tags[pl.ds(set_of * TAG + 4, 1), pl.ds(0, BLOCK)].astype(jnp.float32) - 1.0
        bins, _ = bin_of(tag)
        if odd:
            bins = jnp.where(odd_here[0] > 0, bins, -2.0)
        bins = jnp.concatenate([bins] * (size // BLOCK), axis=1)
        one = jnp.zeros((8, size), jnp.float32)
        zero = jnp.zeros((8, size), jnp.float32)
        n_one = jnp.zeros((1, size), jnp.float32)
        n_zero = jnp.zeros((1, size), jnp.float32)
        for low in range(0, depth, 2 * BLOCK):
            high = depth if depth - low < 4 * BLOCK and depth % (2 * BLOCK) else low + 2 * BLOCK
            if low and high == depth and low > high - 2 * BLOCK and depth % (2 * BLOCK):
                break
            products = lax.dot_general(
                cols_at[pl.ds(low, high - low), :],
                rows_at[pl.ds(first, size), :],
                (((1,), (1,)), ((), ())),
                preferred_element_type=jnp.float32,
            )
            shifted = products + 32.0
            cubes = shifted * shifted * shifted
            for group in range(low // PIECE, high // PIECE):
                if odd and group == apart:
                    continue
                block = cubes[group * PIECE - low : (group + 1) * PIECE - low]
                if first == 0 and group < BLOCK // PIECE:
                    lane = lax.broadcasted_iota(jnp.int32, block.shape, 1)
                    sub = lax.broadcasted_iota(jnp.int32, block.shape, 0)
                    block = jnp.where(lane == sub + group * PIECE, 0.0, block)
                part = (block[0:8] + block[8:16]) + (block[16:24] + block[24:32])
                row = group // 4 * TAG + group % 4
                code = col_tags[pl.ds(row, 1), pl.ds(0, size)].astype(jnp.float32) - 1.0
                bin_id, source = bin_of(code)
                match = (bins == bin_id).astype(jnp.float32)
                is_one = match * source
                is_zero = match - is_one
                one += is_one * part
                zero += is_zero * part
                n_one += is_one
                n_zero += is_zero
        lanes = pl.ds(first, size)
        out[0:1, lanes] = jnp.sum(one, axis=0, keepdims=True)
        out[1:2, lanes] = jnp.sum(zero, axis=0, keepdims=True)
        out[2:3, lanes] = n_one
        out[3:4, lanes] = n_zero


def pair_sums(odd_here, args, row_cuts, tag_cuts, cols, apart):
    col_sizes = tuple(size for _, size in cols)
    total, depth = sum(size for _, _, size in row_cuts), sum(col_sizes)
    feats = args[0].shape[1]
    hbm = pl.BlockSpec(memory_space=pl.ANY)
    return pl.pallas_call(
        functools.partial(
            pair_kernel,
            row_cuts=tuple(row_cuts),
            tag_cuts=tuple(tag_cuts),
            col_sizes=col_sizes,
            n_args=len(args),
            apart=apart,
        ),
        in_specs=[pl.BlockSpec(memory_space=pltpu.SMEM)] + [hbm] * (len(args) + len(cols)),
        out_specs=pl.BlockSpec(memory_space=pltpu.VMEM),
        out_shape=jax.ShapeDtypeStruct((4, total), jnp.float32),
        scratch_shapes=[
            pltpu.VMEM((total, feats), jnp.bfloat16),
            pltpu.VMEM((depth, feats), jnp.bfloat16),
            pltpu.VMEM((TAG * len(tag_cuts), feats), jnp.bfloat16),
            pltpu.VMEM((TAG * len(cols), feats), jnp.bfloat16),
            pltpu.SemaphoreType.DMA((len(row_cuts),)),
            pltpu.SemaphoreType.DMA((len(cols),)),
            pltpu.SemaphoreType.DMA((len(cols) + len(tag_cuts),)),
        ],
        compiler_params=pltpu.CompilerParams(vmem_limit_bytes=58 * 2**20),
        cost_estimate=pl.CostEstimate(
            flops=2 * total * depth * feats,
            bytes_accessed=2 * (total + depth) * feats,
            transcendentals=0,
        ),
        name="pairs",
    )(odd_here, *args, *[c for c, _ in cols])


def shards(showers, geometry, pattern, bins, sources):
    y = lax.axis_index("layer")
    s = lax.axis_index("shower")
    x, z, c = s // (NZ * NC), (s // NC) % NZ, s % NC
    feats = geometry.shape[1]
    blocks = bins.shape[0]

    codes = (bins + BINS * sources + 1).astype(jnp.float32)
    line = lax.broadcasted_iota(jnp.int32, (TAG, feats), 0)
    lane = lax.broadcasted_iota(jnp.int32, (TAG, feats), 1) // PIECE
    which = jnp.where(line == blocks, lane, line)
    tag = jnp.zeros((TAG, feats), jnp.float32)
    for group in range(blocks):
        tag = jnp.where(which == group, codes[group], tag)
    tag = tag.astype(jnp.bfloat16)

    partial_sums = raw_partial(showers, geometry, pattern).reshape(blocks, NY, PIECE, feats)

    def share(turn):
        part = lax.dynamic_index_in_dim(partial_sums, (y + turn) % NY, 1, keepdims=False)
        return part.reshape(BLOCK, feats)

    raw = share(0)
    arrived = [permute(share(turn).astype(jnp.float16), along_y(turn)) for turn in (2, 1, 3)]
    for part in arrived:
        raw = raw + part.astype(jnp.float32)
    scale = lax.rsqrt(jnp.mean(raw * raw, axis=1, keepdims=True) + 1e-05)
    own = jnp.concatenate([tag, (raw * scale).astype(jnp.bfloat16)], axis=0)

    rows_of = lambda value: value[TAG:]
    same = [permute(own, same_core)]
    cross = [permute(own, cross_core)]
    x1 = permute(own, swap_x)
    ya = permute(rows_of(own), along_y(1))
    yb = permute(rows_of(own), along_y(3))
    same.append(permute(same[0], same_core))
    cross.append(permute(cross[0], same_core))
    y_way = lambda y, x, z, c: ((y + 1 - 2 * c) % NY, x, z, c)
    y2 = permute(jnp.where(c == 0, ya, yb), y_way)
    xx = permute(jnp.concatenate([ya, yb], axis=0), swap_x)
    near = permute(jnp.concatenate([own, x1, ya, yb], axis=0), swap_core)
    same.append(permute(same[1], same_core))
    cross.append(permute(cross[1], same_core))
    w2 = permute(jnp.where(c == 0, xx[:BLOCK], xx[BLOCK:]), y_way)
    far = permute(jnp.concatenate([xx, y2, w2], axis=0), swap_core)
    same.append(permute(same[2], same_core))

    head = TAG + PIECE
    held = [own, same[0], same[1], same[2], same[2], cross[2], cross[1], cross[0]]
    piece = lax.select_n(z, *[value[:head] for value in held])
    to_one = lambda y, x, z, c: (y, 1, z, c)
    side = lambda z: 0 if z < 4 else 1
    piece_near = permute(
        piece, to_one, keep=lambda y, x, z, c: x == 2 and z != 4 and c == side(z)
    )
    piece_far = permute(
        piece,
        lambda y, x, z, c: (y, 1, z + 1, c),
        keep=lambda y, x, z, c: x == 2 and z == 3 and c == 0,
    )
    piece = piece_near + piece_far
    odd = jnp.concatenate(
        [own[TAG:head], yb[:PIECE], y2[:PIECE], ya[:PIECE]], axis=0
    )
    at_start = lambda y, x, z, c: z == 0 and c == 0
    odd = permute(odd, to_one, keep=lambda *a: a[1] == 2 and at_start(*a))
    odd = odd + permute(odd, swap_x, keep=lambda *a: a[1] == 1 and at_start(*a))
    odd = odd + permute(odd, swap_core, keep=lambda *a: a[1] < 2 and at_start(*a))

    args = [own, x1, ya, yb, y2, xx, w2, near, far, odd]
    tagged = BLOCK + TAG
    tag_cuts = [(0, 0), (1, 0), (7, 0), (7, tagged)]
    row_cuts = [(0, TAG, BLOCK), (3, 0, BLOCK), (4, 0, BLOCK), (2, 0, BLOCK)]
    row_cuts += [(1, TAG, BLOCK), (5, BLOCK, BLOCK), (6, 0, BLOCK), (5, 0, BLOCK)]
    row_cuts += [(7, TAG, BLOCK), (7, 2 * tagged + BLOCK, BLOCK)]
    row_cuts += [(8, 2 * BLOCK, BLOCK), (7, 2 * tagged, BLOCK)]
    row_cuts += [(7, tagged + TAG, BLOCK), (8, BLOCK, BLOCK)]
    row_cuts += [(8, 3 * BLOCK, BLOCK), (8, 0, BLOCK), (9, 0, BLOCK)]
    cols = [own, same[0], cross[0], same[1], cross[1], same[2], cross[2], same[3]]
    cols = [(value, BLOCK) for value in cols] + [(piece, PIECE)]
    odd_here = ((x < 2) & (z == 0)).astype(jnp.int32).reshape(1)
    stats = pair_sums(odd_here, args, row_cuts, tag_cuts, cols, 8 * BLOCK // PIECE)

    theirs = permute(stats[:, 2 * CHUNK :], swap_core)
    mine = stats[:, : 2 * CHUNK] + theirs[:, : 2 * CHUNK]
    odd_stats = stats[:, 4 * CHUNK :] + theirs[:, 2 * CHUNK :]
    kept = mine[:, :CHUNK] + permute(mine[:, CHUNK:], swap_x)
    odd_total = jnp.zeros_like(odd_stats)
    for start in (0, 1):
        odd_total = odd_total + permute(
            odd_stats,
            lambda y, x, z, c: (y, 2, z, c),
            keep=lambda *a, start=start: a[1] == start and at_start(*a),
        )
    odd_total = odd_total.reshape(4, NY, PIECE)
    kept = kept.reshape(4, NY, BLOCK) + jnp.pad(odd_total, ((0, 0), (0, 0), (0, BLOCK - PIECE)))
    total = kept
    for turn in (2, 1, 3):
        total = total + jnp.roll(permute(kept, along_y(turn)), -turn, axis=1)
    weight = 1.0 / (PIECE * 32.0**3)
    proof = (total[0] / total[2] - total[1] / total[3]) * weight
    proof = jnp.concatenate([proof, proof], axis=0)
    proof = lax.dynamic_slice_in_dim(proof, (NY - y) % NY, NY, 0).reshape(NY, blocks, PIECE)
    return jnp.transpose(proof, (1, 0, 2)).reshape(-1)


def solution(mesh):
    placed = (P("shower", "layer"), P("layer", None), P("layer", None), P("shower"), P("shower"))
    return jax.shard_map(shards, mesh=mesh, in_specs=placed, out_specs=P("shower"), check_vma=False)
```

time: 238 us -> 108 us (0.45)
  waiting for transfers between devices: 150 us -> 43.9 us
  starting transfers between devices: 0.04 us -> 32 us
  blocking collectives: 30.2 us -> 0 us
  matrix products: 25.5 us -> 0 us
  Pallas kernels: 0 us -> 16.1 us
  between operations: 14.1 us -> 0.44 us
  local copies, waits for them, and re-layouts: 8.35 us -> 4.07 us
  other arithmetic: 7.97 us -> 11 us
    all_gather x1 -> x0, waiting for transfers between devices: 83.4 us -> none  [shards(): piece = lax.all_gather(quarter, 'shower', axis=0, tiled=True)]
    psum x1 -> x0, waiting for transfers between devices: 66.8 us -> none  [shards(): summed = lax.psum(partial_sums, 'layer')]
    ppermute x0 -> x30, waiting for transfers between devices: none -> 43.9 us  [permute(): return lax.ppermute(value, AXES, pairs)]
    ppermute x0 -> x30, starting transfers between devices: none -> 32 us  [permute(): return lax.ppermute(value, AXES, pairs)]
    dot_general x5 -> x0, matrix products: 25.5 us -> none  [the longest x4 22.1 us: tile_sums(): lax.dot_general(own_feats, columns, (((1,), (1,)), ((), ())), preferred_e...]
    unnamed x1 -> x0, blocking collectives: 19.2 us -> none
    pallas_call x0 -> x2, Pallas kernels: none -> 16.1 us  [the longest x1 10.7 us: pair_sums(): pl.pallas_call(functools.partial(pair_kernel, row_cuts=tuple(row_cuts), t...]
    psum x1 -> x0, blocking collectives: 11.1 us -> none  [shards(): return lax.psum(partial_proof, 'layer')]
  transfers between devices with their start and end apart: 2 -> 30, of which waited for: 2 -> 17; matrix products, arithmetic and copies ran while one was open for 1% -> 9% of each run, Pallas kernels for 0% -> 0%
where the time goes in v3:
time: 108 us
  waiting for transfers between devices  43.9 us (41%)
  starting transfers between devices  32 us (30%)
  Pallas kernels  16.1 us (15%)
  other arithmetic  11 us (10%)
  local copies, waits for them, and re-layouts  4.07 us (4%)
    ppermute x30, waiting for transfers between devices, permute(): return lax.ppermute(value, AXES, pairs)  43.9 us
    ppermute x30, starting transfers between devices, permute(): return lax.ppermute(value, AXES, pairs)  32 us
    pallas_call x1, Pallas kernels, pair_sums(): pl.pallas_call(functools.partial(pair_kernel, row_cuts=tuple(row_cuts), t...  10.7 us
    pallas_call x1, Pallas kernels, raw_partial(): pl.pallas_call(raw_kernel, grid=(feats // width,), in_specs=[pl.BlockSpec...  5.48 us
    unnamed x2, other arithmetic  4.02 us
  transfers between devices with their start and end apart: 30, of which 17 were waited for; matrix products, arithmetic and copies ran while one was open for 9% of the time, Pallas kernels for 0%

profile of v3, /device:TPU:4, one launch (start us, length us, event | category | flops | bytes accessed | tf_op | source)
XLA Modules:
  0.0 107.6 jit_solution(10608861073832232243)
XLA Ops:
  0.0 5.5 %raw.1 = f32[512,1024]{1,0:T(8,128)} custom-call(s32[8,11]{1,0:T(8,128)} %bitcast.40, bf16[1584,512]{1,0:T(8,128)(2,1)} %bitcast.34, bf16[1584,1024]{1,0:T(8,128)(2,1)} %geometry.1), custom_call_target="tpu_custom_call" | custom-call | flops 1660944384 | bytes 8388608 | tf_op jit(solution)/shard_map/raw/pallas_call | solution.py:83
  5.5 1.7 %constant_dynamic-slice_fusion.1 = (f32[4,1,32,1024]{3,2,1,0:T(8,128)S(1)}, f16[4,1,32,1024]{3,2,0,1:T(8,128)(2,1)S(1)}, f16[4,1,32,1024]{3,2,0,1:T(8,128)(2,1)S(1)}, f16[4,1,32,1024]{3,2,0,1:T(8,128)(2,1)S(1)}) fusion(f32[4,4,32,1024]{3,2,1,0:T(8,128)} %bitcast.33, s32[]{:T(128)S(6)} %select_n.172, s32[]{:T(128)S(6)} %select_n.176, s32[]{:T(128)S(6)} %select_n.174, ...), kind=kLoop, calls=%fused_computation.55 | loop fusion | flops 393216 | bytes 3407888 | tf_op jit(solution)/shard_map/jit(dynamic_index_in_dim)/dynamic_slice | solution.py:244
  7.2 3.1 %collective-permute-start.2 = (f16[128,1024]{1,0:T(8,128)(2,1)S(1)}, f16[128,1024]{1,0:T(8,128)(2,1)S(1)}, u32[]{:S(2)}, u32[]{:S(2)}) collective-permute-start(f16[128,1024]{1,0:T(8,128)(2,1)S(1)} %bitcast.37), channel_id=1, source_target_pairs={{0,192},{1,193},{2,194},{3,195},{4,196},{5,197},{6,198},{7,199},{8... | collective-permute-start | bytes 786440 | tf_op jit(solution)/shard_map/ppermute | solution.py:32
  10.3 2.2 %collective-permute-start = (f16[128,1024]{1,0:T(8,128)(2,1)S(1)}, f16[128,1024]{1,0:T(8,128)(2,1)S(1)}, u32[]{:S(2)}, u32[]{:S(2)}) collective-permute-start(f16[128,1024]{1,0:T(8,128)(2,1)S(1)} %bitcast.35), channel_id=1, source_target_pairs={{0,128},{1,129},{2,130},{3,131},{4,132},{5,133},{6,134},{7,135},{8... | collective-permute-start | bytes 786440 | tf_op jit(solution)/shard_map/ppermute | solution.py:32
  13.2 3.2 %constant_dynamic-update-slice_fusion.4 = (bf16[544,1024]{1,0:T(8,128)(2,1)}, bf16[16,1024]{1,0:T(8,128)(2,1)S(1)}) fusion(bf16[]{:T(256)} %bitcast.4, bf16[]{:T(256)} %bitcast.3, bf16[]{:T(256)} %bitcast.2, bf16[]{:T(256)} %bitcast.1, s32[1024]{0:T(1024)S(1)} %get-tuple-element.21, s32[1024]{0:T(1024)S(1)} %get-tuple-element.22, ...), kind=kLoop, calls=%fused_computation.35 | loop fusion | flops 163839 | bytes 74776
  16.4 5.1 %collective-permute-done.2 = f16[128,1024]{1,0:T(8,128)(2,1)S(1)} collective-permute-done((f16[128,1024]{1,0:T(8,128)(2,1)S(1)}, f16[128,1024]{1,0:T(8,128)(2,1)S(1)}, u32[]{:S(2)}, u32[]{:S(2)}) %collective-permute-start.2) | collective-permute-done | bytes 262176 | tf_op jit(solution)/shard_map/ppermute | solution.py:32
  21.5 3.4 %collective-permute-done.1 = f16[128,1024]{1,0:T(8,128)(2,1)S(1)} collective-permute-done((f16[128,1024]{1,0:T(8,128)(2,1)S(1)}, f16[128,1024]{1,0:T(8,128)(2,1)S(1)}, u32[]{:S(2)}, u32[]{:S(2)}) %collective-permute-start.1) | collective-permute-done | bytes 262176 | tf_op jit(solution)/shard_map/ppermute | solution.py:32
  26.0 3.2 %collective-permute-start.5 = (bf16[128,1024]{1,0:T(8,128)(2,1)S(1)}, bf16[128,1024]{1,0:T(8,128)(2,1)S(1)}, u32[]{:S(2)}, u32[]{:S(2)}) collective-permute-start(bf16[128,1024]{1,0:T(8,128)(2,1)S(1)} %get-tuple-element.20), channel_id=1, source_target_pairs={{0,192},{1,193},{2,194},{3,195},{4,196},{5,197},{6,198},{7,199},{8... | collective-permute-start | bytes 786440 | tf_op jit(solution)/shard_map/ppermute | solution.py:32
  29.3 1.3 %collective-permute-start.3 = (bf16[144,1024]{1,0:T(8,128)(2,1)S(1)}, bf16[144,1024]{1,0:T(8,128)(2,1)S(1)}, u32[]{:S(2)}, u32[]{:S(2)}) collective-permute-start(bf16[144,1024]{1,0:T(8,128)(2,1)S(1)} %pad_maximum_fusion.2.refs_1_.refs_11_), channel_id=1, source_target_pairs={{0,16},{1,17},{2,18},{3,19},{4,20},{5,21},{6,22},{7,23},{8,24},{9,... | collective-permute-start | bytes 884744 | tf_op jit(solution)/shard_map/ppermute | solution.py:32
  30.6 3.0 %collective-permute-done.4.refs_3_ = bf16[128,1024]{1,0:T(8,128)(2,1)S(1)} collective-permute-done((bf16[128,1024]{1,0:T(8,128)(2,1)S(1)}, bf16[128,1024]{1,0:T(8,128)(2,1)S(1)}, u32[]{:S(2)}, u32[]{:S(2)}) %collective-permute-start.4) | collective-permute-done | bytes 262176 | tf_op jit(solution)/shard_map/ppermute | solution.py:32
  33.7 1.3 %collective-permute-start.7 = (bf16[256,1024]{1,0:T(8,128)(2,1)S(1)}, bf16[256,1024]{1,0:T(8,128)(2,1)S(1)}, u32[]{:S(2)}, u32[]{:S(2)}) collective-permute-start(bf16[256,1024]{1,0:T(8,128)(2,1)S(1)} %pad_maximum_fusion.1), channel_id=1, source_target_pairs={{0,16},{1,17},{2,18},{3,19},{4,20},{5,21},{6,22},{7,23},{8,24},{9,... | collective-permute-start | bytes 1572872 | tf_op jit(solution)/shard_map/ppermute | solution.py:32
  34.9 1.9 %collective-permute-start.14 = (bf16[144,1024]{1,0:T(8,128)(2,1)S(1)}, bf16[144,1024]{1,0:T(8,128)(2,1)S(1)}, u32[]{:S(2)}, u32[]{:S(2)}) collective-permute-start(bf16[144,1024]{1,0:T(8,128)(2,1)S(1)} %pad_maximum_fusion.2.refs_1_.refs_11_), channel_id=1, source_target_pairs={{0,2},{1,15},{2,4},{3,1},{4,6},{5,3},{6,8},{7,5},{8,10},{9,7},{10,... | collective-permute-start | bytes 884744 | tf_op jit(solution)/shard_map/ppermute | solution.py:32
  37.4 1.9 %collective-permute-done.3.refs_2_ = bf16[144,1024]{1,0:T(8,128)(2,1)S(1)} collective-permute-done((bf16[144,1024]{1,0:T(8,128)(2,1)S(1)}, bf16[144,1024]{1,0:T(8,128)(2,1)S(1)}, u32[]{:S(2)}, u32[]{:S(2)}) %collective-permute-start.3) | collective-permute-done | bytes 294944 | tf_op jit(solution)/shard_map/ppermute | solution.py:32
  41.5 5.7 %collective-permute-done.7.refs_6_ = bf16[256,1024]{1,0:T(8,128)(2,1)S(1)} collective-permute-done((bf16[256,1024]{1,0:T(8,128)(2,1)S(1)}, bf16[256,1024]{1,0:T(8,128)(2,1)S(1)}, u32[]{:S(2)}, u32[]{:S(2)}) %collective-permute-start.7) | collective-permute-done | bytes 524320 | tf_op jit(solution)/shard_map/ppermute | solution.py:32
  47.6 2.0 %collective-permute-start.16 = (bf16[144,1024]{1,0:T(8,128)(2,1)S(1)}, bf16[144,1024]{1,0:T(8,128)(2,1)S(1)}, u32[]{:S(2)}, u32[]{:S(2)}) collective-permute-start(bf16[144,1024]{1,0:T(8,128)(2,1)S(1)} %collective-permute-done.14.refs_12_), channel_id=1, source_target_pairs={{0,2},{1,15},{2,4},{3,1},{4,6},{5,3},{6,8},{7,5},{8,10},{9,7},{10,... | collective-permute-start | bytes 884744 | tf_op jit(solution)/shard_map/ppermute | solution.py:32
  49.5 1.9 %collective-permute-start.17 = (bf16[144,1024]{1,0:T(8,128)(2,1)S(1)}, bf16[144,1024]{1,0:T(8,128)(2,1)S(1)}, u32[]{:S(2)}, u32[]{:S(2)}) collective-permute-start(bf16[144,1024]{1,0:T(8,128)(2,1)S(1)} %collective-permute-done.15.refs_13_), channel_id=1, source_target_pairs={{0,2},{1,15},{2,4},{3,1},{4,6},{5,3},{6,8},{7,5},{8,10},{9,7},{10,... | collective-permute-start | bytes 884744 | tf_op jit(solution)/shard_map/ppermute | solution.py:32
  51.5 3.5 %collective-permute-done.8.refs_7_ = bf16[128,1024]{1,0:T(8,128)(2,1)S(1)} collective-permute-done((bf16[128,1024]{1,0:T(8,128)(2,1)S(1)}, bf16[128,1024]{1,0:T(8,128)(2,1)S(1)}, u32[]{:S(2)}, u32[]{:S(2)}) %collective-permute-start.8) | collective-permute-done | bytes 262176 | tf_op jit(solution)/shard_map/ppermute | solution.py:32
  55.7 2.4 %collective-permute-start.11 = (bf16[128,1024]{1,0:T(8,128)(2,1)S(1)}, bf16[128,1024]{1,0:T(8,128)(2,1)S(1)}, u32[]{:S(2)}, u32[]{:S(2)}) collective-permute-start(bf16[128,1024]{1,0:T(8,128)(2,1)S(1)} %pad_maximum_fusion.3), channel_id=1, source_target_pairs={{32,16},{96,80},{160,144},{224,208}} | collective-permute-start | bytes 786440 | tf_op jit(solution)/shard_map/ppermute | solution.py:32
  58.3 3.0 %collective-permute-done.17.refs_15_ = bf16[144,1024]{1,0:T(8,128)(2,1)S(1)} collective-permute-done((bf16[144,1024]{1,0:T(8,128)(2,1)S(1)}, bf16[144,1024]{1,0:T(8,128)(2,1)S(1)}, u32[]{:S(2)}, u32[]{:S(2)}) %collective-permute-start.17) | collective-permute-done | bytes 294944 | tf_op jit(solution)/shard_map/ppermute | solution.py:32
  62.7 4.4 %collective-permute-done.18.refs_16_ = bf16[144,1024]{1,0:T(8,128)(2,1)} collective-permute-done((bf16[144,1024]{1,0:T(8,128)(2,1)S(1)}, bf16[144,1024]{1,0:T(8,128)(2,1)}, u32[]{:S(2)}, u32[]{:S(2)}) %collective-permute-start.18) | collective-permute-done | bytes 294944 | tf_op jit(solution)/shard_map/ppermute | solution.py:32
  67.8 2.4 %collective-permute-done.19.refs_17_ = bf16[144,1024]{1,0:T(8,128)(2,1)} collective-permute-done((bf16[144,1024]{1,0:T(8,128)(2,1)S(1)}, bf16[144,1024]{1,0:T(8,128)(2,1)}, u32[]{:S(2)}, u32[]{:S(2)}) %collective-permute-start.19) | collective-permute-done | bytes 294944 | tf_op jit(solution)/shard_map/ppermute | solution.py:32
  70.2 1.1 %fusion.5 = bf16[48,1024]{1,0:T(8,128)(2,1)S(1)} fusion(bf16[128,1024]{1,0:T(8,128)(2,1)S(1)} %get-tuple-element.20, bf16[16,1024]{1,0:T(8,128)(2,1)S(1)} %get-tuple-element.12, bf16[144,1024]{1,0:T(8,128)(2,1)} %copy-done.8, bf16[144,1024]{1,0:T(8,128)(2,1)S(1)} %collective-permute-done.17.refs_15_, bf16[144,1024]{1,0:T(8,128)(2,1)} %collective-permute-done.19.refs_17_, ...), kind=kLoop, calls=%fused_computation.19 | loop fusion | flops 540672 | bytes 983047 | tf_op jit(solution)/shard_map/select_n | solution.py:274
  71.3 3.3 %collective-permute-start.21 = (bf16[48,1024]{1,0:T(8,128)(2,1)S(1)}, bf16[48,1024]{1,0:T(8,128)(2,1)S(1)}, u32[]{:S(2)}, u32[]{:S(2)}) collective-permute-start(bf16[48,1024]{1,0:T(8,128)(2,1)S(1)} %fusion.5), channel_id=1, source_target_pairs={{32,16},{34,18},{36,20},{38,22},{43,27},{45,29},{47,31},{96,80},{9... | collective-permute-start | bytes 294920 | tf_op jit(solution)/shard_map/ppermute | solution.py:32
  74.7 2.2 %collective-permute-done.21 = bf16[48,1024]{1,0:T(8,128)(2,1)S(1)} collective-permute-done((bf16[48,1024]{1,0:T(8,128)(2,1)S(1)}, bf16[48,1024]{1,0:T(8,128)(2,1)S(1)}, u32[]{:S(2)}, u32[]{:S(2)}) %collective-permute-start.21) | collective-permute-done | bytes 98336 | tf_op jit(solution)/shard_map/ppermute | solution.py:32
  79.1 10.7 %pairs.1 = f32[4,2176]{1,0:T(4,128)} custom-call(s32[1]{0:T(128)} %bitcast.refs_0_, bf16[144,1024]{1,0:T(8,128)(2,1)} %copy-done.4, bf16[144,1024]{1,0:T(8,128)(2,1)} %copy-done.5, bf16[128,1024]{1,0:T(8,128)(2,1)} %copy-done, bf16[128,1024]{1,0:T(8,128)(2,1)} %copy-done.2, bf16[128,1024]{1,0:T(8,128)(2,1)} %copy-done.3, bf16[256,1024]{1,0:T(8,128)(2,1)} %copy-done.1, ...), custom_call_target="tpu_custom_call" | custom-call | flops 4706009088 | bytes 6619136 | tf_op jit(solution)/shard_map/pairs/pallas_call | solution.py:194
  90.5 1.2 %collective-permute-done.23 = f32[4,1152]{1,0:T(4,128)S(1)} collective-permute-done((f32[4,1152]{1,0:T(4,128)S(1)}, f32[4,1152]{1,0:T(4,128)S(1)}, u32[]{:S(2)}, u32[]{:S(2)}) %collective-permute-start.23) | collective-permute-done | bytes 18464 | tf_op jit(solution)/shard_map/ppermute | solution.py:32
  93.0 1.3 %collective-permute-start.25 = (f32[4,128]{1,0:T(4,128)S(1)}, f32[4,128]{1,0:T(4,128)S(1)}, u32[]{:S(2)}, u32[]{:S(2)}) collective-permute-start(f32[4,128]{1,0:T(4,128)S(1)} %slice_add_fusion.2), channel_id=1, source_target_pairs={{0,32},{64,96},{128,160},{192,224}} | collective-permute-start | bytes 6152 | tf_op jit(solution)/shard_map/ppermute | solution.py:32
  94.3 1.3 %collective-permute-start.26 = (f32[4,128]{1,0:T(4,128)S(1)}, f32[4,128]{1,0:T(4,128)S(1)}, u32[]{:S(2)}, u32[]{:S(2)}) collective-permute-start(f32[4,128]{1,0:T(4,128)S(1)} %slice_add_fusion.2), channel_id=1, source_target_pairs={{16,32},{80,96},{144,160},{208,224}} | collective-permute-start | bytes 6152 | tf_op jit(solution)/shard_map/ppermute | solution.py:32
  95.6 4.4 %collective-permute-done.25 = f32[4,128]{1,0:T(4,128)S(1)} collective-permute-done((f32[4,128]{1,0:T(4,128)S(1)}, f32[4,128]{1,0:T(4,128)S(1)}, u32[]{:S(2)}, u32[]{:S(2)}) %collective-permute-start.25) | collective-permute-done | bytes 2080 | tf_op jit(solution)/shard_map/ppermute | solution.py:32
  100.6 2.5 %collective-permute-start.28 = (f32[4,4,128]{2,1,0:T(4,128)S(1)}, f32[4,4,128]{2,1,0:T(4,128)S(1)}, u32[]{:S(2)}, u32[]{:S(2)}) collective-permute-start(f32[4,4,128]{2,1,0:T(4,128)S(1)} %pad_add_fusion), channel_id=1, source_target_pairs={{0,64},{1,65},{2,66},{3,67},{4,68},{5,69},{6,70},{7,71},{8,72},{9,... | collective-permute-start | bytes 24584 | tf_op jit(solution)/shard_map/ppermute | solution.py:32
  103.8 1.6 %collective-permute-done.27 = f32[4,4,128]{2,1,0:T(4,128)S(1)} collective-permute-done((f32[4,4,128]{2,1,0:T(4,128)S(1)}, f32[4,4,128]{2,1,0:T(4,128)S(1)}, u32[]{:S(2)}, u32[]{:S(2)}) %collective-permute-start.27) | collective-permute-done | bytes 8224 | tf_op jit(solution)/shard_map/ppermute | solution.py:32
  105.5 1.2 %collective-permute-done.29 = f32[4,4,128]{2,1,0:T(4,128)S(1)} collective-permute-done((f32[4,4,128]{2,1,0:T(4,128)S(1)}, f32[4,4,128]{2,1,0:T(4,128)S(1)}, u32[]{:S(2)}, u32[]{:S(2)}) %collective-permute-start.29) | collective-permute-done | bytes 8224 | tf_op jit(solution)/shard_map/ppermute | solution.py:32
  (104 shorter events, 14.1 us)
Async XLA Ops:
  7.2 14.3 %collective-permute-start.2 = (f16[128,1024]{1,0:T(8,128)(2,1)S(1)}, f16[128,1024]{1,0:T(8,128)(2,1)S(1)}, u32[]{:S(2)}, u32[]{:S(2)}) collective-permute-start(f16[128,1024]{1,0:T(8,128)(2,1)S(1)} %bitcast.37), channel_id=1, source_target_pairs={{0,192},{1,193},{2,194},{3,195},{4,196},{5,197},{6,198},{7,199},{8... | collective-permute-start | bytes 786440 | tf_op jit(solution)/shard_map/ppermute | solution.py:32
  10.3 14.6 %collective-permute-start.1 = (f16[128,1024]{1,0:T(8,128)(2,1)S(1)}, f16[128,1024]{1,0:T(8,128)(2,1)S(1)}, u32[]{:S(2)}, u32[]{:S(2)}) collective-permute-start(f16[128,1024]{1,0:T(8,128)(2,1)S(1)} %bitcast.36), channel_id=1, source_target_pairs={{0,64},{1,65},{2,66},{3,67},{4,68},{5,69},{6,70},{7,71},{8,72},{9,... | collective-permute-start | bytes 786440 | tf_op jit(solution)/shard_map/ppermute | solution.py:32
  10.3 14.6 %collective-permute-start = (f16[128,1024]{1,0:T(8,128)(2,1)S(1)}, f16[128,1024]{1,0:T(8,128)(2,1)S(1)}, u32[]{:S(2)}, u32[]{:S(2)}) collective-permute-start(f16[128,1024]{1,0:T(8,128)(2,1)S(1)} %bitcast.35), channel_id=1, source_target_pairs={{0,128},{1,129},{2,130},{3,131},{4,132},{5,133},{6,134},{7,135},{8... | collective-permute-start | bytes 786440 | tf_op jit(solution)/shard_map/ppermute | solution.py:32
  26.0 7.6 %collective-permute-start.4 = (bf16[128,1024]{1,0:T(8,128)(2,1)S(1)}, bf16[128,1024]{1,0:T(8,128)(2,1)S(1)}, u32[]{:S(2)}, u32[]{:S(2)}) collective-permute-start(bf16[128,1024]{1,0:T(8,128)(2,1)S(1)} %get-tuple-element.20), channel_id=1, source_target_pairs={{0,64},{1,65},{2,66},{3,67},{4,68},{5,69},{6,70},{7,71},{8,72},{9,... | collective-permute-start | bytes 786440 | tf_op jit(solution)/shard_map/ppermute | solution.py:32
  26.0 7.6 %collective-permute-start.5 = (bf16[128,1024]{1,0:T(8,128)(2,1)S(1)}, bf16[128,1024]{1,0:T(8,128)(2,1)S(1)}, u32[]{:S(2)}, u32[]{:S(2)}) collective-permute-start(bf16[128,1024]{1,0:T(8,128)(2,1)S(1)} %get-tuple-element.20), channel_id=1, source_target_pairs={{0,192},{1,193},{2,194},{3,195},{4,196},{5,197},{6,198},{7,199},{8... | collective-permute-start | bytes 786440 | tf_op jit(solution)/shard_map/ppermute | solution.py:32
  29.3 10.0 %collective-permute-start.3 = (bf16[144,1024]{1,0:T(8,128)(2,1)S(1)}, bf16[144,1024]{1,0:T(8,128)(2,1)S(1)}, u32[]{:S(2)}, u32[]{:S(2)}) collective-permute-start(bf16[144,1024]{1,0:T(8,128)(2,1)S(1)} %pad_maximum_fusion.2.refs_1_.refs_11_), channel_id=1, source_target_pairs={{0,16},{1,17},{2,18},{3,19},{4,20},{5,21},{6,22},{7,23},{8,24},{9,... | collective-permute-start | bytes 884744 | tf_op jit(solution)/shard_map/ppermute | solution.py:32
  33.7 13.6 %collective-permute-start.7 = (bf16[256,1024]{1,0:T(8,128)(2,1)S(1)}, bf16[256,1024]{1,0:T(8,128)(2,1)S(1)}, u32[]{:S(2)}, u32[]{:S(2)}) collective-permute-start(bf16[256,1024]{1,0:T(8,128)(2,1)S(1)} %pad_maximum_fusion.1), channel_id=1, source_target_pairs={{0,16},{1,17},{2,18},{3,19},{4,20},{5,21},{6,22},{7,23},{8,24},{9,... | collective-permute-start | bytes 1572872 | tf_op jit(solution)/shard_map/ppermute | solution.py:32
  34.9 12.6 %collective-permute-start.14 = (bf16[144,1024]{1,0:T(8,128)(2,1)S(1)}, bf16[144,1024]{1,0:T(8,128)(2,1)S(1)}, u32[]{:S(2)}, u32[]{:S(2)}) collective-permute-start(bf16[144,1024]{1,0:T(8,128)(2,1)S(1)} %pad_maximum_fusion.2.refs_1_.refs_11_), channel_id=1, source_target_pairs={{0,2},{1,15},{2,4},{3,1},{4,6},{5,3},{6,8},{7,5},{8,10},{9,7},{10,... | collective-permute-start | bytes 884744 | tf_op jit(solution)/shard_map/ppermute | solution.py:32
  36.9 12.7 %collective-permute-start.15 = (bf16[144,1024]{1,0:T(8,128)(2,1)S(1)}, bf16[144,1024]{1,0:T(8,128)(2,1)S(1)}, u32[]{:S(2)}, u32[]{:S(2)}) collective-permute-start(bf16[144,1024]{1,0:T(8,128)(2,1)S(1)} %pad_maximum_fusion.2.refs_1_.refs_11_), channel_id=1, source_target_pairs={{0,15},{1,2},{2,1},{3,4},{4,3},{5,6},{6,5},{7,8},{8,7},{9,10},{10,... | collective-permute-start | bytes 884744 | tf_op jit(solution)/shard_map/ppermute | solution.py:32
  41.5 10.0 %collective-permute-start.6 = (bf16[128,1024]{1,0:T(8,128)(2,1)S(1)}, bf16[128,1024]{1,0:T(8,128)(2,1)S(1)}, u32[]{:S(2)}, u32[]{:S(2)}) collective-permute-start(bf16[128,1024]{1,0:T(8,128)(2,1)S(1)} %get-tuple-element.10), channel_id=1, source_target_pairs={{0,64},{1,193},{2,66},{3,195},{4,68},{5,197},{6,70},{7,199},{8,72}... | collective-permute-start | bytes 786440 | tf_op jit(solution)/shard_map/ppermute | solution.py:32
  47.3 7.7 %collective-permute-start.8 = (bf16[128,1024]{1,0:T(8,128)(2,1)S(1)}, bf16[128,1024]{1,0:T(8,128)(2,1)S(1)}, u32[]{:S(2)}, u32[]{:S(2)}) collective-permute-start(bf16[128,1024]{1,0:T(8,128)(2,1)S(1)} %slice_select_fusion), channel_id=1, source_target_pairs={{0,64},{1,193},{2,66},{3,195},{4,68},{5,197},{6,70},{7,199},{8,72}... | collective-permute-start | bytes 786440 | tf_op jit(solution)/shard_map/ppermute | solution.py:32
  47.4 31.6 %collective-permute-start.9 = (bf16[544,1024]{1,0:T(8,128)(2,1)}, bf16[544,1024]{1,0:T(8,128)(2,1)}, u32[]{:S(2)}, u32[]{:S(2)}) collective-permute-start(bf16[544,1024]{1,0:T(8,128)(2,1)} %get-tuple-element.9), channel_id=1, source_target_pairs={{0,1},{1,0},{2,3},{3,2},{4,5},{5,4},{6,7},{7,6},{8,9},{9,8},{10,11... | collective-permute-start | bytes 3342344 | tf_op jit(solution)/shard_map/ppermute | solution.py:32
  47.5 22.7 %copy-start.7 = (bf16[144,1024]{1,0:T(8,128)(2,1)}, bf16[144,1024]{1,0:T(8,128)(2,1)S(1)}, u32[]{:S(2)}) copy-start(bf16[144,1024]{1,0:T(8,128)(2,1)S(1)} %collective-permute-done.14.refs_12_) | copy-start | bytes 884740
  47.6 10.6 %collective-permute-start.16 = (bf16[144,1024]{1,0:T(8,128)(2,1)S(1)}, bf16[144,1024]{1,0:T(8,128)(2,1)S(1)}, u32[]{:S(2)}, u32[]{:S(2)}) collective-permute-start(bf16[144,1024]{1,0:T(8,128)(2,1)S(1)} %collective-permute-done.14.refs_12_), channel_id=1, source_target_pairs={{0,2},{1,15},{2,4},{3,1},{4,6},{5,3},{6,8},{7,5},{8,10},{9,7},{10,... | collective-permute-start | bytes 884744 | tf_op jit(solution)/shard_map/ppermute | solution.py:32
  49.5 11.8 %collective-permute-start.17 = (bf16[144,1024]{1,0:T(8,128)(2,1)S(1)}, bf16[144,1024]{1,0:T(8,128)(2,1)S(1)}, u32[]{:S(2)}, u32[]{:S(2)}) collective-permute-start(bf16[144,1024]{1,0:T(8,128)(2,1)S(1)} %collective-permute-done.15.refs_13_), channel_id=1, source_target_pairs={{0,2},{1,15},{2,4},{3,1},{4,6},{5,3},{6,8},{7,5},{8,10},{9,7},{10,... | collective-permute-start | bytes 884744 | tf_op jit(solution)/shard_map/ppermute | solution.py:32
  55.1 24.0 %collective-permute-start.10 = (bf16[512,1024]{1,0:T(8,128)(2,1)S(1)}, bf16[512,1024]{1,0:T(8,128)(2,1)}, u32[]{:S(2)}, u32[]{:S(2)}) collective-permute-start(bf16[512,1024]{1,0:T(8,128)(2,1)S(1)} %pad_maximum_fusion), channel_id=1, source_target_pairs={{0,1},{1,0},{2,3},{3,2},{4,5},{5,4},{6,7},{7,6},{8,9},{9,8},{10,11... | collective-permute-start | bytes 3145736 | tf_op jit(solution)/shard_map/ppermute | solution.py:32
  55.7 6.3 %collective-permute-start.11 = (bf16[128,1024]{1,0:T(8,128)(2,1)S(1)}, bf16[128,1024]{1,0:T(8,128)(2,1)S(1)}, u32[]{:S(2)}, u32[]{:S(2)}) collective-permute-start(bf16[128,1024]{1,0:T(8,128)(2,1)S(1)} %pad_maximum_fusion.3), channel_id=1, source_target_pairs={{32,16},{96,80},{160,144},{224,208}} | collective-permute-start | bytes 786440 | tf_op jit(solution)/shard_map/ppermute | solution.py:32
  58.2 20.8 %copy-start.9 = (bf16[144,1024]{1,0:T(8,128)(2,1)}, bf16[144,1024]{1,0:T(8,128)(2,1)S(1)}, u32[]{:S(2)}) copy-start(bf16[144,1024]{1,0:T(8,128)(2,1)S(1)} %collective-permute-done.16.refs_14_) | copy-start | bytes 884740
  58.2 8.9 %collective-permute-start.18 = (bf16[144,1024]{1,0:T(8,128)(2,1)S(1)}, bf16[144,1024]{1,0:T(8,128)(2,1)}, u32[]{:S(2)}, u32[]{:S(2)}) collective-permute-start(bf16[144,1024]{1,0:T(8,128)(2,1)S(1)} %collective-permute-done.16.refs_14_), channel_id=1, source_target_pairs={{0,2},{1,15},{2,4},{3,1},{4,6},{5,3},{6,8},{7,5},{8,10},{9,7},{10,... | collective-permute-start | bytes 884744 | tf_op jit(solution)/shard_map/ppermute | solution.py:32
  61.3 8.9 %collective-permute-start.19 = (bf16[144,1024]{1,0:T(8,128)(2,1)S(1)}, bf16[144,1024]{1,0:T(8,128)(2,1)}, u32[]{:S(2)}, u32[]{:S(2)}) collective-permute-start(bf16[144,1024]{1,0:T(8,128)(2,1)S(1)} %collective-permute-done.17.refs_15_), channel_id=1, source_target_pairs={{0,2},{1,15},{2,4},{3,1},{4,6},{5,3},{6,8},{7,5},{8,10},{9,7},{10,... | collective-permute-start | bytes 884744 | tf_op jit(solution)/shard_map/ppermute | solution.py:32
  62.0 5.1 %collective-permute-start.12 = (bf16[128,1024]{1,0:T(8,128)(2,1)S(1)}, bf16[128,1024]{1,0:T(8,128)(2,1)S(1)}, u32[]{:S(2)}, u32[]{:S(2)}) collective-permute-start(bf16[128,1024]{1,0:T(8,128)(2,1)S(1)} %collective-permute-done.11), channel_id=1, source_target_pairs={{16,0},{80,64},{144,128},{208,192}} | collective-permute-start | bytes 786440 | tf_op jit(solution)/shard_map/ppermute | solution.py:32
  67.1 12.0 %collective-permute-start.20 = (bf16[144,1024]{1,0:T(8,128)(2,1)}, bf16[144,1024]{1,0:T(8,128)(2,1)}, u32[]{:S(2)}, u32[]{:S(2)}) collective-permute-start(bf16[144,1024]{1,0:T(8,128)(2,1)} %collective-permute-done.18.refs_16_), channel_id=1, source_target_pairs={{0,2},{1,15},{2,4},{3,1},{4,6},{5,3},{6,8},{7,5},{8,10},{9,7},{10,... | collective-permute-start | bytes 884744 | tf_op jit(solution)/shard_map/ppermute | solution.py:32
  67.2 11.1 %collective-permute-start.13 = (bf16[128,1024]{1,0:T(8,128)(2,1)S(1)}, bf16[128,1024]{1,0:T(8,128)(2,1)S(1)}, u32[]{:S(2)}, u32[]{:S(2)}) collective-permute-start(bf16[128,1024]{1,0:T(8,128)(2,1)S(1)} %add.132), channel_id=1, source_target_pairs={{0,1},{16,17},{64,65},{80,81},{128,129},{144,145},{192,193},{208,2... | collective-permute-start | bytes 786440 | tf_op jit(solution)/shard_map/ppermute | solution.py:32
  71.3 5.5 %collective-permute-start.21 = (bf16[48,1024]{1,0:T(8,128)(2,1)S(1)}, bf16[48,1024]{1,0:T(8,128)(2,1)S(1)}, u32[]{:S(2)}, u32[]{:S(2)}) collective-permute-start(bf16[48,1024]{1,0:T(8,128)(2,1)S(1)} %fusion.5), channel_id=1, source_target_pairs={{32,16},{34,18},{36,20},{38,22},{43,27},{45,29},{47,31},{96,80},{9... | collective-permute-start | bytes 294920 | tf_op jit(solution)/shard_map/ppermute | solution.py:32
  76.9 0.7 collective-permute-start.22
  90.5 1.2 %collective-permute-start.23 = (f32[4,1152]{1,0:T(4,128)S(1)}, f32[4,1152]{1,0:T(4,128)S(1)}, u32[]{:S(2)}, u32[]{:S(2)}) collective-permute-start(f32[4,1152]{1,0:T(4,128)S(1)} %slice.158), channel_id=1, source_target_pairs={{0,1},{1,0},{2,3},{3,2},{4,5},{5,4},{6,7},{7,6},{8,9},{9,8},{10,11... | collective-permute-start | bytes 55304 | tf_op jit(solution)/shard_map/ppermute | solution.py:32
  92.4 7.7 %collective-permute-start.24 = (f32[4,512]{1,0:T(4,128)S(1)}, f32[4,512]{1,0:T(4,128)S(1)}, u32[]{:S(2)}, u32[]{:S(2)}) collective-permute-start(f32[4,512]{1,0:T(4,128)S(1)} %slice.161), channel_id=1, source_target_pairs={{0,16},{1,17},{2,18},{3,19},{4,20},{5,21},{6,22},{7,23},{8,24},{9,... | collective-permute-start | bytes 24584 | tf_op jit(solution)/shard_map/ppermute | solution.py:32
  93.0 7.0 %collective-permute-start.25 = (f32[4,128]{1,0:T(4,128)S(1)}, f32[4,128]{1,0:T(4,128)S(1)}, u32[]{:S(2)}, u32[]{:S(2)}) collective-permute-start(f32[4,128]{1,0:T(4,128)S(1)} %slice_add_fusion.2), channel_id=1, source_target_pairs={{0,32},{64,96},{128,160},{192,224}} | collective-permute-start | bytes 6152 | tf_op jit(solution)/shard_map/ppermute | solution.py:32
  94.3 5.7 %collective-permute-start.26 = (f32[4,128]{1,0:T(4,128)S(1)}, f32[4,128]{1,0:T(4,128)S(1)}, u32[]{:S(2)}, u32[]{:S(2)}) collective-permute-start(f32[4,128]{1,0:T(4,128)S(1)} %slice_add_fusion.2), channel_id=1, source_target_pairs={{16,32},{80,96},{144,160},{208,224}} | collective-permute-start | bytes 6152 | tf_op jit(solution)/shard_map/ppermute | solution.py:32
  100.2 5.2 %collective-permute-start.27 = (f32[4,4,128]{2,1,0:T(4,128)S(1)}, f32[4,4,128]{2,1,0:T(4,128)S(1)}, u32[]{:S(2)}, u32[]{:S(2)}) collective-permute-start(f32[4,4,128]{2,1,0:T(4,128)S(1)} %pad_add_fusion), channel_id=1, source_target_pairs={{0,128},{1,129},{2,130},{3,131},{4,132},{5,133},{6,134},{7,135},{8... | collective-permute-start | bytes 24584 | tf_op jit(solution)/shard_map/ppermute | solution.py:32
  100.6 4.9 %collective-permute-start.28 = (f32[4,4,128]{2,1,0:T(4,128)S(1)}, f32[4,4,128]{2,1,0:T(4,128)S(1)}, u32[]{:S(2)}, u32[]{:S(2)}) collective-permute-start(f32[4,4,128]{2,1,0:T(4,128)S(1)} %pad_add_fusion), channel_id=1, source_target_pairs={{0,64},{1,65},{2,66},{3,67},{4,68},{5,69},{6,70},{7,71},{8,72},{9,... | collective-permute-start | bytes 24584 | tf_op jit(solution)/shard_map/ppermute | solution.py:32
  103.1 3.7 %collective-permute-start.29 = (f32[4,4,128]{2,1,0:T(4,128)S(1)}, f32[4,4,128]{2,1,0:T(4,128)S(1)}, u32[]{:S(2)}, u32[]{:S(2)}) collective-permute-start(f32[4,4,128]{2,1,0:T(4,128)S(1)} %pad_add_fusion), channel_id=1, source_target_pairs={{0,192},{1,193},{2,194},{3,195},{4,196},{5,197},{6,198},{7,199},{8... | collective-permute-start | bytes 24584 | tf_op jit(solution)/shard_map/ppermute | solution.py:32
  (13 other events, 113.0 us)

commit v4 on v3

--- a/solution.py
+++ b/solution.py
@@ -99,12 +99,12 @@
     )(pattern.T, showers.T, geometry)
 
 
-def pair_kernel(*refs, row_cuts, tag_cuts, col_sizes, n_args, apart):
+def pair_kernel(*refs, row_cuts, tag_cuts, col_sizes, n_args, apart, diag):
     n_cols = len(col_sizes)
-    odd_here = refs[0]
-    args = refs[1 : 1 + n_args]
-    cols = refs[1 + n_args : 1 + n_args + n_cols]
-    out, rows_at, cols_at, row_tags, col_tags, row_sems, col_sems, tag_sems = refs[1 + n_args + n_cols :]
+    odd_here, before = refs[:2]
+    args = refs[2 : 2 + n_args]
+    cols = refs[2 + n_args : 2 + n_args + n_cols]
+    out, rows_at, cols_at, row_tags, col_tags, row_sems, col_sems, tag_sems = refs[2 + n_args + n_cols :]
 
     def start(source, first, size, target, place, sem):
         copy = pltpu.make_async_copy(
@@ -137,7 +137,7 @@
         while waited < len(row_copies) and row_copies[waited][0] < first + size:
             row_copies[waited][1].wait()
             waited += 1
-        odd = first >= 4 * CHUNK
+        odd = first >= 2 * CHUNK
         set_of = 0 if odd else first // CHUNK
         tag = row_tags[pl.ds(set_of * TAG + 4, 1), pl.ds(0, BLOCK)].astype(jnp.float32) - 1.0
         bins, _ = bin_of(tag)
@@ -164,7 +164,7 @@
                 if odd and group == apart:
                     continue
                 block = cubes[group * PIECE - low : (group + 1) * PIECE - low]
-                if first == 0 and group < BLOCK // PIECE:
+                if diag and first == 0 and group < BLOCK // PIECE:
                     lane = lax.broadcasted_iota(jnp.int32, block.shape, 1)
                     sub = lax.broadcasted_iota(jnp.int32, block.shape, 0)
                     block = jnp.where(lane == sub + group * PIECE, 0.0, block)
@@ -180,13 +180,13 @@
                 n_one += is_one
                 n_zero += is_zero
         lanes = pl.ds(first, size)
-        out[0:1, lanes] = jnp.sum(one, axis=0, keepdims=True)
-        out[1:2, lanes] = jnp.sum(zero, axis=0, keepdims=True)
-        out[2:3, lanes] = n_one
-        out[3:4, lanes] = n_zero
-
-
-def pair_sums(odd_here, args, row_cuts, tag_cuts, cols, apart):
+        out[0:1, lanes] = before[0:1, lanes] + jnp.sum(one, axis=0, keepdims=True)
+        out[1:2, lanes] = before[1:2, lanes] + jnp.sum(zero, axis=0, keepdims=True)
+        out[2:3, lanes] = before[2:3, lanes] + n_one
+        out[3:4, lanes] = before[3:4, lanes] + n_zero
+
+
+def pair_sums(odd_here, before, args, row_cuts, tag_cuts, cols, apart, diag, name):
     col_sizes = tuple(size for _, size in cols)
     total, depth = sum(size for _, _, size in row_cuts), sum(col_sizes)
     feats = args[0].shape[1]
@@ -199,8 +199,10 @@
             col_sizes=col_sizes,
             n_args=len(args),
             apart=apart,
+            diag=diag,
         ),
-        in_specs=[pl.BlockSpec(memory_space=pltpu.SMEM)] + [hbm] * (len(args) + len(cols)),
+        in_specs=[pl.BlockSpec(memory_space=pltpu.SMEM), pl.BlockSpec(memory_space=pltpu.VMEM)]
+        + [hbm] * (len(args) + len(cols)),
         out_specs=pl.BlockSpec(memory_space=pltpu.VMEM),
         out_shape=jax.ShapeDtypeStruct((4, total), jnp.float32),
         scratch_shapes=[
@@ -218,8 +220,8 @@
             bytes_accessed=2 * (total + depth) * feats,
             transcendentals=0,
         ),
-        name="pairs",
-    )(odd_here, *args, *[c for c, _ in cols])
+        name=name,
+    )(odd_here, before, *args, *[c for c, _ in cols])
 
 
 def shards(showers, geometry, pattern, bins, sources):
@@ -252,22 +254,23 @@
     own = jnp.concatenate([tag, (raw * scale).astype(jnp.bfloat16)], axis=0)
 
     rows_of = lambda value: value[TAG:]
-    same = [permute(own, same_core)]
-    cross = [permute(own, cross_core)]
+    same, cross = [], []
+    for turn in range(4):
+        same.append(permute(same[-1] if same else own, same_core))
+        if turn < 3:
+            cross.append(permute(cross[-1], same_core) if cross else permute(own, cross_core))
+    own_other = permute(own, swap_core)
+    same_other = [permute(value, swap_core) for value in same]
+    cross_other = [permute(value, swap_core) for value in cross]
+
+    y_way = lambda y, x, z, c: ((y + 1 - 2 * c) % NY, x, z, c)
     x1 = permute(own, swap_x)
     ya = permute(rows_of(own), along_y(1))
     yb = permute(rows_of(own), along_y(3))
-    same.append(permute(same[0], same_core))
-    cross.append(permute(cross[0], same_core))
-    y_way = lambda y, x, z, c: ((y + 1 - 2 * c) % NY, x, z, c)
     y2 = permute(jnp.where(c == 0, ya, yb), y_way)
-    xx = permute(jnp.concatenate([ya, yb], axis=0), swap_x)
-    near = permute(jnp.concatenate([own, x1, ya, yb], axis=0), swap_core)
-    same.append(permute(same[1], same_core))
-    cross.append(permute(cross[1], same_core))
-    w2 = permute(jnp.where(c == 0, xx[:BLOCK], xx[BLOCK:]), y_way)
-    far = permute(jnp.concatenate([xx, y2, w2], axis=0), swap_core)
-    same.append(permute(same[2], same_core))
+    xa = permute(ya, swap_x)
+    xb = permute(yb, swap_x)
+    w2 = permute(jnp.where(c == 0, xa, xb), y_way)
 
     head = TAG + PIECE
     held = [own, same[0], same[1], same[2], same[2], cross[2], cross[1], cross[0]]
@@ -283,32 +286,30 @@
         keep=lambda y, x, z, c: x == 2 and z == 3 and c == 0,
     )
     piece = piece_near + piece_far
-    odd = jnp.concatenate(
-        [own[TAG:head], yb[:PIECE], y2[:PIECE], ya[:PIECE]], axis=0
-    )
+    piece = piece + permute(piece, swap_core)
+    odd = jnp.concatenate([own[TAG:head], yb[:PIECE], y2[:PIECE], ya[:PIECE]], axis=0)
     at_start = lambda y, x, z, c: z == 0 and c == 0
     odd = permute(odd, to_one, keep=lambda *a: a[1] == 2 and at_start(*a))
     odd = odd + permute(odd, swap_x, keep=lambda *a: a[1] == 1 and at_start(*a))
-    odd = odd + permute(odd, swap_core, keep=lambda *a: a[1] < 2 and at_start(*a))
-
-    args = [own, x1, ya, yb, y2, xx, w2, near, far, odd]
-    tagged = BLOCK + TAG
-    tag_cuts = [(0, 0), (1, 0), (7, 0), (7, tagged)]
-    row_cuts = [(0, TAG, BLOCK), (3, 0, BLOCK), (4, 0, BLOCK), (2, 0, BLOCK)]
-    row_cuts += [(1, TAG, BLOCK), (5, BLOCK, BLOCK), (6, 0, BLOCK), (5, 0, BLOCK)]
-    row_cuts += [(7, TAG, BLOCK), (7, 2 * tagged + BLOCK, BLOCK)]
-    row_cuts += [(8, 2 * BLOCK, BLOCK), (7, 2 * tagged, BLOCK)]
-    row_cuts += [(7, tagged + TAG, BLOCK), (8, BLOCK, BLOCK)]
-    row_cuts += [(8, 3 * BLOCK, BLOCK), (8, 0, BLOCK), (9, 0, BLOCK)]
-    cols = [own, same[0], cross[0], same[1], cross[1], same[2], cross[2], same[3]]
-    cols = [(value, BLOCK) for value in cols] + [(piece, PIECE)]
-    odd_here = ((x < 2) & (z == 0)).astype(jnp.int32).reshape(1)
-    stats = pair_sums(odd_here, args, row_cuts, tag_cuts, cols, 8 * BLOCK // PIECE)
-
-    theirs = permute(stats[:, 2 * CHUNK :], swap_core)
-    mine = stats[:, : 2 * CHUNK] + theirs[:, : 2 * CHUNK]
-    odd_stats = stats[:, 4 * CHUNK :] + theirs[:, 2 * CHUNK :]
-    kept = mine[:, :CHUNK] + permute(mine[:, CHUNK:], swap_x)
+
+    args = [own, x1, ya, yb, y2, xa, xb, w2, odd]
+    tag_cuts = [(0, 0), (1, 0)]
+    row_cuts = [(0, TAG), (3, 0), (4, 0), (2, 0), (1, TAG), (6, 0), (7, 0), (5, 0), (8, 0)]
+    row_cuts = [(arg, first, BLOCK) for arg, first in row_cuts]
+    whole = lambda values: [(value, BLOCK) for value in values]
+    early = whole([own, own_other])
+    for turn in range(2):
+        early += whole([same[turn], cross[turn], same_other[turn], cross_other[turn]])
+    late = whole([same[2], cross[2], same_other[2], cross_other[2], same[3], same_other[3]])
+    late = late + [(piece, PIECE)]
+    odd_here = ((x < 2) & (z == 0) & (c == 0)).astype(jnp.int32).reshape(1)
+    blank = jnp.zeros((4, 2 * CHUNK + BLOCK), jnp.float32)
+    stats = pair_sums(odd_here, blank, args, row_cuts, tag_cuts, early, -1, True, "early")
+    apart = 6 * BLOCK // PIECE
+    stats = pair_sums(odd_here, stats, args, row_cuts, tag_cuts, late, apart, False, "late")
+
+    kept = stats[:, :CHUNK] + permute(stats[:, CHUNK : 2 * CHUNK], swap_x)
+    odd_stats = stats[:, 2 * CHUNK :]
     odd_total = jnp.zeros_like(odd_stats)
     for start in (0, 1):
         odd_total = odd_total + permute(

time: 108 us -> 109 us (level)
  Pallas kernels: 16.1 us -> 20.9 us
  waiting for transfers between devices: 43.9 us -> 40.2 us
  other arithmetic: 11 us -> 8.07 us
  starting transfers between devices: 32 us -> 34.8 us
    pallas_call x1 -> x2, Pallas kernels: 10.7 us -> 15.4 us  [pair_sums(): pl.pallas_call(functools.partial(pair_kernel, row_cuts=tuple(row_cuts), t...]
    unnamed x2 -> x0, other arithmetic: 4.02 us -> none
    ppermute x30 -> x36, waiting for transfers between devices: 43.9 us -> 40.2 us  [permute(): return lax.ppermute(value, AXES, pairs)]
    ppermute x30 -> x36, starting transfers between devices: 32 us -> 34.8 us  [permute(): return lax.ppermute(value, AXES, pairs)]
    convert_element_type x0 -> x2, other arithmetic: none -> 2.69 us  [the longest x1 2.55 us: shards(): tag = tag.astype(jnp.bfloat16)]
    add x4 -> x2, other arithmetic: 2.18 us -> 1.36 us  [the longest x1 0.7 us: shards(): kept = stats[:, :CHUNK] + permute(stats[:, CHUNK:2 * CHUNK], swap_x)]
  transfers between devices with their start and end apart: 30 -> 36, of which waited for: 17 -> 12; matrix products, arithmetic and copies ran while one was open for 9% -> 7% of each run, Pallas kernels for 0% -> 8%
where the time goes in v4:
time: 109 us
  waiting for transfers between devices  40.2 us (37%)
  starting transfers between devices  34.8 us (32%)
  Pallas kernels  20.9 us (19%)
  other arithmetic  8.07 us (7%)
  local copies, waits for them, and re-layouts  4.29 us (4%)
    ppermute x36, waiting for transfers between devices, permute(): return lax.ppermute(value, AXES, pairs)  40.2 us
    ppermute x36, starting transfers between devices, permute(): return lax.ppermute(value, AXES, pairs)  34.8 us
    pallas_call x2, Pallas kernels, pair_sums(): pl.pallas_call(functools.partial(pair_kernel, row_cuts=tuple(row_cuts), t...  15.4 us
    pallas_call x1, Pallas kernels, raw_partial(): pl.pallas_call(raw_kernel, grid=(feats // width,), in_specs=[pl.BlockSpec...  5.48 us
    convert_element_type x1, other arithmetic, shards(): tag = tag.astype(jnp.bfloat16)  2.55 us
  transfers between devices with their start and end apart: 36, of which 12 were waited for; matrix products, arithmetic and copies ran while one was open for 7% of the time, Pallas kernels for 8%

profile of v4, /device:TPU:4, one launch (start us, length us, event | category | flops | bytes accessed | tf_op | source)
XLA Modules:
  0.0 108.7 jit_solution(11837670251965575636)
XLA Ops:
  0.0 5.5 %raw.1 = f32[512,1024]{1,0:T(8,128)} custom-call(s32[8,11]{1,0:T(8,128)} %bitcast.40, bf16[1584,512]{1,0:T(8,128)(2,1)} %bitcast.34, bf16[1584,1024]{1,0:T(8,128)(2,1)} %geometry.1), custom_call_target="tpu_custom_call" | custom-call | flops 1660944384 | bytes 8388608 | tf_op jit(solution)/shard_map/raw/pallas_call | solution.py:83
  5.5 1.7 %constant_dynamic-slice_fusion.1 = (f32[4,1,32,1024]{3,2,1,0:T(8,128)S(1)}, f16[4,1,32,1024]{3,2,0,1:T(8,128)(2,1)S(1)}, f16[4,1,32,1024]{3,2,0,1:T(8,128)(2,1)S(1)}, f16[4,1,32,1024]{3,2,0,1:T(8,128)(2,1)S(1)}) fusion(f32[4,4,32,1024]{3,2,1,0:T(8,128)} %bitcast.33, s32[]{:T(128)S(6)} %select_n.173, s32[]{:T(128)S(6)} %select_n.177, s32[]{:T(128)S(6)} %select_n.175, ...), kind=kLoop, calls=%fused_computation.46 | loop fusion | flops 393216 | bytes 3407888 | tf_op jit(solution)/shard_map/jit(dynamic_index_in_dim)/dynamic_slice | solution.py:246
  7.2 3.1 %collective-permute-start.2 = (f16[128,1024]{1,0:T(8,128)(2,1)S(1)}, f16[128,1024]{1,0:T(8,128)(2,1)S(1)}, u32[]{:S(2)}, u32[]{:S(2)}) collective-permute-start(f16[128,1024]{1,0:T(8,128)(2,1)S(1)} %bitcast.37), channel_id=1, source_target_pairs={{0,192},{1,193},{2,194},{3,195},{4,196},{5,197},{6,198},{7,199},{8... | collective-permute-start | bytes 786440 | tf_op jit(solution)/shard_map/ppermute | solution.py:32
  10.3 2.2 %collective-permute-start = (f16[128,1024]{1,0:T(8,128)(2,1)S(1)}, f16[128,1024]{1,0:T(8,128)(2,1)S(1)}, u32[]{:S(2)}, u32[]{:S(2)}) collective-permute-start(f16[128,1024]{1,0:T(8,128)(2,1)S(1)} %bitcast.35), channel_id=1, source_target_pairs={{0,128},{1,129},{2,130},{3,131},{4,132},{5,133},{6,134},{7,135},{8... | collective-permute-start | bytes 786440 | tf_op jit(solution)/shard_map/ppermute | solution.py:32
  13.2 8.3 %collective-permute-done.2 = f16[128,1024]{1,0:T(8,128)(2,1)S(1)} collective-permute-done((f16[128,1024]{1,0:T(8,128)(2,1)S(1)}, f16[128,1024]{1,0:T(8,128)(2,1)S(1)}, u32[]{:S(2)}, u32[]{:S(2)}) %collective-permute-start.2) | collective-permute-done | bytes 262176 | tf_op jit(solution)/shard_map/ppermute | solution.py:32
  21.5 3.4 %collective-permute-done.1 = f16[128,1024]{1,0:T(8,128)(2,1)S(1)} collective-permute-done((f16[128,1024]{1,0:T(8,128)(2,1)S(1)}, f16[128,1024]{1,0:T(8,128)(2,1)S(1)}, u32[]{:S(2)}, u32[]{:S(2)}) %collective-permute-start.1) | collective-permute-done | bytes 262176 | tf_op jit(solution)/shard_map/ppermute | solution.py:32
  25.4 3.2 %collective-permute-start.5 = (bf16[128,1024]{1,0:T(8,128)(2,1)S(1)}, bf16[128,1024]{1,0:T(8,128)(2,1)S(1)}, u32[]{:S(2)}, u32[]{:S(2)}) collective-permute-start(bf16[128,1024]{1,0:T(8,128)(2,1)S(1)} %multiply_convert_fusion), channel_id=1, source_target_pairs={{0,192},{1,193},{2,194},{3,195},{4,196},{5,197},{6,198},{7,199},{8... | collective-permute-start | bytes 786440 | tf_op jit(solution)/shard_map/ppermute | solution.py:32
  28.6 2.5 %select_convert_fusion = bf16[16,1024]{1,0:T(8,128)(2,1)S(1)} fusion(bf16[]{:T(256)} %bitcast.4, bf16[]{:T(256)} %bitcast.3, bf16[]{:T(256)} %bitcast.2, bf16[]{:T(256)} %bitcast.1, s32[1024]{0:T(1024)S(1)} %get-tuple-element.15, s32[1024]{0:T(1024)S(1)} %get-tuple-element.16, pred[16]{0:T(512)(128)(4,1)S(1)} %iota_compare_fusion, pred[1024]{0:T(1024)(128)(4,1)S(1)} %fusion.15), kind=kLoop, calls=%fused_computation.22 | loop fusion | flops 163840 | bytes 42008 | tf_op jit(solution)/shard_map/convert_element_type | solution.py:241
  31.2 1.3 %collective-permute-start.3 = (bf16[144,1024]{1,0:T(8,128)(2,1)S(1)}, bf16[144,1024]{1,0:T(8,128)(2,1)S(1)}, u32[]{:S(2)}, u32[]{:S(2)}) collective-permute-start(bf16[144,1024]{1,0:T(8,128)(2,1)S(1)} %pad_maximum_fusion.refs_2_.refs_11_), channel_id=1, source_target_pairs={{0,16},{1,17},{2,18},{3,19},{4,20},{5,21},{6,22},{7,23},{8,24},{9,... | collective-permute-start | bytes 884744 | tf_op jit(solution)/shard_map/ppermute | solution.py:32
  32.5 1.9 %collective-permute-start.13 = (bf16[144,1024]{1,0:T(8,128)(2,1)S(1)}, bf16[144,1024]{1,0:T(8,128)(2,1)S(1)}, u32[]{:S(2)}, u32[]{:S(2)}) collective-permute-start(bf16[144,1024]{1,0:T(8,128)(2,1)S(1)} %pad_maximum_fusion.refs_2_.refs_11_), channel_id=1, source_target_pairs={{0,2},{1,15},{2,4},{3,1},{4,6},{5,3},{6,8},{7,5},{8,10},{9,7},{10,... | collective-permute-start | bytes 884744 | tf_op jit(solution)/shard_map/ppermute | solution.py:32
  34.4 1.1 %collective-permute-start.14 = (bf16[144,1024]{1,0:T(8,128)(2,1)S(1)}, bf16[144,1024]{1,0:T(8,128)(2,1)S(1)}, u32[]{:S(2)}, u32[]{:S(2)}) collective-permute-start(bf16[144,1024]{1,0:T(8,128)(2,1)S(1)} %pad_maximum_fusion.refs_2_.refs_11_), channel_id=1, source_target_pairs={{0,15},{1,2},{2,1},{3,4},{4,3},{5,6},{6,5},{7,8},{8,7},{9,10},{10,... | collective-permute-start | bytes 884744 | tf_op jit(solution)/shard_map/ppermute | solution.py:32
  35.6 1.0 collective-permute-start.12
  36.7 8.2 %collective-permute-done.13.refs_13_ = bf16[144,1024]{1,0:T(8,128)(2,1)S(1)} collective-permute-done((bf16[144,1024]{1,0:T(8,128)(2,1)S(1)}, bf16[144,1024]{1,0:T(8,128)(2,1)S(1)}, u32[]{:S(2)}, u32[]{:S(2)}) %collective-permute-start.13) | collective-permute-done | bytes 294944 | tf_op jit(solution)/shard_map/ppermute | solution.py:32
  45.0 0.9 collective-permute-start.7
  46.0 1.2 %collective-permute-start.8 = (bf16[128,1024]{1,0:T(8,128)(2,1)S(1)}, bf16[128,1024]{1,0:T(8,128)(2,1)S(1)}, u32[]{:S(2)}, u32[]{:S(2)}) collective-permute-start(bf16[128,1024]{1,0:T(8,128)(2,1)S(1)} %collective-permute-done.5.refs_5_), channel_id=1, source_target_pairs={{0,16},{1,17},{2,18},{3,19},{4,20},{5,21},{6,22},{7,23},{8,24},{9,... | collective-permute-start | bytes 786440 | tf_op jit(solution)/shard_map/ppermute | solution.py:32
  47.3 7.0 %collective-permute-done.7.refs_7_ = bf16[128,1024]{1,0:T(8,128)(2,1)S(1)} collective-permute-done((bf16[128,1024]{1,0:T(8,128)(2,1)S(1)}, bf16[128,1024]{1,0:T(8,128)(2,1)S(1)}, u32[]{:S(2)}, u32[]{:S(2)}) %collective-permute-start.7) | collective-permute-done | bytes 262176 | tf_op jit(solution)/shard_map/ppermute | solution.py:32
  54.3 2.3 %collective-permute-start.21 = (bf16[144,1024]{1,0:T(8,128)(2,1)S(1)}, bf16[144,1024]{1,0:T(8,128)(2,1)}, u32[]{:S(2)}, u32[]{:S(2)}) collective-permute-start(bf16[144,1024]{1,0:T(8,128)(2,1)S(1)} %collective-permute-done.17.refs_17_), channel_id=1, source_target_pairs={{0,2},{1,15},{2,4},{3,1},{4,6},{5,3},{6,8},{7,5},{8,10},{9,7},{10,... | collective-permute-start | bytes 884744 | tf_op jit(solution)/shard_map/ppermute | solution.py:32
  56.7 2.1 %collective-permute-start.22 = (bf16[144,1024]{1,0:T(8,128)(2,1)}, bf16[144,1024]{1,0:T(8,128)(2,1)}, u32[]{:S(2)}, u32[]{:S(2)}) collective-permute-start(bf16[144,1024]{1,0:T(8,128)(2,1)} %collective-permute-done.18.refs_18_), channel_id=1, source_target_pairs={{0,2},{1,15},{2,4},{3,1},{4,6},{5,3},{6,8},{7,5},{8,10},{9,7},{10,... | collective-permute-start | bytes 884744 | tf_op jit(solution)/shard_map/ppermute | solution.py:32
  59.0 1.8 %collective-permute-start.10 = (bf16[128,1024]{1,0:T(8,128)(2,1)S(1)}, bf16[128,1024]{1,0:T(8,128)(2,1)S(1)}, u32[]{:S(2)}, u32[]{:S(2)}) collective-permute-start(bf16[128,1024]{1,0:T(8,128)(2,1)S(1)} %pad_maximum_fusion.1), channel_id=1, source_target_pairs={{32,16},{96,80},{160,144},{224,208}} | collective-permute-start | bytes 786440 | tf_op jit(solution)/shard_map/ppermute | solution.py:32
  61.5 3.1 %collective-permute-done.10 = bf16[128,1024]{1,0:T(8,128)(2,1)S(1)} collective-permute-done((bf16[128,1024]{1,0:T(8,128)(2,1)S(1)}, bf16[128,1024]{1,0:T(8,128)(2,1)S(1)}, u32[]{:S(2)}, u32[]{:S(2)}) %collective-permute-start.10) | collective-permute-done | bytes 262176 | tf_op jit(solution)/shard_map/ppermute | solution.py:32
  65.6 1.0 collective-permute-start.25
  66.6 1.1 %fusion.5 = bf16[48,1024]{1,0:T(8,128)(2,1)S(1)} fusion(bf16[128,1024]{1,0:T(8,128)(2,1)S(1)} %multiply_convert_fusion, bf16[16,1024]{1,0:T(8,128)(2,1)S(1)} %select_convert_fusion, bf16[144,1024]{1,0:T(8,128)(2,1)S(1)} %collective-permute-done.14.refs_14_, bf16[144,1024]{1,0:T(8,128)(2,1)} %collective-permute-done.18.refs_18_, ...), kind=kLoop, calls=%fused_computation.17 | loop fusion | flops 540672 | bytes 983047 | tf_op jit(solution)/shard_map/select_n | solution.py:277
  67.7 1.5 %collective-permute-done.9.refs_9_ = bf16[128,1024]{1,0:T(8,128)(2,1)} collective-permute-done((bf16[128,1024]{1,0:T(8,128)(2,1)S(1)}, bf16[128,1024]{1,0:T(8,128)(2,1)}, u32[]{:S(2)}, u32[]{:S(2)}) %collective-permute-start.9) | collective-permute-done | bytes 262176 | tf_op jit(solution)/shard_map/ppermute | solution.py:32
  69.2 2.3 %collective-permute-start.27 = (bf16[48,1024]{1,0:T(8,128)(2,1)S(1)}, bf16[48,1024]{1,0:T(8,128)(2,1)S(1)}, u32[]{:S(2)}, u32[]{:S(2)}) collective-permute-start(bf16[48,1024]{1,0:T(8,128)(2,1)S(1)} %fusion.5), channel_id=1, source_target_pairs={{32,16},{34,18},{36,20},{38,22},{43,27},{45,29},{47,31},{96,80},{9... | collective-permute-start | bytes 294920 | tf_op jit(solution)/shard_map/ppermute | solution.py:32
  71.5 2.2 %collective-permute-done.27 = bf16[48,1024]{1,0:T(8,128)(2,1)S(1)} collective-permute-done((bf16[48,1024]{1,0:T(8,128)(2,1)S(1)}, bf16[48,1024]{1,0:T(8,128)(2,1)S(1)}, u32[]{:S(2)}, u32[]{:S(2)}) %collective-permute-start.27) | collective-permute-done | bytes 98336 | tf_op jit(solution)/shard_map/ppermute | solution.py:32
  77.2 8.6 %early.1.refs_1_ = f32[4,1152]{1,0:T(4,128)} custom-call(s32[1]{0:T(128)} %bitcast.refs_0_, f32[4,1152]{1,0:T(4,128)} %broadcast_in_dim.20.refs_1_, bf16[144,1024]{1,0:T(8,128)(2,1)} %copy-done.2, bf16[144,1024]{1,0:T(8,128)(2,1)} %copy-done.9, bf16[128,1024]{1,0:T(8,128)(2,1)} %copy-done, bf16[128,1024]{1,0:T(8,128)(2,1)} %copy-done.1, ...), custom_call_target="tpu_custom_call" | custom-call | flops 3019898880 | bytes 4980736 | tf_op jit(solution)/shard_map/early/pallas_call | solution.py:194
  86.5 6.8 %late.1 = f32[4,1152]{1,0:T(4,128)} custom-call(s32[1]{0:T(128)} %bitcast.refs_0_, f32[4,1152]{1,0:T(4,128)} %early.1.refs_1_, bf16[144,1024]{1,0:T(8,128)(2,1)} %copy-done.2, bf16[144,1024]{1,0:T(8,128)(2,1)} %copy-done.9, bf16[128,1024]{1,0:T(8,128)(2,1)} %copy-done, bf16[128,1024]{1,0:T(8,128)(2,1)} %copy-done.1, bf16[128,1024]{1,0:T(8,128)(2,1)} %copy-done.8, ...), custom_call_target="tpu_custom_call" | custom-call | flops 1887436800 | bytes 3997696 | tf_op jit(solution)/shard_map/late/pallas_call | solution.py:194
  94.7 1.3 %collective-permute-start.31 = (f32[4,128]{1,0:T(4,128)S(1)}, f32[4,128]{1,0:T(4,128)S(1)}, u32[]{:S(2)}, u32[]{:S(2)}) collective-permute-start(f32[4,128]{1,0:T(4,128)S(1)} %slice.133), channel_id=1, source_target_pairs={{0,32},{64,96},{128,160},{192,224}} | collective-permute-start | bytes 6152 | tf_op jit(solution)/shard_map/ppermute | solution.py:32
  96.0 1.3 %collective-permute-start.32 = (f32[4,128]{1,0:T(4,128)S(1)}, f32[4,128]{1,0:T(4,128)S(1)}, u32[]{:S(2)}, u32[]{:S(2)}) collective-permute-start(f32[4,128]{1,0:T(4,128)S(1)} %slice.133), channel_id=1, source_target_pairs={{16,32},{80,96},{144,160},{208,224}} | collective-permute-start | bytes 6152 | tf_op jit(solution)/shard_map/ppermute | solution.py:32
  97.3 4.4 %collective-permute-done.31 = f32[4,128]{1,0:T(4,128)S(1)} collective-permute-done((f32[4,128]{1,0:T(4,128)S(1)}, f32[4,128]{1,0:T(4,128)S(1)}, u32[]{:S(2)}, u32[]{:S(2)}) %collective-permute-start.31) | collective-permute-done | bytes 2080 | tf_op jit(solution)/shard_map/ppermute | solution.py:32
  103.6 2.6 %collective-permute-start.35 = (f32[4,4,128]{2,1,0:T(4,128)S(1)}, f32[4,4,128]{2,1,0:T(4,128)S(1)}, u32[]{:S(2)}, u32[]{:S(2)}) collective-permute-start(f32[4,4,128]{2,1,0:T(4,128)S(1)} %pad_add_fusion), channel_id=1, source_target_pairs={{0,192},{1,193},{2,194},{3,195},{4,196},{5,197},{6,198},{7,199},{8... | collective-permute-start | bytes 24584 | tf_op jit(solution)/shard_map/ppermute | solution.py:32
  106.2 1.6 %collective-permute-done.33 = f32[4,4,128]{2,1,0:T(4,128)S(1)} collective-permute-done((f32[4,4,128]{2,1,0:T(4,128)S(1)}, f32[4,4,128]{2,1,0:T(4,128)S(1)}, u32[]{:S(2)}, u32[]{:S(2)}) %collective-permute-start.33) | collective-permute-done | bytes 8224 | tf_op jit(solution)/shard_map/ppermute | solution.py:32
  (112 shorter events, 11.7 us)
Async XLA Ops:
  7.2 14.3 %collective-permute-start.2 = (f16[128,1024]{1,0:T(8,128)(2,1)S(1)}, f16[128,1024]{1,0:T(8,128)(2,1)S(1)}, u32[]{:S(2)}, u32[]{:S(2)}) collective-permute-start(f16[128,1024]{1,0:T(8,128)(2,1)S(1)} %bitcast.37), channel_id=1, source_target_pairs={{0,192},{1,193},{2,194},{3,195},{4,196},{5,197},{6,198},{7,199},{8... | collective-permute-start | bytes 786440 | tf_op jit(solution)/shard_map/ppermute | solution.py:32
  10.3 14.6 %collective-permute-start.1 = (f16[128,1024]{1,0:T(8,128)(2,1)S(1)}, f16[128,1024]{1,0:T(8,128)(2,1)S(1)}, u32[]{:S(2)}, u32[]{:S(2)}) collective-permute-start(f16[128,1024]{1,0:T(8,128)(2,1)S(1)} %bitcast.36), channel_id=1, source_target_pairs={{0,64},{1,65},{2,66},{3,67},{4,68},{5,69},{6,70},{7,71},{8,72},{9,... | collective-permute-start | bytes 786440 | tf_op jit(solution)/shard_map/ppermute | solution.py:32
  10.3 14.6 %collective-permute-start = (f16[128,1024]{1,0:T(8,128)(2,1)S(1)}, f16[128,1024]{1,0:T(8,128)(2,1)S(1)}, u32[]{:S(2)}, u32[]{:S(2)}) collective-permute-start(f16[128,1024]{1,0:T(8,128)(2,1)S(1)} %bitcast.35), channel_id=1, source_target_pairs={{0,128},{1,129},{2,130},{3,131},{4,132},{5,133},{6,134},{7,135},{8... | collective-permute-start | bytes 786440 | tf_op jit(solution)/shard_map/ppermute | solution.py:32
  25.3 10.2 %collective-permute-start.4 = (bf16[128,1024]{1,0:T(8,128)(2,1)S(1)}, bf16[128,1024]{1,0:T(8,128)(2,1)S(1)}, u32[]{:S(2)}, u32[]{:S(2)}) collective-permute-start(bf16[128,1024]{1,0:T(8,128)(2,1)S(1)} %multiply_convert_fusion), channel_id=1, source_target_pairs={{0,64},{1,65},{2,66},{3,67},{4,68},{5,69},{6,70},{7,71},{8,72},{9,... | collective-permute-start | bytes 786440 | tf_op jit(solution)/shard_map/ppermute | solution.py:32
  25.4 10.1 %collective-permute-start.5 = (bf16[128,1024]{1,0:T(8,128)(2,1)S(1)}, bf16[128,1024]{1,0:T(8,128)(2,1)S(1)}, u32[]{:S(2)}, u32[]{:S(2)}) collective-permute-start(bf16[128,1024]{1,0:T(8,128)(2,1)S(1)} %multiply_convert_fusion), channel_id=1, source_target_pairs={{0,192},{1,193},{2,194},{3,195},{4,196},{5,197},{6,198},{7,199},{8... | collective-permute-start | bytes 786440 | tf_op jit(solution)/shard_map/ppermute | solution.py:32
  31.2 13.8 %collective-permute-start.3 = (bf16[144,1024]{1,0:T(8,128)(2,1)S(1)}, bf16[144,1024]{1,0:T(8,128)(2,1)S(1)}, u32[]{:S(2)}, u32[]{:S(2)}) collective-permute-start(bf16[144,1024]{1,0:T(8,128)(2,1)S(1)} %pad_maximum_fusion.refs_2_.refs_11_), channel_id=1, source_target_pairs={{0,16},{1,17},{2,18},{3,19},{4,20},{5,21},{6,22},{7,23},{8,24},{9,... | collective-permute-start | bytes 884744 | tf_op jit(solution)/shard_map/ppermute | solution.py:32
  32.5 12.4 %collective-permute-start.13 = (bf16[144,1024]{1,0:T(8,128)(2,1)S(1)}, bf16[144,1024]{1,0:T(8,128)(2,1)S(1)}, u32[]{:S(2)}, u32[]{:S(2)}) collective-permute-start(bf16[144,1024]{1,0:T(8,128)(2,1)S(1)} %pad_maximum_fusion.refs_2_.refs_11_), channel_id=1, source_target_pairs={{0,2},{1,15},{2,4},{3,1},{4,6},{5,3},{6,8},{7,5},{8,10},{9,7},{10,... | collective-permute-start | bytes 884744 | tf_op jit(solution)/shard_map/ppermute | solution.py:32
  34.4 10.5 %collective-permute-start.14 = (bf16[144,1024]{1,0:T(8,128)(2,1)S(1)}, bf16[144,1024]{1,0:T(8,128)(2,1)S(1)}, u32[]{:S(2)}, u32[]{:S(2)}) collective-permute-start(bf16[144,1024]{1,0:T(8,128)(2,1)S(1)} %pad_maximum_fusion.refs_2_.refs_11_), channel_id=1, source_target_pairs={{0,15},{1,2},{2,1},{3,4},{4,3},{5,6},{6,5},{7,8},{8,7},{9,10},{10,... | collective-permute-start | bytes 884744 | tf_op jit(solution)/shard_map/ppermute | solution.py:32
  35.5 10.4 %collective-permute-start.6 = (bf16[128,1024]{1,0:T(8,128)(2,1)S(1)}, bf16[128,1024]{1,0:T(8,128)(2,1)S(1)}, u32[]{:S(2)}, u32[]{:S(2)}) collective-permute-start(bf16[128,1024]{1,0:T(8,128)(2,1)S(1)} %broadcast_select_fusion.1), channel_id=1, source_target_pairs={{0,64},{1,193},{2,66},{3,195},{4,68},{5,197},{6,70},{7,199},{8,72}... | collective-permute-start | bytes 786440 | tf_op jit(solution)/shard_map/ppermute | solution.py:32
  35.6 11.6 %collective-permute-start.12 = (bf16[144,1024]{1,0:T(8,128)(2,1)S(1)}, bf16[144,1024]{1,0:T(8,128)(2,1)S(1)}, u32[]{:S(2)}, u32[]{:S(2)}) collective-permute-start(bf16[144,1024]{1,0:T(8,128)(2,1)S(1)} %pad_maximum_fusion.refs_2_.refs_11_), channel_id=1, source_target_pairs={{0,1},{1,0},{2,3},{3,2},{4,5},{5,4},{6,7},{7,6},{8,9},{9,8},{10,11... | collective-permute-start | bytes 884744 | tf_op jit(solution)/shard_map/ppermute | solution.py:32
  44.9 9.4 %collective-permute-start.17 = (bf16[144,1024]{1,0:T(8,128)(2,1)S(1)}, bf16[144,1024]{1,0:T(8,128)(2,1)S(1)}, u32[]{:S(2)}, u32[]{:S(2)}) collective-permute-start(bf16[144,1024]{1,0:T(8,128)(2,1)S(1)} %collective-permute-done.13.refs_13_), channel_id=1, source_target_pairs={{0,2},{1,15},{2,4},{3,1},{4,6},{5,3},{6,8},{7,5},{8,10},{9,7},{10,... | collective-permute-start | bytes 884744 | tf_op jit(solution)/shard_map/ppermute | solution.py:32
  44.9 11.7 %collective-permute-start.18 = (bf16[144,1024]{1,0:T(8,128)(2,1)S(1)}, bf16[144,1024]{1,0:T(8,128)(2,1)}, u32[]{:S(2)}, u32[]{:S(2)}) collective-permute-start(bf16[144,1024]{1,0:T(8,128)(2,1)S(1)} %collective-permute-done.14.refs_14_), channel_id=1, source_target_pairs={{0,2},{1,15},{2,4},{3,1},{4,6},{5,3},{6,8},{7,5},{8,10},{9,7},{10,... | collective-permute-start | bytes 884744 | tf_op jit(solution)/shard_map/ppermute | solution.py:32
  45.0 9.3 %collective-permute-start.7 = (bf16[128,1024]{1,0:T(8,128)(2,1)S(1)}, bf16[128,1024]{1,0:T(8,128)(2,1)S(1)}, u32[]{:S(2)}, u32[]{:S(2)}) collective-permute-start(bf16[128,1024]{1,0:T(8,128)(2,1)S(1)} %collective-permute-done.4.refs_4_), channel_id=1, source_target_pairs={{0,16},{1,17},{2,18},{3,19},{4,20},{5,21},{6,22},{7,23},{8,24},{9,... | collective-permute-start | bytes 786440 | tf_op jit(solution)/shard_map/ppermute | solution.py:32
  46.0 13.0 %collective-permute-start.8 = (bf16[128,1024]{1,0:T(8,128)(2,1)S(1)}, bf16[128,1024]{1,0:T(8,128)(2,1)S(1)}, u32[]{:S(2)}, u32[]{:S(2)}) collective-permute-start(bf16[128,1024]{1,0:T(8,128)(2,1)S(1)} %collective-permute-done.5.refs_5_), channel_id=1, source_target_pairs={{0,16},{1,17},{2,18},{3,19},{4,20},{5,21},{6,22},{7,23},{8,24},{9,... | collective-permute-start | bytes 786440 | tf_op jit(solution)/shard_map/ppermute | solution.py:32
  47.2 13.5 %collective-permute-start.15 = (bf16[144,1024]{1,0:T(8,128)(2,1)S(1)}, bf16[144,1024]{1,0:T(8,128)(2,1)S(1)}, u32[]{:S(2)}, u32[]{:S(2)}) collective-permute-start(bf16[144,1024]{1,0:T(8,128)(2,1)S(1)} %collective-permute-done.13.refs_13_), channel_id=1, source_target_pairs={{0,1},{1,0},{2,3},{3,2},{4,5},{5,4},{6,7},{7,6},{8,9},{9,8},{10,11... | collective-permute-start | bytes 884744 | tf_op jit(solution)/shard_map/ppermute | solution.py:32
  54.3 7.2 %collective-permute-start.16 = (bf16[144,1024]{1,0:T(8,128)(2,1)S(1)}, bf16[144,1024]{1,0:T(8,128)(2,1)}, u32[]{:S(2)}, u32[]{:S(2)}) collective-permute-start(bf16[144,1024]{1,0:T(8,128)(2,1)S(1)} %collective-permute-done.14.refs_14_), channel_id=1, source_target_pairs={{0,1},{1,0},{2,3},{3,2},{4,5},{5,4},{6,7},{7,6},{8,9},{9,8},{10,11... | collective-permute-start | bytes 884744 | tf_op jit(solution)/shard_map/ppermute | solution.py:32
  54.3 10.3 %collective-permute-start.21 = (bf16[144,1024]{1,0:T(8,128)(2,1)S(1)}, bf16[144,1024]{1,0:T(8,128)(2,1)}, u32[]{:S(2)}, u32[]{:S(2)}) collective-permute-start(bf16[144,1024]{1,0:T(8,128)(2,1)S(1)} %collective-permute-done.17.refs_17_), channel_id=1, source_target_pairs={{0,2},{1,15},{2,4},{3,1},{4,6},{5,3},{6,8},{7,5},{8,10},{9,7},{10,... | collective-permute-start | bytes 884744 | tf_op jit(solution)/shard_map/ppermute | solution.py:32
  56.7 8.9 %collective-permute-start.22 = (bf16[144,1024]{1,0:T(8,128)(2,1)}, bf16[144,1024]{1,0:T(8,128)(2,1)}, u32[]{:S(2)}, u32[]{:S(2)}) collective-permute-start(bf16[144,1024]{1,0:T(8,128)(2,1)} %collective-permute-done.18.refs_18_), channel_id=1, source_target_pairs={{0,2},{1,15},{2,4},{3,1},{4,6},{5,3},{6,8},{7,5},{8,10},{9,7},{10,... | collective-permute-start | bytes 884744 | tf_op jit(solution)/shard_map/ppermute | solution.py:32
  59.0 5.6 %collective-permute-start.10 = (bf16[128,1024]{1,0:T(8,128)(2,1)S(1)}, bf16[128,1024]{1,0:T(8,128)(2,1)S(1)}, u32[]{:S(2)}, u32[]{:S(2)}) collective-permute-start(bf16[128,1024]{1,0:T(8,128)(2,1)S(1)} %pad_maximum_fusion.1), channel_id=1, source_target_pairs={{32,16},{96,80},{160,144},{224,208}} | collective-permute-start | bytes 786440 | tf_op jit(solution)/shard_map/ppermute | solution.py:32
  61.5 7.7 %collective-permute-start.9 = (bf16[128,1024]{1,0:T(8,128)(2,1)S(1)}, bf16[128,1024]{1,0:T(8,128)(2,1)}, u32[]{:S(2)}, u32[]{:S(2)}) collective-permute-start(bf16[128,1024]{1,0:T(8,128)(2,1)S(1)} %broadcast_select_fusion), channel_id=1, source_target_pairs={{0,64},{1,193},{2,66},{3,195},{4,68},{5,197},{6,70},{7,199},{8,72}... | collective-permute-start | bytes 786440 | tf_op jit(solution)/shard_map/ppermute | solution.py:32
  61.5 14.4 %collective-permute-start.19 = (bf16[144,1024]{1,0:T(8,128)(2,1)S(1)}, bf16[144,1024]{1,0:T(8,128)(2,1)}, u32[]{:S(2)}, u32[]{:S(2)}) collective-permute-start(bf16[144,1024]{1,0:T(8,128)(2,1)S(1)} %collective-permute-done.17.refs_17_), channel_id=1, source_target_pairs={{0,1},{1,0},{2,3},{3,2},{4,5},{5,4},{6,7},{7,6},{8,9},{9,8},{10,11... | collective-permute-start | bytes 884744 | tf_op jit(solution)/shard_map/ppermute | solution.py:32
  64.6 12.0 %collective-permute-start.20 = (bf16[144,1024]{1,0:T(8,128)(2,1)}, bf16[144,1024]{1,0:T(8,128)(2,1)}, u32[]{:S(2)}, u32[]{:S(2)}) collective-permute-start(bf16[144,1024]{1,0:T(8,128)(2,1)} %collective-permute-done.18.refs_18_), channel_id=1, source_target_pairs={{0,1},{1,0},{2,3},{3,2},{4,5},{5,4},{6,7},{7,6},{8,9},{9,8},{10,11... | collective-permute-start | bytes 884744 | tf_op jit(solution)/shard_map/ppermute | solution.py:32
  64.6 9.9 %collective-permute-start.11 = (bf16[128,1024]{1,0:T(8,128)(2,1)S(1)}, bf16[128,1024]{1,0:T(8,128)(2,1)S(1)}, u32[]{:S(2)}, u32[]{:S(2)}) collective-permute-start(bf16[128,1024]{1,0:T(8,128)(2,1)S(1)} %collective-permute-done.10), channel_id=1, source_target_pairs={{16,0},{80,64},{144,128},{208,192}} | collective-permute-start | bytes 786440 | tf_op jit(solution)/shard_map/ppermute | solution.py:32
  65.6 9.4 %collective-permute-start.25 = (bf16[144,1024]{1,0:T(8,128)(2,1)}, bf16[144,1024]{1,0:T(8,128)(2,1)}, u32[]{:S(2)}, u32[]{:S(2)}) collective-permute-start(bf16[144,1024]{1,0:T(8,128)(2,1)} %collective-permute-done.21.refs_11_), channel_id=1, source_target_pairs={{0,2},{1,15},{2,4},{3,1},{4,6},{5,3},{6,8},{7,5},{8,10},{9,7},{10,... | collective-permute-start | bytes 884744 | tf_op jit(solution)/shard_map/ppermute | solution.py:32
  74.4 12.1 %collective-permute-start.23 = (bf16[144,1024]{1,0:T(8,128)(2,1)}, bf16[144,1024]{1,0:T(8,128)(2,1)}, u32[]{:S(2)}, u32[]{:S(2)}) collective-permute-start(bf16[144,1024]{1,0:T(8,128)(2,1)} %collective-permute-done.21.refs_11_), channel_id=1, source_target_pairs={{0,1},{1,0},{2,3},{3,2},{4,5},{5,4},{6,7},{7,6},{8,9},{9,8},{10,11... | collective-permute-start | bytes 884744 | tf_op jit(solution)/shard_map/ppermute | solution.py:32
  74.5 12.0 %collective-permute-start.24 = (bf16[144,1024]{1,0:T(8,128)(2,1)}, bf16[144,1024]{1,0:T(8,128)(2,1)}, u32[]{:S(2)}, u32[]{:S(2)}) collective-permute-start(bf16[144,1024]{1,0:T(8,128)(2,1)} %collective-permute-done.22.refs_12_), channel_id=1, source_target_pairs={{0,1},{1,0},{2,3},{3,2},{4,5},{5,4},{6,7},{7,6},{8,9},{9,8},{10,11... | collective-permute-start | bytes 884744 | tf_op jit(solution)/shard_map/ppermute | solution.py:32
  75.0 11.5 %collective-permute-start.26 = (bf16[144,1024]{1,0:T(8,128)(2,1)}, bf16[144,1024]{1,0:T(8,128)(2,1)}, u32[]{:S(2)}, u32[]{:S(2)}) collective-permute-start(bf16[144,1024]{1,0:T(8,128)(2,1)} %collective-permute-done.25.refs_15_), channel_id=1, source_target_pairs={{0,1},{1,0},{2,3},{3,2},{4,5},{5,4},{6,7},{7,6},{8,9},{9,8},{10,11... | collective-permute-start | bytes 884744 | tf_op jit(solution)/shard_map/ppermute | solution.py:32
  75.9 9.9 %collective-permute-start.29 = (bf16[48,1024]{1,0:T(8,128)(2,1)S(1)}, bf16[48,1024]{1,0:T(8,128)(2,1)S(1)}, u32[]{:S(2)}, u32[]{:S(2)}) collective-permute-start(bf16[48,1024]{1,0:T(8,128)(2,1)S(1)} %add.127), channel_id=1, source_target_pairs={{0,1},{1,0},{2,3},{3,2},{4,5},{5,4},{6,7},{7,6},{8,9},{9,8},{10,11... | collective-permute-start | bytes 294920 | tf_op jit(solution)/shard_map/ppermute | solution.py:32
  94.0 7.7 %collective-permute-start.30 = (f32[4,512]{1,0:T(4,128)S(1)}, f32[4,512]{1,0:T(4,128)S(1)}, u32[]{:S(2)}, u32[]{:S(2)}) collective-permute-start(f32[4,512]{1,0:T(4,128)S(1)} %slice.132), channel_id=1, source_target_pairs={{0,16},{1,17},{2,18},{3,19},{4,20},{5,21},{6,22},{7,23},{8,24},{9,... | collective-permute-start | bytes 24584 | tf_op jit(solution)/shard_map/ppermute | solution.py:32
  94.7 7.0 %collective-permute-start.31 = (f32[4,128]{1,0:T(4,128)S(1)}, f32[4,128]{1,0:T(4,128)S(1)}, u32[]{:S(2)}, u32[]{:S(2)}) collective-permute-start(f32[4,128]{1,0:T(4,128)S(1)} %slice.133), channel_id=1, source_target_pairs={{0,32},{64,96},{128,160},{192,224}} | collective-permute-start | bytes 6152 | tf_op jit(solution)/shard_map/ppermute | solution.py:32
  96.0 5.7 %collective-permute-start.32 = (f32[4,128]{1,0:T(4,128)S(1)}, f32[4,128]{1,0:T(4,128)S(1)}, u32[]{:S(2)}, u32[]{:S(2)}) collective-permute-start(f32[4,128]{1,0:T(4,128)S(1)} %slice.133), channel_id=1, source_target_pairs={{16,32},{80,96},{144,160},{208,224}} | collective-permute-start | bytes 6152 | tf_op jit(solution)/shard_map/ppermute | solution.py:32
  102.5 5.2 %collective-permute-start.33 = (f32[4,4,128]{2,1,0:T(4,128)S(1)}, f32[4,4,128]{2,1,0:T(4,128)S(1)}, u32[]{:S(2)}, u32[]{:S(2)}) collective-permute-start(f32[4,4,128]{2,1,0:T(4,128)S(1)} %pad_add_fusion), channel_id=1, source_target_pairs={{0,128},{1,129},{2,130},{3,131},{4,132},{5,133},{6,134},{7,135},{8... | collective-permute-start | bytes 24584 | tf_op jit(solution)/shard_map/ppermute | solution.py:32
  (18 other events, 319.3 us)

commit v5 on v3

v5 whole, which is shorter than its diff:
```python
import functools

import jax
import jax.numpy as jnp
from jax import lax
from jax.experimental import pallas as pl
from jax.experimental.pallas import tpu as pltpu
from jax.sharding import PartitionSpec as P

BLOCK = 128
PIECE = 32
TAG = 16
BINS = 8
CHUNK = 512
AXES = ("layer", "shower")
NY, NX, NZ, NC = 4, 4, 8, 2


def flat(y, x, z, c):
    return y * (NX * NZ * NC) + (x * NZ + z) * NC + c


def permute(value, move, keep=lambda y, x, z, c: True):
    pairs = [
        (flat(y, x, z, c), flat(*move(y, x, z, c)))
        for y in range(NY)
        for x in range(NX)
        for z in range(NZ)
        for c in range(NC)
        if keep(y, x, z, c)
    ]
    return lax.ppermute(value, AXES, pairs)


def along_y(step):
    return lambda y, x, z, c: ((y + step) % NY, x, z, c)


def along_z(step):
    return lambda y, x, z, c: (y, x, (z + step) % NZ, c)


def flip_z(bit):
    return lambda y, x, z, c: (y, x, z ^ bit, c)


def swap_x(y, x, z, c):
    return (y, x ^ 1, z, c)


def swap_core(y, x, z, c):
    return (y, x, z, 1 - c)


def same_core(y, x, z, c):
    return (y, x, (z + 1 - 2 * c) % NZ, c)


def cross_core(y, x, z, c):
    return (y, x, (z - 1 + 2 * c) % NZ, 1 - c)


def raw_kernel(pattern, showers, geometry, out, masked, *, part_of):
    layers = pattern.shape[1]
    cells = geometry.shape[0] // layers
    per = geometry.shape[1] // BLOCK
    for layer in range(layers):
        for part in range(per):
            rows = pl.ds(layer * cells, cells)
            cols = pl.ds(part * BLOCK, BLOCK)
            on = pattern[part_of * per + part, layer].astype(jnp.float32).astype(jnp.bfloat16)
            masked[rows, cols] = geometry[rows, cols] * on
    out[...] = lax.dot_general(
        showers[...], masked[...], (((0,), (0,)), ((), ())), preferred_element_type=jnp.float32
    )


def raw_partial(showers, geometry, pattern, part_of):
    rows, depth = showers.shape
    width = CHUNK
    return pl.pallas_call(
        functools.partial(raw_kernel, part_of=part_of),
        grid=(1,),
        in_specs=[
            pl.BlockSpec(memory_space=pltpu.SMEM),
            pl.BlockSpec((depth, rows), lambda i: (0, 0)),
            pl.BlockSpec((depth, width), lambda i: (0, part_of)),
        ],
        out_specs=pl.BlockSpec((rows, width), lambda i: (0, 0)),
        out_shape=jax.ShapeDtypeStruct((rows, width), jnp.float32),
        scratch_shapes=[pltpu.VMEM((depth, width), jnp.bfloat16)],
        compiler_params=pltpu.CompilerParams(vmem_limit_bytes=60 * 2**20),
        cost_estimate=pl.CostEstimate(
            flops=2 * rows * depth * width, bytes_accessed=5 * 2**20, transcendentals=0
        ),
        name="raw",
    )(pattern.T, showers.T, geometry)


def pair_kernel(*refs, row_cuts, tag_cuts, col_sizes, n_args):
    n_cols = len(col_sizes)
    odd_here = refs[0]
    args = refs[1 : 1 + n_args]
    cols = refs[1 + n_args : 1 + n_args + n_cols]
    outs = refs[1 + n_args + n_cols : 4 + n_args + n_cols]
    (
        rows_at, cols_at, row_tags, col_tags, sums, counts, row_sems, col_sems, tag_sems, row_tag_sems,
    ) = refs[4 + n_args + n_cols :]

    def start(source, first, size, target, place, sem):
        copy = pltpu.make_async_copy(
            source.at[pl.ds(first, size), :], target.at[pl.ds(place, size), :], sem
        )
        copy.start()
        return copy

    starts = [sum(col_sizes[:at]) for at in range(n_cols)]
    depth = sum(col_sizes)

    def col_copies(at):
        return [
            start(cols[at], TAG, col_sizes[at], cols_at, starts[at], col_sems.at[at]),
            start(cols[at], 0, TAG, col_tags, at * TAG, tag_sems.at[at]),
        ]

    held = {at: col_copies(at) for at in range(2)}
    tag_copies = [
        start(args[arg], first, TAG, row_tags, at * TAG, row_tag_sems.at[at])
        for at, (arg, first) in enumerate(tag_cuts)
    ]
    row_copies, total = [], 0
    for at, (arg, first, size) in enumerate(row_cuts):
        row_copies.append((total, start(args[arg], first, size, rows_at, total, row_sems.at[at])))
        total += size
    for at in range(2, n_cols):
        held[at] = col_copies(at)
    sums[...] = jnp.zeros_like(sums)
    counts[...] = jnp.zeros_like(counts)
    for copy in tag_copies:
        copy.wait()

    def bin_of(code):
        source = (code >= BINS).astype(jnp.float32)
        return code - BINS * source, source

    waited_rows = waited_cols = 0
    low = 0
    while low < depth:
        high = depth if depth - low < 3 * BLOCK else low + 2 * BLOCK
        while waited_cols < n_cols and starts[waited_cols] < high:
            for copy in held[waited_cols]:
                copy.wait()
            waited_cols += 1
        for first in range(0, total, CHUNK):
            size = min(CHUNK, total - first)
            while waited_rows < len(row_copies) and row_copies[waited_rows][0] < first + size:
                row_copies[waited_rows][1].wait()
                waited_rows += 1
            odd = first >= 2 * CHUNK
            set_of = 0 if odd else first // CHUNK
            tag = row_tags[pl.ds(set_of * TAG + 4, 1), pl.ds(0, BLOCK)].astype(jnp.float32) - 1.0
            bins, _ = bin_of(tag)
            if odd:
                bins = jnp.where(odd_here[0] > 0, bins, -2.0)
            bins = jnp.concatenate([bins] * (size // BLOCK), axis=1)
            lanes = pl.ds(first, size)
            products = lax.dot_general(
                cols_at[pl.ds(low, high - low), :],
                rows_at[lanes, :],
                (((1,), (1,)), ((), ())),
                preferred_element_type=jnp.float32,
            )
            shifted = products + 32.0
            cubes = shifted * shifted * shifted
            one = jnp.zeros((8, size), jnp.float32)
            zero = jnp.zeros((8, size), jnp.float32)
            n_one = jnp.zeros((1, size), jnp.float32)
            n_zero = jnp.zeros((1, size), jnp.float32)
            for group in range(low // PIECE, high // PIECE):
                at = group * PIECE // BLOCK
                if odd and col_sizes[at] == PIECE:
                    continue
                block = cubes[group * PIECE - low : (group + 1) * PIECE - low]
                if first == 0 and at == 0:
                    lane = lax.broadcasted_iota(jnp.int32, block.shape, 1)
                    sub = lax.broadcasted_iota(jnp.int32, block.shape, 0)
                    block = jnp.where(lane == sub + group * PIECE, 0.0, block)
                part = (block[0:8] + block[8:16]) + (block[16:24] + block[24:32])
                row = at * TAG + group % 4
                code = col_tags[pl.ds(row, 1), pl.ds(0, size)].astype(jnp.float32) - 1.0
                bin_id, source = bin_of(code)
                match = (bins == bin_id).astype(jnp.float32)
                is_one = match * source
                is_zero = match - is_one
                one += is_one * part
                zero += is_zero * part
                n_one += is_one
                n_zero += is_zero
            sums[0:8, lanes] += one
            sums[8:16, lanes] += zero
            counts[0:1, lanes] += n_one
            counts[1:2, lanes] += n_zero
        low = high
    for out, first in zip(outs, range(0, total, CHUNK)):
        lanes = pl.ds(first, out.shape[1])
        out[0:1, :] = jnp.sum(sums[0:8, lanes], axis=0, keepdims=True)
        out[1:2, :] = jnp.sum(sums[8:16, lanes], axis=0, keepdims=True)
        out[2:4, :] = counts[0:2, lanes]


def pair_sums(odd_here, args, row_cuts, tag_cuts, cols):
    col_sizes = tuple(size for _, size in cols)
    total, depth = sum(size for _, _, size in row_cuts), sum(col_sizes)
    feats = args[0].shape[1]
    hbm = pl.BlockSpec(memory_space=pl.ANY)
    vmem = pl.BlockSpec(memory_space=pltpu.VMEM)
    widths = [min(CHUNK, total - first) for first in range(0, total, CHUNK)]
    dma = pltpu.SemaphoreType.DMA
    return pl.pallas_call(
        functools.partial(
            pair_kernel,
            row_cuts=tuple(row_cuts),
            tag_cuts=tuple(tag_cuts),
            col_sizes=col_sizes,
            n_args=len(args),
        ),
        in_specs=[pl.BlockSpec(memory_space=pltpu.SMEM)] + [hbm] * (len(args) + len(cols)),
        out_specs=[vmem] * len(widths),
        out_shape=[jax.ShapeDtypeStruct((4, width), jnp.float32) for width in widths],
        scratch_shapes=[
            pltpu.VMEM((total, feats), jnp.bfloat16),
            pltpu.VMEM((depth, feats), jnp.bfloat16),
            pltpu.VMEM((TAG * len(tag_cuts), feats), jnp.bfloat16),
            pltpu.VMEM((TAG * len(cols), feats), jnp.bfloat16),
            pltpu.VMEM((16, total), jnp.float32),
            pltpu.VMEM((8, total), jnp.float32),
            dma((len(row_cuts),)),
            dma((len(cols),)),
            dma((len(cols),)),
            dma((len(tag_cuts),)),
        ],
        compiler_params=pltpu.CompilerParams(vmem_limit_bytes=58 * 2**20),
        cost_estimate=pl.CostEstimate(
            flops=2 * total * depth * feats,
            bytes_accessed=2 * (total + depth) * feats,
            transcendentals=0,
        ),
        name="pairs",
    )(odd_here, *args, *[c for c, _ in cols])


def shards(showers, geometry, pattern, bins, sources):
    y = lax.axis_index("layer")
    s = lax.axis_index("shower")
    x, z, c = s // (NZ * NC), (s // NC) % NZ, s % NC
    feats = geometry.shape[1]
    blocks = bins.shape[0]

    codes = (bins + BINS * sources + 1).astype(jnp.float32)
    line = lax.broadcasted_iota(jnp.int32, (TAG, feats), 0)
    lane = lax.broadcasted_iota(jnp.int32, (TAG, feats), 1) // PIECE
    which = jnp.where(line == blocks, lane, line)
    tag = jnp.zeros((TAG, feats), jnp.float32)
    for group in range(blocks):
        tag = jnp.where(which == group, codes[group], tag)
    tag = tag.astype(jnp.bfloat16)

    halves = []
    for part_of in range(feats // CHUNK):
        partial_sums = raw_partial(showers, geometry, pattern, part_of)
        partial_sums = partial_sums.reshape(blocks, NY, PIECE, CHUNK)

        def share(turn):
            part = lax.dynamic_index_in_dim(partial_sums, (y + turn) % NY, 1, keepdims=False)
            return part.reshape(BLOCK, CHUNK)

        raw = share(0)
        arrived = [permute(share(turn).astype(jnp.float16), along_y(turn)) for turn in (2, 1, 3)]
        halves.append((raw, arrived))
    raws = []
    for raw, arrived in halves:
        for part in arrived:
            raw = raw + part.astype(jnp.float32)
        raws.append(raw)
    square = sum(jnp.sum(raw * raw, axis=1, keepdims=True) for raw in raws)
    scale = lax.rsqrt(square / feats + 1e-05)
    own = jnp.concatenate([(raw * scale).astype(jnp.bfloat16) for raw in raws], axis=1)
    own = lax.optimization_barrier(jnp.concatenate([tag, own], axis=0))

    y_way = lambda y, x, z, c: ((y + 1 - 2 * c) % NY, x, z, c)
    fence = lambda *values: lax.optimization_barrier(values)
    same, cross = [permute(own, same_core)], [permute(own, cross_core)]
    ya = permute(own[TAG:], along_y(1))
    yb = permute(own[TAG:], along_y(3))
    x1 = permute(own, swap_x)
    same[0], cross[0], ya, yb, x1, own = fence(same[0], cross[0], ya, yb, x1, own)

    same.append(permute(same[0], same_core))
    cross.append(permute(cross[0], same_core))
    y2 = permute(jnp.where(c == 0, ya, yb), y_way)
    xa = permute(ya, swap_x)
    own_other = permute(own, swap_core)
    same[1], cross[1], y2, xa, own_other, yb, same[0], cross[0] = fence(
        same[1], cross[1], y2, xa, own_other, yb, same[0], cross[0]
    )

    same.append(permute(same[1], same_core))
    cross.append(permute(cross[1], same_core))
    xb = permute(yb, swap_x)
    same_other, cross_other = [permute(same[0], swap_core)], [permute(cross[0], swap_core)]
    same[2], cross[2], xb, same_other[0], cross_other[0], same[1], cross[1], y2, yb, ya = fence(
        same[2], cross[2], xb, same_other[0], cross_other[0], same[1], cross[1], y2, yb, ya
    )

    same.append(permute(same[2], same_core))
    w2 = permute(jnp.where(c == 0, xa, xb), y_way)
    for turn in (1, 2):
        same_other.append(permute(same[turn], swap_core))
        cross_other.append(permute(cross[turn], swap_core))
    same_other.append(permute(same[3], swap_core))

    head = TAG + PIECE
    held = [own, same[0], same[1], same[2], same[2], cross[2], cross[1], cross[0]]
    piece = lax.select_n(z, *[value[:head] for value in held])
    to_one = lambda y, x, z, c: (y, 1, z, c)
    side = lambda z: 0 if z < 4 else 1
    piece_near = permute(
        piece, to_one, keep=lambda y, x, z, c: x == 2 and z != 4 and c == side(z)
    )
    piece_far = permute(
        piece,
        lambda y, x, z, c: (y, 1, z + 1, c),
        keep=lambda y, x, z, c: x == 2 and z == 3 and c == 0,
    )
    piece = piece_near + piece_far
    piece = piece + permute(piece, swap_core)
    odd = jnp.concatenate([own[TAG:head], yb[:PIECE], y2[:PIECE], ya[:PIECE]], axis=0)
    at_start = lambda y, x, z, c: z == 0 and c == 0
    odd = permute(odd, to_one, keep=lambda *a: a[1] == 2 and at_start(*a))
    odd = odd + permute(odd, swap_x, keep=lambda *a: a[1] == 1 and at_start(*a))

    args = [own, x1, ya, yb, y2, xa, xb, w2, odd]
    tag_cuts = [(0, 0), (1, 0)]
    row_cuts = [(0, TAG), (3, 0), (4, 0), (2, 0), (1, TAG), (6, 0), (7, 0), (5, 0), (8, 0)]
    row_cuts = [(arg, first, BLOCK) for arg, first in row_cuts]
    cols = [own, own_other]
    for turn in range(3):
        cols += [same[turn], cross[turn], same_other[turn], cross_other[turn]]
    cols += [same[3], same_other[3]]
    cols = [(value, BLOCK) for value in cols] + [(piece, PIECE)]
    odd_here = ((x < 2) & (z == 0) & (c == 0)).astype(jnp.int32).reshape(1)
    stats, stats_x, odd_stats = pair_sums(odd_here, args, row_cuts, tag_cuts, cols)

    kept = stats + permute(stats_x, swap_x)
    odd_total = jnp.zeros_like(odd_stats)
    for start in (0, 1):
        odd_total = odd_total + permute(
            odd_stats,
            lambda y, x, z, c: (y, 2, z, c),
            keep=lambda *a, start=start: a[1] == start and at_start(*a),
        )
    odd_total = odd_total.reshape(4, NY, PIECE)
    kept = kept.reshape(4, NY, BLOCK) + jnp.pad(odd_total, ((0, 0), (0, 0), (0, BLOCK - PIECE)))
    total = kept
    for turn in (2, 1, 3):
        total = total + jnp.roll(permute(kept, along_y(turn)), -turn, axis=1)
    weight = 1.0 / (PIECE * 32.0**3)
    proof = (total[0] / total[2] - total[1] / total[3]) * weight
    proof = jnp.concatenate([proof, proof], axis=0)
    proof = lax.dynamic_slice_in_dim(proof, (NY - y) % NY, NY, 0).reshape(NY, blocks, PIECE)
    return jnp.transpose(proof, (1, 0, 2)).reshape(-1)


def solution(mesh):
    placed = (P("shower", "layer"), P("layer", None), P("layer", None), P("shower"), P("shower"))
    return jax.shard_map(shards, mesh=mesh, in_specs=placed, out_specs=P("shower"), check_vma=False)
```

time: 108 us -> 123 us (1.14)
  starting transfers between devices: 32 us -> 43.4 us
  Pallas kernels: 16.1 us -> 21.6 us
  other arithmetic: 11 us -> 8.77 us
  waiting for transfers between devices: 43.9 us -> 45.3 us
    ppermute x30 -> x39, starting transfers between devices: 32 us -> 43.4 us  [permute(): return lax.ppermute(value, AXES, pairs)]
    unnamed x2 -> x0, other arithmetic: 4.02 us -> none
    pallas_call x1 -> x2, Pallas kernels: 5.48 us -> 8.45 us  [raw_partial(): pl.pallas_call(functools.partial(raw_kernel, part_of=part_of), grid=(1,),...]
    convert_element_type x0 -> x2, other arithmetic: none -> 2.65 us  [the longest x1 2.52 us: shards(): tag = tag.astype(jnp.bfloat16)]
    pallas_call x1, Pallas kernels: 10.7 us -> 13.1 us  [pair_sums(): pl.pallas_call(functools.partial(pair_kernel, row_cuts=tuple(row_cuts), t...]
    ppermute x30 -> x39, waiting for transfers between devices: 43.9 us -> 45.3 us  [permute(): return lax.ppermute(value, AXES, pairs)]
    dynamic_slice x1 -> x2, other arithmetic: 1.74 us -> 2.56 us  [share(): lax.dynamic_index_in_dim(partial_sums, (y + turn) % NY, 1, keepdims=False)]
  transfers between devices with their start and end apart: 30 -> 39, of which waited for: 17 -> 16; matrix products, arithmetic and copies ran while one was open for 9% -> 6% of each run, Pallas kernels for 0% -> 3%
where the time goes in v5:
time: 123 us
  waiting for transfers between devices  45.3 us (37%)
  starting transfers between devices  43.4 us (35%)
  Pallas kernels  21.6 us (18%)
  other arithmetic  8.77 us (7%)
  local copies, waits for them, and re-layouts  3.37 us (3%)
    ppermute x39, waiting for transfers between devices, permute(): return lax.ppermute(value, AXES, pairs)  45.3 us
    ppermute x39, starting transfers between devices, permute(): return lax.ppermute(value, AXES, pairs)  43.4 us
    pallas_call x1, Pallas kernels, pair_sums(): pl.pallas_call(functools.partial(pair_kernel, row_cuts=tuple(row_cuts), t...  13.1 us
    pallas_call x2, Pallas kernels, raw_partial(): pl.pallas_call(functools.partial(raw_kernel, part_of=part_of), grid=(1,),...  8.45 us
    dynamic_slice x2, other arithmetic, share(): lax.dynamic_index_in_dim(partial_sums, (y + turn) % NY, 1, keepdims=False)  2.56 us
    convert_element_type x1, other arithmetic, shards(): tag = tag.astype(jnp.bfloat16)  2.52 us
  transfers between devices with their start and end apart: 39, of which 16 were waited for; matrix products, arithmetic and copies ran while one was open for 6% of the time, Pallas kernels for 3%

profile of v5, /device:TPU:4, one launch (start us, length us, event | category | flops | bytes accessed | tf_op | source)
XLA Modules:
  0.0 123.0 jit_solution(13715515132249832258)
XLA Ops:
  0.0 4.2 %raw.3 = f32[512,512]{1,0:T(8,128)} custom-call(s32[8,11]{1,0:T(8,128)} %bitcast.66, bf16[1584,512]{1,0:T(8,128)(2,1)} %bitcast.55, bf16[1584,1024]{1,0:T(8,128)(2,1)} %geometry.3), custom_call_target="tpu_custom_call" | custom-call | flops 830472192 | bytes 5242880 | tf_op jit(solution)/shard_map/raw/pallas_call | solution.py:81
  4.2 1.3 %constant_dynamic-slice_fusion.1 = (f32[4,1,32,512]{3,2,1,0:T(8,128)S(1)}, f16[4,1,32,512]{3,2,0,1:T(8,128)(2,1)S(1)}, f16[4,1,32,512]{3,2,0,1:T(8,128)(2,1)S(1)}, f16[4,1,32,512]{3,2,0,1:T(8,128)(2,1)S(1)}) fusion(f32[4,4,32,512]{3,2,1,0:T(8,128)} %bitcast.58, s32[]{:T(128)S(6)} %select_n.185, s32[]{:T(128)S(6)} %select_n.189, s32[]{:T(128)S(6)} %select_n.187, ...), kind=kLoop, calls=%fused_computation.39 | loop fusion | flops 196608 | bytes 1703952 | tf_op jit(solution)/shard_map/jit(dynamic_index_in_dim)/dynamic_slice | solution.py:274
  5.5 3.3 %collective-permute-start.3 = (f16[128,512]{1,0:T(8,128)(2,1)S(1)}, f16[128,512]{1,0:T(8,128)(2,1)S(1)}, u32[]{:S(2)}, u32[]{:S(2)}) collective-permute-start(f16[128,512]{1,0:T(8,128)(2,1)S(1)} %bitcast.63), channel_id=1, source_target_pairs={{0,128},{1,129},{2,130},{3,131},{4,132},{5,133},{6,134},{7,135},{8... | collective-permute-start | bytes 393224 | tf_op jit(solution)/shard_map/ppermute | solution.py:32
  9.5 2.6 %collective-permute-start.5 = (f16[128,512]{1,0:T(8,128)(2,1)S(1)}, f16[128,512]{1,0:T(8,128)(2,1)S(1)}, u32[]{:S(2)}, u32[]{:S(2)}) collective-permute-start(f16[128,512]{1,0:T(8,128)(2,1)S(1)} %bitcast.59), channel_id=1, source_target_pairs={{0,192},{1,193},{2,194},{3,195},{4,196},{5,197},{6,198},{7,199},{8... | collective-permute-start | bytes 393224 | tf_op jit(solution)/shard_map/ppermute | solution.py:32
  12.0 4.2 %raw.2 = f32[512,512]{1,0:T(8,128)} custom-call(s32[8,11]{1,0:T(8,128)} %bitcast.67, bf16[1584,512]{1,0:T(8,128)(2,1)} %bitcast.56, bf16[1584,1024]{1,0:T(8,128)(2,1)} %geometry.3), custom_call_target="tpu_custom_call" | custom-call | flops 830472192 | bytes 5242880 | tf_op jit(solution)/shard_map/raw/pallas_call | solution.py:81
  16.3 1.3 %constant_dynamic-slice_fusion.2 = (f32[4,1,32,512]{3,2,1,0:T(8,128)S(1)}, f16[4,1,32,512]{3,2,0,1:T(8,128)(2,1)S(1)}, f16[4,1,32,512]{3,2,0,1:T(8,128)(2,1)S(1)}, f16[4,1,32,512]{3,2,0,1:T(8,128)(2,1)S(1)}) fusion(f32[4,4,32,512]{3,2,1,0:T(8,128)} %bitcast.57, s32[]{:T(128)S(6)} %select_n.185, s32[]{:T(128)S(6)} %select_n.189, s32[]{:T(128)S(6)} %select_n.187, ...), kind=kLoop, calls=%fused_computation.40 | loop fusion | flops 196608 | bytes 1703952 | tf_op jit(solution)/shard_map/jit(dynamic_index_in_dim)/dynamic_slice | solution.py:274
  19.2 2.5 %select_convert_fusion = bf16[16,1024]{1,0:T(8,128)(2,1)S(1)} fusion(bf16[]{:T(256)} %bitcast.4, bf16[]{:T(256)} %bitcast.3, bf16[]{:T(256)} %bitcast.2, bf16[]{:T(256)} %bitcast.1, s32[1024]{0:T(1024)S(1)} %get-tuple-element.75, s32[1024]{0:T(1024)S(1)} %get-tuple-element.76, pred[16]{0:T(512)(128)(4,1)S(1)} %iota_compare_fusion, pred[1024]{0:T(1024)(128)(4,1)S(1)} %fusion.12), kind=kLoop, calls=%fused_computation.21 | loop fusion | flops 163840 | bytes 42008 | tf_op jit(solution)/shard_map/convert_element_type | solution.py:266
  21.7 2.5 %collective-permute-start.2 = (f16[128,512]{1,0:T(8,128)(2,1)S(1)}, f16[128,512]{1,0:T(8,128)(2,1)S(1)}, u32[]{:S(2)}, u32[]{:S(2)}) collective-permute-start(f16[128,512]{1,0:T(8,128)(2,1)S(1)} %bitcast.61), channel_id=1, source_target_pairs={{0,192},{1,193},{2,194},{3,195},{4,196},{5,197},{6,198},{7,199},{8... | collective-permute-start | bytes 393224 | tf_op jit(solution)/shard_map/ppermute | solution.py:32
  26.1 1.2 collective-permute-done.2
  27.7 1.3 %collective-permute-start.10 = (bf16[144,1024]{1,0:T(8,128)(2,1)S(1)}, bf16[144,1024]{1,0:T(8,128)(2,1)S(1)}, u32[]{:S(2)}, u32[]{:S(2)}) collective-permute-start(bf16[144,1024]{1,0:T(8,128)(2,1)S(1)} %maximum_maximum_fusion.refs_1_.refs_10_), channel_id=1, source_target_pairs={{0,16},{1,17},{2,18},{3,19},{4,20},{5,21},{6,22},{7,23},{8,24},{9,... | collective-permute-start | bytes 884744 | tf_op jit(solution)/shard_map/ppermute | solution.py:32
  29.0 3.5 %collective-permute-start.7 = (bf16[144,1024]{1,0:T(8,128)(2,1)S(1)}, bf16[144,1024]{1,0:T(8,128)(2,1)S(1)}, u32[]{:S(2)}, u32[]{:S(2)}) collective-permute-start(bf16[144,1024]{1,0:T(8,128)(2,1)S(1)} %maximum_maximum_fusion.refs_1_.refs_10_), channel_id=1, source_target_pairs={{0,15},{1,2},{2,1},{3,4},{4,3},{5,6},{6,5},{7,8},{8,7},{9,10},{10,... | collective-permute-start | bytes 884744 | tf_op jit(solution)/shard_map/ppermute | solution.py:32
  32.5 2.4 %collective-permute-start.9 = (bf16[128,1024]{1,0:T(8,128)(2,1)S(1)}, bf16[128,1024]{1,0:T(8,128)(2,1)S(1)}, u32[]{:S(2)}, u32[]{:S(2)}) collective-permute-start(bf16[128,1024]{1,0:T(8,128)(2,1)S(1)} %slice.112), channel_id=1, source_target_pairs={{0,192},{1,193},{2,194},{3,195},{4,196},{5,197},{6,198},{7,199},{8... | collective-permute-start | bytes 786440 | tf_op jit(solution)/shard_map/ppermute | solution.py:32
  34.9 6.1 %collective-permute-done.9.refs_4_ = bf16[128,1024]{1,0:T(8,128)(2,1)S(1)} collective-permute-done((bf16[128,1024]{1,0:T(8,128)(2,1)S(1)}, bf16[128,1024]{1,0:T(8,128)(2,1)S(1)}, u32[]{:S(2)}, u32[]{:S(2)}) %collective-permute-start.9) | collective-permute-done | bytes 262176 | tf_op jit(solution)/shard_map/ppermute | solution.py:32
  40.9 3.4 %collective-permute-done.8.refs_3_ = bf16[128,1024]{1,0:T(8,128)(2,1)S(1)} collective-permute-done((bf16[128,1024]{1,0:T(8,128)(2,1)S(1)}, bf16[128,1024]{1,0:T(8,128)(2,1)S(1)}, u32[]{:S(2)}, u32[]{:S(2)}) %collective-permute-start.8) | collective-permute-done | bytes 262176 | tf_op jit(solution)/shard_map/ppermute | solution.py:32
  46.0 1.9 %collective-permute-start.12 = (bf16[144,1024]{1,0:T(8,128)(2,1)S(1)}, bf16[144,1024]{1,0:T(8,128)(2,1)S(1)}, u32[]{:S(2)}, u32[]{:S(2)}) collective-permute-start(bf16[144,1024]{1,0:T(8,128)(2,1)S(1)} %collective-permute-done.7.refs_13_), channel_id=1, source_target_pairs={{0,2},{1,15},{2,4},{3,1},{4,6},{5,3},{6,8},{7,5},{8,10},{9,7},{10,... | collective-permute-start | bytes 884744 | tf_op jit(solution)/shard_map/ppermute | solution.py:32
  47.9 2.1 %collective-permute-start.15 = (bf16[144,1024]{1,0:T(8,128)(2,1)S(1)}, bf16[144,1024]{1,0:T(8,128)(2,1)S(1)}, u32[]{:S(2)}, u32[]{:S(2)}) collective-permute-start(bf16[144,1024]{1,0:T(8,128)(2,1)S(1)} %maximum_maximum_fusion.refs_1_.refs_10_), channel_id=1, source_target_pairs={{0,1},{1,0},{2,3},{3,2},{4,5},{5,4},{6,7},{7,6},{8,9},{9,8},{10,11... | collective-permute-start | bytes 884744 | tf_op jit(solution)/shard_map/ppermute | solution.py:32
  51.0 6.7 %collective-permute-done.13.refs_5_ = bf16[128,1024]{1,0:T(8,128)(2,1)S(1)} collective-permute-done((bf16[128,1024]{1,0:T(8,128)(2,1)S(1)}, bf16[128,1024]{1,0:T(8,128)(2,1)S(1)}, u32[]{:S(2)}, u32[]{:S(2)}) %collective-permute-start.13) | collective-permute-done | bytes 262176 | tf_op jit(solution)/shard_map/ppermute | solution.py:32
  58.6 1.6 %collective-permute-start.16 = (bf16[144,1024]{1,0:T(8,128)(2,1)S(1)}, bf16[144,1024]{1,0:T(8,128)(2,1)S(1)}, u32[]{:S(2)}, u32[]{:S(2)}) collective-permute-start(bf16[144,1024]{1,0:T(8,128)(2,1)S(1)} %collective-permute-done.11.refs_16_), channel_id=1, source_target_pairs={{0,2},{1,15},{2,4},{3,1},{4,6},{5,3},{6,8},{7,5},{8,10},{9,7},{10,... | collective-permute-start | bytes 884744 | tf_op jit(solution)/shard_map/ppermute | solution.py:32
  60.1 1.5 %collective-permute-start.17 = (bf16[144,1024]{1,0:T(8,128)(2,1)S(1)}, bf16[144,1024]{1,0:T(8,128)(2,1)S(1)}, u32[]{:S(2)}, u32[]{:S(2)}) collective-permute-start(bf16[144,1024]{1,0:T(8,128)(2,1)S(1)} %collective-permute-done.12.refs_17_), channel_id=1, source_target_pairs={{0,2},{1,15},{2,4},{3,1},{4,6},{5,3},{6,8},{7,5},{8,10},{9,7},{10,... | collective-permute-start | bytes 884744 | tf_op jit(solution)/shard_map/ppermute | solution.py:32
  62.9 7.4 %collective-permute-done.18.refs_7_ = bf16[128,1024]{1,0:T(8,128)(2,1)S(1)} collective-permute-done((bf16[128,1024]{1,0:T(8,128)(2,1)S(1)}, bf16[128,1024]{1,0:T(8,128)(2,1)S(1)}, u32[]{:S(2)}, u32[]{:S(2)}) %collective-permute-start.18) | collective-permute-done | bytes 262176 | tf_op jit(solution)/shard_map/ppermute | solution.py:32
  71.3 1.8 %collective-permute-start.22 = (bf16[128,1024]{1,0:T(8,128)(2,1)S(1)}, bf16[128,1024]{1,0:T(8,128)(2,1)S(1)}, u32[]{:S(2)}, u32[]{:S(2)}) collective-permute-start(bf16[128,1024]{1,0:T(8,128)(2,1)S(1)} %pad_maximum_fusion), channel_id=1, source_target_pairs={{32,16},{96,80},{160,144},{224,208}} | collective-permute-start | bytes 786440 | tf_op jit(solution)/shard_map/ppermute | solution.py:32
  73.5 3.4 %collective-permute-done.22 = bf16[128,1024]{1,0:T(8,128)(2,1)S(1)} collective-permute-done((bf16[128,1024]{1,0:T(8,128)(2,1)S(1)}, bf16[128,1024]{1,0:T(8,128)(2,1)S(1)}, u32[]{:S(2)}, u32[]{:S(2)}) %collective-permute-start.22) | collective-permute-done | bytes 262176 | tf_op jit(solution)/shard_map/ppermute | solution.py:32
  79.2 5.0 %collective-permute-start.30 = (bf16[48,1024]{1,0:T(8,128)(2,1)S(1)}, bf16[48,1024]{1,0:T(8,128)(2,1)S(1)}, u32[]{:S(2)}, u32[]{:S(2)}) collective-permute-start(bf16[48,1024]{1,0:T(8,128)(2,1)S(1)} %select_select_fusion), channel_id=1, source_target_pairs={{32,16},{34,18},{36,20},{38,22},{43,27},{45,29},{47,31},{96,80},{9... | collective-permute-start | bytes 294920 | tf_op jit(solution)/shard_map/ppermute | solution.py:32
  84.2 2.2 %collective-permute-done.30 = bf16[48,1024]{1,0:T(8,128)(2,1)S(1)} collective-permute-done((bf16[48,1024]{1,0:T(8,128)(2,1)S(1)}, bf16[48,1024]{1,0:T(8,128)(2,1)S(1)}, u32[]{:S(2)}, u32[]{:S(2)}) %collective-permute-start.30) | collective-permute-done | bytes 98336 | tf_op jit(solution)/shard_map/ppermute | solution.py:32
  91.1 13.1 %pairs.1 = (f32[4,512]{1,0:T(4,128)}, f32[4,512]{1,0:T(4,128)}, f32[4,128]{1,0:T(4,128)}) custom-call(s32[1]{0:T(128)} %bitcast.refs_0_, bf16[144,1024]{1,0:T(8,128)(2,1)} %copy-done, bf16[144,1024]{1,0:T(8,128)(2,1)} %copy-done.12, bf16[128,1024]{1,0:T(8,128)(2,1)} %copy-done.2, bf16[128,1024]{1,0:T(8,128)(2,1)} %copy-done.1, bf16[128,1024]{1,0:T(8,128)(2,1)} %copy-done.11, ...), custom_call_target="tpu_custom_call" | custom-call | flops 4907335680 | bytes 6619136 | tf_op jit(solution)/shard_map/pairs/pallas_call | solution.py:219
  104.3 1.3 %collective-permute-start.35 = (f32[4,128]{1,0:T(4,128)}, f32[4,128]{1,0:T(4,128)S(1)}, u32[]{:S(2)}, u32[]{:S(2)}) collective-permute-start(f32[4,128]{1,0:T(4,128)} %get-tuple-element.58), channel_id=1, source_target_pairs={{16,32},{80,96},{144,160},{208,224}} | collective-permute-start | bytes 6152 | tf_op jit(solution)/shard_map/ppermute | solution.py:32
  105.6 1.3 %collective-permute-start.34 = (f32[4,128]{1,0:T(4,128)}, f32[4,128]{1,0:T(4,128)S(1)}, u32[]{:S(2)}, u32[]{:S(2)}) collective-permute-start(f32[4,128]{1,0:T(4,128)} %get-tuple-element.58), channel_id=1, source_target_pairs={{0,32},{64,96},{128,160},{192,224}} | collective-permute-start | bytes 6152 | tf_op jit(solution)/shard_map/ppermute | solution.py:32
  106.9 3.1 %collective-permute-done.35 = f32[4,128]{1,0:T(4,128)S(1)} collective-permute-done((f32[4,128]{1,0:T(4,128)}, f32[4,128]{1,0:T(4,128)S(1)}, u32[]{:S(2)}, u32[]{:S(2)}) %collective-permute-start.35) | collective-permute-done | bytes 2080 | tf_op jit(solution)/shard_map/ppermute | solution.py:32
  110.0 2.8 %collective-permute-done.34 = f32[4,128]{1,0:T(4,128)S(1)} collective-permute-done((f32[4,128]{1,0:T(4,128)}, f32[4,128]{1,0:T(4,128)S(1)}, u32[]{:S(2)}, u32[]{:S(2)}) %collective-permute-start.34) | collective-permute-done | bytes 2080 | tf_op jit(solution)/shard_map/ppermute | solution.py:32
  113.7 3.2 %collective-permute-start.38 = (f32[4,4,128]{2,1,0:T(4,128)S(1)}, f32[4,4,128]{2,1,0:T(4,128)S(1)}, u32[]{:S(2)}, u32[]{:S(2)}) collective-permute-start(f32[4,4,128]{2,1,0:T(4,128)S(1)} %pad_add_fusion), channel_id=1, source_target_pairs={{0,192},{1,193},{2,194},{3,195},{4,196},{5,197},{6,198},{7,199},{8... | collective-permute-start | bytes 24584 | tf_op jit(solution)/shard_map/ppermute | solution.py:32
  117.0 1.6 %collective-permute-done.37 = f32[4,4,128]{2,1,0:T(4,128)S(1)} collective-permute-done((f32[4,4,128]{2,1,0:T(4,128)S(1)}, f32[4,4,128]{2,1,0:T(4,128)S(1)}, u32[]{:S(2)}, u32[]{:S(2)}) %collective-permute-start.37) | collective-permute-done | bytes 8224 | tf_op jit(solution)/shard_map/ppermute | solution.py:32
  118.6 3.5 %collective-permute-done.36 = f32[4,4,128]{2,1,0:T(4,128)S(1)} collective-permute-done((f32[4,4,128]{2,1,0:T(4,128)S(1)}, f32[4,4,128]{2,1,0:T(4,128)S(1)}, u32[]{:S(2)}, u32[]{:S(2)}) %collective-permute-start.36) | collective-permute-done | bytes 8224 | tf_op jit(solution)/shard_map/ppermute | solution.py:32
  (128 shorter events, 19.4 us)
Async XLA Ops:
  5.5 16.2 %collective-permute-start.3 = (f16[128,512]{1,0:T(8,128)(2,1)S(1)}, f16[128,512]{1,0:T(8,128)(2,1)S(1)}, u32[]{:S(2)}, u32[]{:S(2)}) collective-permute-start(f16[128,512]{1,0:T(8,128)(2,1)S(1)} %bitcast.63), channel_id=1, source_target_pairs={{0,128},{1,129},{2,130},{3,131},{4,132},{5,133},{6,134},{7,135},{8... | collective-permute-start | bytes 393224 | tf_op jit(solution)/shard_map/ppermute | solution.py:32
  8.8 15.4 %collective-permute-start.4 = (f16[128,512]{1,0:T(8,128)(2,1)S(1)}, f16[128,512]{1,0:T(8,128)(2,1)S(1)}, u32[]{:S(2)}, u32[]{:S(2)}) collective-permute-start(f16[128,512]{1,0:T(8,128)(2,1)S(1)} %bitcast.60), channel_id=1, source_target_pairs={{0,64},{1,65},{2,66},{3,67},{4,68},{5,69},{6,70},{7,71},{8,72},{9,... | collective-permute-start | bytes 393224 | tf_op jit(solution)/shard_map/ppermute | solution.py:32
  9.5 14.7 %collective-permute-start.5 = (f16[128,512]{1,0:T(8,128)(2,1)S(1)}, f16[128,512]{1,0:T(8,128)(2,1)S(1)}, u32[]{:S(2)}, u32[]{:S(2)}) collective-permute-start(f16[128,512]{1,0:T(8,128)(2,1)S(1)} %bitcast.59), channel_id=1, source_target_pairs={{0,192},{1,193},{2,194},{3,195},{4,196},{5,197},{6,198},{7,199},{8... | collective-permute-start | bytes 393224 | tf_op jit(solution)/shard_map/ppermute | solution.py:32
  17.5 7.5 %collective-permute-start = (f16[128,512]{1,0:T(8,128)(2,1)S(1)}, f16[128,512]{1,0:T(8,128)(2,1)S(1)}, u32[]{:S(2)}, u32[]{:S(2)}) collective-permute-start(f16[128,512]{1,0:T(8,128)(2,1)S(1)} %bitcast.64), channel_id=1, source_target_pairs={{0,128},{1,129},{2,130},{3,131},{4,132},{5,133},{6,134},{7,135},{8... | collective-permute-start | bytes 393224 | tf_op jit(solution)/shard_map/ppermute | solution.py:32
  17.6 8.5 %collective-permute-start.1 = (f16[128,512]{1,0:T(8,128)(2,1)S(1)}, f16[128,512]{1,0:T(8,128)(2,1)S(1)}, u32[]{:S(2)}, u32[]{:S(2)}) collective-permute-start(f16[128,512]{1,0:T(8,128)(2,1)S(1)} %bitcast.62), channel_id=1, source_target_pairs={{0,64},{1,65},{2,66},{3,67},{4,68},{5,69},{6,70},{7,71},{8,72},{9,... | collective-permute-start | bytes 393224 | tf_op jit(solution)/shard_map/ppermute | solution.py:32
  21.7 5.6 %collective-permute-start.2 = (f16[128,512]{1,0:T(8,128)(2,1)S(1)}, f16[128,512]{1,0:T(8,128)(2,1)S(1)}, u32[]{:S(2)}, u32[]{:S(2)}) collective-permute-start(f16[128,512]{1,0:T(8,128)(2,1)S(1)} %bitcast.61), channel_id=1, source_target_pairs={{0,192},{1,193},{2,194},{3,195},{4,196},{5,197},{6,198},{7,199},{8... | collective-permute-start | bytes 393224 | tf_op jit(solution)/shard_map/ppermute | solution.py:32
  27.7 16.7 %collective-permute-start.10 = (bf16[144,1024]{1,0:T(8,128)(2,1)S(1)}, bf16[144,1024]{1,0:T(8,128)(2,1)S(1)}, u32[]{:S(2)}, u32[]{:S(2)}) collective-permute-start(bf16[144,1024]{1,0:T(8,128)(2,1)S(1)} %maximum_maximum_fusion.refs_1_.refs_10_), channel_id=1, source_target_pairs={{0,16},{1,17},{2,18},{3,19},{4,20},{5,21},{6,22},{7,23},{8,24},{9,... | collective-permute-start | bytes 884744 | tf_op jit(solution)/shard_map/ppermute | solution.py:32
  29.0 15.4 %collective-permute-start.7 = (bf16[144,1024]{1,0:T(8,128)(2,1)S(1)}, bf16[144,1024]{1,0:T(8,128)(2,1)S(1)}, u32[]{:S(2)}, u32[]{:S(2)}) collective-permute-start(bf16[144,1024]{1,0:T(8,128)(2,1)S(1)} %maximum_maximum_fusion.refs_1_.refs_10_), channel_id=1, source_target_pairs={{0,15},{1,2},{2,1},{3,4},{4,3},{5,6},{6,5},{7,8},{8,7},{9,10},{10,... | collective-permute-start | bytes 884744 | tf_op jit(solution)/shard_map/ppermute | solution.py:32
  32.4 12.7 %collective-permute-start.6 = (bf16[144,1024]{1,0:T(8,128)(2,1)S(1)}, bf16[144,1024]{1,0:T(8,128)(2,1)S(1)}, u32[]{:S(2)}, u32[]{:S(2)}) collective-permute-start(bf16[144,1024]{1,0:T(8,128)(2,1)S(1)} %maximum_maximum_fusion.refs_1_.refs_10_), channel_id=1, source_target_pairs={{0,2},{1,15},{2,4},{3,1},{4,6},{5,3},{6,8},{7,5},{8,10},{9,7},{10,... | collective-permute-start | bytes 884744 | tf_op jit(solution)/shard_map/ppermute | solution.py:32
  32.5 8.5 %collective-permute-start.9 = (bf16[128,1024]{1,0:T(8,128)(2,1)S(1)}, bf16[128,1024]{1,0:T(8,128)(2,1)S(1)}, u32[]{:S(2)}, u32[]{:S(2)}) collective-permute-start(bf16[128,1024]{1,0:T(8,128)(2,1)S(1)} %slice.112), channel_id=1, source_target_pairs={{0,192},{1,193},{2,194},{3,195},{4,196},{5,197},{6,198},{7,199},{8... | collective-permute-start | bytes 786440 | tf_op jit(solution)/shard_map/ppermute | solution.py:32
  34.9 9.5 %collective-permute-start.8 = (bf16[128,1024]{1,0:T(8,128)(2,1)S(1)}, bf16[128,1024]{1,0:T(8,128)(2,1)S(1)}, u32[]{:S(2)}, u32[]{:S(2)}) collective-permute-start(bf16[128,1024]{1,0:T(8,128)(2,1)S(1)} %slice.112), channel_id=1, source_target_pairs={{0,64},{1,65},{2,66},{3,67},{4,68},{5,69},{6,70},{7,71},{8,72},{9,... | collective-permute-start | bytes 786440 | tf_op jit(solution)/shard_map/ppermute | solution.py:32
  45.1 13.4 %collective-permute-start.11 = (bf16[144,1024]{1,0:T(8,128)(2,1)S(1)}, bf16[144,1024]{1,0:T(8,128)(2,1)S(1)}, u32[]{:S(2)}, u32[]{:S(2)}) collective-permute-start(bf16[144,1024]{1,0:T(8,128)(2,1)S(1)} %collective-permute-done.6.refs_12_), channel_id=1, source_target_pairs={{0,2},{1,15},{2,4},{3,1},{4,6},{5,3},{6,8},{7,5},{8,10},{9,7},{10,... | collective-permute-start | bytes 884744 | tf_op jit(solution)/shard_map/ppermute | solution.py:32
  46.0 12.5 %collective-permute-start.12 = (bf16[144,1024]{1,0:T(8,128)(2,1)S(1)}, bf16[144,1024]{1,0:T(8,128)(2,1)S(1)}, u32[]{:S(2)}, u32[]{:S(2)}) collective-permute-start(bf16[144,1024]{1,0:T(8,128)(2,1)S(1)} %collective-permute-done.7.refs_13_), channel_id=1, source_target_pairs={{0,2},{1,15},{2,4},{3,1},{4,6},{5,3},{6,8},{7,5},{8,10},{9,7},{10,... | collective-permute-start | bytes 884744 | tf_op jit(solution)/shard_map/ppermute | solution.py:32
  47.9 10.6 %collective-permute-start.15 = (bf16[144,1024]{1,0:T(8,128)(2,1)S(1)}, bf16[144,1024]{1,0:T(8,128)(2,1)S(1)}, u32[]{:S(2)}, u32[]{:S(2)}) collective-permute-start(bf16[144,1024]{1,0:T(8,128)(2,1)S(1)} %maximum_maximum_fusion.refs_1_.refs_10_), channel_id=1, source_target_pairs={{0,1},{1,0},{2,3},{3,2},{4,5},{5,4},{6,7},{7,6},{8,9},{9,8},{10,11... | collective-permute-start | bytes 884744 | tf_op jit(solution)/shard_map/ppermute | solution.py:32
  50.0 7.7 %collective-permute-start.13 = (bf16[128,1024]{1,0:T(8,128)(2,1)S(1)}, bf16[128,1024]{1,0:T(8,128)(2,1)S(1)}, u32[]{:S(2)}, u32[]{:S(2)}) collective-permute-start(bf16[128,1024]{1,0:T(8,128)(2,1)S(1)} %broadcast_select_fusion.1), channel_id=1, source_target_pairs={{0,64},{1,193},{2,66},{3,195},{4,68},{5,197},{6,70},{7,199},{8,72}... | collective-permute-start | bytes 786440 | tf_op jit(solution)/shard_map/ppermute | solution.py:32
  50.1 8.4 %collective-permute-start.14 = (bf16[128,1024]{1,0:T(8,128)(2,1)S(1)}, bf16[128,1024]{1,0:T(8,128)(2,1)S(1)}, u32[]{:S(2)}, u32[]{:S(2)}) collective-permute-start(bf16[128,1024]{1,0:T(8,128)(2,1)S(1)} %collective-permute-done.8.refs_3_), channel_id=1, source_target_pairs={{0,16},{1,17},{2,18},{3,19},{4,20},{5,21},{6,22},{7,23},{8,24},{9,... | collective-permute-start | bytes 786440 | tf_op jit(solution)/shard_map/ppermute | solution.py:32
  58.6 11.7 %collective-permute-start.16 = (bf16[144,1024]{1,0:T(8,128)(2,1)S(1)}, bf16[144,1024]{1,0:T(8,128)(2,1)S(1)}, u32[]{:S(2)}, u32[]{:S(2)}) collective-permute-start(bf16[144,1024]{1,0:T(8,128)(2,1)S(1)} %collective-permute-done.11.refs_16_), channel_id=1, source_target_pairs={{0,2},{1,15},{2,4},{3,1},{4,6},{5,3},{6,8},{7,5},{8,10},{9,7},{10,... | collective-permute-start | bytes 884744 | tf_op jit(solution)/shard_map/ppermute | solution.py:32
  60.1 10.2 %collective-permute-start.17 = (bf16[144,1024]{1,0:T(8,128)(2,1)S(1)}, bf16[144,1024]{1,0:T(8,128)(2,1)S(1)}, u32[]{:S(2)}, u32[]{:S(2)}) collective-permute-start(bf16[144,1024]{1,0:T(8,128)(2,1)S(1)} %collective-permute-done.12.refs_17_), channel_id=1, source_target_pairs={{0,2},{1,15},{2,4},{3,1},{4,6},{5,3},{6,8},{7,5},{8,10},{9,7},{10,... | collective-permute-start | bytes 884744 | tf_op jit(solution)/shard_map/ppermute | solution.py:32
  61.6 8.8 %collective-permute-start.19 = (bf16[144,1024]{1,0:T(8,128)(2,1)S(1)}, bf16[144,1024]{1,0:T(8,128)(2,1)S(1)}, u32[]{:S(2)}, u32[]{:S(2)}) collective-permute-start(bf16[144,1024]{1,0:T(8,128)(2,1)S(1)} %collective-permute-done.6.refs_12_), channel_id=1, source_target_pairs={{0,1},{1,0},{2,3},{3,2},{4,5},{5,4},{6,7},{7,6},{8,9},{9,8},{10,11... | collective-permute-start | bytes 884744 | tf_op jit(solution)/shard_map/ppermute | solution.py:32
  61.6 8.8 %collective-permute-start.20 = (bf16[144,1024]{1,0:T(8,128)(2,1)S(1)}, bf16[144,1024]{1,0:T(8,128)(2,1)S(1)}, u32[]{:S(2)}, u32[]{:S(2)}) collective-permute-start(bf16[144,1024]{1,0:T(8,128)(2,1)S(1)} %collective-permute-done.7.refs_13_), channel_id=1, source_target_pairs={{0,1},{1,0},{2,3},{3,2},{4,5},{5,4},{6,7},{7,6},{8,9},{9,8},{10,11... | collective-permute-start | bytes 884744 | tf_op jit(solution)/shard_map/ppermute | solution.py:32
  62.1 8.2 %collective-permute-start.18 = (bf16[128,1024]{1,0:T(8,128)(2,1)S(1)}, bf16[128,1024]{1,0:T(8,128)(2,1)S(1)}, u32[]{:S(2)}, u32[]{:S(2)}) collective-permute-start(bf16[128,1024]{1,0:T(8,128)(2,1)S(1)} %collective-permute-done.9.refs_4_), channel_id=1, source_target_pairs={{0,16},{1,17},{2,18},{3,19},{4,20},{5,21},{6,22},{7,23},{8,24},{9,... | collective-permute-start | bytes 786440 | tf_op jit(solution)/shard_map/ppermute | solution.py:32
  71.3 5.6 %collective-permute-start.22 = (bf16[128,1024]{1,0:T(8,128)(2,1)S(1)}, bf16[128,1024]{1,0:T(8,128)(2,1)S(1)}, u32[]{:S(2)}, u32[]{:S(2)}) collective-permute-start(bf16[128,1024]{1,0:T(8,128)(2,1)S(1)} %pad_maximum_fusion), channel_id=1, source_target_pairs={{32,16},{96,80},{160,144},{224,208}} | collective-permute-start | bytes 786440 | tf_op jit(solution)/shard_map/ppermute | solution.py:32
  73.1 14.9 %collective-permute-start.21 = (bf16[128,1024]{1,0:T(8,128)(2,1)S(1)}, bf16[128,1024]{1,0:T(8,128)(2,1)S(1)}, u32[]{:S(2)}, u32[]{:S(2)}) collective-permute-start(bf16[128,1024]{1,0:T(8,128)(2,1)S(1)} %broadcast_select_fusion), channel_id=1, source_target_pairs={{0,64},{1,193},{2,66},{3,195},{4,68},{5,197},{6,70},{7,199},{8,72}... | collective-permute-start | bytes 786440 | tf_op jit(solution)/shard_map/ppermute | solution.py:32
  73.2 15.1 %collective-permute-start.28 = (bf16[144,1024]{1,0:T(8,128)(2,1)S(1)}, bf16[144,1024]{1,0:T(8,128)(2,1)}, u32[]{:S(2)}, u32[]{:S(2)}) collective-permute-start(bf16[144,1024]{1,0:T(8,128)(2,1)S(1)} %collective-permute-done.16.refs_20_), channel_id=1, source_target_pairs={{0,2},{1,15},{2,4},{3,1},{4,6},{5,3},{6,8},{7,5},{8,10},{9,7},{10,... | collective-permute-start | bytes 884744 | tf_op jit(solution)/shard_map/ppermute | solution.py:32
  76.9 11.6 %collective-permute-start.23 = (bf16[128,1024]{1,0:T(8,128)(2,1)S(1)}, bf16[128,1024]{1,0:T(8,128)(2,1)S(1)}, u32[]{:S(2)}, u32[]{:S(2)}) collective-permute-start(bf16[128,1024]{1,0:T(8,128)(2,1)S(1)} %collective-permute-done.22), channel_id=1, source_target_pairs={{16,0},{80,64},{144,128},{208,192}} | collective-permute-start | bytes 786440 | tf_op jit(solution)/shard_map/ppermute | solution.py:32
  78.5 5.7 %collective-permute-start.31 = (bf16[48,1024]{1,0:T(8,128)(2,1)S(1)}, bf16[48,1024]{1,0:T(8,128)(2,1)S(1)}, u32[]{:S(2)}, u32[]{:S(2)}) collective-permute-start(bf16[48,1024]{1,0:T(8,128)(2,1)S(1)} %select_select_fusion), channel_id=1, source_target_pairs={{38,24},{102,88},{166,152},{230,216}} | collective-permute-start | bytes 294920 | tf_op jit(solution)/shard_map/ppermute | solution.py:32
  79.2 7.2 %collective-permute-start.30 = (bf16[48,1024]{1,0:T(8,128)(2,1)S(1)}, bf16[48,1024]{1,0:T(8,128)(2,1)S(1)}, u32[]{:S(2)}, u32[]{:S(2)}) collective-permute-start(bf16[48,1024]{1,0:T(8,128)(2,1)S(1)} %select_select_fusion), channel_id=1, source_target_pairs={{32,16},{34,18},{36,20},{38,22},{43,27},{45,29},{47,31},{96,80},{9... | collective-permute-start | bytes 294920 | tf_op jit(solution)/shard_map/ppermute | solution.py:32
  104.2 8.7 %collective-permute-start.33 = (f32[4,512]{1,0:T(4,128)}, f32[4,512]{1,0:T(4,128)S(1)}, u32[]{:S(2)}, u32[]{:S(2)}) collective-permute-start(f32[4,512]{1,0:T(4,128)} %get-tuple-element.57), channel_id=1, source_target_pairs={{0,16},{1,17},{2,18},{3,19},{4,20},{5,21},{6,22},{7,23},{8,24},{9,... | collective-permute-start | bytes 24584 | tf_op jit(solution)/shard_map/ppermute | solution.py:32
  104.3 5.7 %collective-permute-start.35 = (f32[4,128]{1,0:T(4,128)}, f32[4,128]{1,0:T(4,128)S(1)}, u32[]{:S(2)}, u32[]{:S(2)}) collective-permute-start(f32[4,128]{1,0:T(4,128)} %get-tuple-element.58), channel_id=1, source_target_pairs={{16,32},{80,96},{144,160},{208,224}} | collective-permute-start | bytes 6152 | tf_op jit(solution)/shard_map/ppermute | solution.py:32
  105.6 7.2 %collective-permute-start.34 = (f32[4,128]{1,0:T(4,128)}, f32[4,128]{1,0:T(4,128)S(1)}, u32[]{:S(2)}, u32[]{:S(2)}) collective-permute-start(f32[4,128]{1,0:T(4,128)} %get-tuple-element.58), channel_id=1, source_target_pairs={{0,32},{64,96},{128,160},{192,224}} | collective-permute-start | bytes 6152 | tf_op jit(solution)/shard_map/ppermute | solution.py:32
  113.7 4.9 %collective-permute-start.37 = (f32[4,4,128]{2,1,0:T(4,128)S(1)}, f32[4,4,128]{2,1,0:T(4,128)S(1)}, u32[]{:S(2)}, u32[]{:S(2)}) collective-permute-start(f32[4,4,128]{2,1,0:T(4,128)S(1)} %pad_add_fusion), channel_id=1, source_target_pairs={{0,64},{1,65},{2,66},{3,67},{4,68},{5,69},{6,70},{7,71},{8,72},{9,... | collective-permute-start | bytes 24584 | tf_op jit(solution)/shard_map/ppermute | solution.py:32
  117.0 5.2 %collective-permute-start.36 = (f32[4,4,128]{2,1,0:T(4,128)S(1)}, f32[4,4,128]{2,1,0:T(4,128)S(1)}, u32[]{:S(2)}, u32[]{:S(2)}) collective-permute-start(f32[4,4,128]{2,1,0:T(4,128)S(1)} %pad_add_fusion), channel_id=1, source_target_pairs={{0,128},{1,129},{2,130},{3,131},{4,132},{5,133},{6,134},{7,135},{8... | collective-permute-start | bytes 24584 | tf_op jit(solution)/shard_map/ppermute | solution.py:32
  (26 other events, 458.5 us)

commit v6 on v3

v6 whole, which is shorter than its diff:
```python
import functools

import jax
import jax.numpy as jnp
from jax import lax
from jax.experimental import pallas as pl
from jax.experimental.pallas import tpu as pltpu
from jax.sharding import PartitionSpec as P

BLOCK = 128
PIECE = 32
TAG = 16
BINS = 8
CHUNK = 512
AXES = ("layer", "shower")
NY, NX, NZ, NC = 4, 4, 8, 2


def flat(y, x, z, c):
    return y * (NX * NZ * NC) + (x * NZ + z) * NC + c


def permute(value, move, keep=lambda y, x, z, c: True):
    pairs = [
        (flat(y, x, z, c), flat(*move(y, x, z, c)))
        for y in range(NY)
        for x in range(NX)
        for z in range(NZ)
        for c in range(NC)
        if keep(y, x, z, c)
    ]
    return lax.ppermute(value, AXES, pairs)


def along_y(step):
    return lambda y, x, z, c: ((y + step) % NY, x, z, c)


def along_z(step):
    return lambda y, x, z, c: (y, x, (z + step) % NZ, c)


def flip_z(bit):
    return lambda y, x, z, c: (y, x, z ^ bit, c)


def swap_x(y, x, z, c):
    return (y, x ^ 1, z, c)


def swap_core(y, x, z, c):
    return (y, x, z, 1 - c)


def same_core(y, x, z, c):
    return (y, x, (z + 1 - 2 * c) % NZ, c)


def cross_core(y, x, z, c):
    return (y, x, (z - 1 + 2 * c) % NZ, 1 - c)


def raw_kernel(pattern, showers, geometry, out, masked):
    step = pl.program_id(0)
    layers = pattern.shape[1]
    cells = geometry.shape[0] // layers
    per = geometry.shape[1] // BLOCK
    for layer in range(layers):
        for part in range(per):
            rows = pl.ds(layer * cells, cells)
            cols = pl.ds(part * BLOCK, BLOCK)
            on = pattern[step * per + part, layer].astype(jnp.float32).astype(jnp.bfloat16)
            masked[rows, cols] = geometry[rows, cols] * on
    out[...] = lax.dot_general(
        showers[...], masked[...], (((0,), (0,)), ((), ())), preferred_element_type=jnp.float32
    )


def raw_partial(showers, geometry, pattern):
    rows, depth = showers.shape
    feats = geometry.shape[1]
    width = 512
    return pl.pallas_call(
        raw_kernel,
        grid=(feats // width,),
        in_specs=[
            pl.BlockSpec(memory_space=pltpu.SMEM),
            pl.BlockSpec((depth, rows), lambda i: (0, 0)),
            pl.BlockSpec((depth, width), lambda i: (0, i)),
        ],
        out_specs=pl.BlockSpec((rows, width), lambda i: (0, i)),
        out_shape=jax.ShapeDtypeStruct((rows, feats), jnp.float32),
        scratch_shapes=[pltpu.VMEM((depth, width), jnp.bfloat16)],
        compiler_params=pltpu.CompilerParams(vmem_limit_bytes=60 * 2**20),
        cost_estimate=pl.CostEstimate(
            flops=2 * rows * depth * feats, bytes_accessed=8 * 2**20, transcendentals=0
        ),
        name="raw",
    )(pattern.T, showers.T, geometry)


def pair_kernel(*refs, tag_cuts, col_cuts, n_args):
    n_cols = len(col_cuts)
    place = refs[0]
    args = refs[1 : 1 + n_args]
    out_near, out_far, out_theirs, out_odd = refs[1 + n_args : 5 + n_args]
    rows_at, cols_at, row_tags, col_tags, row_sems, col_sems, tag_sems = refs[5 + n_args :]
    odd_here, core = place[0], place[1]
    tagged = BLOCK + TAG
    row_args = args[n_cols_args(col_cuts) :]

    def start(source, first, size, target, at, sem):
        copy = pltpu.make_async_copy(
            source.at[pl.ds(first, size), :], target.at[pl.ds(at, size), :], sem
        )
        copy.start()
        return copy

    waits, depth = [], 0
    for at, (arg, first, size) in enumerate(col_cuts):
        waits.append(start(args[arg], first, size, cols_at, depth, col_sems.at[at]))
        waits.append(start(args[arg], first - TAG, TAG, col_tags, at * TAG, tag_sems.at[at]))
        depth += size
    for at, (arg, first) in enumerate(tag_cuts):
        waits.append(start(args[arg], first, TAG, row_tags, at * TAG, tag_sems.at[n_cols + at]))

    own, own_t, x1, x1_t, y1, y1_t, y2, y2_t, xx, xx_t, w2, w2_t, odd_rows = row_args
    turn = jnp.where(core == 0, 3, 1)
    side = [4 * CHUNK // 2 * jnp.where(core == b, 0, 1) for b in range(NC)]
    made = []

    def rows(source, first, at):
        at = at if isinstance(at, int) else pl.multiple_of(at, BLOCK)
        made.append(start(source, first, BLOCK, rows_at, at, row_sems.at[len(made)]))

    rows(own, TAG, 0)
    rows(y2, 0, 2 * BLOCK)
    for b in range(NC):
        rows(y1, TAG + b * tagged, side[b] + turn * BLOCK)
        rows(y1_t, TAG + b * tagged, side[b] + (NY - turn) * BLOCK)
    rows(own_t, TAG, 2 * CHUNK)
    rows(y2_t, 0, 2 * CHUNK + 2 * BLOCK)
    n_near = len(made)
    rows(x1, TAG, CHUNK)
    rows(w2, 0, CHUNK + 2 * BLOCK)
    for b in range(NC):
        rows(xx, TAG + b * tagged, CHUNK + side[b] + turn * BLOCK)
        rows(xx_t, TAG + b * tagged, CHUNK + side[b] + (NY - turn) * BLOCK)
    rows(x1_t, TAG, 3 * CHUNK)
    rows(w2_t, 0, 3 * CHUNK + 2 * BLOCK)
    rows(odd_rows, 0, 4 * CHUNK)
    for copy in waits:
        copy.wait()

    def bin_of(code):
        source = (code >= BINS).astype(jnp.float32)
        return code - BINS * source, source

    for chunk in (0, 2, 1, 3, 4):
        if chunk == 0:
            for copy in made[:n_near]:
                copy.wait()
        if chunk == 1:
            for copy in made[n_near:]:
                copy.wait()
        first = chunk * CHUNK
        odd = chunk == 4
        size = BLOCK if odd else CHUNK
        set_of = 0 if odd else chunk
        tag = row_tags[pl.ds(set_of * TAG + 4, 1), pl.ds(0, BLOCK)].astype(jnp.float32) - 1.0
        bins, _ = bin_of(tag)
        if odd:
            bins = jnp.where(odd_here > 0, bins, -2.0)
        bins = jnp.concatenate([bins] * (size // BLOCK), axis=1)
        one = jnp.zeros((8, size), jnp.float32)
        zero = jnp.zeros((8, size), jnp.float32)
        n_one = jnp.zeros((1, size), jnp.float32)
        n_zero = jnp.zeros((1, size), jnp.float32)
        low = 0
        while low < depth:
            high = depth if depth - low < 3 * BLOCK else low + 2 * BLOCK
            products = lax.dot_general(
                cols_at[pl.ds(low, high - low), :],
                rows_at[pl.ds(first, size), :],
                (((1,), (1,)), ((), ())),
                preferred_element_type=jnp.float32,
            )
            shifted = products + 32.0
            cubes = shifted * shifted * shifted
            for group in range(low // PIECE, high // PIECE):
                at = group * PIECE // BLOCK
                if odd and col_cuts[at][2] == PIECE:
                    continue
                block = cubes[group * PIECE - low : (group + 1) * PIECE - low]
                if first == 0 and at == 0:
                    lane = lax.broadcasted_iota(jnp.int32, block.shape, 1)
                    sub = lax.broadcasted_iota(jnp.int32, block.shape, 0)
                    block = jnp.where(lane == sub + group * PIECE, 0.0, block)
                part = (block[0:8] + block[8:16]) + (block[16:24] + block[24:32])
                row = at * TAG + group % 4
                code = col_tags[pl.ds(row, 1), pl.ds(0, size)].astype(jnp.float32) - 1.0
                bin_id, source = bin_of(code)
                match = (bins == bin_id).astype(jnp.float32)
                is_one = match * source
                is_zero = match - is_one
                one += is_one * part
                zero += is_zero * part
                n_one += is_one
                n_zero += is_zero
            low = high
        targets = {0: [(out_near, 0)], 1: [(out_far, 0)], 2: [(out_theirs, 0)]}
        targets |= {3: [(out_theirs, CHUNK)], 4: [(out_theirs, 2 * CHUNK), (out_odd, 0)]}
        for out, place_at in targets[chunk]:
            lanes = pl.ds(place_at, size)
            out[0:1, lanes] = jnp.sum(one, axis=0, keepdims=True)
            out[1:2, lanes] = jnp.sum(zero, axis=0, keepdims=True)
            out[2:3, lanes] = n_one
            out[3:4, lanes] = n_zero


def n_cols_args(col_cuts):
    return 1 + max(arg for arg, _, _ in col_cuts)


def pair_sums(place, col_args, row_args, col_cuts, tag_cuts):
    args = col_args + row_args
    total, depth = 4 * CHUNK + BLOCK, sum(size for _, _, size in col_cuts)
    feats = args[0].shape[1]
    hbm = pl.BlockSpec(memory_space=pl.ANY)
    vmem = pl.BlockSpec(memory_space=pltpu.VMEM)
    dma = pltpu.SemaphoreType.DMA
    widths = [CHUNK, CHUNK, 2 * CHUNK + BLOCK, BLOCK]
    return pl.pallas_call(
        functools.partial(
            pair_kernel, tag_cuts=tuple(tag_cuts), col_cuts=tuple(col_cuts), n_args=len(args)
        ),
        in_specs=[pl.BlockSpec(memory_space=pltpu.SMEM)] + [hbm] * len(args),
        out_specs=[vmem] * len(widths),
        out_shape=[jax.ShapeDtypeStruct((4, width), jnp.float32) for width in widths],
        scratch_shapes=[
            pltpu.VMEM((total, feats), jnp.bfloat16),
            pltpu.VMEM((depth, feats), jnp.bfloat16),
            pltpu.VMEM((TAG * len(tag_cuts), feats), jnp.bfloat16),
            pltpu.VMEM((TAG * len(col_cuts), feats), jnp.bfloat16),
            dma((17,)),
            dma((len(col_cuts),)),
            dma((len(col_cuts) + len(tag_cuts),)),
        ],
        compiler_params=pltpu.CompilerParams(vmem_limit_bytes=58 * 2**20),
        cost_estimate=pl.CostEstimate(
            flops=2 * total * depth * feats,
            bytes_accessed=2 * (total + depth) * feats,
            transcendentals=0,
        ),
        name="pairs",
    )(place, *args)


def shards(showers, geometry, pattern, bins, sources):
    y = lax.axis_index("layer")
    s = lax.axis_index("shower")
    x, z, c = s // (NZ * NC), (s // NC) % NZ, s % NC
    feats = geometry.shape[1]
    blocks = bins.shape[0]

    codes = (bins + BINS * sources + 1).astype(jnp.float32)
    line = lax.broadcasted_iota(jnp.int32, (TAG, feats), 0)
    lane = lax.broadcasted_iota(jnp.int32, (TAG, feats), 1) // PIECE
    which = jnp.where(line == blocks, lane, line)
    tag = jnp.zeros((TAG, feats), jnp.float32)
    for group in range(blocks):
        tag = jnp.where(which == group, codes[group], tag)
    tag = tag.astype(jnp.bfloat16)

    partial_sums = raw_partial(showers, geometry, pattern).reshape(blocks, NY, PIECE, feats)

    def share(turn):
        part = lax.dynamic_index_in_dim(partial_sums, (y + turn) % NY, 1, keepdims=False)
        return part.reshape(BLOCK, feats)

    raw = share(0)
    arrived = [permute(share(turn).astype(jnp.float16), along_y(turn)) for turn in (2, 1, 3)]
    for part in arrived:
        raw = raw + part.astype(jnp.float32)
    scale = lax.rsqrt(jnp.mean(raw * raw, axis=1, keepdims=True) + 1e-05)
    own = jnp.concatenate([tag, (raw * scale).astype(jnp.bfloat16)], axis=0)

    fence = lambda *values: lax.optimization_barrier(values)
    tagged = BLOCK + TAG
    y_way = lambda y, x, z, c: ((y + 1 - 2 * c) % NY, x, z, c)
    own_t = permute(own, swap_core)
    chip = jnp.where(c == 0, jnp.concatenate([own, own_t]), jnp.concatenate([own_t, own]))
    z1 = permute(chip, same_core)
    y1 = permute(chip, y_way)
    x1 = permute(own, swap_x)
    z1, y1, x1 = fence(z1, y1, x1)

    z2 = permute(z1, same_core)
    y2 = permute(jnp.where(c == 0, y1[TAG:tagged], y1[tagged + TAG :]), y_way)
    xx = permute(y1, swap_x)
    y1_t = permute(y1, swap_core)
    x1_t = permute(x1, swap_core)
    z1, z2, y2, xx, y1_t, x1_t = fence(z1, z2, y2, xx, y1_t, x1_t)

    z3 = permute(z2, same_core)
    w2 = permute(y2, swap_x)
    head = TAG + PIECE
    odd_rows = jnp.concatenate([own[TAG:head], y1_t[TAG:head], y2[:PIECE], y1[TAG:head]], axis=0)
    at_start = lambda y, x, z, c: z == 0 and c == 0
    odd_at = [
        permute(
            odd_rows,
            lambda y, x, z, c, to=to: (y, to, z, c),
            keep=lambda *a: a[1] == 2 and at_start(*a),
        )
        for to in (1, 0)
    ]
    y2_t = permute(y2, swap_core)
    z2, z3, w2, y2_t, *odd_at = fence(z2, z3, w2, y2_t, *odd_at)

    z4 = permute(jnp.where(c == 0, z3[:tagged], z3[tagged:]), same_core)
    held = [own, z1, z2, z3, z3, z3, z2, z1]
    piece = lax.select_n(z, *[value[:head] for value in held])
    side = lambda z: 0 if z < 4 else 1
    piece_near = permute(
        piece,
        lambda y, x, z, c: (y, 1, z, c),
        keep=lambda y, x, z, c: x == 2 and z != 4 and c == side(z),
    )
    piece_far = permute(
        piece,
        lambda y, x, z, c: (y, 1, z + 1, c),
        keep=lambda y, x, z, c: x == 2 and z == 3 and c == 0,
    )
    xx_t = permute(xx, swap_core)
    w2_t = permute(w2, swap_core)
    odd_rows = odd_at[0] + odd_at[1]
    odd_rows = odd_rows + permute(
        odd_rows, swap_core, keep=lambda *a: a[1] < 2 and at_start(*a)
    )
    piece = piece_near + piece_far

    col_args = [own, z1, z2, z3, z4, piece]
    col_cuts = [(0, TAG, BLOCK)]
    for arg in (1, 2, 3):
        col_cuts += [(arg, TAG, BLOCK), (arg, tagged + TAG, BLOCK)]
    col_cuts += [(4, TAG, BLOCK), (5, TAG, PIECE)]
    row_args = [own, own_t, x1, x1_t, y1, y1_t, y2, y2_t, xx, xx_t, w2, w2_t, odd_rows]
    tag_cuts = [(6, 0), (8, 0), (7, 0), (9, 0)]
    place = jnp.stack([((x < 2) & (z == 0)).astype(jnp.int32), c.astype(jnp.int32)])
    near, far, theirs, odd_stats = pair_sums(place, col_args, row_args, col_cuts, tag_cuts)

    theirs = permute(theirs, swap_core)
    kept = near + theirs[:, :CHUNK] + permute(far + theirs[:, CHUNK : 2 * CHUNK], swap_x)
    odd_stats = odd_stats + theirs[:, 2 * CHUNK :]
    odd_total = jnp.zeros_like(odd_stats)
    for start in (0, 1):
        odd_total = odd_total + permute(
            odd_stats,
            lambda y, x, z, c: (y, 2, z, c),
            keep=lambda *a, start=start: a[1] == start and at_start(*a),
        )
    odd_total = odd_total.reshape(4, NY, PIECE)
    kept = kept.reshape(4, NY, BLOCK) + jnp.pad(odd_total, ((0, 0), (0, 0), (0, BLOCK - PIECE)))
    total = kept
    for turn in (2, 1, 3):
        total = total + jnp.roll(permute(kept, along_y(turn)), -turn, axis=1)
    weight = 1.0 / (PIECE * 32.0**3)
    proof = (total[0] / total[2] - total[1] / total[3]) * weight
    proof = jnp.concatenate([proof, proof], axis=0)
    proof = lax.dynamic_slice_in_dim(proof, (NY - y) % NY, NY, 0).reshape(NY, blocks, PIECE)
    return jnp.transpose(proof, (1, 0, 2)).reshape(-1)


def solution(mesh):
    placed = (P("shower", "layer"), P("layer", None), P("layer", None), P("shower"), P("shower"))
    return jax.shard_map(shards, mesh=mesh, in_specs=placed, out_specs=P("shower"), check_vma=False)
```

time: 108 us -> 115 us (1.065)
  waiting for transfers between devices: 43.9 us -> 54.6 us
  starting transfers between devices: 32 us -> 30.2 us
    ppermute x30, waiting for transfers between devices: 43.9 us -> 54.6 us  [permute(): return lax.ppermute(value, AXES, pairs)]
    unnamed x2 -> x0, other arithmetic: 4.02 us -> none
    convert_element_type x0 -> x2, other arithmetic: none -> 2.72 us  [the longest x1 2.57 us: shards(): tag = tag.astype(jnp.bfloat16)]
    ppermute x30, starting transfers between devices: 32 us -> 30.2 us  [permute(): return lax.ppermute(value, AXES, pairs)]
  transfers between devices with their start and end apart: 30 -> 30, of which waited for: 17 -> 18; matrix products, arithmetic and copies ran while one was open for 9% -> 6% of each run, Pallas kernels for 0% -> 0%
where the time goes in v6:
time: 115 us
  waiting for transfers between devices  54.6 us (47%)
  starting transfers between devices  30.2 us (26%)
  Pallas kernels  16.2 us (14%)
  other arithmetic  10.2 us (9%)
  local copies, waits for them, and re-layouts  3.14 us (3%)
    ppermute x30, waiting for transfers between devices, permute(): return lax.ppermute(value, AXES, pairs)  54.6 us
    ppermute x30, starting transfers between devices, permute(): return lax.ppermute(value, AXES, pairs)  30.2 us
    pallas_call x1, Pallas kernels, pair_sums(): pl.pallas_call(functools.partial(pair_kernel, tag_cuts=tuple(tag_cuts), c...  10.7 us
    pallas_call x1, Pallas kernels, raw_partial(): pl.pallas_call(raw_kernel, grid=(feats // width,), in_specs=[pl.BlockSpec...  5.5 us
    convert_element_type x1, other arithmetic, shards(): tag = tag.astype(jnp.bfloat16)  2.57 us
  transfers between devices with their start and end apart: 30, of which 18 were waited for; matrix products, arithmetic and copies ran while one was open for 6% of the time, Pallas kernels for 0%

profile of v6, /device:TPU:4, one launch (start us, length us, event | category | flops | bytes accessed | tf_op | source)
XLA Modules:
  0.0 114.9 jit_solution(10368670658645341315)
XLA Ops:
  0.0 5.5 %raw.1 = f32[512,1024]{1,0:T(8,128)} custom-call(s32[8,11]{1,0:T(8,128)} %bitcast.41, bf16[1584,512]{1,0:T(8,128)(2,1)} %bitcast.35, bf16[1584,1024]{1,0:T(8,128)(2,1)} %geometry.1), custom_call_target="tpu_custom_call" | custom-call | flops 1660944384 | bytes 8388608 | tf_op jit(solution)/shard_map/raw/pallas_call | solution.py:83
  5.5 1.7 %constant_dynamic-slice_fusion.1 = (f32[4,1,32,1024]{3,2,1,0:T(8,128)S(1)}, f16[4,1,32,1024]{3,2,0,1:T(8,128)(2,1)S(1)}, f16[4,1,32,1024]{3,2,0,1:T(8,128)(2,1)S(1)}, f16[4,1,32,1024]{3,2,0,1:T(8,128)(2,1)S(1)}) fusion(f32[4,4,32,1024]{3,2,1,0:T(8,128)} %bitcast.34, s32[]{:T(128)S(6)} %select_n.179, s32[]{:T(128)S(6)} %select_n.183, s32[]{:T(128)S(6)} %select_n.181, ...), kind=kLoop, calls=%fused_computation.46 | loop fusion | flops 393216 | bytes 3407888 | tf_op jit(solution)/shard_map/jit(dynamic_index_in_dim)/dynamic_slice | solution.py:278
  7.2 3.3 %collective-permute-start = (f16[128,1024]{1,0:T(8,128)(2,1)S(1)}, f16[128,1024]{1,0:T(8,128)(2,1)S(1)}, u32[]{:S(2)}, u32[]{:S(2)}) collective-permute-start(f16[128,1024]{1,0:T(8,128)(2,1)S(1)} %bitcast.38), channel_id=1, source_target_pairs={{0,128},{1,129},{2,130},{3,131},{4,132},{5,133},{6,134},{7,135},{8... | collective-permute-start | bytes 786440 | tf_op jit(solution)/shard_map/ppermute | solution.py:32
  11.2 2.6 %collective-permute-start.2 = (f16[128,1024]{1,0:T(8,128)(2,1)S(1)}, f16[128,1024]{1,0:T(8,128)(2,1)S(1)}, u32[]{:S(2)}, u32[]{:S(2)}) collective-permute-start(f16[128,1024]{1,0:T(8,128)(2,1)S(1)} %bitcast.36), channel_id=1, source_target_pairs={{0,192},{1,193},{2,194},{3,195},{4,196},{5,197},{6,198},{7,199},{8... | collective-permute-start | bytes 786440 | tf_op jit(solution)/shard_map/ppermute | solution.py:32
  14.5 2.6 %select_convert_fusion = bf16[16,1024]{1,0:T(8,128)(2,1)S(1)} fusion(bf16[]{:T(256)} %bitcast.5, bf16[]{:T(256)} %bitcast.4, bf16[]{:T(256)} %bitcast.3, bf16[]{:T(256)} %bitcast.2, s32[1024]{0:T(1024)S(1)} %get-tuple-element.53, s32[1024]{0:T(1024)S(1)} %get-tuple-element.54, pred[16]{0:T(512)(128)(4,1)S(1)} %iota_compare_fusion, pred[1024]{0:T(1024)(128)(4,1)S(1)} %fusion.15), kind=kLoop, calls=%fused_computation.19 | loop fusion | flops 163840 | bytes 42008 | tf_op jit(solution)/shard_map/convert_element_type | solution.py:273
  18.1 4.4 %collective-permute-done.1 = f16[128,1024]{1,0:T(8,128)(2,1)S(1)} collective-permute-done((f16[128,1024]{1,0:T(8,128)(2,1)S(1)}, f16[128,1024]{1,0:T(8,128)(2,1)S(1)}, u32[]{:S(2)}, u32[]{:S(2)}) %collective-permute-start.1) | collective-permute-done | bytes 262176 | tf_op jit(solution)/shard_map/ppermute | solution.py:32
  23.4 1.6 %collective-permute-done.3.refs_8_ = bf16[144,1024]{1,0:T(8,128)(2,1)S(1)} collective-permute-done((bf16[144,1024]{1,0:T(8,128)(2,1)S(1)}, bf16[144,1024]{1,0:T(8,128)(2,1)S(1)}, u32[]{:S(2)}, u32[]{:S(2)}) %collective-permute-start.3) | collective-permute-done | bytes 294944 | tf_op jit(solution)/shard_map/ppermute | solution.py:32
  25.2 1.4 %collective-permute-start.5 = (bf16[288,1024]{1,0:T(8,128)(2,1)S(1)}, bf16[288,1024]{1,0:T(8,128)(2,1)S(1)}, u32[]{:S(2)}, u32[]{:S(2)}) collective-permute-start(bf16[288,1024]{1,0:T(8,128)(2,1)S(1)} %maximum_select_fusion), channel_id=1, source_target_pairs={{0,64},{1,193},{2,66},{3,195},{4,68},{5,197},{6,70},{7,199},{8,72}... | collective-permute-start | bytes 1769480 | tf_op jit(solution)/shard_map/ppermute | solution.py:32
  26.6 1.9 %collective-permute-start.4 = (bf16[288,1024]{1,0:T(8,128)(2,1)S(1)}, bf16[288,1024]{1,0:T(8,128)(2,1)S(1)}, u32[]{:S(2)}, u32[]{:S(2)}) collective-permute-start(bf16[288,1024]{1,0:T(8,128)(2,1)S(1)} %maximum_select_fusion), channel_id=1, source_target_pairs={{0,2},{1,15},{2,4},{3,1},{4,6},{5,3},{6,8},{7,5},{8,10},{9,7},{10,... | collective-permute-start | bytes 1769480 | tf_op jit(solution)/shard_map/ppermute | solution.py:32
  28.5 1.2 %collective-permute-start.6 = (bf16[144,1024]{1,0:T(8,128)(2,1)S(1)}, bf16[144,1024]{1,0:T(8,128)(2,1)S(1)}, u32[]{:S(2)}, u32[]{:S(2)}) collective-permute-start(bf16[144,1024]{1,0:T(8,128)(2,1)S(1)} %pad_maximum_fusion.refs_1_.refs_7_), channel_id=1, source_target_pairs={{0,16},{1,17},{2,18},{3,19},{4,20},{5,21},{6,22},{7,23},{8,24},{9,... | collective-permute-start | bytes 884744 | tf_op jit(solution)/shard_map/ppermute | solution.py:32
  29.7 5.5 %collective-permute-done.6.refs_9_ = bf16[144,1024]{1,0:T(8,128)(2,1)S(1)} collective-permute-done((bf16[144,1024]{1,0:T(8,128)(2,1)S(1)}, bf16[144,1024]{1,0:T(8,128)(2,1)S(1)}, u32[]{:S(2)}, u32[]{:S(2)}) %collective-permute-start.6) | collective-permute-done | bytes 294944 | tf_op jit(solution)/shard_map/ppermute | solution.py:32
  36.4 4.0 %collective-permute-done.4.refs_2_ = bf16[288,1024]{1,0:T(8,128)(2,1)S(1)} collective-permute-done((bf16[288,1024]{1,0:T(8,128)(2,1)S(1)}, bf16[288,1024]{1,0:T(8,128)(2,1)S(1)}, u32[]{:S(2)}, u32[]{:S(2)}) %collective-permute-start.4) | collective-permute-done | bytes 589856 | tf_op jit(solution)/shard_map/ppermute | solution.py:32
  40.3 2.9 %collective-permute-start.10 = (bf16[288,1024]{1,0:T(8,128)(2,1)S(1)}, bf16[288,1024]{1,0:T(8,128)(2,1)S(1)}, u32[]{:S(2)}, u32[]{:S(2)}) collective-permute-start(bf16[288,1024]{1,0:T(8,128)(2,1)S(1)} %collective-permute-done.5.refs_11_), channel_id=1, source_target_pairs={{0,1},{1,0},{2,3},{3,2},{4,5},{5,4},{6,7},{7,6},{8,9},{9,8},{10,11... | collective-permute-start | bytes 1769480 | tf_op jit(solution)/shard_map/ppermute | solution.py:32
  43.3 1.2 %collective-permute-start.9 = (bf16[288,1024]{1,0:T(8,128)(2,1)S(1)}, bf16[288,1024]{1,0:T(8,128)(2,1)}, u32[]{:S(2)}, u32[]{:S(2)}) collective-permute-start(bf16[288,1024]{1,0:T(8,128)(2,1)S(1)} %collective-permute-done.5.refs_11_), channel_id=1, source_target_pairs={{0,16},{1,17},{2,18},{3,19},{4,20},{5,21},{6,22},{7,23},{8,24},{9,... | collective-permute-start | bytes 1769480 | tf_op jit(solution)/shard_map/ppermute | solution.py:32
  44.6 7.6 %collective-permute-done.8.refs_13_ = bf16[128,1024]{1,0:T(8,128)(2,1)S(1)} collective-permute-done((bf16[128,1024]{1,0:T(8,128)(2,1)S(1)}, bf16[128,1024]{1,0:T(8,128)(2,1)S(1)}, u32[]{:S(2)}, u32[]{:S(2)}) %collective-permute-start.8) | collective-permute-done | bytes 262176 | tf_op jit(solution)/shard_map/ppermute | solution.py:32
  53.0 5.6 %collective-permute-done.9.refs_15_ = bf16[288,1024]{1,0:T(8,128)(2,1)} collective-permute-done((bf16[288,1024]{1,0:T(8,128)(2,1)S(1)}, bf16[288,1024]{1,0:T(8,128)(2,1)}, u32[]{:S(2)}, u32[]{:S(2)}) %collective-permute-start.9) | collective-permute-done | bytes 589856 | tf_op jit(solution)/shard_map/ppermute | solution.py:32
  58.7 2.4 %collective-permute-start.16 = (bf16[128,1024]{1,0:T(8,128)(2,1)S(1)}, bf16[128,1024]{1,0:T(8,128)(2,1)S(1)}, u32[]{:S(2)}, u32[]{:S(2)}) collective-permute-start(bf16[128,1024]{1,0:T(8,128)(2,1)S(1)} %pad_maximum_fusion.1), channel_id=1, source_target_pairs={{32,0},{96,64},{160,128},{224,192}} | collective-permute-start | bytes 786440 | tf_op jit(solution)/shard_map/ppermute | solution.py:32
  61.2 1.3 %collective-permute-start.15 = (bf16[128,1024]{1,0:T(8,128)(2,1)S(1)}, bf16[128,1024]{1,0:T(8,128)(2,1)S(1)}, u32[]{:S(2)}, u32[]{:S(2)}) collective-permute-start(bf16[128,1024]{1,0:T(8,128)(2,1)S(1)} %pad_maximum_fusion.1), channel_id=1, source_target_pairs={{32,16},{96,80},{160,144},{224,208}} | collective-permute-start | bytes 786440 | tf_op jit(solution)/shard_map/ppermute | solution.py:32
  62.7 3.8 %collective-permute-done.16 = bf16[128,1024]{1,0:T(8,128)(2,1)S(1)} collective-permute-done((bf16[128,1024]{1,0:T(8,128)(2,1)S(1)}, bf16[128,1024]{1,0:T(8,128)(2,1)S(1)}, u32[]{:S(2)}, u32[]{:S(2)}) %collective-permute-start.16) | collective-permute-done | bytes 262176 | tf_op jit(solution)/shard_map/ppermute | solution.py:32
  66.5 4.9 %collective-permute-done.13.refs_17_ = bf16[128,1024]{1,0:T(8,128)(2,1)} collective-permute-done((bf16[128,1024]{1,0:T(8,128)(2,1)S(1)}, bf16[128,1024]{1,0:T(8,128)(2,1)}, u32[]{:S(2)}, u32[]{:S(2)}) %collective-permute-start.13) | collective-permute-done | bytes 262176 | tf_op jit(solution)/shard_map/ppermute | solution.py:32
  74.1 1.6 %collective-permute-start.18 = (bf16[48,1024]{1,0:T(8,128)(2,1)S(1)}, bf16[48,1024]{1,0:T(8,128)(2,1)S(1)}, u32[]{:S(2)}, u32[]{:S(2)}) collective-permute-start(bf16[48,1024]{1,0:T(8,128)(2,1)S(1)} %fusion.5), channel_id=1, source_target_pairs={{32,16},{34,18},{36,20},{38,22},{43,27},{45,29},{47,31},{96,80},{9... | collective-permute-start | bytes 294920 | tf_op jit(solution)/shard_map/ppermute | solution.py:32
  76.3 1.6 %collective-permute-done.18 = bf16[48,1024]{1,0:T(8,128)(2,1)S(1)} collective-permute-done((bf16[48,1024]{1,0:T(8,128)(2,1)S(1)}, bf16[48,1024]{1,0:T(8,128)(2,1)S(1)}, u32[]{:S(2)}, u32[]{:S(2)}) %collective-permute-start.18) | collective-permute-done | bytes 98336 | tf_op jit(solution)/shard_map/ppermute | solution.py:32
  81.1 10.7 %pairs.1 = (f32[4,512]{1,0:T(4,128)}, f32[4,512]{1,0:T(4,128)}, f32[4,1152]{1,0:T(4,128)}, f32[4,128]{1,0:T(4,128)}) custom-call(s32[2]{0:T(128)} %pad_add_fusion.1.refs_0_, bf16[144,1024]{1,0:T(8,128)(2,1)} %copy-done.2, bf16[288,1024]{1,0:T(8,128)(2,1)} %copy-done.5, bf16[288,1024]{1,0:T(8,128)(2,1)} %collective-permute-done.7.refs_3_, ...), custom_call_target="tpu_custom_call" | custom-call | flops 4706009088 | bytes 6619136 | tf_op jit(solution)/shard_map/pairs/pallas_call | solution.py:233
  91.9 1.4 %collective-permute-done.23 = f32[4,1152]{1,0:T(4,128)S(1)} collective-permute-done((f32[4,1152]{1,0:T(4,128)}, f32[4,1152]{1,0:T(4,128)S(1)}, u32[]{:S(2)}, u32[]{:S(2)}) %collective-permute-start.23) | collective-permute-done | bytes 18464 | tf_op jit(solution)/shard_map/ppermute | solution.py:32
  94.0 1.8 %collective-permute-start.24 = (f32[4,512]{1,0:T(4,128)S(1)}, f32[4,512]{1,0:T(4,128)S(1)}, u32[]{:S(2)}, u32[]{:S(2)}) collective-permute-start(f32[4,512]{1,0:T(4,128)S(1)} %slice_add_fusion), channel_id=1, source_target_pairs={{0,16},{1,17},{2,18},{3,19},{4,20},{5,21},{6,22},{7,23},{8,24},{9,... | collective-permute-start | bytes 24584 | tf_op jit(solution)/shard_map/ppermute | solution.py:32
  96.5 1.3 %collective-permute-start.26 = (f32[4,128]{1,0:T(4,128)S(1)}, f32[4,128]{1,0:T(4,128)S(1)}, u32[]{:S(2)}, u32[]{:S(2)}) collective-permute-start(f32[4,128]{1,0:T(4,128)S(1)} %slice_add_fusion.2), channel_id=1, source_target_pairs={{16,32},{80,96},{144,160},{208,224}} | collective-permute-start | bytes 6152 | tf_op jit(solution)/shard_map/ppermute | solution.py:32
  97.8 1.3 %collective-permute-start.25 = (f32[4,128]{1,0:T(4,128)S(1)}, f32[4,128]{1,0:T(4,128)S(1)}, u32[]{:S(2)}, u32[]{:S(2)}) collective-permute-start(f32[4,128]{1,0:T(4,128)S(1)} %slice_add_fusion.2), channel_id=1, source_target_pairs={{0,32},{64,96},{128,160},{192,224}} | collective-permute-start | bytes 6152 | tf_op jit(solution)/shard_map/ppermute | solution.py:32
  99.1 2.9 %collective-permute-done.26 = f32[4,128]{1,0:T(4,128)S(1)} collective-permute-done((f32[4,128]{1,0:T(4,128)S(1)}, f32[4,128]{1,0:T(4,128)S(1)}, u32[]{:S(2)}, u32[]{:S(2)}) %collective-permute-start.26) | collective-permute-done | bytes 2080 | tf_op jit(solution)/shard_map/ppermute | solution.py:32
  102.0 2.8 %collective-permute-done.25 = f32[4,128]{1,0:T(4,128)S(1)} collective-permute-done((f32[4,128]{1,0:T(4,128)S(1)}, f32[4,128]{1,0:T(4,128)S(1)}, u32[]{:S(2)}, u32[]{:S(2)}) %collective-permute-start.25) | collective-permute-done | bytes 2080 | tf_op jit(solution)/shard_map/ppermute | solution.py:32
  105.7 3.2 %collective-permute-start.29 = (f32[4,4,128]{2,1,0:T(4,128)S(1)}, f32[4,4,128]{2,1,0:T(4,128)S(1)}, u32[]{:S(2)}, u32[]{:S(2)}) collective-permute-start(f32[4,4,128]{2,1,0:T(4,128)S(1)} %pad_add_fusion), channel_id=1, source_target_pairs={{0,192},{1,193},{2,194},{3,195},{4,196},{5,197},{6,198},{7,199},{8... | collective-permute-start | bytes 24584 | tf_op jit(solution)/shard_map/ppermute | solution.py:32
  108.9 1.6 %collective-permute-done.28 = f32[4,4,128]{2,1,0:T(4,128)S(1)} collective-permute-done((f32[4,4,128]{2,1,0:T(4,128)S(1)}, f32[4,4,128]{2,1,0:T(4,128)S(1)}, u32[]{:S(2)}, u32[]{:S(2)}) %collective-permute-start.28) | collective-permute-done | bytes 8224 | tf_op jit(solution)/shard_map/ppermute | solution.py:32
  110.5 3.5 %collective-permute-done.27 = f32[4,4,128]{2,1,0:T(4,128)S(1)} collective-permute-done((f32[4,4,128]{2,1,0:T(4,128)S(1)}, f32[4,4,128]{2,1,0:T(4,128)S(1)}, u32[]{:S(2)}, u32[]{:S(2)}) %collective-permute-start.27) | collective-permute-done | bytes 8224 | tf_op jit(solution)/shard_map/ppermute | solution.py:32
  (96 shorter events, 15.3 us)
Async XLA Ops:
  7.2 10.8 %collective-permute-start = (f16[128,1024]{1,0:T(8,128)(2,1)S(1)}, f16[128,1024]{1,0:T(8,128)(2,1)S(1)}, u32[]{:S(2)}, u32[]{:S(2)}) collective-permute-start(f16[128,1024]{1,0:T(8,128)(2,1)S(1)} %bitcast.38), channel_id=1, source_target_pairs={{0,128},{1,129},{2,130},{3,131},{4,132},{5,133},{6,134},{7,135},{8... | collective-permute-start | bytes 786440 | tf_op jit(solution)/shard_map/ppermute | solution.py:32
  10.5 12.0 %collective-permute-start.1 = (f16[128,1024]{1,0:T(8,128)(2,1)S(1)}, f16[128,1024]{1,0:T(8,128)(2,1)S(1)}, u32[]{:S(2)}, u32[]{:S(2)}) collective-permute-start(f16[128,1024]{1,0:T(8,128)(2,1)S(1)} %bitcast.37), channel_id=1, source_target_pairs={{0,64},{1,65},{2,66},{3,67},{4,68},{5,69},{6,70},{7,71},{8,72},{9,... | collective-permute-start | bytes 786440 | tf_op jit(solution)/shard_map/ppermute | solution.py:32
  11.2 11.7 %collective-permute-start.2 = (f16[128,1024]{1,0:T(8,128)(2,1)S(1)}, f16[128,1024]{1,0:T(8,128)(2,1)S(1)}, u32[]{:S(2)}, u32[]{:S(2)}) collective-permute-start(f16[128,1024]{1,0:T(8,128)(2,1)S(1)} %bitcast.36), channel_id=1, source_target_pairs={{0,192},{1,193},{2,194},{3,195},{4,196},{5,197},{6,198},{7,199},{8... | collective-permute-start | bytes 786440 | tf_op jit(solution)/shard_map/ppermute | solution.py:32
  23.3 35.3 %copy-start.2 = (bf16[144,1024]{1,0:T(8,128)(2,1)}, bf16[144,1024]{1,0:T(8,128)(2,1)S(1)}, u32[]{:S(2)}) copy-start(bf16[144,1024]{1,0:T(8,128)(2,1)S(1)} %pad_maximum_fusion.refs_1_.refs_7_) | copy-start | bytes 884740
  23.3 1.7 %collective-permute-start.3 = (bf16[144,1024]{1,0:T(8,128)(2,1)S(1)}, bf16[144,1024]{1,0:T(8,128)(2,1)S(1)}, u32[]{:S(2)}, u32[]{:S(2)}) collective-permute-start(bf16[144,1024]{1,0:T(8,128)(2,1)S(1)} %pad_maximum_fusion.refs_1_.refs_7_), channel_id=1, source_target_pairs={{0,1},{1,0},{2,3},{3,2},{4,5},{5,4},{6,7},{7,6},{8,9},{9,8},{10,11... | collective-permute-start | bytes 884744 | tf_op jit(solution)/shard_map/ppermute | solution.py:32
  25.2 11.2 %collective-permute-start.5 = (bf16[288,1024]{1,0:T(8,128)(2,1)S(1)}, bf16[288,1024]{1,0:T(8,128)(2,1)S(1)}, u32[]{:S(2)}, u32[]{:S(2)}) collective-permute-start(bf16[288,1024]{1,0:T(8,128)(2,1)S(1)} %maximum_select_fusion), channel_id=1, source_target_pairs={{0,64},{1,193},{2,66},{3,195},{4,68},{5,197},{6,70},{7,199},{8,72}... | collective-permute-start | bytes 1769480 | tf_op jit(solution)/shard_map/ppermute | solution.py:32
  26.6 13.7 %collective-permute-start.4 = (bf16[288,1024]{1,0:T(8,128)(2,1)S(1)}, bf16[288,1024]{1,0:T(8,128)(2,1)S(1)}, u32[]{:S(2)}, u32[]{:S(2)}) collective-permute-start(bf16[288,1024]{1,0:T(8,128)(2,1)S(1)} %maximum_select_fusion), channel_id=1, source_target_pairs={{0,2},{1,15},{2,4},{3,1},{4,6},{5,3},{6,8},{7,5},{8,10},{9,7},{10,... | collective-permute-start | bytes 1769480 | tf_op jit(solution)/shard_map/ppermute | solution.py:32
  28.5 6.7 %collective-permute-start.6 = (bf16[144,1024]{1,0:T(8,128)(2,1)S(1)}, bf16[144,1024]{1,0:T(8,128)(2,1)S(1)}, u32[]{:S(2)}, u32[]{:S(2)}) collective-permute-start(bf16[144,1024]{1,0:T(8,128)(2,1)S(1)} %pad_maximum_fusion.refs_1_.refs_7_), channel_id=1, source_target_pairs={{0,16},{1,17},{2,18},{3,19},{4,20},{5,21},{6,22},{7,23},{8,24},{9,... | collective-permute-start | bytes 884744 | tf_op jit(solution)/shard_map/ppermute | solution.py:32
  35.3 45.1 %copy-start.7 = (bf16[144,1024]{1,0:T(8,128)(2,1)}, bf16[144,1024]{1,0:T(8,128)(2,1)S(1)}, u32[]{:S(2)}) copy-start(bf16[144,1024]{1,0:T(8,128)(2,1)S(1)} %collective-permute-done.6.refs_9_) | copy-start | bytes 884740
  40.3 11.8 %collective-permute-start.7 = (bf16[288,1024]{1,0:T(8,128)(2,1)S(1)}, bf16[288,1024]{1,0:T(8,128)(2,1)}, u32[]{:S(2)}, u32[]{:S(2)}) collective-permute-start(bf16[288,1024]{1,0:T(8,128)(2,1)S(1)} %collective-permute-done.4.refs_2_), channel_id=1, source_target_pairs={{0,2},{1,15},{2,4},{3,1},{4,6},{5,3},{6,8},{7,5},{8,10},{9,7},{10,... | collective-permute-start | bytes 1769480 | tf_op jit(solution)/shard_map/ppermute | solution.py:32
  40.3 11.8 %collective-permute-start.10 = (bf16[288,1024]{1,0:T(8,128)(2,1)S(1)}, bf16[288,1024]{1,0:T(8,128)(2,1)S(1)}, u32[]{:S(2)}, u32[]{:S(2)}) collective-permute-start(bf16[288,1024]{1,0:T(8,128)(2,1)S(1)} %collective-permute-done.5.refs_11_), channel_id=1, source_target_pairs={{0,1},{1,0},{2,3},{3,2},{4,5},{5,4},{6,7},{7,6},{8,9},{9,8},{10,11... | collective-permute-start | bytes 1769480 | tf_op jit(solution)/shard_map/ppermute | solution.py:32
  43.3 15.3 %collective-permute-start.9 = (bf16[288,1024]{1,0:T(8,128)(2,1)S(1)}, bf16[288,1024]{1,0:T(8,128)(2,1)}, u32[]{:S(2)}, u32[]{:S(2)}) collective-permute-start(bf16[288,1024]{1,0:T(8,128)(2,1)S(1)} %collective-permute-done.5.refs_11_), channel_id=1, source_target_pairs={{0,16},{1,17},{2,18},{3,19},{4,20},{5,21},{6,22},{7,23},{8,24},{9,... | collective-permute-start | bytes 1769480 | tf_op jit(solution)/shard_map/ppermute | solution.py:32
  44.5 7.7 %collective-permute-start.11 = (bf16[144,1024]{1,0:T(8,128)(2,1)S(1)}, bf16[144,1024]{1,0:T(8,128)(2,1)S(1)}, u32[]{:S(2)}, u32[]{:S(2)}) collective-permute-start(bf16[144,1024]{1,0:T(8,128)(2,1)S(1)} %collective-permute-done.6.refs_9_), channel_id=1, source_target_pairs={{0,1},{1,0},{2,3},{3,2},{4,5},{5,4},{6,7},{7,6},{8,9},{9,8},{10,11... | collective-permute-start | bytes 884744 | tf_op jit(solution)/shard_map/ppermute | solution.py:32
  44.5 7.7 %collective-permute-start.8 = (bf16[128,1024]{1,0:T(8,128)(2,1)S(1)}, bf16[128,1024]{1,0:T(8,128)(2,1)S(1)}, u32[]{:S(2)}, u32[]{:S(2)}) collective-permute-start(bf16[128,1024]{1,0:T(8,128)(2,1)S(1)} %slice_select_fusion.1), channel_id=1, source_target_pairs={{0,64},{1,193},{2,66},{3,195},{4,68},{5,197},{6,70},{7,199},{8,72}... | collective-permute-start | bytes 786440 | tf_op jit(solution)/shard_map/ppermute | solution.py:32
  58.6 12.8 %collective-permute-start.12 = (bf16[288,1024]{1,0:T(8,128)(2,1)}, bf16[288,1024]{1,0:T(8,128)(2,1)S(1)}, u32[]{:S(2)}, u32[]{:S(2)}) collective-permute-start(bf16[288,1024]{1,0:T(8,128)(2,1)} %collective-permute-done.7.refs_3_), channel_id=1, source_target_pairs={{0,2},{1,15},{2,4},{3,1},{4,6},{5,3},{6,8},{7,5},{8,10},{9,7},{10,... | collective-permute-start | bytes 1769480 | tf_op jit(solution)/shard_map/ppermute | solution.py:32
  58.7 7.8 %collective-permute-start.16 = (bf16[128,1024]{1,0:T(8,128)(2,1)S(1)}, bf16[128,1024]{1,0:T(8,128)(2,1)S(1)}, u32[]{:S(2)}, u32[]{:S(2)}) collective-permute-start(bf16[128,1024]{1,0:T(8,128)(2,1)S(1)} %pad_maximum_fusion.1), channel_id=1, source_target_pairs={{32,0},{96,64},{160,128},{224,192}} | collective-permute-start | bytes 786440 | tf_op jit(solution)/shard_map/ppermute | solution.py:32
  61.2 5.4 %collective-permute-start.15 = (bf16[128,1024]{1,0:T(8,128)(2,1)S(1)}, bf16[128,1024]{1,0:T(8,128)(2,1)S(1)}, u32[]{:S(2)}, u32[]{:S(2)}) collective-permute-start(bf16[128,1024]{1,0:T(8,128)(2,1)S(1)} %pad_maximum_fusion.1), channel_id=1, source_target_pairs={{32,16},{96,80},{160,144},{224,208}} | collective-permute-start | bytes 786440 | tf_op jit(solution)/shard_map/ppermute | solution.py:32
  62.5 4.1 %collective-permute-start.14 = (bf16[128,1024]{1,0:T(8,128)(2,1)S(1)}, bf16[128,1024]{1,0:T(8,128)(2,1)}, u32[]{:S(2)}, u32[]{:S(2)}) collective-permute-start(bf16[128,1024]{1,0:T(8,128)(2,1)S(1)} %collective-permute-done.8.refs_13_), channel_id=1, source_target_pairs={{0,1},{1,0},{2,3},{3,2},{4,5},{5,4},{6,7},{7,6},{8,9},{9,8},{10,11... | collective-permute-start | bytes 786440 | tf_op jit(solution)/shard_map/ppermute | solution.py:32
  62.6 8.8 %collective-permute-start.13 = (bf16[128,1024]{1,0:T(8,128)(2,1)S(1)}, bf16[128,1024]{1,0:T(8,128)(2,1)}, u32[]{:S(2)}, u32[]{:S(2)}) collective-permute-start(bf16[128,1024]{1,0:T(8,128)(2,1)S(1)} %collective-permute-done.8.refs_13_), channel_id=1, source_target_pairs={{0,16},{1,17},{2,18},{3,19},{4,20},{5,21},{6,22},{7,23},{8,24},{9,... | collective-permute-start | bytes 786440 | tf_op jit(solution)/shard_map/ppermute | solution.py:32
  66.5 12.8 %collective-permute-start.20 = (bf16[288,1024]{1,0:T(8,128)(2,1)}, bf16[288,1024]{1,0:T(8,128)(2,1)}, u32[]{:S(2)}, u32[]{:S(2)}) collective-permute-start(bf16[288,1024]{1,0:T(8,128)(2,1)} %collective-permute-done.9.refs_15_), channel_id=1, source_target_pairs={{0,1},{1,0},{2,3},{3,2},{4,5},{5,4},{6,7},{7,6},{8,9},{9,8},{10,11... | collective-permute-start | bytes 1769480 | tf_op jit(solution)/shard_map/ppermute | solution.py:32
  71.5 7.1 %collective-permute-start.22 = (bf16[128,1024]{1,0:T(8,128)(2,1)S(1)}, bf16[128,1024]{1,0:T(8,128)(2,1)S(1)}, u32[]{:S(2)}, u32[]{:S(2)}) collective-permute-start(bf16[128,1024]{1,0:T(8,128)(2,1)S(1)} %add.136), channel_id=1, source_target_pairs={{0,1},{16,17},{64,65},{80,81},{128,129},{144,145},{192,193},{208,2... | collective-permute-start | bytes 786440 | tf_op jit(solution)/shard_map/ppermute | solution.py:32
  72.2 7.2 %collective-permute-start.21 = (bf16[128,1024]{1,0:T(8,128)(2,1)}, bf16[128,1024]{1,0:T(8,128)(2,1)}, u32[]{:S(2)}, u32[]{:S(2)}) collective-permute-start(bf16[128,1024]{1,0:T(8,128)(2,1)} %collective-permute-done.13.refs_17_), channel_id=1, source_target_pairs={{0,1},{1,0},{2,3},{3,2},{4,5},{5,4},{6,7},{7,6},{8,9},{9,8},{10,11... | collective-permute-start | bytes 786440 | tf_op jit(solution)/shard_map/ppermute | solution.py:32
  72.3 8.0 %collective-permute-start.17 = (bf16[144,1024]{1,0:T(8,128)(2,1)S(1)}, bf16[144,1024]{1,0:T(8,128)(2,1)S(1)}, u32[]{:S(2)}, u32[]{:S(2)}) collective-permute-start(bf16[144,1024]{1,0:T(8,128)(2,1)S(1)} %slice_select_fusion), channel_id=1, source_target_pairs={{0,2},{1,15},{2,4},{3,1},{4,6},{5,3},{6,8},{7,5},{8,10},{9,7},{10,... | collective-permute-start | bytes 884744 | tf_op jit(solution)/shard_map/ppermute | solution.py:32
  73.4 0.7 collective-permute-start.19
  74.1 3.8 %collective-permute-start.18 = (bf16[48,1024]{1,0:T(8,128)(2,1)S(1)}, bf16[48,1024]{1,0:T(8,128)(2,1)S(1)}, u32[]{:S(2)}, u32[]{:S(2)}) collective-permute-start(bf16[48,1024]{1,0:T(8,128)(2,1)S(1)} %fusion.5), channel_id=1, source_target_pairs={{32,16},{34,18},{36,20},{38,22},{43,27},{45,29},{47,31},{96,80},{9... | collective-permute-start | bytes 294920 | tf_op jit(solution)/shard_map/ppermute | solution.py:32
  91.8 1.5 %collective-permute-start.23 = (f32[4,1152]{1,0:T(4,128)}, f32[4,1152]{1,0:T(4,128)S(1)}, u32[]{:S(2)}, u32[]{:S(2)}) collective-permute-start(f32[4,1152]{1,0:T(4,128)} %get-tuple-element.40), channel_id=1, source_target_pairs={{0,1},{1,0},{2,3},{3,2},{4,5},{5,4},{6,7},{7,6},{8,9},{9,8},{10,11... | collective-permute-start | bytes 55304 | tf_op jit(solution)/shard_map/ppermute | solution.py:32
  94.0 10.9 %collective-permute-start.24 = (f32[4,512]{1,0:T(4,128)S(1)}, f32[4,512]{1,0:T(4,128)S(1)}, u32[]{:S(2)}, u32[]{:S(2)}) collective-permute-start(f32[4,512]{1,0:T(4,128)S(1)} %slice_add_fusion), channel_id=1, source_target_pairs={{0,16},{1,17},{2,18},{3,19},{4,20},{5,21},{6,22},{7,23},{8,24},{9,... | collective-permute-start | bytes 24584 | tf_op jit(solution)/shard_map/ppermute | solution.py:32
  96.5 5.5 %collective-permute-start.26 = (f32[4,128]{1,0:T(4,128)S(1)}, f32[4,128]{1,0:T(4,128)S(1)}, u32[]{:S(2)}, u32[]{:S(2)}) collective-permute-start(f32[4,128]{1,0:T(4,128)S(1)} %slice_add_fusion.2), channel_id=1, source_target_pairs={{16,32},{80,96},{144,160},{208,224}} | collective-permute-start | bytes 6152 | tf_op jit(solution)/shard_map/ppermute | solution.py:32
  97.8 7.0 %collective-permute-start.25 = (f32[4,128]{1,0:T(4,128)S(1)}, f32[4,128]{1,0:T(4,128)S(1)}, u32[]{:S(2)}, u32[]{:S(2)}) collective-permute-start(f32[4,128]{1,0:T(4,128)S(1)} %slice_add_fusion.2), channel_id=1, source_target_pairs={{0,32},{64,96},{128,160},{192,224}} | collective-permute-start | bytes 6152 | tf_op jit(solution)/shard_map/ppermute | solution.py:32
  105.6 4.9 %collective-permute-start.28 = (f32[4,4,128]{2,1,0:T(4,128)S(1)}, f32[4,4,128]{2,1,0:T(4,128)S(1)}, u32[]{:S(2)}, u32[]{:S(2)}) collective-permute-start(f32[4,4,128]{2,1,0:T(4,128)S(1)} %pad_add_fusion), channel_id=1, source_target_pairs={{0,64},{1,65},{2,66},{3,67},{4,68},{5,69},{6,70},{7,71},{8,72},{9,... | collective-permute-start | bytes 24584 | tf_op jit(solution)/shard_map/ppermute | solution.py:32
  105.7 4.9 %collective-permute-start.29 = (f32[4,4,128]{2,1,0:T(4,128)S(1)}, f32[4,4,128]{2,1,0:T(4,128)S(1)}, u32[]{:S(2)}, u32[]{:S(2)}) collective-permute-start(f32[4,4,128]{2,1,0:T(4,128)S(1)} %pad_add_fusion), channel_id=1, source_target_pairs={{0,192},{1,193},{2,194},{3,195},{4,196},{5,197},{6,198},{7,199},{8... | collective-permute-start | bytes 24584 | tf_op jit(solution)/shard_map/ppermute | solution.py:32
  108.9 5.2 %collective-permute-start.27 = (f32[4,4,128]{2,1,0:T(4,128)S(1)}, f32[4,4,128]{2,1,0:T(4,128)S(1)}, u32[]{:S(2)}, u32[]{:S(2)}) collective-permute-start(f32[4,4,128]{2,1,0:T(4,128)S(1)} %pad_add_fusion), channel_id=1, source_target_pairs={{0,128},{1,129},{2,130},{3,131},{4,132},{5,133},{6,134},{7,135},{8... | collective-permute-start | bytes 24584 | tf_op jit(solution)/shard_map/ppermute | solution.py:32
  (10 other events, 146.8 us)

commit v7 on v6

--- a/solution.py
+++ b/solution.py
@@ -116,15 +116,23 @@
         copy.start()
         return copy
 
-    waits, depth = [], 0
-    for at, (arg, first, size) in enumerate(col_cuts):
-        waits.append(start(args[arg], first, size, cols_at, depth, col_sems.at[at]))
-        waits.append(start(args[arg], first - TAG, TAG, col_tags, at * TAG, tag_sems.at[at]))
-        depth += size
+    starts = [sum(size for _, _, size in col_cuts[:at]) for at in range(n_cols)]
+    depth = sum(size for _, _, size in col_cuts)
+
+    def load_col(at):
+        arg, first, size = col_cuts[at]
+        return [
+            start(args[arg], first, size, cols_at, starts[at], col_sems.at[at]),
+            start(args[arg], first - TAG, TAG, col_tags, at * TAG, tag_sems.at[at]),
+        ]
+
+    held = {at: load_col(at) for at in range(2)}
+    waits = []
     for at, (arg, first) in enumerate(tag_cuts):
         waits.append(start(args[arg], first, TAG, row_tags, at * TAG, tag_sems.at[n_cols + at]))
 
-    own, own_t, x1, x1_t, y1, y1_t, y2, y2_t, xx, xx_t, w2, w2_t, odd_rows = row_args
+    own, own_t, x1, x1_t, y1, y1_t, y2, y2_t = row_args[:8]
+    xa, xb, xa_t, xb_t, w2, w2_t, odd_rows = row_args[8:]
     turn = jnp.where(core == 0, 3, 1)
     side = [4 * CHUNK // 2 * jnp.where(core == b, 0, 1) for b in range(NC)]
     made = []
@@ -138,31 +146,31 @@
     for b in range(NC):
         rows(y1, TAG + b * tagged, side[b] + turn * BLOCK)
         rows(y1_t, TAG + b * tagged, side[b] + (NY - turn) * BLOCK)
+    n_near = len(made)
+    for copy in waits + made:
+        copy.wait()
+    for at in range(2, n_cols):
+        held[at] = load_col(at)
     rows(own_t, TAG, 2 * CHUNK)
     rows(y2_t, 0, 2 * CHUNK + 2 * BLOCK)
-    n_near = len(made)
+    n_far = len(made)
     rows(x1, TAG, CHUNK)
     rows(w2, 0, CHUNK + 2 * BLOCK)
     for b in range(NC):
-        rows(xx, TAG + b * tagged, CHUNK + side[b] + turn * BLOCK)
-        rows(xx_t, TAG + b * tagged, CHUNK + side[b] + (NY - turn) * BLOCK)
+        rows((xa, xb)[b], 0, CHUNK + side[b] + turn * BLOCK)
+        rows((xa_t, xb_t)[b], 0, CHUNK + side[b] + (NY - turn) * BLOCK)
     rows(x1_t, TAG, 3 * CHUNK)
     rows(w2_t, 0, 3 * CHUNK + 2 * BLOCK)
     rows(odd_rows, 0, 4 * CHUNK)
-    for copy in waits:
-        copy.wait()
+    waited = 0
 
     def bin_of(code):
         source = (code >= BINS).astype(jnp.float32)
         return code - BINS * source, source
 
     for chunk in (0, 2, 1, 3, 4):
-        if chunk == 0:
-            for copy in made[:n_near]:
-                copy.wait()
-        if chunk == 1:
-            for copy in made[n_near:]:
-                copy.wait()
+        for copy in {2: made[n_near:n_far], 1: made[n_far:]}.get(chunk, []):
+            copy.wait()
         first = chunk * CHUNK
         odd = chunk == 4
         size = BLOCK if odd else CHUNK
@@ -179,6 +187,10 @@
         low = 0
         while low < depth:
             high = depth if depth - low < 3 * BLOCK else low + 2 * BLOCK
+            while waited < n_cols and starts[waited] < high:
+                for copy in held[waited]:
+                    copy.wait()
+                waited += 1
             products = lax.dot_general(
                 cols_at[pl.ds(low, high - low), :],
                 rows_at[pl.ds(first, size), :],
@@ -297,13 +309,13 @@
 
     z2 = permute(z1, same_core)
     y2 = permute(jnp.where(c == 0, y1[TAG:tagged], y1[tagged + TAG :]), y_way)
-    xx = permute(y1, swap_x)
+    xa = permute(y1[TAG:tagged], swap_x)
     y1_t = permute(y1, swap_core)
     x1_t = permute(x1, swap_core)
-    z1, z2, y2, xx, y1_t, x1_t = fence(z1, z2, y2, xx, y1_t, x1_t)
+    z1, z2, y2, xa, y1_t, x1_t, y1 = fence(z1, z2, y2, xa, y1_t, x1_t, y1)
 
     z3 = permute(z2, same_core)
-    w2 = permute(y2, swap_x)
+    xb = permute(y1[tagged + TAG :], swap_x)
     head = TAG + PIECE
     odd_rows = jnp.concatenate([own[TAG:head], y1_t[TAG:head], y2[:PIECE], y1[TAG:head]], axis=0)
     at_start = lambda y, x, z, c: z == 0 and c == 0
@@ -316,36 +328,31 @@
         for to in (1, 0)
     ]
     y2_t = permute(y2, swap_core)
-    z2, z3, w2, y2_t, *odd_at = fence(z2, z3, w2, y2_t, *odd_at)
+    z2, z3, y2, xb, xa, y2_t, *odd_at = fence(z2, z3, y2, xb, xa, y2_t, *odd_at)
 
     z4 = permute(jnp.where(c == 0, z3[:tagged], z3[tagged:]), same_core)
-    held = [own, z1, z2, z3, z3, z3, z2, z1]
-    piece = lax.select_n(z, *[value[:head] for value in held])
-    side = lambda z: 0 if z < 4 else 1
-    piece_near = permute(
-        piece,
-        lambda y, x, z, c: (y, 1, z, c),
-        keep=lambda y, x, z, c: x == 2 and z != 4 and c == side(z),
+    held = [chip, z1, z2, z3, z3, z3, z2, z1]
+    piece = permute(
+        lax.select_n(z, *[value[:head] for value in held]),
+        lambda y, x, z, c: (y, 1, z + 1 - c, c),
+        keep=lambda y, x, z, c: x == 2 and (z < 4 if c == 0 else z == 0 or z > 4),
     )
-    piece_far = permute(
-        piece,
-        lambda y, x, z, c: (y, 1, z + 1, c),
-        keep=lambda y, x, z, c: x == 2 and z == 3 and c == 0,
-    )
-    xx_t = permute(xx, swap_core)
+    w2 = permute(y2, swap_x)
+    xa_t = permute(xa, swap_core)
+    xb_t = permute(xb, swap_core)
     w2_t = permute(w2, swap_core)
     odd_rows = odd_at[0] + odd_at[1]
     odd_rows = odd_rows + permute(
         odd_rows, swap_core, keep=lambda *a: a[1] < 2 and at_start(*a)
     )
-    piece = piece_near + piece_far
 
     col_args = [own, z1, z2, z3, z4, piece]
     col_cuts = [(0, TAG, BLOCK)]
     for arg in (1, 2, 3):
         col_cuts += [(arg, TAG, BLOCK), (arg, tagged + TAG, BLOCK)]
     col_cuts += [(4, TAG, BLOCK), (5, TAG, PIECE)]
-    row_args = [own, own_t, x1, x1_t, y1, y1_t, y2, y2_t, xx, xx_t, w2, w2_t, odd_rows]
+    row_args = [own, own_t, x1, x1_t, y1, y1_t, y2, y2_t]
+    row_args += [xa, xb, xa_t, xb_t, w2, w2_t, odd_rows]
     tag_cuts = [(6, 0), (8, 0), (7, 0), (9, 0)]
     place = jnp.stack([((x < 2) & (z == 0)).astype(jnp.int32), c.astype(jnp.int32)])
     near, far, theirs, odd_stats = pair_sums(place, col_args, row_args, col_cuts, tag_cuts)
@@ -363,8 +370,8 @@
     odd_total = odd_total.reshape(4, NY, PIECE)
     kept = kept.reshape(4, NY, BLOCK) + jnp.pad(odd_total, ((0, 0), (0, 0), (0, BLOCK - PIECE)))
     total = kept
-    for turn in (2, 1, 3):
-        total = total + jnp.roll(permute(kept, along_y(turn)), -turn, axis=1)
+    for turn in (1, 2):
+        total = total + jnp.roll(permute(total, along_y(turn)), -turn, axis=1)
     weight = 1.0 / (PIECE * 32.0**3)
     proof = (total[0] / total[2] - total[1] / total[3]) * weight
     proof = jnp.concatenate([proof, proof], axis=0)

time: 115 us -> 114 us (level)
  waiting for transfers between devices: 54.6 us -> 51.1 us
  local copies, waits for them, and re-layouts: 3.14 us -> 4.54 us
    ppermute x30, waiting for transfers between devices: 54.6 us -> 51.1 us  [permute(): return lax.ppermute(value, AXES, pairs)]
    unnamed x24 -> x44, local copies, waits for them, and re-layouts: 1.58 us -> 2.96 us
  transfers between devices with their start and end apart: 30 -> 30, of which waited for: 18 -> 17; matrix products, arithmetic and copies ran while one was open for 6% -> 6% of each run, Pallas kernels for 0% -> 0%
where the time goes in v7:
time: 114 us; the launch traced here: 113 us
  waiting for transfers between devices  51.1 us (45%)
  starting transfers between devices  30.7 us (27%)
  Pallas kernels  16.7 us (15%)
  other arithmetic  9.61 us (8%)
  local copies, waits for them, and re-layouts  4.54 us (4%)
    ppermute x30, waiting for transfers between devices, permute(): return lax.ppermute(value, AXES, pairs)  51.1 us
    ppermute x30, starting transfers between devices, permute(): return lax.ppermute(value, AXES, pairs)  30.7 us
    pallas_call x1, Pallas kernels, pair_sums(): pl.pallas_call(functools.partial(pair_kernel, tag_cuts=tuple(tag_cuts), c...  11.2 us
    pallas_call x1, Pallas kernels, raw_partial(): pl.pallas_call(raw_kernel, grid=(feats // width,), in_specs=[pl.BlockSpec...  5.49 us
    unnamed x44, local copies, waits for them, and re-layouts  2.96 us
    convert_element_type x1, other arithmetic, shards(): tag = tag.astype(jnp.bfloat16)  2.63 us
  transfers between devices with their start and end apart: 30, of which 17 were waited for; matrix products, arithmetic and copies ran while one was open for 6% of the time, Pallas kernels for 0%

profile of v7, /device:TPU:4, one launch (start us, length us, event | category | flops | bytes accessed | tf_op | source)
XLA Modules:
  0.0 113.1 jit_solution(16812284735459642443)
XLA Ops:
  0.0 5.5 %raw.1 = f32[512,1024]{1,0:T(8,128)} custom-call(s32[8,11]{1,0:T(8,128)} %bitcast.39, bf16[1584,512]{1,0:T(8,128)(2,1)} %bitcast.34, bf16[1584,1024]{1,0:T(8,128)(2,1)} %geometry.1), custom_call_target="tpu_custom_call" | custom-call | flops 1660944384 | bytes 8388608 | tf_op jit(solution)/shard_map/raw/pallas_call | solution.py:83
  5.5 1.7 %constant_dynamic-slice_fusion.1 = (f32[4,1,32,1024]{3,2,1,0:T(8,128)S(1)}, f16[4,1,32,1024]{3,2,0,1:T(8,128)(2,1)S(1)}, f16[4,1,32,1024]{3,2,0,1:T(8,128)(2,1)S(1)}, f16[4,1,32,1024]{3,2,0,1:T(8,128)(2,1)S(1)}) fusion(f32[4,4,32,1024]{3,2,1,0:T(8,128)} %bitcast.33, s32[]{:T(128)S(6)} %select_n.179, s32[]{:T(128)S(6)} %select_n.183, s32[]{:T(128)S(6)} %select_n.181, ...), kind=kLoop, calls=%fused_computation.42 | loop fusion | flops 393216 | bytes 3407888 | tf_op jit(solution)/shard_map/jit(dynamic_index_in_dim)/dynamic_slice | solution.py:290
  7.2 3.3 %collective-permute-start = (f16[128,1024]{1,0:T(8,128)(2,1)S(1)}, f16[128,1024]{1,0:T(8,128)(2,1)S(1)}, u32[]{:S(2)}, u32[]{:S(2)}) collective-permute-start(f16[128,1024]{1,0:T(8,128)(2,1)S(1)} %bitcast.37), channel_id=1, source_target_pairs={{0,128},{1,129},{2,130},{3,131},{4,132},{5,133},{6,134},{7,135},{8... | collective-permute-start | bytes 786440 | tf_op jit(solution)/shard_map/ppermute | solution.py:32
  11.2 2.6 %collective-permute-start.2 = (f16[128,1024]{1,0:T(8,128)(2,1)S(1)}, f16[128,1024]{1,0:T(8,128)(2,1)S(1)}, u32[]{:S(2)}, u32[]{:S(2)}) collective-permute-start(f16[128,1024]{1,0:T(8,128)(2,1)S(1)} %bitcast.35), channel_id=1, source_target_pairs={{0,192},{1,193},{2,194},{3,195},{4,196},{5,197},{6,198},{7,199},{8... | collective-permute-start | bytes 786440 | tf_op jit(solution)/shard_map/ppermute | solution.py:32
  14.5 2.6 %select_convert_fusion = bf16[16,1024]{1,0:T(8,128)(2,1)S(1)} fusion(bf16[]{:T(256)} %bitcast.5, bf16[]{:T(256)} %bitcast.4, bf16[]{:T(256)} %bitcast.3, bf16[]{:T(256)} %bitcast.2, s32[1024]{0:T(1024)S(1)} %get-tuple-element.61, s32[1024]{0:T(1024)S(1)} %get-tuple-element.62, pred[16]{0:T(512)(128)(4,1)S(1)} %iota_compare_fusion, pred[1024]{0:T(1024)(128)(4,1)S(1)} %fusion.11), kind=kLoop, calls=%fused_computation.16 | loop fusion | flops 163840 | bytes 42008 | tf_op jit(solution)/shard_map/convert_element_type | solution.py:285
  18.1 4.4 %collective-permute-done.1 = f16[128,1024]{1,0:T(8,128)(2,1)S(1)} collective-permute-done((f16[128,1024]{1,0:T(8,128)(2,1)S(1)}, f16[128,1024]{1,0:T(8,128)(2,1)S(1)}, u32[]{:S(2)}, u32[]{:S(2)}) %collective-permute-start.1) | collective-permute-done | bytes 262176 | tf_op jit(solution)/shard_map/ppermute | solution.py:32
  23.4 1.6 %collective-permute-done.3.refs_8_ = bf16[144,1024]{1,0:T(8,128)(2,1)S(1)} collective-permute-done((bf16[144,1024]{1,0:T(8,128)(2,1)S(1)}, bf16[144,1024]{1,0:T(8,128)(2,1)S(1)}, u32[]{:S(2)}, u32[]{:S(2)}) %collective-permute-start.3) | collective-permute-done | bytes 294944 | tf_op jit(solution)/shard_map/ppermute | solution.py:32
  25.2 2.0 %collective-permute-start.4 = (bf16[288,1024]{1,0:T(8,128)(2,1)S(1)}, bf16[288,1024]{1,0:T(8,128)(2,1)S(1)}, u32[]{:S(2)}, u32[]{:S(2)}) collective-permute-start(bf16[288,1024]{1,0:T(8,128)(2,1)S(1)} %maximum_select_fusion), channel_id=1, source_target_pairs={{0,2},{1,15},{2,4},{3,1},{4,6},{5,3},{6,8},{7,5},{8,10},{9,7},{10,... | collective-permute-start | bytes 1769480 | tf_op jit(solution)/shard_map/ppermute | solution.py:32
  27.2 1.4 %collective-permute-start.5 = (bf16[288,1024]{1,0:T(8,128)(2,1)S(1)}, bf16[288,1024]{1,0:T(8,128)(2,1)S(1)}, u32[]{:S(2)}, u32[]{:S(2)}) collective-permute-start(bf16[288,1024]{1,0:T(8,128)(2,1)S(1)} %maximum_select_fusion), channel_id=1, source_target_pairs={{0,64},{1,193},{2,66},{3,195},{4,68},{5,197},{6,70},{7,199},{8,72}... | collective-permute-start | bytes 1769480 | tf_op jit(solution)/shard_map/ppermute | solution.py:32
  28.5 1.2 %collective-permute-start.6 = (bf16[144,1024]{1,0:T(8,128)(2,1)S(1)}, bf16[144,1024]{1,0:T(8,128)(2,1)S(1)}, u32[]{:S(2)}, u32[]{:S(2)}) collective-permute-start(bf16[144,1024]{1,0:T(8,128)(2,1)S(1)} %pad_maximum_fusion.refs_1_.refs_7_), channel_id=1, source_target_pairs={{0,16},{1,17},{2,18},{3,19},{4,20},{5,21},{6,22},{7,23},{8,24},{9,... | collective-permute-start | bytes 884744 | tf_op jit(solution)/shard_map/ppermute | solution.py:32
  29.7 5.5 %collective-permute-done.6.refs_9_ = bf16[144,1024]{1,0:T(8,128)(2,1)S(1)} collective-permute-done((bf16[144,1024]{1,0:T(8,128)(2,1)S(1)}, bf16[144,1024]{1,0:T(8,128)(2,1)S(1)}, u32[]{:S(2)}, u32[]{:S(2)}) %collective-permute-start.6) | collective-permute-done | bytes 294944 | tf_op jit(solution)/shard_map/ppermute | solution.py:32
  35.2 3.7 %collective-permute-done.4.refs_2_ = bf16[288,1024]{1,0:T(8,128)(2,1)S(1)} collective-permute-done((bf16[288,1024]{1,0:T(8,128)(2,1)S(1)}, bf16[288,1024]{1,0:T(8,128)(2,1)S(1)}, u32[]{:S(2)}, u32[]{:S(2)}) %collective-permute-start.4) | collective-permute-done | bytes 589856 | tf_op jit(solution)/shard_map/ppermute | solution.py:32
  39.0 1.2 %collective-permute-start.10 = (bf16[288,1024]{1,0:T(8,128)(2,1)S(1)}, bf16[288,1024]{1,0:T(8,128)(2,1)S(1)}, u32[]{:S(2)}, u32[]{:S(2)}) collective-permute-start(bf16[288,1024]{1,0:T(8,128)(2,1)S(1)} %collective-permute-done.5.refs_11_), channel_id=1, source_target_pairs={{0,1},{1,0},{2,3},{3,2},{4,5},{5,4},{6,7},{7,6},{8,9},{9,8},{10,11... | collective-permute-start | bytes 1769480 | tf_op jit(solution)/shard_map/ppermute | solution.py:32
  40.2 2.3 %collective-permute-start.11 = (bf16[144,1024]{1,0:T(8,128)(2,1)S(1)}, bf16[144,1024]{1,0:T(8,128)(2,1)S(1)}, u32[]{:S(2)}, u32[]{:S(2)}) collective-permute-start(bf16[144,1024]{1,0:T(8,128)(2,1)S(1)} %collective-permute-done.6.refs_9_), channel_id=1, source_target_pairs={{0,1},{1,0},{2,3},{3,2},{4,5},{5,4},{6,7},{7,6},{8,9},{9,8},{10,11... | collective-permute-start | bytes 884744 | tf_op jit(solution)/shard_map/ppermute | solution.py:32
  43.1 1.2 %collective-permute-start.9 = (bf16[128,1024]{1,0:T(8,128)(2,1)S(1)}, bf16[128,1024]{1,0:T(8,128)(2,1)S(1)}, u32[]{:S(2)}, u32[]{:S(2)}) collective-permute-start(bf16[128,1024]{1,0:T(8,128)(2,1)S(1)} %get-tuple-element.53), channel_id=1, source_target_pairs={{0,16},{1,17},{2,18},{3,19},{4,20},{5,21},{6,22},{7,23},{8,24},{9,... | collective-permute-start | bytes 786440 | tf_op jit(solution)/shard_map/ppermute | solution.py:32
  44.3 5.9 %collective-permute-done.8.refs_13_ = bf16[128,1024]{1,0:T(8,128)(2,1)S(1)} collective-permute-done((bf16[128,1024]{1,0:T(8,128)(2,1)S(1)}, bf16[128,1024]{1,0:T(8,128)(2,1)S(1)}, u32[]{:S(2)}, u32[]{:S(2)}) %collective-permute-start.8) | collective-permute-done | bytes 262176 | tf_op jit(solution)/shard_map/ppermute | solution.py:32
  50.2 2.0 %collective-permute-done.9.refs_15_ = bf16[128,1024]{1,0:T(8,128)(2,1)S(1)} collective-permute-done((bf16[128,1024]{1,0:T(8,128)(2,1)S(1)}, bf16[128,1024]{1,0:T(8,128)(2,1)S(1)}, u32[]{:S(2)}, u32[]{:S(2)}) %collective-permute-start.9) | collective-permute-done | bytes 262176 | tf_op jit(solution)/shard_map/ppermute | solution.py:32
  53.0 2.6 %collective-permute-start.15 = (bf16[128,1024]{1,0:T(8,128)(2,1)S(1)}, bf16[128,1024]{1,0:T(8,128)(2,1)S(1)}, u32[]{:S(2)}, u32[]{:S(2)}) collective-permute-start(bf16[128,1024]{1,0:T(8,128)(2,1)S(1)} %pad_maximum_fusion.1), channel_id=1, source_target_pairs={{32,16},{96,80},{160,144},{224,208}} | collective-permute-start | bytes 786440 | tf_op jit(solution)/shard_map/ppermute | solution.py:32
  55.6 1.3 %collective-permute-start.16 = (bf16[128,1024]{1,0:T(8,128)(2,1)S(1)}, bf16[128,1024]{1,0:T(8,128)(2,1)S(1)}, u32[]{:S(2)}, u32[]{:S(2)}) collective-permute-start(bf16[128,1024]{1,0:T(8,128)(2,1)S(1)} %pad_maximum_fusion.1), channel_id=1, source_target_pairs={{32,0},{96,64},{160,128},{224,192}} | collective-permute-start | bytes 786440 | tf_op jit(solution)/shard_map/ppermute | solution.py:32
  57.3 2.1 %collective-permute-done.15 = bf16[128,1024]{1,0:T(8,128)(2,1)S(1)} collective-permute-done((bf16[128,1024]{1,0:T(8,128)(2,1)S(1)}, bf16[128,1024]{1,0:T(8,128)(2,1)S(1)}, u32[]{:S(2)}, u32[]{:S(2)}) %collective-permute-start.15) | collective-permute-done | bytes 262176 | tf_op jit(solution)/shard_map/ppermute | solution.py:32
  59.5 3.4 %collective-permute-done.16 = bf16[128,1024]{1,0:T(8,128)(2,1)S(1)} collective-permute-done((bf16[128,1024]{1,0:T(8,128)(2,1)S(1)}, bf16[128,1024]{1,0:T(8,128)(2,1)S(1)}, u32[]{:S(2)}, u32[]{:S(2)}) %collective-permute-start.16) | collective-permute-done | bytes 262176 | tf_op jit(solution)/shard_map/ppermute | solution.py:32
  62.9 2.8 %collective-permute-done.13.refs_16_ = bf16[128,1024]{1,0:T(8,128)(2,1)S(1)} collective-permute-done((bf16[128,1024]{1,0:T(8,128)(2,1)S(1)}, bf16[128,1024]{1,0:T(8,128)(2,1)S(1)}, u32[]{:S(2)}, u32[]{:S(2)}) %collective-permute-start.13) | collective-permute-done | bytes 262176 | tf_op jit(solution)/shard_map/ppermute | solution.py:32
  66.4 2.5 %collective-permute-start.21 = (bf16[128,1024]{1,0:T(8,128)(2,1)S(1)}, bf16[128,1024]{1,0:T(8,128)(2,1)}, u32[]{:S(2)}, u32[]{:S(2)}) collective-permute-start(bf16[128,1024]{1,0:T(8,128)(2,1)S(1)} %collective-permute-done.8.refs_13_), channel_id=1, source_target_pairs={{0,16},{1,17},{2,18},{3,19},{4,20},{5,21},{6,22},{7,23},{8,24},{9,... | collective-permute-start | bytes 786440 | tf_op jit(solution)/shard_map/ppermute | solution.py:32
  70.4 2.9 %collective-permute-done.21.refs_19_ = bf16[128,1024]{1,0:T(8,128)(2,1)} collective-permute-done((bf16[128,1024]{1,0:T(8,128)(2,1)S(1)}, bf16[128,1024]{1,0:T(8,128)(2,1)}, u32[]{:S(2)}, u32[]{:S(2)}) %collective-permute-start.21) | collective-permute-done | bytes 262176 | tf_op jit(solution)/shard_map/ppermute | solution.py:32
  74.3 1.3 %collective-permute-start.18 = (bf16[48,1024]{1,0:T(8,128)(2,1)S(1)}, bf16[48,1024]{1,0:T(8,128)(2,1)S(1)}, u32[]{:S(2)}, u32[]{:S(2)}) collective-permute-start(bf16[48,1024]{1,0:T(8,128)(2,1)S(1)} %fusion.3), channel_id=1, source_target_pairs={{32,18},{33,17},{34,20},{36,22},{38,24},{43,27},{45,29},{47,31},{9... | collective-permute-start | bytes 294920 | tf_op jit(solution)/shard_map/ppermute | solution.py:32
  79.4 11.2 %pairs.1 = (f32[4,512]{1,0:T(4,128)}, f32[4,512]{1,0:T(4,128)}, f32[4,1152]{1,0:T(4,128)}, f32[4,128]{1,0:T(4,128)}) custom-call(s32[2]{0:T(128)} %pad_add_fusion.1.refs_0_, bf16[144,1024]{1,0:T(8,128)(2,1)} %copy-done.2, bf16[288,1024]{1,0:T(8,128)(2,1)} %copy-done.5, bf16[288,1024]{1,0:T(8,128)(2,1)} %copy-done.6, bf16[288,1024]{1,0:T(8,128)(2,1)} %copy-done.1, ...), custom_call_target="tpu_custom_call" | custom-call | flops 4706009088 | bytes 6619136 | tf_op jit(solution)/shard_map/pairs/pallas_call | solution.py:245
  91.2 1.1 collective-permute-done.24
  94.3 1.3 %collective-permute-start.26 = (f32[4,128]{1,0:T(4,128)S(1)}, f32[4,128]{1,0:T(4,128)S(1)}, u32[]{:S(2)}, u32[]{:S(2)}) collective-permute-start(f32[4,128]{1,0:T(4,128)S(1)} %slice_add_fusion.2), channel_id=1, source_target_pairs={{0,32},{64,96},{128,160},{192,224}} | collective-permute-start | bytes 6152 | tf_op jit(solution)/shard_map/ppermute | solution.py:32
  95.5 1.3 %collective-permute-start.27 = (f32[4,128]{1,0:T(4,128)S(1)}, f32[4,128]{1,0:T(4,128)S(1)}, u32[]{:S(2)}, u32[]{:S(2)}) collective-permute-start(f32[4,128]{1,0:T(4,128)S(1)} %slice_add_fusion.2), channel_id=1, source_target_pairs={{16,32},{80,96},{144,160},{208,224}} | collective-permute-start | bytes 6152 | tf_op jit(solution)/shard_map/ppermute | solution.py:32
  96.8 4.4 %collective-permute-done.26 = f32[4,128]{1,0:T(4,128)S(1)} collective-permute-done((f32[4,128]{1,0:T(4,128)S(1)}, f32[4,128]{1,0:T(4,128)S(1)}, u32[]{:S(2)}, u32[]{:S(2)}) %collective-permute-start.26) | collective-permute-done | bytes 2080 | tf_op jit(solution)/shard_map/ppermute | solution.py:32
  103.0 4.0 %collective-permute-done.28 = f32[4,4,128]{2,1,0:T(4,128)S(1)} collective-permute-done((f32[4,4,128]{2,1,0:T(4,128)S(1)}, f32[4,4,128]{2,1,0:T(4,128)S(1)}, u32[]{:S(2)}, u32[]{:S(2)}) %collective-permute-start.28) | collective-permute-done | bytes 8224 | tf_op jit(solution)/shard_map/ppermute | solution.py:32
  107.1 5.1 %collective-permute-done.29 = f32[4,4,128]{2,1,0:T(4,128)S(1)} collective-permute-done((f32[4,4,128]{2,1,0:T(4,128)S(1)}, f32[4,4,128]{2,1,0:T(4,128)S(1)}, u32[]{:S(2)}, u32[]{:S(2)}) %collective-permute-start.29) | collective-permute-done | bytes 8224 | tf_op jit(solution)/shard_map/ppermute | solution.py:32
  (116 shorter events, 17.3 us)
Async XLA Ops:
  7.2 10.8 %collective-permute-start = (f16[128,1024]{1,0:T(8,128)(2,1)S(1)}, f16[128,1024]{1,0:T(8,128)(2,1)S(1)}, u32[]{:S(2)}, u32[]{:S(2)}) collective-permute-start(f16[128,1024]{1,0:T(8,128)(2,1)S(1)} %bitcast.37), channel_id=1, source_target_pairs={{0,128},{1,129},{2,130},{3,131},{4,132},{5,133},{6,134},{7,135},{8... | collective-permute-start | bytes 786440 | tf_op jit(solution)/shard_map/ppermute | solution.py:32
  10.5 12.0 %collective-permute-start.1 = (f16[128,1024]{1,0:T(8,128)(2,1)S(1)}, f16[128,1024]{1,0:T(8,128)(2,1)S(1)}, u32[]{:S(2)}, u32[]{:S(2)}) collective-permute-start(f16[128,1024]{1,0:T(8,128)(2,1)S(1)} %bitcast.36), channel_id=1, source_target_pairs={{0,64},{1,65},{2,66},{3,67},{4,68},{5,69},{6,70},{7,71},{8,72},{9,... | collective-permute-start | bytes 786440 | tf_op jit(solution)/shard_map/ppermute | solution.py:32
  11.2 11.7 %collective-permute-start.2 = (f16[128,1024]{1,0:T(8,128)(2,1)S(1)}, f16[128,1024]{1,0:T(8,128)(2,1)S(1)}, u32[]{:S(2)}, u32[]{:S(2)}) collective-permute-start(f16[128,1024]{1,0:T(8,128)(2,1)S(1)} %bitcast.35), channel_id=1, source_target_pairs={{0,192},{1,193},{2,194},{3,195},{4,196},{5,197},{6,198},{7,199},{8... | collective-permute-start | bytes 786440 | tf_op jit(solution)/shard_map/ppermute | solution.py:32
  23.3 29.6 %copy-start.2 = (bf16[144,1024]{1,0:T(8,128)(2,1)}, bf16[144,1024]{1,0:T(8,128)(2,1)S(1)}, u32[]{:S(2)}) copy-start(bf16[144,1024]{1,0:T(8,128)(2,1)S(1)} %pad_maximum_fusion.refs_1_.refs_7_) | copy-start | bytes 884740
  23.3 1.7 %collective-permute-start.3 = (bf16[144,1024]{1,0:T(8,128)(2,1)S(1)}, bf16[144,1024]{1,0:T(8,128)(2,1)S(1)}, u32[]{:S(2)}, u32[]{:S(2)}) collective-permute-start(bf16[144,1024]{1,0:T(8,128)(2,1)S(1)} %pad_maximum_fusion.refs_1_.refs_7_), channel_id=1, source_target_pairs={{0,1},{1,0},{2,3},{3,2},{4,5},{5,4},{6,7},{7,6},{8,9},{9,8},{10,11... | collective-permute-start | bytes 884744 | tf_op jit(solution)/shard_map/ppermute | solution.py:32
  25.2 13.8 %collective-permute-start.4 = (bf16[288,1024]{1,0:T(8,128)(2,1)S(1)}, bf16[288,1024]{1,0:T(8,128)(2,1)S(1)}, u32[]{:S(2)}, u32[]{:S(2)}) collective-permute-start(bf16[288,1024]{1,0:T(8,128)(2,1)S(1)} %maximum_select_fusion), channel_id=1, source_target_pairs={{0,2},{1,15},{2,4},{3,1},{4,6},{5,3},{6,8},{7,5},{8,10},{9,7},{10,... | collective-permute-start | bytes 1769480 | tf_op jit(solution)/shard_map/ppermute | solution.py:32
  27.2 11.8 %collective-permute-start.5 = (bf16[288,1024]{1,0:T(8,128)(2,1)S(1)}, bf16[288,1024]{1,0:T(8,128)(2,1)S(1)}, u32[]{:S(2)}, u32[]{:S(2)}) collective-permute-start(bf16[288,1024]{1,0:T(8,128)(2,1)S(1)} %maximum_select_fusion), channel_id=1, source_target_pairs={{0,64},{1,193},{2,66},{3,195},{4,68},{5,197},{6,70},{7,199},{8,72}... | collective-permute-start | bytes 1769480 | tf_op jit(solution)/shard_map/ppermute | solution.py:32
  28.5 6.7 %collective-permute-start.6 = (bf16[144,1024]{1,0:T(8,128)(2,1)S(1)}, bf16[144,1024]{1,0:T(8,128)(2,1)S(1)}, u32[]{:S(2)}, u32[]{:S(2)}) collective-permute-start(bf16[144,1024]{1,0:T(8,128)(2,1)S(1)} %pad_maximum_fusion.refs_1_.refs_7_), channel_id=1, source_target_pairs={{0,16},{1,17},{2,18},{3,19},{4,20},{5,21},{6,22},{7,23},{8,24},{9,... | collective-permute-start | bytes 884744 | tf_op jit(solution)/shard_map/ppermute | solution.py:32
  39.0 34.4 %copy-start.5 = (bf16[288,1024]{1,0:T(8,128)(2,1)}, bf16[288,1024]{1,0:T(8,128)(2,1)S(1)}, u32[]{:S(2)}) copy-start(bf16[288,1024]{1,0:T(8,128)(2,1)S(1)} %collective-permute-done.4.refs_2_) | copy-start | bytes 1769476
  39.0 13.3 %collective-permute-start.10 = (bf16[288,1024]{1,0:T(8,128)(2,1)S(1)}, bf16[288,1024]{1,0:T(8,128)(2,1)S(1)}, u32[]{:S(2)}, u32[]{:S(2)}) collective-permute-start(bf16[288,1024]{1,0:T(8,128)(2,1)S(1)} %collective-permute-done.5.refs_11_), channel_id=1, source_target_pairs={{0,1},{1,0},{2,3},{3,2},{4,5},{5,4},{6,7},{7,6},{8,9},{9,8},{10,11... | collective-permute-start | bytes 1769480 | tf_op jit(solution)/shard_map/ppermute | solution.py:32
  40.1 12.1 %collective-permute-start.7 = (bf16[288,1024]{1,0:T(8,128)(2,1)S(1)}, bf16[288,1024]{1,0:T(8,128)(2,1)S(1)}, u32[]{:S(2)}, u32[]{:S(2)}) collective-permute-start(bf16[288,1024]{1,0:T(8,128)(2,1)S(1)} %collective-permute-done.4.refs_2_), channel_id=1, source_target_pairs={{0,2},{1,15},{2,4},{3,1},{4,6},{5,3},{6,8},{7,5},{8,10},{9,7},{10,... | collective-permute-start | bytes 1769480 | tf_op jit(solution)/shard_map/ppermute | solution.py:32
  40.2 12.0 %collective-permute-start.11 = (bf16[144,1024]{1,0:T(8,128)(2,1)S(1)}, bf16[144,1024]{1,0:T(8,128)(2,1)S(1)}, u32[]{:S(2)}, u32[]{:S(2)}) collective-permute-start(bf16[144,1024]{1,0:T(8,128)(2,1)S(1)} %collective-permute-done.6.refs_9_), channel_id=1, source_target_pairs={{0,1},{1,0},{2,3},{3,2},{4,5},{5,4},{6,7},{7,6},{8,9},{9,8},{10,11... | collective-permute-start | bytes 884744 | tf_op jit(solution)/shard_map/ppermute | solution.py:32
  42.6 7.7 %collective-permute-start.8 = (bf16[128,1024]{1,0:T(8,128)(2,1)S(1)}, bf16[128,1024]{1,0:T(8,128)(2,1)S(1)}, u32[]{:S(2)}, u32[]{:S(2)}) collective-permute-start(bf16[128,1024]{1,0:T(8,128)(2,1)S(1)} %get-tuple-element.54), channel_id=1, source_target_pairs={{0,64},{1,193},{2,66},{3,195},{4,68},{5,197},{6,70},{7,199},{8,72}... | collective-permute-start | bytes 786440 | tf_op jit(solution)/shard_map/ppermute | solution.py:32
  43.1 9.1 %collective-permute-start.9 = (bf16[128,1024]{1,0:T(8,128)(2,1)S(1)}, bf16[128,1024]{1,0:T(8,128)(2,1)S(1)}, u32[]{:S(2)}, u32[]{:S(2)}) collective-permute-start(bf16[128,1024]{1,0:T(8,128)(2,1)S(1)} %get-tuple-element.53), channel_id=1, source_target_pairs={{0,16},{1,17},{2,18},{3,19},{4,20},{5,21},{6,22},{7,23},{8,24},{9,... | collective-permute-start | bytes 786440 | tf_op jit(solution)/shard_map/ppermute | solution.py:32
  52.9 12.8 %collective-permute-start.12 = (bf16[288,1024]{1,0:T(8,128)(2,1)S(1)}, bf16[288,1024]{1,0:T(8,128)(2,1)S(1)}, u32[]{:S(2)}, u32[]{:S(2)}) collective-permute-start(bf16[288,1024]{1,0:T(8,128)(2,1)S(1)} %collective-permute-done.7.refs_3_), channel_id=1, source_target_pairs={{0,2},{1,15},{2,4},{3,1},{4,6},{5,3},{6,8},{7,5},{8,10},{9,7},{10,... | collective-permute-start | bytes 1769480 | tf_op jit(solution)/shard_map/ppermute | solution.py:32
  53.0 6.4 %collective-permute-start.15 = (bf16[128,1024]{1,0:T(8,128)(2,1)S(1)}, bf16[128,1024]{1,0:T(8,128)(2,1)S(1)}, u32[]{:S(2)}, u32[]{:S(2)}) collective-permute-start(bf16[128,1024]{1,0:T(8,128)(2,1)S(1)} %pad_maximum_fusion.1), channel_id=1, source_target_pairs={{32,16},{96,80},{160,144},{224,208}} | collective-permute-start | bytes 786440 | tf_op jit(solution)/shard_map/ppermute | solution.py:32
  55.6 7.3 %collective-permute-start.16 = (bf16[128,1024]{1,0:T(8,128)(2,1)S(1)}, bf16[128,1024]{1,0:T(8,128)(2,1)S(1)}, u32[]{:S(2)}, u32[]{:S(2)}) collective-permute-start(bf16[128,1024]{1,0:T(8,128)(2,1)S(1)} %pad_maximum_fusion.1), channel_id=1, source_target_pairs={{32,0},{96,64},{160,128},{224,192}} | collective-permute-start | bytes 786440 | tf_op jit(solution)/shard_map/ppermute | solution.py:32
  57.0 8.7 %collective-permute-start.13 = (bf16[128,1024]{1,0:T(8,128)(2,1)S(1)}, bf16[128,1024]{1,0:T(8,128)(2,1)S(1)}, u32[]{:S(2)}, u32[]{:S(2)}) collective-permute-start(bf16[128,1024]{1,0:T(8,128)(2,1)S(1)} %slice.99), channel_id=1, source_target_pairs={{0,16},{1,17},{2,18},{3,19},{4,20},{5,21},{6,22},{7,23},{8,24},{9,... | collective-permute-start | bytes 786440 | tf_op jit(solution)/shard_map/ppermute | solution.py:32
  57.1 8.6 %collective-permute-start.14 = (bf16[128,1024]{1,0:T(8,128)(2,1)S(1)}, bf16[128,1024]{1,0:T(8,128)(2,1)S(1)}, u32[]{:S(2)}, u32[]{:S(2)}) collective-permute-start(bf16[128,1024]{1,0:T(8,128)(2,1)S(1)} %collective-permute-done.8.refs_13_), channel_id=1, source_target_pairs={{0,1},{1,0},{2,3},{3,2},{4,5},{5,4},{6,7},{7,6},{8,9},{9,8},{10,11... | collective-permute-start | bytes 786440 | tf_op jit(solution)/shard_map/ppermute | solution.py:32
  66.4 7.0 %collective-permute-start.21 = (bf16[128,1024]{1,0:T(8,128)(2,1)S(1)}, bf16[128,1024]{1,0:T(8,128)(2,1)}, u32[]{:S(2)}, u32[]{:S(2)}) collective-permute-start(bf16[128,1024]{1,0:T(8,128)(2,1)S(1)} %collective-permute-done.8.refs_13_), channel_id=1, source_target_pairs={{0,16},{1,17},{2,18},{3,19},{4,20},{5,21},{6,22},{7,23},{8,24},{9,... | collective-permute-start | bytes 786440 | tf_op jit(solution)/shard_map/ppermute | solution.py:32
  69.0 5.3 %collective-permute-start.23 = (bf16[128,1024]{1,0:T(8,128)(2,1)S(1)}, bf16[128,1024]{1,0:T(8,128)(2,1)S(1)}, u32[]{:S(2)}, u32[]{:S(2)}) collective-permute-start(bf16[128,1024]{1,0:T(8,128)(2,1)S(1)} %add.129), channel_id=1, source_target_pairs={{0,1},{16,17},{64,65},{80,81},{128,129},{144,145},{192,193},{208,2... | collective-permute-start | bytes 786440 | tf_op jit(solution)/shard_map/ppermute | solution.py:32
  69.7 8.1 %collective-permute-start.17 = (bf16[144,1024]{1,0:T(8,128)(2,1)S(1)}, bf16[144,1024]{1,0:T(8,128)(2,1)S(1)}, u32[]{:S(2)}, u32[]{:S(2)}) collective-permute-start(bf16[144,1024]{1,0:T(8,128)(2,1)S(1)} %slice_select_fusion), channel_id=1, source_target_pairs={{0,2},{1,15},{2,4},{3,1},{4,6},{5,3},{6,8},{7,5},{8,10},{9,7},{10,... | collective-permute-start | bytes 884744 | tf_op jit(solution)/shard_map/ppermute | solution.py:32
  69.8 8.0 %collective-permute-start.19 = (bf16[128,1024]{1,0:T(8,128)(2,1)S(1)}, bf16[128,1024]{1,0:T(8,128)(2,1)S(1)}, u32[]{:S(2)}, u32[]{:S(2)}) collective-permute-start(bf16[128,1024]{1,0:T(8,128)(2,1)S(1)} %copy-done.12), channel_id=1, source_target_pairs={{0,1},{1,0},{2,3},{3,2},{4,5},{5,4},{6,7},{7,6},{8,9},{9,8},{10,11... | collective-permute-start | bytes 786440 | tf_op jit(solution)/shard_map/ppermute | solution.py:32
  69.9 7.9 %collective-permute-start.20 = (bf16[128,1024]{1,0:T(8,128)(2,1)S(1)}, bf16[128,1024]{1,0:T(8,128)(2,1)S(1)}, u32[]{:S(2)}, u32[]{:S(2)}) collective-permute-start(bf16[128,1024]{1,0:T(8,128)(2,1)S(1)} %copy-done.14), channel_id=1, source_target_pairs={{0,1},{1,0},{2,3},{3,2},{4,5},{5,4},{6,7},{7,6},{8,9},{9,8},{10,11... | collective-permute-start | bytes 786440 | tf_op jit(solution)/shard_map/ppermute | solution.py:32
  73.3 4.5 %collective-permute-start.22 = (bf16[128,1024]{1,0:T(8,128)(2,1)}, bf16[128,1024]{1,0:T(8,128)(2,1)S(1)}, u32[]{:S(2)}, u32[]{:S(2)}) collective-permute-start(bf16[128,1024]{1,0:T(8,128)(2,1)} %collective-permute-done.21.refs_19_), channel_id=1, source_target_pairs={{0,1},{1,0},{2,3},{3,2},{4,5},{5,4},{6,7},{7,6},{8,9},{9,8},{10,11... | collective-permute-start | bytes 786440 | tf_op jit(solution)/shard_map/ppermute | solution.py:32
  74.3 3.5 %collective-permute-start.18 = (bf16[48,1024]{1,0:T(8,128)(2,1)S(1)}, bf16[48,1024]{1,0:T(8,128)(2,1)S(1)}, u32[]{:S(2)}, u32[]{:S(2)}) collective-permute-start(bf16[48,1024]{1,0:T(8,128)(2,1)S(1)} %fusion.3), channel_id=1, source_target_pairs={{32,18},{33,17},{34,20},{36,22},{38,24},{43,27},{45,29},{47,31},{9... | collective-permute-start | bytes 294920 | tf_op jit(solution)/shard_map/ppermute | solution.py:32
  90.6 1.6 %collective-permute-start.24 = (f32[4,1152]{1,0:T(4,128)}, f32[4,1152]{1,0:T(4,128)S(1)}, u32[]{:S(2)}, u32[]{:S(2)}) collective-permute-start(f32[4,1152]{1,0:T(4,128)} %get-tuple-element.46), channel_id=1, source_target_pairs={{0,1},{1,0},{2,3},{3,2},{4,5},{5,4},{6,7},{7,6},{8,9},{9,8},{10,11... | collective-permute-start | bytes 55304 | tf_op jit(solution)/shard_map/ppermute | solution.py:32
  92.9 8.4 %collective-permute-start.25 = (f32[4,512]{1,0:T(4,128)S(1)}, f32[4,512]{1,0:T(4,128)S(1)}, u32[]{:S(2)}, u32[]{:S(2)}) collective-permute-start(f32[4,512]{1,0:T(4,128)S(1)} %slice_add_fusion), channel_id=1, source_target_pairs={{0,16},{1,17},{2,18},{3,19},{4,20},{5,21},{6,22},{7,23},{8,24},{9,... | collective-permute-start | bytes 24584 | tf_op jit(solution)/shard_map/ppermute | solution.py:32
  94.3 7.0 %collective-permute-start.26 = (f32[4,128]{1,0:T(4,128)S(1)}, f32[4,128]{1,0:T(4,128)S(1)}, u32[]{:S(2)}, u32[]{:S(2)}) collective-permute-start(f32[4,128]{1,0:T(4,128)S(1)} %slice_add_fusion.2), channel_id=1, source_target_pairs={{0,32},{64,96},{128,160},{192,224}} | collective-permute-start | bytes 6152 | tf_op jit(solution)/shard_map/ppermute | solution.py:32
  95.5 5.7 %collective-permute-start.27 = (f32[4,128]{1,0:T(4,128)S(1)}, f32[4,128]{1,0:T(4,128)S(1)}, u32[]{:S(2)}, u32[]{:S(2)}) collective-permute-start(f32[4,128]{1,0:T(4,128)S(1)} %slice_add_fusion.2), channel_id=1, source_target_pairs={{16,32},{80,96},{144,160},{208,224}} | collective-permute-start | bytes 6152 | tf_op jit(solution)/shard_map/ppermute | solution.py:32
  102.1 4.9 %collective-permute-start.28 = (f32[4,4,128]{2,1,0:T(4,128)S(1)}, f32[4,4,128]{2,1,0:T(4,128)S(1)}, u32[]{:S(2)}, u32[]{:S(2)}) collective-permute-start(f32[4,4,128]{2,1,0:T(4,128)S(1)} %pad_add_fusion), channel_id=1, source_target_pairs={{0,64},{1,65},{2,66},{3,67},{4,68},{5,69},{6,70},{7,71},{8,72},{9,... | collective-permute-start | bytes 24584 | tf_op jit(solution)/shard_map/ppermute | solution.py:32
  107.0 5.2 %collective-permute-start.29 = (f32[4,4,128]{2,1,0:T(4,128)S(1)}, f32[4,4,128]{2,1,0:T(4,128)S(1)}, u32[]{:S(2)}, u32[]{:S(2)}) collective-permute-start(f32[4,4,128]{2,1,0:T(4,128)S(1)} %maximum_add_fusion), channel_id=1, source_target_pairs={{0,128},{1,129},{2,130},{3,131},{4,132},{5,133},{6,134},{7,135},{8... | collective-permute-start | bytes 24584 | tf_op jit(solution)/shard_map/ppermute | solution.py:32
  (20 other events, 182.9 us)

commit v8 on v7

--- a/solution.py
+++ b/solution.py
@@ -12,6 +12,7 @@
 TAG = 16
 BINS = 8
 CHUNK = 512
+EARLY = 7
 AXES = ("layer", "shower")
 NY, NX, NZ, NC = 4, 4, 8, 2
 
@@ -99,15 +100,21 @@
     )(pattern.T, showers.T, geometry)
 
 
-def pair_kernel(*refs, tag_cuts, col_cuts, n_args):
+NAMES = ("own", "own_t", "y1", "y1_t", "y2", "y2_t", "x1", "x1_t", "xa", "xb", "xa_t", "xb_t", "w2", "w2_t", "odd")
+TAG_OF = ("own", "x1", "own_t", "x1_t", "own")
+
+
+def pair_kernel(*refs, col_cuts, n_cols_args, late):
     n_cols = len(col_cuts)
-    place = refs[0]
-    args = refs[1 : 1 + n_args]
-    out_near, out_far, out_theirs, out_odd = refs[1 + n_args : 5 + n_args]
-    rows_at, cols_at, row_tags, col_tags, row_sems, col_sems, tag_sems = refs[5 + n_args :]
+    names = NAMES if late else NAMES[:6]
+    place, refs = refs[0], refs[1:]
+    before, refs = refs[: 2 * late], refs[2 * late :]
+    col_args, refs = refs[:n_cols_args], refs[n_cols_args:]
+    held, refs = dict(zip(names, refs)), refs[len(names) :]
+    outs, refs = refs[: 4 if late else 2], refs[4 if late else 2 :]
+    rows_at, cols_at, row_tags, col_tags, row_sems, col_sems, tag_sems = refs
     odd_here, core = place[0], place[1]
     tagged = BLOCK + TAG
-    row_args = args[n_cols_args(col_cuts) :]
 
     def start(source, first, size, target, at, sem):
         copy = pltpu.make_async_copy(
@@ -118,64 +125,62 @@
 
     starts = [sum(size for _, _, size in col_cuts[:at]) for at in range(n_cols)]
     depth = sum(size for _, _, size in col_cuts)
-
-    def load_col(at):
-        arg, first, size = col_cuts[at]
-        return [
-            start(args[arg], first, size, cols_at, starts[at], col_sems.at[at]),
-            start(args[arg], first - TAG, TAG, col_tags, at * TAG, tag_sems.at[at]),
-        ]
-
-    held = {at: load_col(at) for at in range(2)}
-    waits = []
-    for at, (arg, first) in enumerate(tag_cuts):
-        waits.append(start(args[arg], first, TAG, row_tags, at * TAG, tag_sems.at[n_cols + at]))
-
-    own, own_t, x1, x1_t, y1, y1_t, y2, y2_t = row_args[:8]
-    xa, xb, xa_t, xb_t, w2, w2_t, odd_rows = row_args[8:]
+    loads = []
+    for at, (arg, first, size) in enumerate(col_cuts):
+        source = col_args[arg]
+        loads.append(
+            [
+                start(source, first, size, cols_at, starts[at], col_sems.at[at]),
+                start(source, first - TAG, TAG, col_tags, at * TAG, tag_sems.at[at]),
+            ]
+        )
+    chunks = (0, 2, 1, 3, 4) if late else (0, 2)
+    tags = {
+        chunk: start(
+            held[TAG_OF[chunk]], 0, TAG, row_tags, chunk * TAG, tag_sems.at[n_cols + chunk]
+        )
+        for chunk in chunks
+    }
     turn = jnp.where(core == 0, 3, 1)
-    side = [4 * CHUNK // 2 * jnp.where(core == b, 0, 1) for b in range(NC)]
+    side = [2 * CHUNK * jnp.where(core == b, 0, 1) for b in range(NC)]
     made = []
 
-    def rows(source, first, at):
+    def rows(name, first, at):
         at = at if isinstance(at, int) else pl.multiple_of(at, BLOCK)
-        made.append(start(source, first, BLOCK, rows_at, at, row_sems.at[len(made)]))
-
-    rows(own, TAG, 0)
-    rows(y2, 0, 2 * BLOCK)
+        made.append(start(held[name], first, BLOCK, rows_at, at, row_sems.at[len(made)]))
+
+    rows("own", TAG, 0)
+    rows("y2", 0, 2 * BLOCK)
     for b in range(NC):
-        rows(y1, TAG + b * tagged, side[b] + turn * BLOCK)
-        rows(y1_t, TAG + b * tagged, side[b] + (NY - turn) * BLOCK)
+        rows("y1", TAG + b * tagged, side[b] + turn * BLOCK)
+        rows("y1_t", TAG + b * tagged, side[b] + (NY - turn) * BLOCK)
     n_near = len(made)
-    for copy in waits + made:
-        copy.wait()
-    for at in range(2, n_cols):
-        held[at] = load_col(at)
-    rows(own_t, TAG, 2 * CHUNK)
-    rows(y2_t, 0, 2 * CHUNK + 2 * BLOCK)
+    rows("own_t", TAG, 2 * CHUNK)
+    rows("y2_t", 0, 2 * CHUNK + 2 * BLOCK)
     n_far = len(made)
-    rows(x1, TAG, CHUNK)
-    rows(w2, 0, CHUNK + 2 * BLOCK)
-    for b in range(NC):
-        rows((xa, xb)[b], 0, CHUNK + side[b] + turn * BLOCK)
-        rows((xa_t, xb_t)[b], 0, CHUNK + side[b] + (NY - turn) * BLOCK)
-    rows(x1_t, TAG, 3 * CHUNK)
-    rows(w2_t, 0, 3 * CHUNK + 2 * BLOCK)
-    rows(odd_rows, 0, 4 * CHUNK)
-    waited = 0
+    if late:
+        rows("x1", TAG, CHUNK)
+        rows("w2", 0, CHUNK + 2 * BLOCK)
+        for b in range(NC):
+            rows(("xa", "xb")[b], 0, CHUNK + side[b] + turn * BLOCK)
+            rows(("xa_t", "xb_t")[b], 0, CHUNK + side[b] + (NY - turn) * BLOCK)
+        rows("x1_t", TAG, 3 * CHUNK)
+        rows("w2_t", 0, 3 * CHUNK + 2 * BLOCK)
+        rows("odd", 0, 4 * CHUNK)
+    waited = set()
 
     def bin_of(code):
         source = (code >= BINS).astype(jnp.float32)
         return code - BINS * source, source
 
-    for chunk in (0, 2, 1, 3, 4):
-        for copy in {2: made[n_near:n_far], 1: made[n_far:]}.get(chunk, []):
+    for chunk in chunks:
+        tags[chunk].wait()
+        for copy in {0: made[:n_near], 2: made[n_near:n_far], 1: made[n_far:]}.get(chunk, []):
             copy.wait()
         first = chunk * CHUNK
         odd = chunk == 4
         size = BLOCK if odd else CHUNK
-        set_of = 0 if odd else chunk
-        tag = row_tags[pl.ds(set_of * TAG + 4, 1), pl.ds(0, BLOCK)].astype(jnp.float32) - 1.0
+        tag = row_tags[pl.ds(chunk * TAG + 4, 1), pl.ds(0, BLOCK)].astype(jnp.float32) - 1.0
         bins, _ = bin_of(tag)
         if odd:
             bins = jnp.where(odd_here > 0, bins, -2.0)
@@ -184,13 +189,14 @@
         zero = jnp.zeros((8, size), jnp.float32)
         n_one = jnp.zeros((1, size), jnp.float32)
         n_zero = jnp.zeros((1, size), jnp.float32)
-        low = 0
+        low = EARLY * BLOCK if late and chunk in (0, 2) else 0
         while low < depth:
             high = depth if depth - low < 3 * BLOCK else low + 2 * BLOCK
-            while waited < n_cols and starts[waited] < high:
-                for copy in held[waited]:
-                    copy.wait()
-                waited += 1
+            for at in range(n_cols):
+                if low <= starts[at] < high and at not in waited:
+                    waited.add(at)
+                    for copy in loads[at]:
+                        copy.wait()
             products = lax.dot_general(
                 cols_at[pl.ds(low, high - low), :],
                 rows_at[pl.ds(first, size), :],
@@ -220,52 +226,59 @@
                 n_one += is_one
                 n_zero += is_zero
             low = high
-        targets = {0: [(out_near, 0)], 1: [(out_far, 0)], 2: [(out_theirs, 0)]}
-        targets |= {3: [(out_theirs, CHUNK)], 4: [(out_theirs, 2 * CHUNK), (out_odd, 0)]}
+        one = jnp.sum(one, axis=0, keepdims=True)
+        zero = jnp.sum(zero, axis=0, keepdims=True)
+        if late:
+            targets = {0: [(outs[0], 0)], 1: [(outs[1], 0)], 2: [(outs[2], 0)]}
+            targets |= {3: [(outs[2], CHUNK)], 4: [(outs[2], 2 * CHUNK), (outs[3], 0)]}
+            earlier = {0: before[0], 2: before[1]}.get(chunk)
+        else:
+            targets, earlier = {0: [(outs[0], 0)], 2: [(outs[1], 0)]}, None
+        values = [one, zero, n_one, n_zero]
+        if earlier is not None:
+            values = [earlier[i : i + 1, :] + value for i, value in enumerate(values)]
         for out, place_at in targets[chunk]:
-            lanes = pl.ds(place_at, size)
-            out[0:1, lanes] = jnp.sum(one, axis=0, keepdims=True)
-            out[1:2, lanes] = jnp.sum(zero, axis=0, keepdims=True)
-            out[2:3, lanes] = n_one
-            out[3:4, lanes] = n_zero
-
-
-def n_cols_args(col_cuts):
-    return 1 + max(arg for arg, _, _ in col_cuts)
-
-
-def pair_sums(place, col_args, row_args, col_cuts, tag_cuts):
-    args = col_args + row_args
-    total, depth = 4 * CHUNK + BLOCK, sum(size for _, _, size in col_cuts)
-    feats = args[0].shape[1]
+            for i, value in enumerate(values):
+                out[i : i + 1, pl.ds(place_at, size)] = value
+
+
+def pair_sums(place, col_args, row_args, col_cuts, before):
+    late = before is not None
+    total = 4 * CHUNK + BLOCK if late else 3 * CHUNK
+    used, depth = (5 if late else 2) * CHUNK, sum(size for _, _, size in col_cuts)
+    feats = col_args[0].shape[1]
     hbm = pl.BlockSpec(memory_space=pl.ANY)
     vmem = pl.BlockSpec(memory_space=pltpu.VMEM)
     dma = pltpu.SemaphoreType.DMA
-    widths = [CHUNK, CHUNK, 2 * CHUNK + BLOCK, BLOCK]
+    widths = [CHUNK, CHUNK, 2 * CHUNK + BLOCK, BLOCK] if late else [CHUNK, CHUNK]
+    names = NAMES if late else NAMES[:6]
+    before = list(before or [])
     return pl.pallas_call(
         functools.partial(
-            pair_kernel, tag_cuts=tuple(tag_cuts), col_cuts=tuple(col_cuts), n_args=len(args)
+            pair_kernel, col_cuts=tuple(col_cuts), n_cols_args=len(col_args), late=late
         ),
-        in_specs=[pl.BlockSpec(memory_space=pltpu.SMEM)] + [hbm] * len(args),
+        in_specs=[pl.BlockSpec(memory_space=pltpu.SMEM)]
+        + [vmem] * len(before)
+        + [hbm] * (len(col_args) + len(names)),
         out_specs=[vmem] * len(widths),
         out_shape=[jax.ShapeDtypeStruct((4, width), jnp.float32) for width in widths],
         scratch_shapes=[
             pltpu.VMEM((total, feats), jnp.bfloat16),
             pltpu.VMEM((depth, feats), jnp.bfloat16),
-            pltpu.VMEM((TAG * len(tag_cuts), feats), jnp.bfloat16),
+            pltpu.VMEM((TAG * 5, feats), jnp.bfloat16),
             pltpu.VMEM((TAG * len(col_cuts), feats), jnp.bfloat16),
             dma((17,)),
             dma((len(col_cuts),)),
-            dma((len(col_cuts) + len(tag_cuts),)),
+            dma((len(col_cuts) + 5,)),
         ],
         compiler_params=pltpu.CompilerParams(vmem_limit_bytes=58 * 2**20),
         cost_estimate=pl.CostEstimate(
-            flops=2 * total * depth * feats,
-            bytes_accessed=2 * (total + depth) * feats,
+            flops=6 * used * depth * feats,
+            bytes_accessed=6 * (used + depth) * feats,
             transcendentals=0,
         ),
-        name="pairs",
-    )(place, *args)
+        name="late" if late else "early",
+    )(place, *before, *col_args, *[row_args[name] for name in names])
 
 
 def shards(showers, geometry, pattern, bins, sources):
@@ -328,7 +341,8 @@
         for to in (1, 0)
     ]
     y2_t = permute(y2, swap_core)
-    z2, z3, y2, xb, xa, y2_t, *odd_at = fence(z2, z3, y2, xb, xa, y2_t, *odd_at)
+    xa_t = permute(xa, swap_core)
+    z2, z3, y2, xb, xa_t, y2_t, *odd_at = fence(z2, z3, y2, xb, xa_t, y2_t, *odd_at)
 
     z4 = permute(jnp.where(c == 0, z3[:tagged], z3[tagged:]), same_core)
     held = [chip, z1, z2, z3, z3, z3, z2, z1]
@@ -338,24 +352,26 @@
         keep=lambda y, x, z, c: x == 2 and (z < 4 if c == 0 else z == 0 or z > 4),
     )
     w2 = permute(y2, swap_x)
-    xa_t = permute(xa, swap_core)
     xb_t = permute(xb, swap_core)
+    col_args = [own, z1, z2, z3]
+    col_cuts = [(0, TAG, BLOCK)]
+    for arg in (1, 2, 3):
+        col_cuts += [(arg, TAG, BLOCK), (arg, tagged + TAG, BLOCK)]
+    row_args = dict(own=own, own_t=own_t, y1=y1, y1_t=y1_t, y2=y2, y2_t=y2_t)
+    place = jnp.stack([((x < 2) & (z == 0)).astype(jnp.int32), c.astype(jnp.int32)])
+    early = pair_sums(place, col_args, row_args, col_cuts, None)
+    w2, odd_at[0], odd_at[1], early, piece = fence(w2, odd_at[0], odd_at[1], early, piece)
     w2_t = permute(w2, swap_core)
     odd_rows = odd_at[0] + odd_at[1]
     odd_rows = odd_rows + permute(
         odd_rows, swap_core, keep=lambda *a: a[1] < 2 and at_start(*a)
     )
-
-    col_args = [own, z1, z2, z3, z4, piece]
-    col_cuts = [(0, TAG, BLOCK)]
-    for arg in (1, 2, 3):
-        col_cuts += [(arg, TAG, BLOCK), (arg, tagged + TAG, BLOCK)]
+    row_args |= dict(x1=x1, x1_t=x1_t, xa=xa, xb=xb, xa_t=xa_t, xb_t=xb_t, w2=w2, w2_t=w2_t)
+    row_args["odd"] = odd_rows
     col_cuts += [(4, TAG, BLOCK), (5, TAG, PIECE)]
-    row_args = [own, own_t, x1, x1_t, y1, y1_t, y2, y2_t]
-    row_args += [xa, xb, xa_t, xb_t, w2, w2_t, odd_rows]
-    tag_cuts = [(6, 0), (8, 0), (7, 0), (9, 0)]
-    place = jnp.stack([((x < 2) & (z == 0)).astype(jnp.int32), c.astype(jnp.int32)])
-    near, far, theirs, odd_stats = pair_sums(place, col_args, row_args, col_cuts, tag_cuts)
+    near, far, theirs, odd_stats = pair_sums(
+        place, col_args + [z4, piece], row_args, col_cuts, early
+    )
 
     theirs = permute(theirs, swap_core)
     kept = near + theirs[:, :CHUNK] + permute(far + theirs[:, CHUNK : 2 * CHUNK], swap_x)
@@ -370,8 +386,8 @@
     odd_total = odd_total.reshape(4, NY, PIECE)
     kept = kept.reshape(4, NY, BLOCK) + jnp.pad(odd_total, ((0, 0), (0, 0), (0, BLOCK - PIECE)))
     total = kept
-    for turn in (1, 2):
-        total = total + jnp.roll(permute(total, along_y(turn)), -turn, axis=1)
+    for turn in (2, 1, 3):
+        total = total + jnp.roll(permute(kept, along_y(turn)), -turn, axis=1)
     weight = 1.0 / (PIECE * 32.0**3)
     proof = (total[0] / total[2] - total[1] / total[3]) * weight
     proof = jnp.concatenate([proof, proof], axis=0)

time: 114 us -> 110 us (0.965)
  waiting for transfers between devices: 51.1 us -> 40.5 us
  Pallas kernels: 16.7 us -> 22.4 us
  starting transfers between devices: 30.7 us -> 33 us
    ppermute x30 -> x31, waiting for transfers between devices: 51.1 us -> 40.5 us  [permute(): return lax.ppermute(value, AXES, pairs)]
    pallas_call x1 -> x2, Pallas kernels: 11.2 us -> 17 us  [pair_sums(): pl.pallas_call(functools.partial(pair_kernel, col_cuts=tuple(col_cuts), n...]
    ppermute x30 -> x31, starting transfers between devices: 30.7 us -> 33 us  [permute(): return lax.ppermute(value, AXES, pairs)]
    unnamed x44 -> x32, local copies, waits for them, and re-layouts: 2.96 us -> 2.29 us
  transfers between devices with their start and end apart: 30 -> 31, of which waited for: 17 -> 17; matrix products, arithmetic and copies ran while one was open for 6% -> 5% of each run, Pallas kernels for 0% -> 6%
where the time goes in v8:
time: 110 us
  waiting for transfers between devices  40.5 us (37%)
  starting transfers between devices  33 us (30%)
  Pallas kernels  22.4 us (20%)
  other arithmetic  9.6 us (9%)
  local copies, waits for them, and re-layouts  3.86 us (4%)
    ppermute x31, waiting for transfers between devices, permute(): return lax.ppermute(value, AXES, pairs)  40.5 us
    ppermute x31, starting transfers between devices, permute(): return lax.ppermute(value, AXES, pairs)  33 us
    pallas_call x2, Pallas kernels, pair_sums(): pl.pallas_call(functools.partial(pair_kernel, col_cuts=tuple(col_cuts), n...  17 us
    pallas_call x1, Pallas kernels, raw_partial(): pl.pallas_call(raw_kernel, grid=(feats // width,), in_specs=[pl.BlockSpec...  5.48 us
    convert_element_type x1, other arithmetic, shards(): tag = tag.astype(jnp.bfloat16)  2.55 us
    unnamed x32, local copies, waits for them, and re-layouts  2.29 us
  transfers between devices with their start and end apart: 31, of which 17 were waited for; matrix products, arithmetic and copies ran while one was open for 5% of the time, Pallas kernels for 6%

profile of v8, /device:TPU:4, one launch (start us, length us, event | category | flops | bytes accessed | tf_op | source)
XLA Modules:
  0.0 109.9 jit_solution(4185744278802345184)
XLA Ops:
  0.0 5.5 %raw.1 = f32[512,1024]{1,0:T(8,128)} custom-call(s32[8,11]{1,0:T(8,128)} %bitcast.41, bf16[1584,512]{1,0:T(8,128)(2,1)} %bitcast.35, bf16[1584,1024]{1,0:T(8,128)(2,1)} %geometry.1), custom_call_target="tpu_custom_call" | custom-call | flops 1660944384 | bytes 8388608 | tf_op jit(solution)/shard_map/raw/pallas_call | solution.py:84
  5.5 1.7 %constant_dynamic-slice_fusion.1 = (f32[4,1,32,1024]{3,2,1,0:T(8,128)S(1)}, f16[4,1,32,1024]{3,2,0,1:T(8,128)(2,1)S(1)}, f16[4,1,32,1024]{3,2,0,1:T(8,128)(2,1)S(1)}, f16[4,1,32,1024]{3,2,0,1:T(8,128)(2,1)S(1)}) fusion(f32[4,4,32,1024]{3,2,1,0:T(8,128)} %bitcast.34, s32[]{:T(128)S(6)} %select_n.180, s32[]{:T(128)S(6)} %select_n.184, s32[]{:T(128)S(6)} %select_n.182, ...), kind=kLoop, calls=%fused_computation.43 | loop fusion | flops 393216 | bytes 3407888 | tf_op jit(solution)/shard_map/jit(dynamic_index_in_dim)/dynamic_slice | solution.py:303
  7.2 3.3 %collective-permute-start = (f16[128,1024]{1,0:T(8,128)(2,1)S(1)}, f16[128,1024]{1,0:T(8,128)(2,1)S(1)}, u32[]{:S(2)}, u32[]{:S(2)}) collective-permute-start(f16[128,1024]{1,0:T(8,128)(2,1)S(1)} %bitcast.38), channel_id=1, source_target_pairs={{0,128},{1,129},{2,130},{3,131},{4,132},{5,133},{6,134},{7,135},{8... | collective-permute-start | bytes 786440 | tf_op jit(solution)/shard_map/ppermute | solution.py:33
  11.2 2.6 %collective-permute-start.2 = (f16[128,1024]{1,0:T(8,128)(2,1)S(1)}, f16[128,1024]{1,0:T(8,128)(2,1)S(1)}, u32[]{:S(2)}, u32[]{:S(2)}) collective-permute-start(f16[128,1024]{1,0:T(8,128)(2,1)S(1)} %bitcast.36), channel_id=1, source_target_pairs={{0,192},{1,193},{2,194},{3,195},{4,196},{5,197},{6,198},{7,199},{8... | collective-permute-start | bytes 786440 | tf_op jit(solution)/shard_map/ppermute | solution.py:33
  14.5 2.5 %select_convert_fusion = bf16[16,1024]{1,0:T(8,128)(2,1)S(1)} fusion(bf16[]{:T(256)} %bitcast.5, bf16[]{:T(256)} %bitcast.4, bf16[]{:T(256)} %bitcast.3, bf16[]{:T(256)} %bitcast.2, s32[1024]{0:T(1024)S(1)} %get-tuple-element.77, s32[1024]{0:T(1024)S(1)} %get-tuple-element.78, pred[16]{0:T(512)(128)(4,1)S(1)} %iota_compare_fusion, pred[1024]{0:T(1024)(128)(4,1)S(1)} %fusion.13), kind=kLoop, calls=%fused_computation.16 | loop fusion | flops 163840 | bytes 42008 | tf_op jit(solution)/shard_map/convert_element_type | solution.py:298
  18.1 4.4 %collective-permute-done.1 = f16[128,1024]{1,0:T(8,128)(2,1)S(1)} collective-permute-done((f16[128,1024]{1,0:T(8,128)(2,1)S(1)}, f16[128,1024]{1,0:T(8,128)(2,1)S(1)}, u32[]{:S(2)}, u32[]{:S(2)}) %collective-permute-start.1) | collective-permute-done | bytes 262176 | tf_op jit(solution)/shard_map/ppermute | solution.py:33
  23.4 1.6 %collective-permute-done.3.refs_6_.refs_10_ = bf16[144,1024]{1,0:T(8,128)(2,1)S(1)} collective-permute-done((bf16[144,1024]{1,0:T(8,128)(2,1)S(1)}, bf16[144,1024]{1,0:T(8,128)(2,1)S(1)}, u32[]{:S(2)}, u32[]{:S(2)}) %collective-permute-start.3) | collective-permute-done | bytes 294944 | tf_op jit(solution)/shard_map/ppermute | solution.py:33
  25.2 2.0 %collective-permute-start.4 = (bf16[288,1024]{1,0:T(8,128)(2,1)S(1)}, bf16[288,1024]{1,0:T(8,128)(2,1)S(1)}, u32[]{:S(2)}, u32[]{:S(2)}) collective-permute-start(bf16[288,1024]{1,0:T(8,128)(2,1)S(1)} %maximum_select_fusion), channel_id=1, source_target_pairs={{0,2},{1,15},{2,4},{3,1},{4,6},{5,3},{6,8},{7,5},{8,10},{9,7},{10,... | collective-permute-start | bytes 1769480 | tf_op jit(solution)/shard_map/ppermute | solution.py:33
  27.2 1.4 %collective-permute-start.5 = (bf16[288,1024]{1,0:T(8,128)(2,1)S(1)}, bf16[288,1024]{1,0:T(8,128)(2,1)S(1)}, u32[]{:S(2)}, u32[]{:S(2)}) collective-permute-start(bf16[288,1024]{1,0:T(8,128)(2,1)S(1)} %maximum_select_fusion), channel_id=1, source_target_pairs={{0,64},{1,193},{2,66},{3,195},{4,68},{5,197},{6,70},{7,199},{8,72}... | collective-permute-start | bytes 1769480 | tf_op jit(solution)/shard_map/ppermute | solution.py:33
  28.5 1.2 %collective-permute-start.6 = (bf16[144,1024]{1,0:T(8,128)(2,1)S(1)}, bf16[144,1024]{1,0:T(8,128)(2,1)S(1)}, u32[]{:S(2)}, u32[]{:S(2)}) collective-permute-start(bf16[144,1024]{1,0:T(8,128)(2,1)S(1)} %pad_maximum_fusion.refs_1_.refs_5_.refs_3_.refs_9_), channel_id=1, source_target_pairs={{0,16},{1,17},{2,18},{3,19},{4,20},{5,21},{6,22},{7,23},{8,24},{9,... | collective-permute-start | bytes 884744 | tf_op jit(solution)/shard_map/ppermute | solution.py:33
  29.7 5.5 %collective-permute-done.6.refs_15_ = bf16[144,1024]{1,0:T(8,128)(2,1)S(1)} collective-permute-done((bf16[144,1024]{1,0:T(8,128)(2,1)S(1)}, bf16[144,1024]{1,0:T(8,128)(2,1)S(1)}, u32[]{:S(2)}, u32[]{:S(2)}) %collective-permute-start.6) | collective-permute-done | bytes 294944 | tf_op jit(solution)/shard_map/ppermute | solution.py:33
  35.2 3.7 %collective-permute-done.4.refs_2_.refs_4_ = bf16[288,1024]{1,0:T(8,128)(2,1)S(1)} collective-permute-done((bf16[288,1024]{1,0:T(8,128)(2,1)S(1)}, bf16[288,1024]{1,0:T(8,128)(2,1)S(1)}, u32[]{:S(2)}, u32[]{:S(2)}) %collective-permute-start.4) | collective-permute-done | bytes 589856 | tf_op jit(solution)/shard_map/ppermute | solution.py:33
  40.2 2.3 %collective-permute-start.11 = (bf16[144,1024]{1,0:T(8,128)(2,1)S(1)}, bf16[144,1024]{1,0:T(8,128)(2,1)S(1)}, u32[]{:S(2)}, u32[]{:S(2)}) collective-permute-start(bf16[144,1024]{1,0:T(8,128)(2,1)S(1)} %collective-permute-done.6.refs_15_), channel_id=1, source_target_pairs={{0,1},{1,0},{2,3},{3,2},{4,5},{5,4},{6,7},{7,6},{8,9},{9,8},{10,11... | collective-permute-start | bytes 884744 | tf_op jit(solution)/shard_map/ppermute | solution.py:33
  43.1 1.2 %collective-permute-start.9 = (bf16[128,1024]{1,0:T(8,128)(2,1)S(1)}, bf16[128,1024]{1,0:T(8,128)(2,1)}, u32[]{:S(2)}, u32[]{:S(2)}) collective-permute-start(bf16[128,1024]{1,0:T(8,128)(2,1)S(1)} %get-tuple-element.69), channel_id=1, source_target_pairs={{0,16},{1,17},{2,18},{3,19},{4,20},{5,21},{6,22},{7,23},{8,24},{9,... | collective-permute-start | bytes 786440 | tf_op jit(solution)/shard_map/ppermute | solution.py:33
  44.3 5.9 %collective-permute-done.8.refs_9_.refs_13_ = bf16[128,1024]{1,0:T(8,128)(2,1)S(1)} collective-permute-done((bf16[128,1024]{1,0:T(8,128)(2,1)S(1)}, bf16[128,1024]{1,0:T(8,128)(2,1)S(1)}, u32[]{:S(2)}, u32[]{:S(2)}) %collective-permute-start.8) | collective-permute-done | bytes 262176 | tf_op jit(solution)/shard_map/ppermute | solution.py:33
  50.2 2.1 %collective-permute-done.9.refs_17_ = bf16[128,1024]{1,0:T(8,128)(2,1)} collective-permute-done((bf16[128,1024]{1,0:T(8,128)(2,1)S(1)}, bf16[128,1024]{1,0:T(8,128)(2,1)}, u32[]{:S(2)}, u32[]{:S(2)}) %collective-permute-start.9) | collective-permute-done | bytes 262176 | tf_op jit(solution)/shard_map/ppermute | solution.py:33
  53.3 2.5 %collective-permute-start.16 = (bf16[128,1024]{1,0:T(8,128)(2,1)S(1)}, bf16[128,1024]{1,0:T(8,128)(2,1)S(1)}, u32[]{:S(2)}, u32[]{:S(2)}) collective-permute-start(bf16[128,1024]{1,0:T(8,128)(2,1)S(1)} %pad_maximum_fusion.1), channel_id=1, source_target_pairs={{32,16},{96,80},{160,144},{224,208}} | collective-permute-start | bytes 786440 | tf_op jit(solution)/shard_map/ppermute | solution.py:33
  55.8 1.3 %collective-permute-start.17 = (bf16[128,1024]{1,0:T(8,128)(2,1)S(1)}, bf16[128,1024]{1,0:T(8,128)(2,1)S(1)}, u32[]{:S(2)}, u32[]{:S(2)}) collective-permute-start(bf16[128,1024]{1,0:T(8,128)(2,1)S(1)} %pad_maximum_fusion.1), channel_id=1, source_target_pairs={{32,0},{96,64},{160,128},{224,192}} | collective-permute-start | bytes 786440 | tf_op jit(solution)/shard_map/ppermute | solution.py:33
  57.3 2.3 %collective-permute-done.16 = bf16[128,1024]{1,0:T(8,128)(2,1)S(1)} collective-permute-done((bf16[128,1024]{1,0:T(8,128)(2,1)S(1)}, bf16[128,1024]{1,0:T(8,128)(2,1)S(1)}, u32[]{:S(2)}, u32[]{:S(2)}) %collective-permute-start.16) | collective-permute-done | bytes 262176 | tf_op jit(solution)/shard_map/ppermute | solution.py:33
  60.2 2.8 %collective-permute-done.17 = bf16[128,1024]{1,0:T(8,128)(2,1)S(1)} collective-permute-done((bf16[128,1024]{1,0:T(8,128)(2,1)S(1)}, bf16[128,1024]{1,0:T(8,128)(2,1)S(1)}, u32[]{:S(2)}, u32[]{:S(2)}) %collective-permute-start.17) | collective-permute-done | bytes 262176 | tf_op jit(solution)/shard_map/ppermute | solution.py:33
  63.0 2.8 %collective-permute-done.13.refs_18_ = bf16[128,1024]{1,0:T(8,128)(2,1)} collective-permute-done((bf16[128,1024]{1,0:T(8,128)(2,1)S(1)}, bf16[128,1024]{1,0:T(8,128)(2,1)}, u32[]{:S(2)}, u32[]{:S(2)}) %collective-permute-start.13) | collective-permute-done | bytes 262176 | tf_op jit(solution)/shard_map/ppermute | solution.py:33
  66.9 1.3 %collective-permute-start.19 = (bf16[48,1024]{1,0:T(8,128)(2,1)S(1)}, bf16[48,1024]{1,0:T(8,128)(2,1)S(1)}, u32[]{:S(2)}, u32[]{:S(2)}) collective-permute-start(bf16[48,1024]{1,0:T(8,128)(2,1)S(1)} %fusion.3), channel_id=1, source_target_pairs={{32,18},{33,17},{34,20},{36,22},{38,24},{43,27},{45,29},{47,31},{9... | collective-permute-start | bytes 294920 | tf_op jit(solution)/shard_map/ppermute | solution.py:33
  68.2 2.0 %collective-permute-start.18 = (bf16[128,1024]{1,0:T(8,128)(2,1)S(1)}, bf16[128,1024]{1,0:T(8,128)(2,1)S(1)}, u32[]{:S(2)}, u32[]{:S(2)}) collective-permute-start(bf16[128,1024]{1,0:T(8,128)(2,1)S(1)} %collective-permute-done.8.refs_9_.refs_13_), channel_id=1, source_target_pairs={{0,16},{1,17},{2,18},{3,19},{4,20},{5,21},{6,22},{7,23},{8,24},{9,... | collective-permute-start | bytes 786440 | tf_op jit(solution)/shard_map/ppermute | solution.py:33
  70.3 7.0 %early.1 = (f32[4,512]{1,0:T(4,128)}, f32[4,512]{1,0:T(4,128)}) custom-call(s32[2]{0:T(128)} %pad_add_fusion.1.refs_0_, bf16[144,1024]{1,0:T(8,128)(2,1)} %copy-done.2, bf16[288,1024]{1,0:T(8,128)(2,1)} %copy-done.5, bf16[288,1024]{1,0:T(8,128)(2,1)} %collective-permute-done.7.refs_3_.refs_5_, bf16[288,1024]{1,0:T(8,128)(2,1)} %copy-done.1, ...), custom_call_target="tpu_custom_call" | custom-call | flops 5637144576 | bytes 11796480 | tf_op jit(solution)/shard_map/early/pallas_call | solution.py:256
  81.5 9.9 %late.1 = (f32[4,512]{1,0:T(4,128)}, f32[4,512]{1,0:T(4,128)}, f32[4,1152]{1,0:T(4,128)}, f32[4,128]{1,0:T(4,128)}) custom-call(s32[2]{0:T(128)} %pad_add_fusion.1.refs_0_, f32[4,512]{1,0:T(4,128)} %get-tuple-element.52.refs_1_, f32[4,512]{1,0:T(4,128)} %get-tuple-element.53.refs_2_, bf16[144,1024]{1,0:T(8,128)(2,1)} %copy-done.2, ...), custom_call_target="tpu_custom_call" | custom-call | flops 16609443840 | bytes 22216704 | tf_op jit(solution)/shard_map/late/pallas_call | solution.py:256
  91.7 1.3 %collective-permute-done.24 = f32[4,1152]{1,0:T(4,128)S(1)} collective-permute-done((f32[4,1152]{1,0:T(4,128)}, f32[4,1152]{1,0:T(4,128)S(1)}, u32[]{:S(2)}, u32[]{:S(2)}) %collective-permute-start.24) | collective-permute-done | bytes 18464 | tf_op jit(solution)/shard_map/ppermute | solution.py:33
  94.5 1.3 %collective-permute-start.26 = (f32[4,128]{1,0:T(4,128)S(1)}, f32[4,128]{1,0:T(4,128)S(1)}, u32[]{:S(2)}, u32[]{:S(2)}) collective-permute-start(f32[4,128]{1,0:T(4,128)S(1)} %slice_add_fusion.2), channel_id=1, source_target_pairs={{0,32},{64,96},{128,160},{192,224}} | collective-permute-start | bytes 6152 | tf_op jit(solution)/shard_map/ppermute | solution.py:33
  95.8 1.3 %collective-permute-start.27 = (f32[4,128]{1,0:T(4,128)S(1)}, f32[4,128]{1,0:T(4,128)S(1)}, u32[]{:S(2)}, u32[]{:S(2)}) collective-permute-start(f32[4,128]{1,0:T(4,128)S(1)} %slice_add_fusion.2), channel_id=1, source_target_pairs={{16,32},{80,96},{144,160},{208,224}} | collective-permute-start | bytes 6152 | tf_op jit(solution)/shard_map/ppermute | solution.py:33
  97.1 4.4 %collective-permute-done.26 = f32[4,128]{1,0:T(4,128)S(1)} collective-permute-done((f32[4,128]{1,0:T(4,128)S(1)}, f32[4,128]{1,0:T(4,128)S(1)}, u32[]{:S(2)}, u32[]{:S(2)}) %collective-permute-start.26) | collective-permute-done | bytes 2080 | tf_op jit(solution)/shard_map/ppermute | solution.py:33
  102.3 1.8 %collective-permute-start.28 = (f32[4,4,128]{2,1,0:T(4,128)S(1)}, f32[4,4,128]{2,1,0:T(4,128)S(1)}, u32[]{:S(2)}, u32[]{:S(2)}) collective-permute-start(f32[4,4,128]{2,1,0:T(4,128)S(1)} %pad_add_fusion), channel_id=1, source_target_pairs={{0,128},{1,129},{2,130},{3,131},{4,132},{5,133},{6,134},{7,135},{8... | collective-permute-start | bytes 24584 | tf_op jit(solution)/shard_map/ppermute | solution.py:33
  104.6 2.8 %collective-permute-start.30 = (f32[4,4,128]{2,1,0:T(4,128)S(1)}, f32[4,4,128]{2,1,0:T(4,128)S(1)}, u32[]{:S(2)}, u32[]{:S(2)}) collective-permute-start(f32[4,4,128]{2,1,0:T(4,128)S(1)} %pad_add_fusion), channel_id=1, source_target_pairs={{0,192},{1,193},{2,194},{3,195},{4,196},{5,197},{6,198},{7,199},{8... | collective-permute-start | bytes 24584 | tf_op jit(solution)/shard_map/ppermute | solution.py:33
  107.6 1.4 %collective-permute-done.29 = f32[4,4,128]{2,1,0:T(4,128)S(1)} collective-permute-done((f32[4,4,128]{2,1,0:T(4,128)S(1)}, f32[4,4,128]{2,1,0:T(4,128)S(1)}, u32[]{:S(2)}, u32[]{:S(2)}) %collective-permute-start.29) | collective-permute-done | bytes 8224 | tf_op jit(solution)/shard_map/ppermute | solution.py:33
  (107 shorter events, 16.3 us)
Async XLA Ops:
  7.2 10.8 %collective-permute-start = (f16[128,1024]{1,0:T(8,128)(2,1)S(1)}, f16[128,1024]{1,0:T(8,128)(2,1)S(1)}, u32[]{:S(2)}, u32[]{:S(2)}) collective-permute-start(f16[128,1024]{1,0:T(8,128)(2,1)S(1)} %bitcast.38), channel_id=1, source_target_pairs={{0,128},{1,129},{2,130},{3,131},{4,132},{5,133},{6,134},{7,135},{8... | collective-permute-start | bytes 786440 | tf_op jit(solution)/shard_map/ppermute | solution.py:33
  10.5 12.0 %collective-permute-start.1 = (f16[128,1024]{1,0:T(8,128)(2,1)S(1)}, f16[128,1024]{1,0:T(8,128)(2,1)S(1)}, u32[]{:S(2)}, u32[]{:S(2)}) collective-permute-start(f16[128,1024]{1,0:T(8,128)(2,1)S(1)} %bitcast.37), channel_id=1, source_target_pairs={{0,64},{1,65},{2,66},{3,67},{4,68},{5,69},{6,70},{7,71},{8,72},{9,... | collective-permute-start | bytes 786440 | tf_op jit(solution)/shard_map/ppermute | solution.py:33
  11.2 11.7 %collective-permute-start.2 = (f16[128,1024]{1,0:T(8,128)(2,1)S(1)}, f16[128,1024]{1,0:T(8,128)(2,1)S(1)}, u32[]{:S(2)}, u32[]{:S(2)}) collective-permute-start(f16[128,1024]{1,0:T(8,128)(2,1)S(1)} %bitcast.36), channel_id=1, source_target_pairs={{0,192},{1,193},{2,194},{3,195},{4,196},{5,197},{6,198},{7,199},{8... | collective-permute-start | bytes 786440 | tf_op jit(solution)/shard_map/ppermute | solution.py:33
  23.3 1.7 %collective-permute-start.3 = (bf16[144,1024]{1,0:T(8,128)(2,1)S(1)}, bf16[144,1024]{1,0:T(8,128)(2,1)S(1)}, u32[]{:S(2)}, u32[]{:S(2)}) collective-permute-start(bf16[144,1024]{1,0:T(8,128)(2,1)S(1)} %pad_maximum_fusion.refs_1_.refs_5_.refs_3_.refs_9_), channel_id=1, source_target_pairs={{0,1},{1,0},{2,3},{3,2},{4,5},{5,4},{6,7},{7,6},{8,9},{9,8},{10,11... | collective-permute-start | bytes 884744 | tf_op jit(solution)/shard_map/ppermute | solution.py:33
  25.2 13.8 %collective-permute-start.4 = (bf16[288,1024]{1,0:T(8,128)(2,1)S(1)}, bf16[288,1024]{1,0:T(8,128)(2,1)S(1)}, u32[]{:S(2)}, u32[]{:S(2)}) collective-permute-start(bf16[288,1024]{1,0:T(8,128)(2,1)S(1)} %maximum_select_fusion), channel_id=1, source_target_pairs={{0,2},{1,15},{2,4},{3,1},{4,6},{5,3},{6,8},{7,5},{8,10},{9,7},{10,... | collective-permute-start | bytes 1769480 | tf_op jit(solution)/shard_map/ppermute | solution.py:33
  27.2 11.8 %collective-permute-start.5 = (bf16[288,1024]{1,0:T(8,128)(2,1)S(1)}, bf16[288,1024]{1,0:T(8,128)(2,1)S(1)}, u32[]{:S(2)}, u32[]{:S(2)}) collective-permute-start(bf16[288,1024]{1,0:T(8,128)(2,1)S(1)} %maximum_select_fusion), channel_id=1, source_target_pairs={{0,64},{1,193},{2,66},{3,195},{4,68},{5,197},{6,70},{7,199},{8,72}... | collective-permute-start | bytes 1769480 | tf_op jit(solution)/shard_map/ppermute | solution.py:33
  28.5 6.7 %collective-permute-start.6 = (bf16[144,1024]{1,0:T(8,128)(2,1)S(1)}, bf16[144,1024]{1,0:T(8,128)(2,1)S(1)}, u32[]{:S(2)}, u32[]{:S(2)}) collective-permute-start(bf16[144,1024]{1,0:T(8,128)(2,1)S(1)} %pad_maximum_fusion.refs_1_.refs_5_.refs_3_.refs_9_), channel_id=1, source_target_pairs={{0,16},{1,17},{2,18},{3,19},{4,20},{5,21},{6,22},{7,23},{8,24},{9,... | collective-permute-start | bytes 884744 | tf_op jit(solution)/shard_map/ppermute | solution.py:33
  35.2 42.1 %copy-start.7 = (bf16[144,1024]{1,0:T(8,128)(2,1)}, bf16[144,1024]{1,0:T(8,128)(2,1)S(1)}, u32[]{:S(2)}) copy-start(bf16[144,1024]{1,0:T(8,128)(2,1)S(1)} %collective-permute-done.6.refs_15_) | copy-start | bytes 884740
  39.0 13.4 %collective-permute-start.10 = (bf16[288,1024]{1,0:T(8,128)(2,1)S(1)}, bf16[288,1024]{1,0:T(8,128)(2,1)S(1)}, u32[]{:S(2)}, u32[]{:S(2)}) collective-permute-start(bf16[288,1024]{1,0:T(8,128)(2,1)S(1)} %collective-permute-done.5.refs_7_.refs_11_), channel_id=1, source_target_pairs={{0,1},{1,0},{2,3},{3,2},{4,5},{5,4},{6,7},{7,6},{8,9},{9,8},{10,11... | collective-permute-start | bytes 1769480 | tf_op jit(solution)/shard_map/ppermute | solution.py:33
  40.1 12.2 %collective-permute-start.7 = (bf16[288,1024]{1,0:T(8,128)(2,1)S(1)}, bf16[288,1024]{1,0:T(8,128)(2,1)}, u32[]{:S(2)}, u32[]{:S(2)}) collective-permute-start(bf16[288,1024]{1,0:T(8,128)(2,1)S(1)} %collective-permute-done.4.refs_2_.refs_4_), channel_id=1, source_target_pairs={{0,2},{1,15},{2,4},{3,1},{4,6},{5,3},{6,8},{7,5},{8,10},{9,7},{10,... | collective-permute-start | bytes 1769480 | tf_op jit(solution)/shard_map/ppermute | solution.py:33
  40.2 12.1 %collective-permute-start.11 = (bf16[144,1024]{1,0:T(8,128)(2,1)S(1)}, bf16[144,1024]{1,0:T(8,128)(2,1)S(1)}, u32[]{:S(2)}, u32[]{:S(2)}) collective-permute-start(bf16[144,1024]{1,0:T(8,128)(2,1)S(1)} %collective-permute-done.6.refs_15_), channel_id=1, source_target_pairs={{0,1},{1,0},{2,3},{3,2},{4,5},{5,4},{6,7},{7,6},{8,9},{9,8},{10,11... | collective-permute-start | bytes 884744 | tf_op jit(solution)/shard_map/ppermute | solution.py:33
  42.6 7.7 %collective-permute-start.8 = (bf16[128,1024]{1,0:T(8,128)(2,1)S(1)}, bf16[128,1024]{1,0:T(8,128)(2,1)S(1)}, u32[]{:S(2)}, u32[]{:S(2)}) collective-permute-start(bf16[128,1024]{1,0:T(8,128)(2,1)S(1)} %get-tuple-element.70), channel_id=1, source_target_pairs={{0,64},{1,193},{2,66},{3,195},{4,68},{5,197},{6,70},{7,199},{8,72}... | collective-permute-start | bytes 786440 | tf_op jit(solution)/shard_map/ppermute | solution.py:33
  43.1 9.2 %collective-permute-start.9 = (bf16[128,1024]{1,0:T(8,128)(2,1)S(1)}, bf16[128,1024]{1,0:T(8,128)(2,1)}, u32[]{:S(2)}, u32[]{:S(2)}) collective-permute-start(bf16[128,1024]{1,0:T(8,128)(2,1)S(1)} %get-tuple-element.69), channel_id=1, source_target_pairs={{0,16},{1,17},{2,18},{3,19},{4,20},{5,21},{6,22},{7,23},{8,24},{9,... | collective-permute-start | bytes 786440 | tf_op jit(solution)/shard_map/ppermute | solution.py:33
  53.3 12.6 %collective-permute-start.12 = (bf16[288,1024]{1,0:T(8,128)(2,1)}, bf16[288,1024]{1,0:T(8,128)(2,1)S(1)}, u32[]{:S(2)}, u32[]{:S(2)}) collective-permute-start(bf16[288,1024]{1,0:T(8,128)(2,1)} %collective-permute-done.7.refs_3_.refs_5_), channel_id=1, source_target_pairs={{0,2},{1,15},{2,4},{3,1},{4,6},{5,3},{6,8},{7,5},{8,10},{9,7},{10,... | collective-permute-start | bytes 1769480 | tf_op jit(solution)/shard_map/ppermute | solution.py:33
  53.3 6.3 %collective-permute-start.16 = (bf16[128,1024]{1,0:T(8,128)(2,1)S(1)}, bf16[128,1024]{1,0:T(8,128)(2,1)S(1)}, u32[]{:S(2)}, u32[]{:S(2)}) collective-permute-start(bf16[128,1024]{1,0:T(8,128)(2,1)S(1)} %pad_maximum_fusion.1), channel_id=1, source_target_pairs={{32,16},{96,80},{160,144},{224,208}} | collective-permute-start | bytes 786440 | tf_op jit(solution)/shard_map/ppermute | solution.py:33
  55.8 7.3 %collective-permute-start.17 = (bf16[128,1024]{1,0:T(8,128)(2,1)S(1)}, bf16[128,1024]{1,0:T(8,128)(2,1)S(1)}, u32[]{:S(2)}, u32[]{:S(2)}) collective-permute-start(bf16[128,1024]{1,0:T(8,128)(2,1)S(1)} %pad_maximum_fusion.1), channel_id=1, source_target_pairs={{32,0},{96,64},{160,128},{224,192}} | collective-permute-start | bytes 786440 | tf_op jit(solution)/shard_map/ppermute | solution.py:33
  57.1 8.7 %collective-permute-start.13 = (bf16[128,1024]{1,0:T(8,128)(2,1)S(1)}, bf16[128,1024]{1,0:T(8,128)(2,1)}, u32[]{:S(2)}, u32[]{:S(2)}) collective-permute-start(bf16[128,1024]{1,0:T(8,128)(2,1)S(1)} %slice.107), channel_id=1, source_target_pairs={{0,16},{1,17},{2,18},{3,19},{4,20},{5,21},{6,22},{7,23},{8,24},{9,... | collective-permute-start | bytes 786440 | tf_op jit(solution)/shard_map/ppermute | solution.py:33
  57.2 8.6 %collective-permute-start.14 = (bf16[128,1024]{1,0:T(8,128)(2,1)}, bf16[128,1024]{1,0:T(8,128)(2,1)}, u32[]{:S(2)}, u32[]{:S(2)}) collective-permute-start(bf16[128,1024]{1,0:T(8,128)(2,1)} %collective-permute-done.9.refs_17_), channel_id=1, source_target_pairs={{0,1},{1,0},{2,3},{3,2},{4,5},{5,4},{6,7},{7,6},{8,9},{9,8},{10,11... | collective-permute-start | bytes 786440 | tf_op jit(solution)/shard_map/ppermute | solution.py:33
  59.6 6.2 %collective-permute-start.15 = (bf16[128,1024]{1,0:T(8,128)(2,1)S(1)}, bf16[128,1024]{1,0:T(8,128)(2,1)}, u32[]{:S(2)}, u32[]{:S(2)}) collective-permute-start(bf16[128,1024]{1,0:T(8,128)(2,1)S(1)} %collective-permute-done.8.refs_9_.refs_13_), channel_id=1, source_target_pairs={{0,1},{1,0},{2,3},{3,2},{4,5},{5,4},{6,7},{7,6},{8,9},{9,8},{10,11... | collective-permute-start | bytes 786440 | tf_op jit(solution)/shard_map/ppermute | solution.py:33
  66.9 10.4 %collective-permute-start.19 = (bf16[48,1024]{1,0:T(8,128)(2,1)S(1)}, bf16[48,1024]{1,0:T(8,128)(2,1)S(1)}, u32[]{:S(2)}, u32[]{:S(2)}) collective-permute-start(bf16[48,1024]{1,0:T(8,128)(2,1)S(1)} %fusion.3), channel_id=1, source_target_pairs={{32,18},{33,17},{34,20},{36,22},{38,24},{43,27},{45,29},{47,31},{9... | collective-permute-start | bytes 294920 | tf_op jit(solution)/shard_map/ppermute | solution.py:33
  68.2 9.1 %collective-permute-start.18 = (bf16[128,1024]{1,0:T(8,128)(2,1)S(1)}, bf16[128,1024]{1,0:T(8,128)(2,1)S(1)}, u32[]{:S(2)}, u32[]{:S(2)}) collective-permute-start(bf16[128,1024]{1,0:T(8,128)(2,1)S(1)} %collective-permute-done.8.refs_9_.refs_13_), channel_id=1, source_target_pairs={{0,16},{1,17},{2,18},{3,19},{4,20},{5,21},{6,22},{7,23},{8,24},{9,... | collective-permute-start | bytes 786440 | tf_op jit(solution)/shard_map/ppermute | solution.py:33
  70.3 9.7 %collective-permute-start.20 = (bf16[144,1024]{1,0:T(8,128)(2,1)S(1)}, bf16[144,1024]{1,0:T(8,128)(2,1)S(1)}, u32[]{:S(2)}, u32[]{:S(2)}) collective-permute-start(bf16[144,1024]{1,0:T(8,128)(2,1)S(1)} %slice_select_fusion), channel_id=1, source_target_pairs={{0,2},{1,15},{2,4},{3,1},{4,6},{5,3},{6,8},{7,5},{8,10},{9,7},{10,... | collective-permute-start | bytes 884744 | tf_op jit(solution)/shard_map/ppermute | solution.py:33
  77.5 1.3 %collective-permute-start.23 = (bf16[128,1024]{1,0:T(8,128)(2,1)S(1)}, bf16[128,1024]{1,0:T(8,128)(2,1)S(1)}, u32[]{:S(2)}, u32[]{:S(2)}) collective-permute-start(bf16[128,1024]{1,0:T(8,128)(2,1)S(1)} %add.132), channel_id=1, source_target_pairs={{0,1},{16,17},{64,65},{80,81},{128,129},{144,145},{192,193},{208,2... | collective-permute-start | bytes 786440 | tf_op jit(solution)/shard_map/ppermute | solution.py:33
  78.1 1.8 %collective-permute-start.21 = (bf16[128,1024]{1,0:T(8,128)(2,1)}, bf16[128,1024]{1,0:T(8,128)(2,1)S(1)}, u32[]{:S(2)}, u32[]{:S(2)}) collective-permute-start(bf16[128,1024]{1,0:T(8,128)(2,1)} %collective-permute-done.13.refs_18_), channel_id=1, source_target_pairs={{0,1},{1,0},{2,3},{3,2},{4,5},{5,4},{6,7},{7,6},{8,9},{9,8},{10,11... | collective-permute-start | bytes 786440 | tf_op jit(solution)/shard_map/ppermute | solution.py:33
  78.2 1.9 %collective-permute-start.22 = (bf16[128,1024]{1,0:T(8,128)(2,1)S(1)}, bf16[128,1024]{1,0:T(8,128)(2,1)S(1)}, u32[]{:S(2)}, u32[]{:S(2)}) collective-permute-start(bf16[128,1024]{1,0:T(8,128)(2,1)S(1)} %collective-permute-done.18.refs_21_), channel_id=1, source_target_pairs={{0,1},{1,0},{2,3},{3,2},{4,5},{5,4},{6,7},{7,6},{8,9},{9,8},{10,11... | collective-permute-start | bytes 786440 | tf_op jit(solution)/shard_map/ppermute | solution.py:33
  91.4 1.5 %collective-permute-start.24 = (f32[4,1152]{1,0:T(4,128)}, f32[4,1152]{1,0:T(4,128)S(1)}, u32[]{:S(2)}, u32[]{:S(2)}) collective-permute-start(f32[4,1152]{1,0:T(4,128)} %get-tuple-element.62), channel_id=1, source_target_pairs={{0,1},{1,0},{2,3},{3,2},{4,5},{5,4},{6,7},{7,6},{8,9},{9,8},{10,11... | collective-permute-start | bytes 55304 | tf_op jit(solution)/shard_map/ppermute | solution.py:33
  93.6 8.0 %collective-permute-start.25 = (f32[4,512]{1,0:T(4,128)S(1)}, f32[4,512]{1,0:T(4,128)S(1)}, u32[]{:S(2)}, u32[]{:S(2)}) collective-permute-start(f32[4,512]{1,0:T(4,128)S(1)} %slice_add_fusion), channel_id=1, source_target_pairs={{0,16},{1,17},{2,18},{3,19},{4,20},{5,21},{6,22},{7,23},{8,24},{9,... | collective-permute-start | bytes 24584 | tf_op jit(solution)/shard_map/ppermute | solution.py:33
  94.5 7.0 %collective-permute-start.26 = (f32[4,128]{1,0:T(4,128)S(1)}, f32[4,128]{1,0:T(4,128)S(1)}, u32[]{:S(2)}, u32[]{:S(2)}) collective-permute-start(f32[4,128]{1,0:T(4,128)S(1)} %slice_add_fusion.2), channel_id=1, source_target_pairs={{0,32},{64,96},{128,160},{192,224}} | collective-permute-start | bytes 6152 | tf_op jit(solution)/shard_map/ppermute | solution.py:33
  95.8 5.7 %collective-permute-start.27 = (f32[4,128]{1,0:T(4,128)S(1)}, f32[4,128]{1,0:T(4,128)S(1)}, u32[]{:S(2)}, u32[]{:S(2)}) collective-permute-start(f32[4,128]{1,0:T(4,128)S(1)} %slice_add_fusion.2), channel_id=1, source_target_pairs={{16,32},{80,96},{144,160},{208,224}} | collective-permute-start | bytes 6152 | tf_op jit(solution)/shard_map/ppermute | solution.py:33
  102.3 5.2 %collective-permute-start.28 = (f32[4,4,128]{2,1,0:T(4,128)S(1)}, f32[4,4,128]{2,1,0:T(4,128)S(1)}, u32[]{:S(2)}, u32[]{:S(2)}) collective-permute-start(f32[4,4,128]{2,1,0:T(4,128)S(1)} %pad_add_fusion), channel_id=1, source_target_pairs={{0,128},{1,129},{2,130},{3,131},{4,132},{5,133},{6,134},{7,135},{8... | collective-permute-start | bytes 24584 | tf_op jit(solution)/shard_map/ppermute | solution.py:33
  104.1 4.9 %collective-permute-start.29 = (f32[4,4,128]{2,1,0:T(4,128)S(1)}, f32[4,4,128]{2,1,0:T(4,128)S(1)}, u32[]{:S(2)}, u32[]{:S(2)}) collective-permute-start(f32[4,4,128]{2,1,0:T(4,128)S(1)} %pad_add_fusion), channel_id=1, source_target_pairs={{0,64},{1,65},{2,66},{3,67},{4,68},{5,69},{6,70},{7,71},{8,72},{9,... | collective-permute-start | bytes 24584 | tf_op jit(solution)/shard_map/ppermute | solution.py:33
  104.6 4.4 %collective-permute-start.30 = (f32[4,4,128]{2,1,0:T(4,128)S(1)}, f32[4,4,128]{2,1,0:T(4,128)S(1)}, u32[]{:S(2)}, u32[]{:S(2)}) collective-permute-start(f32[4,4,128]{2,1,0:T(4,128)S(1)} %pad_add_fusion), channel_id=1, source_target_pairs={{0,192},{1,193},{2,194},{3,195},{4,196},{5,197},{6,198},{7,199},{8... | collective-permute-start | bytes 24584 | tf_op jit(solution)/shard_map/ppermute | solution.py:33
  (15 other events, 140.4 us)

commit v9 on v8

--- a/solution.py
+++ b/solution.py
@@ -271,7 +271,7 @@
             dma((len(col_cuts),)),
             dma((len(col_cuts) + 5,)),
         ],
-        compiler_params=pltpu.CompilerParams(vmem_limit_bytes=58 * 2**20),
+        compiler_params=pltpu.CompilerParams(vmem_limit_bytes=18 * 2**20),
         cost_estimate=pl.CostEstimate(
             flops=6 * used * depth * feats,
             bytes_accessed=6 * (used + depth) * feats,

time: 110 us -> 106 us (0.964)
  Pallas kernels: 22.4 us -> 18.4 us
  waiting for transfers between devices: 40.5 us -> 42.3 us
  other arithmetic: 9.6 us -> 7.91 us
    pallas_call x2, Pallas kernels: 17 us -> 12.9 us  [pair_sums(): pl.pallas_call(functools.partial(pair_kernel, col_cuts=tuple(col_cuts), n...]
    ppermute x31, waiting for transfers between devices: 40.5 us -> 42.3 us  [permute(): return lax.ppermute(value, AXES, pairs)]
    unnamed x32 -> x14, local copies, waits for them, and re-layouts: 2.29 us -> 1.58 us
  transfers between devices with their start and end apart: 31 -> 31, of which waited for: 17 -> 19; matrix products, arithmetic and copies ran while one was open for 5% -> 6% of each run, Pallas kernels for 6% -> 5%
where the time goes in v9:
time: 106 us
  waiting for transfers between devices  42.3 us (40%)
  starting transfers between devices  33.5 us (32%)
  Pallas kernels  18.4 us (17%)
  other arithmetic  7.91 us (7%)
  local copies, waits for them, and re-layouts  3.82 us (4%)
    ppermute x31, waiting for transfers between devices, permute(): return lax.ppermute(value, AXES, pairs)  42.3 us
    ppermute x31, starting transfers between devices, permute(): return lax.ppermute(value, AXES, pairs)  33.5 us
    pallas_call x2, Pallas kernels, pair_sums(): pl.pallas_call(functools.partial(pair_kernel, col_cuts=tuple(col_cuts), n...  12.9 us
    pallas_call x1, Pallas kernels, raw_partial(): pl.pallas_call(raw_kernel, grid=(feats // width,), in_specs=[pl.BlockSpec...  5.5 us
    convert_element_type x1, other arithmetic, shards(): tag = tag.astype(jnp.bfloat16)  2.56 us
  transfers between devices with their start and end apart: 31, of which 19 were waited for; matrix products, arithmetic and copies ran while one was open for 6% of the time, Pallas kernels for 5%

profile of v9, /device:TPU:4, one launch (start us, length us, event | category | flops | bytes accessed | tf_op | source)
XLA Modules:
  0.0 106.2 jit_solution(13184996615140668598)
XLA Ops:
  0.0 5.5 %raw.1 = f32[512,1024]{1,0:T(8,128)} custom-call(s32[8,11]{1,0:T(8,128)} %bitcast.41, bf16[1584,512]{1,0:T(8,128)(2,1)} %bitcast.35, bf16[1584,1024]{1,0:T(8,128)(2,1)} %geometry.1), custom_call_target="tpu_custom_call" | custom-call | flops 1660944384 | bytes 8388608 | tf_op jit(solution)/shard_map/raw/pallas_call | solution.py:84
  5.5 1.7 %constant_dynamic-slice_fusion.1 = (f32[4,1,32,1024]{3,2,1,0:T(8,128)S(1)}, f16[4,1,32,1024]{3,2,0,1:T(8,128)(2,1)S(1)}, f16[4,1,32,1024]{3,2,0,1:T(8,128)(2,1)S(1)}, f16[4,1,32,1024]{3,2,0,1:T(8,128)(2,1)S(1)}) fusion(f32[4,4,32,1024]{3,2,1,0:T(8,128)} %bitcast.34, s32[]{:T(128)S(6)} %select_n.180, s32[]{:T(128)S(6)} %select_n.184, s32[]{:T(128)S(6)} %select_n.182, ...), kind=kLoop, calls=%fused_computation.43 | loop fusion | flops 393216 | bytes 3407888 | tf_op jit(solution)/shard_map/jit(dynamic_index_in_dim)/dynamic_slice | solution.py:303
  7.3 3.3 %collective-permute-start = (f16[128,1024]{1,0:T(8,128)(2,1)S(1)}, f16[128,1024]{1,0:T(8,128)(2,1)S(1)}, u32[]{:S(2)}, u32[]{:S(2)}) collective-permute-start(f16[128,1024]{1,0:T(8,128)(2,1)S(1)} %bitcast.38), channel_id=1, source_target_pairs={{0,128},{1,129},{2,130},{3,131},{4,132},{5,133},{6,134},{7,135},{8... | collective-permute-start | bytes 786440 | tf_op jit(solution)/shard_map/ppermute | solution.py:33
  11.2 2.6 %collective-permute-start.2 = (f16[128,1024]{1,0:T(8,128)(2,1)S(1)}, f16[128,1024]{1,0:T(8,128)(2,1)S(1)}, u32[]{:S(2)}, u32[]{:S(2)}) collective-permute-start(f16[128,1024]{1,0:T(8,128)(2,1)S(1)} %bitcast.36), channel_id=1, source_target_pairs={{0,192},{1,193},{2,194},{3,195},{4,196},{5,197},{6,198},{7,199},{8... | collective-permute-start | bytes 786440 | tf_op jit(solution)/shard_map/ppermute | solution.py:33
  14.4 2.6 %select_convert_fusion = bf16[16,1024]{1,0:T(8,128)(2,1)S(1)} fusion(bf16[]{:T(256)} %bitcast.5, bf16[]{:T(256)} %bitcast.4, bf16[]{:T(256)} %bitcast.3, bf16[]{:T(256)} %bitcast.2, s32[1024]{0:T(1024)S(1)} %get-tuple-element.77, s32[1024]{0:T(1024)S(1)} %get-tuple-element.78, pred[16]{0:T(512)(128)(4,1)S(1)} %iota_compare_fusion, pred[1024]{0:T(1024)(128)(4,1)S(1)} %fusion.13), kind=kLoop, calls=%fused_computation.16 | loop fusion | flops 163840 | bytes 42008 | tf_op jit(solution)/shard_map/convert_element_type | solution.py:298
  18.1 4.4 %collective-permute-done.1 = f16[128,1024]{1,0:T(8,128)(2,1)S(1)} collective-permute-done((f16[128,1024]{1,0:T(8,128)(2,1)S(1)}, f16[128,1024]{1,0:T(8,128)(2,1)S(1)}, u32[]{:S(2)}, u32[]{:S(2)}) %collective-permute-start.1) | collective-permute-done | bytes 262176 | tf_op jit(solution)/shard_map/ppermute | solution.py:33
  23.4 1.6 %collective-permute-done.3.refs_6_.refs_10_ = bf16[144,1024]{1,0:T(8,128)(2,1)S(1)} collective-permute-done((bf16[144,1024]{1,0:T(8,128)(2,1)S(1)}, bf16[144,1024]{1,0:T(8,128)(2,1)S(1)}, u32[]{:S(2)}, u32[]{:S(2)}) %collective-permute-start.3) | collective-permute-done | bytes 294944 | tf_op jit(solution)/shard_map/ppermute | solution.py:33
  25.2 2.0 %collective-permute-start.4 = (bf16[288,1024]{1,0:T(8,128)(2,1)S(1)}, bf16[288,1024]{1,0:T(8,128)(2,1)S(1)}, u32[]{:S(2)}, u32[]{:S(2)}) collective-permute-start(bf16[288,1024]{1,0:T(8,128)(2,1)S(1)} %maximum_select_fusion), channel_id=1, source_target_pairs={{0,2},{1,15},{2,4},{3,1},{4,6},{5,3},{6,8},{7,5},{8,10},{9,7},{10,... | collective-permute-start | bytes 1769480 | tf_op jit(solution)/shard_map/ppermute | solution.py:33
  27.2 1.4 %collective-permute-start.5 = (bf16[288,1024]{1,0:T(8,128)(2,1)S(1)}, bf16[288,1024]{1,0:T(8,128)(2,1)S(1)}, u32[]{:S(2)}, u32[]{:S(2)}) collective-permute-start(bf16[288,1024]{1,0:T(8,128)(2,1)S(1)} %maximum_select_fusion), channel_id=1, source_target_pairs={{0,64},{1,193},{2,66},{3,195},{4,68},{5,197},{6,70},{7,199},{8,72}... | collective-permute-start | bytes 1769480 | tf_op jit(solution)/shard_map/ppermute | solution.py:33
  28.5 1.2 %collective-permute-start.6 = (bf16[144,1024]{1,0:T(8,128)(2,1)S(1)}, bf16[144,1024]{1,0:T(8,128)(2,1)S(1)}, u32[]{:S(2)}, u32[]{:S(2)}) collective-permute-start(bf16[144,1024]{1,0:T(8,128)(2,1)S(1)} %pad_maximum_fusion.refs_1_.refs_5_.refs_3_.refs_9_), channel_id=1, source_target_pairs={{0,16},{1,17},{2,18},{3,19},{4,20},{5,21},{6,22},{7,23},{8,24},{9,... | collective-permute-start | bytes 884744 | tf_op jit(solution)/shard_map/ppermute | solution.py:33
  29.7 5.5 %collective-permute-done.6.refs_15_ = bf16[144,1024]{1,0:T(8,128)(2,1)S(1)} collective-permute-done((bf16[144,1024]{1,0:T(8,128)(2,1)S(1)}, bf16[144,1024]{1,0:T(8,128)(2,1)S(1)}, u32[]{:S(2)}, u32[]{:S(2)}) %collective-permute-start.6) | collective-permute-done | bytes 294944 | tf_op jit(solution)/shard_map/ppermute | solution.py:33
  35.3 3.7 %collective-permute-done.4.refs_2_.refs_4_ = bf16[288,1024]{1,0:T(8,128)(2,1)S(1)} collective-permute-done((bf16[288,1024]{1,0:T(8,128)(2,1)S(1)}, bf16[288,1024]{1,0:T(8,128)(2,1)S(1)}, u32[]{:S(2)}, u32[]{:S(2)}) %collective-permute-start.4) | collective-permute-done | bytes 589856 | tf_op jit(solution)/shard_map/ppermute | solution.py:33
  39.0 1.2 %collective-permute-start.10 = (bf16[288,1024]{1,0:T(8,128)(2,1)S(1)}, bf16[288,1024]{1,0:T(8,128)(2,1)S(1)}, u32[]{:S(2)}, u32[]{:S(2)}) collective-permute-start(bf16[288,1024]{1,0:T(8,128)(2,1)S(1)} %collective-permute-done.5.refs_7_.refs_11_), channel_id=1, source_target_pairs={{0,1},{1,0},{2,3},{3,2},{4,5},{5,4},{6,7},{7,6},{8,9},{9,8},{10,11... | collective-permute-start | bytes 1769480 | tf_op jit(solution)/shard_map/ppermute | solution.py:33
  40.2 2.3 %collective-permute-start.11 = (bf16[144,1024]{1,0:T(8,128)(2,1)S(1)}, bf16[144,1024]{1,0:T(8,128)(2,1)S(1)}, u32[]{:S(2)}, u32[]{:S(2)}) collective-permute-start(bf16[144,1024]{1,0:T(8,128)(2,1)S(1)} %collective-permute-done.6.refs_15_), channel_id=1, source_target_pairs={{0,1},{1,0},{2,3},{3,2},{4,5},{5,4},{6,7},{7,6},{8,9},{9,8},{10,11... | collective-permute-start | bytes 884744 | tf_op jit(solution)/shard_map/ppermute | solution.py:33
  43.1 1.2 %collective-permute-start.9 = (bf16[128,1024]{1,0:T(8,128)(2,1)S(1)}, bf16[128,1024]{1,0:T(8,128)(2,1)}, u32[]{:S(2)}, u32[]{:S(2)}) collective-permute-start(bf16[128,1024]{1,0:T(8,128)(2,1)S(1)} %get-tuple-element.69), channel_id=1, source_target_pairs={{0,16},{1,17},{2,18},{3,19},{4,20},{5,21},{6,22},{7,23},{8,24},{9,... | collective-permute-start | bytes 786440 | tf_op jit(solution)/shard_map/ppermute | solution.py:33
  44.3 5.9 %collective-permute-done.8.refs_9_.refs_13_ = bf16[128,1024]{1,0:T(8,128)(2,1)S(1)} collective-permute-done((bf16[128,1024]{1,0:T(8,128)(2,1)S(1)}, bf16[128,1024]{1,0:T(8,128)(2,1)S(1)}, u32[]{:S(2)}, u32[]{:S(2)}) %collective-permute-start.8) | collective-permute-done | bytes 262176 | tf_op jit(solution)/shard_map/ppermute | solution.py:33
  50.2 2.1 %collective-permute-done.9.refs_17_ = bf16[128,1024]{1,0:T(8,128)(2,1)} collective-permute-done((bf16[128,1024]{1,0:T(8,128)(2,1)S(1)}, bf16[128,1024]{1,0:T(8,128)(2,1)}, u32[]{:S(2)}, u32[]{:S(2)}) %collective-permute-start.9) | collective-permute-done | bytes 262176 | tf_op jit(solution)/shard_map/ppermute | solution.py:33
  54.7 3.1 %collective-permute-start.16 = (bf16[128,1024]{1,0:T(8,128)(2,1)}, bf16[128,1024]{1,0:T(8,128)(2,1)}, u32[]{:S(2)}, u32[]{:S(2)}) collective-permute-start(bf16[128,1024]{1,0:T(8,128)(2,1)} %pad_maximum_fusion.1), channel_id=1, source_target_pairs={{32,16},{96,80},{160,144},{224,208}} | collective-permute-start | bytes 786440 | tf_op jit(solution)/shard_map/ppermute | solution.py:33
  57.9 2.0 %collective-permute-start.17 = (bf16[128,1024]{1,0:T(8,128)(2,1)}, bf16[128,1024]{1,0:T(8,128)(2,1)}, u32[]{:S(2)}, u32[]{:S(2)}) collective-permute-start(bf16[128,1024]{1,0:T(8,128)(2,1)} %pad_maximum_fusion.1), channel_id=1, source_target_pairs={{32,0},{96,64},{160,128},{224,192}} | collective-permute-start | bytes 786440 | tf_op jit(solution)/shard_map/ppermute | solution.py:33
  61.4 4.2 %collective-permute-done.17 = bf16[128,1024]{1,0:T(8,128)(2,1)} collective-permute-done((bf16[128,1024]{1,0:T(8,128)(2,1)}, bf16[128,1024]{1,0:T(8,128)(2,1)}, u32[]{:S(2)}, u32[]{:S(2)}) %collective-permute-start.17) | collective-permute-done | bytes 262176 | tf_op jit(solution)/shard_map/ppermute | solution.py:33
  65.6 3.3 %collective-permute-done.13.refs_18_ = bf16[128,1024]{1,0:T(8,128)(2,1)} collective-permute-done((bf16[128,1024]{1,0:T(8,128)(2,1)}, bf16[128,1024]{1,0:T(8,128)(2,1)}, u32[]{:S(2)}, u32[]{:S(2)}) %collective-permute-start.13) | collective-permute-done | bytes 262176 | tf_op jit(solution)/shard_map/ppermute | solution.py:33
  69.9 1.5 %collective-permute-start.19 = (bf16[48,1024]{1,0:T(8,128)(2,1)S(1)}, bf16[48,1024]{1,0:T(8,128)(2,1)S(1)}, u32[]{:S(2)}, u32[]{:S(2)}) collective-permute-start(bf16[48,1024]{1,0:T(8,128)(2,1)S(1)} %fusion.3), channel_id=1, source_target_pairs={{32,18},{33,17},{34,20},{36,22},{38,24},{43,27},{45,29},{47,31},{9... | collective-permute-start | bytes 294920 | tf_op jit(solution)/shard_map/ppermute | solution.py:33
  71.4 1.8 %collective-permute-start.18 = (bf16[128,1024]{1,0:T(8,128)(2,1)S(1)}, bf16[128,1024]{1,0:T(8,128)(2,1)S(1)}, u32[]{:S(2)}, u32[]{:S(2)}) collective-permute-start(bf16[128,1024]{1,0:T(8,128)(2,1)S(1)} %collective-permute-done.8.refs_9_.refs_13_), channel_id=1, source_target_pairs={{0,16},{1,17},{2,18},{3,19},{4,20},{5,21},{6,22},{7,23},{8,24},{9,... | collective-permute-start | bytes 786440 | tf_op jit(solution)/shard_map/ppermute | solution.py:33
  73.2 5.0 %early.1 = (f32[4,512]{1,0:T(4,128)S(1)}, f32[4,512]{1,0:T(4,128)S(1)}) custom-call(s32[2]{0:T(128)S(1)} %pad_add_fusion.1.refs_0_, bf16[144,1024]{1,0:T(8,128)(2,1)S(1)} %pad_maximum_fusion.refs_1_.refs_5_.refs_3_.refs_9_, bf16[288,1024]{1,0:T(8,128)(2,1)S(1)} %collective-permute-done.4.refs_2_.refs_4_, ...), custom_call_target="tpu_custom_call" | custom-call | flops 5637144576 | bytes 11796480 | tf_op jit(solution)/shard_map/early/pallas_call | solution.py:256
  81.3 1.2 %collective-permute-done.21.refs_20_ = bf16[128,1024]{1,0:T(8,128)(2,1)S(1)} collective-permute-done((bf16[128,1024]{1,0:T(8,128)(2,1)}, bf16[128,1024]{1,0:T(8,128)(2,1)S(1)}, u32[]{:S(2)}, u32[]{:S(2)}) %collective-permute-start.21) | collective-permute-done | bytes 262176 | tf_op jit(solution)/shard_map/ppermute | solution.py:33
  82.6 7.9 %late.1 = (f32[4,512]{1,0:T(4,128)S(1)}, f32[4,512]{1,0:T(4,128)S(1)}, f32[4,1152]{1,0:T(4,128)S(1)}, f32[4,128]{1,0:T(4,128)S(1)}) custom-call(s32[2]{0:T(128)S(1)} %pad_add_fusion.1.refs_0_, f32[4,512]{1,0:T(4,128)S(1)} %get-tuple-element.52.refs_1_, f32[4,512]{1,0:T(4,128)S(1)} %get-tuple-element.53.refs_2_, ...), custom_call_target="tpu_custom_call" | custom-call | flops 16609443840 | bytes 22216704 | tf_op jit(solution)/shard_map/late/pallas_call | solution.py:256
  92.5 1.3 %collective-permute-start.26 = (f32[4,128]{1,0:T(4,128)S(1)}, f32[4,128]{1,0:T(4,128)S(1)}, u32[]{:S(2)}, u32[]{:S(2)}) collective-permute-start(f32[4,128]{1,0:T(4,128)S(1)} %slice_add_fusion.2), channel_id=1, source_target_pairs={{0,32},{64,96},{128,160},{192,224}} | collective-permute-start | bytes 6152 | tf_op jit(solution)/shard_map/ppermute | solution.py:33
  93.8 1.3 %collective-permute-start.27 = (f32[4,128]{1,0:T(4,128)S(1)}, f32[4,128]{1,0:T(4,128)S(1)}, u32[]{:S(2)}, u32[]{:S(2)}) collective-permute-start(f32[4,128]{1,0:T(4,128)S(1)} %slice_add_fusion.2), channel_id=1, source_target_pairs={{16,32},{80,96},{144,160},{208,224}} | collective-permute-start | bytes 6152 | tf_op jit(solution)/shard_map/ppermute | solution.py:33
  95.1 4.4 %collective-permute-done.26 = f32[4,128]{1,0:T(4,128)S(1)} collective-permute-done((f32[4,128]{1,0:T(4,128)S(1)}, f32[4,128]{1,0:T(4,128)S(1)}, u32[]{:S(2)}, u32[]{:S(2)}) %collective-permute-start.26) | collective-permute-done | bytes 2080 | tf_op jit(solution)/shard_map/ppermute | solution.py:33
  100.2 1.5 %collective-permute-start.29 = (f32[4,4,128]{2,1,0:T(4,128)S(1)}, f32[4,4,128]{2,1,0:T(4,128)S(1)}, u32[]{:S(2)}, u32[]{:S(2)}) collective-permute-start(f32[4,4,128]{2,1,0:T(4,128)S(1)} %pad_add_fusion), channel_id=1, source_target_pairs={{0,64},{1,65},{2,66},{3,67},{4,68},{5,69},{6,70},{7,71},{8,72},{9,... | collective-permute-start | bytes 24584 | tf_op jit(solution)/shard_map/ppermute | solution.py:33
  101.7 1.7 %collective-permute-start.30 = (f32[4,4,128]{2,1,0:T(4,128)S(1)}, f32[4,4,128]{2,1,0:T(4,128)S(1)}, u32[]{:S(2)}, u32[]{:S(2)}) collective-permute-start(f32[4,4,128]{2,1,0:T(4,128)S(1)} %pad_add_fusion), channel_id=1, source_target_pairs={{0,192},{1,193},{2,194},{3,195},{4,196},{5,197},{6,198},{7,199},{8... | collective-permute-start | bytes 24584 | tf_op jit(solution)/shard_map/ppermute | solution.py:33
  103.5 1.4 %collective-permute-done.28 = f32[4,4,128]{2,1,0:T(4,128)S(1)} collective-permute-done((f32[4,4,128]{2,1,0:T(4,128)S(1)}, f32[4,4,128]{2,1,0:T(4,128)S(1)}, u32[]{:S(2)}, u32[]{:S(2)}) %collective-permute-start.28) | collective-permute-done | bytes 8224 | tf_op jit(solution)/shard_map/ppermute | solution.py:33
  (89 shorter events, 16.2 us)
Async XLA Ops:
  7.3 10.8 %collective-permute-start = (f16[128,1024]{1,0:T(8,128)(2,1)S(1)}, f16[128,1024]{1,0:T(8,128)(2,1)S(1)}, u32[]{:S(2)}, u32[]{:S(2)}) collective-permute-start(f16[128,1024]{1,0:T(8,128)(2,1)S(1)} %bitcast.38), channel_id=1, source_target_pairs={{0,128},{1,129},{2,130},{3,131},{4,132},{5,133},{6,134},{7,135},{8... | collective-permute-start | bytes 786440 | tf_op jit(solution)/shard_map/ppermute | solution.py:33
  10.5 12.0 %collective-permute-start.1 = (f16[128,1024]{1,0:T(8,128)(2,1)S(1)}, f16[128,1024]{1,0:T(8,128)(2,1)S(1)}, u32[]{:S(2)}, u32[]{:S(2)}) collective-permute-start(f16[128,1024]{1,0:T(8,128)(2,1)S(1)} %bitcast.37), channel_id=1, source_target_pairs={{0,64},{1,65},{2,66},{3,67},{4,68},{5,69},{6,70},{7,71},{8,72},{9,... | collective-permute-start | bytes 786440 | tf_op jit(solution)/shard_map/ppermute | solution.py:33
  11.2 11.7 %collective-permute-start.2 = (f16[128,1024]{1,0:T(8,128)(2,1)S(1)}, f16[128,1024]{1,0:T(8,128)(2,1)S(1)}, u32[]{:S(2)}, u32[]{:S(2)}) collective-permute-start(f16[128,1024]{1,0:T(8,128)(2,1)S(1)} %bitcast.36), channel_id=1, source_target_pairs={{0,192},{1,193},{2,194},{3,195},{4,196},{5,197},{6,198},{7,199},{8... | collective-permute-start | bytes 786440 | tf_op jit(solution)/shard_map/ppermute | solution.py:33
  23.3 1.7 %collective-permute-start.3 = (bf16[144,1024]{1,0:T(8,128)(2,1)S(1)}, bf16[144,1024]{1,0:T(8,128)(2,1)S(1)}, u32[]{:S(2)}, u32[]{:S(2)}) collective-permute-start(bf16[144,1024]{1,0:T(8,128)(2,1)S(1)} %pad_maximum_fusion.refs_1_.refs_5_.refs_3_.refs_9_), channel_id=1, source_target_pairs={{0,1},{1,0},{2,3},{3,2},{4,5},{5,4},{6,7},{7,6},{8,9},{9,8},{10,11... | collective-permute-start | bytes 884744 | tf_op jit(solution)/shard_map/ppermute | solution.py:33
  25.2 13.8 %copy-start.4 = (bf16[288,1024]{1,0:T(8,128)(2,1)}, bf16[288,1024]{1,0:T(8,128)(2,1)S(1)}, u32[]{:S(2)}) copy-start(bf16[288,1024]{1,0:T(8,128)(2,1)S(1)} %maximum_select_fusion) | copy-start | bytes 1769476
  25.2 13.8 %collective-permute-start.4 = (bf16[288,1024]{1,0:T(8,128)(2,1)S(1)}, bf16[288,1024]{1,0:T(8,128)(2,1)S(1)}, u32[]{:S(2)}, u32[]{:S(2)}) collective-permute-start(bf16[288,1024]{1,0:T(8,128)(2,1)S(1)} %maximum_select_fusion), channel_id=1, source_target_pairs={{0,2},{1,15},{2,4},{3,1},{4,6},{5,3},{6,8},{7,5},{8,10},{9,7},{10,... | collective-permute-start | bytes 1769480 | tf_op jit(solution)/shard_map/ppermute | solution.py:33
  27.2 11.8 %collective-permute-start.5 = (bf16[288,1024]{1,0:T(8,128)(2,1)S(1)}, bf16[288,1024]{1,0:T(8,128)(2,1)S(1)}, u32[]{:S(2)}, u32[]{:S(2)}) collective-permute-start(bf16[288,1024]{1,0:T(8,128)(2,1)S(1)} %maximum_select_fusion), channel_id=1, source_target_pairs={{0,64},{1,193},{2,66},{3,195},{4,68},{5,197},{6,70},{7,199},{8,72}... | collective-permute-start | bytes 1769480 | tf_op jit(solution)/shard_map/ppermute | solution.py:33
  28.5 6.7 %collective-permute-start.6 = (bf16[144,1024]{1,0:T(8,128)(2,1)S(1)}, bf16[144,1024]{1,0:T(8,128)(2,1)S(1)}, u32[]{:S(2)}, u32[]{:S(2)}) collective-permute-start(bf16[144,1024]{1,0:T(8,128)(2,1)S(1)} %pad_maximum_fusion.refs_1_.refs_5_.refs_3_.refs_9_), channel_id=1, source_target_pairs={{0,16},{1,17},{2,18},{3,19},{4,20},{5,21},{6,22},{7,23},{8,24},{9,... | collective-permute-start | bytes 884744 | tf_op jit(solution)/shard_map/ppermute | solution.py:33
  39.0 14.0 %collective-permute-start.10 = (bf16[288,1024]{1,0:T(8,128)(2,1)S(1)}, bf16[288,1024]{1,0:T(8,128)(2,1)S(1)}, u32[]{:S(2)}, u32[]{:S(2)}) collective-permute-start(bf16[288,1024]{1,0:T(8,128)(2,1)S(1)} %collective-permute-done.5.refs_7_.refs_11_), channel_id=1, source_target_pairs={{0,1},{1,0},{2,3},{3,2},{4,5},{5,4},{6,7},{7,6},{8,9},{9,8},{10,11... | collective-permute-start | bytes 1769480 | tf_op jit(solution)/shard_map/ppermute | solution.py:33
  40.1 12.9 %collective-permute-start.7 = (bf16[288,1024]{1,0:T(8,128)(2,1)S(1)}, bf16[288,1024]{1,0:T(8,128)(2,1)S(1)}, u32[]{:S(2)}, u32[]{:S(2)}) collective-permute-start(bf16[288,1024]{1,0:T(8,128)(2,1)S(1)} %collective-permute-done.4.refs_2_.refs_4_), channel_id=1, source_target_pairs={{0,2},{1,15},{2,4},{3,1},{4,6},{5,3},{6,8},{7,5},{8,10},{9,7},{10,... | collective-permute-start | bytes 1769480 | tf_op jit(solution)/shard_map/ppermute | solution.py:33
  40.2 12.1 %collective-permute-start.11 = (bf16[144,1024]{1,0:T(8,128)(2,1)S(1)}, bf16[144,1024]{1,0:T(8,128)(2,1)S(1)}, u32[]{:S(2)}, u32[]{:S(2)}) collective-permute-start(bf16[144,1024]{1,0:T(8,128)(2,1)S(1)} %collective-permute-done.6.refs_15_), channel_id=1, source_target_pairs={{0,1},{1,0},{2,3},{3,2},{4,5},{5,4},{6,7},{7,6},{8,9},{9,8},{10,11... | collective-permute-start | bytes 884744 | tf_op jit(solution)/shard_map/ppermute | solution.py:33
  42.6 7.7 %collective-permute-start.8 = (bf16[128,1024]{1,0:T(8,128)(2,1)S(1)}, bf16[128,1024]{1,0:T(8,128)(2,1)S(1)}, u32[]{:S(2)}, u32[]{:S(2)}) collective-permute-start(bf16[128,1024]{1,0:T(8,128)(2,1)S(1)} %get-tuple-element.70), channel_id=1, source_target_pairs={{0,64},{1,193},{2,66},{3,195},{4,68},{5,197},{6,70},{7,199},{8,72}... | collective-permute-start | bytes 786440 | tf_op jit(solution)/shard_map/ppermute | solution.py:33
  43.1 9.2 %collective-permute-start.9 = (bf16[128,1024]{1,0:T(8,128)(2,1)S(1)}, bf16[128,1024]{1,0:T(8,128)(2,1)}, u32[]{:S(2)}, u32[]{:S(2)}) collective-permute-start(bf16[128,1024]{1,0:T(8,128)(2,1)S(1)} %get-tuple-element.69), channel_id=1, source_target_pairs={{0,16},{1,17},{2,18},{3,19},{4,20},{5,21},{6,22},{7,23},{8,24},{9,... | collective-permute-start | bytes 786440 | tf_op jit(solution)/shard_map/ppermute | solution.py:33
  53.9 15.1 %collective-permute-start.12 = (bf16[288,1024]{1,0:T(8,128)(2,1)S(1)}, bf16[288,1024]{1,0:T(8,128)(2,1)S(1)}, u32[]{:S(2)}, u32[]{:S(2)}) collective-permute-start(bf16[288,1024]{1,0:T(8,128)(2,1)S(1)} %collective-permute-done.7.refs_3_.refs_5_), channel_id=1, source_target_pairs={{0,2},{1,15},{2,4},{3,1},{4,6},{5,3},{6,8},{7,5},{8,10},{9,7},{10,... | collective-permute-start | bytes 1769480 | tf_op jit(solution)/shard_map/ppermute | solution.py:33
  54.7 6.6 %collective-permute-start.16 = (bf16[128,1024]{1,0:T(8,128)(2,1)}, bf16[128,1024]{1,0:T(8,128)(2,1)}, u32[]{:S(2)}, u32[]{:S(2)}) collective-permute-start(bf16[128,1024]{1,0:T(8,128)(2,1)} %pad_maximum_fusion.1), channel_id=1, source_target_pairs={{32,16},{96,80},{160,144},{224,208}} | collective-permute-start | bytes 786440 | tf_op jit(solution)/shard_map/ppermute | solution.py:33
  57.9 7.8 %collective-permute-start.17 = (bf16[128,1024]{1,0:T(8,128)(2,1)}, bf16[128,1024]{1,0:T(8,128)(2,1)}, u32[]{:S(2)}, u32[]{:S(2)}) collective-permute-start(bf16[128,1024]{1,0:T(8,128)(2,1)} %pad_maximum_fusion.1), channel_id=1, source_target_pairs={{32,0},{96,64},{160,128},{224,192}} | collective-permute-start | bytes 786440 | tf_op jit(solution)/shard_map/ppermute | solution.py:33
  60.6 8.4 %collective-permute-start.13 = (bf16[128,1024]{1,0:T(8,128)(2,1)}, bf16[128,1024]{1,0:T(8,128)(2,1)}, u32[]{:S(2)}, u32[]{:S(2)}) collective-permute-start(bf16[128,1024]{1,0:T(8,128)(2,1)} %slice.107), channel_id=1, source_target_pairs={{0,16},{1,17},{2,18},{3,19},{4,20},{5,21},{6,22},{7,23},{8,24},{9,... | collective-permute-start | bytes 786440 | tf_op jit(solution)/shard_map/ppermute | solution.py:33
  60.6 8.4 %collective-permute-start.14 = (bf16[128,1024]{1,0:T(8,128)(2,1)}, bf16[128,1024]{1,0:T(8,128)(2,1)}, u32[]{:S(2)}, u32[]{:S(2)}) collective-permute-start(bf16[128,1024]{1,0:T(8,128)(2,1)} %collective-permute-done.9.refs_17_), channel_id=1, source_target_pairs={{0,1},{1,0},{2,3},{3,2},{4,5},{5,4},{6,7},{7,6},{8,9},{9,8},{10,11... | collective-permute-start | bytes 786440 | tf_op jit(solution)/shard_map/ppermute | solution.py:33
  61.3 7.6 %collective-permute-start.15 = (bf16[128,1024]{1,0:T(8,128)(2,1)S(1)}, bf16[128,1024]{1,0:T(8,128)(2,1)}, u32[]{:S(2)}, u32[]{:S(2)}) collective-permute-start(bf16[128,1024]{1,0:T(8,128)(2,1)S(1)} %collective-permute-done.8.refs_9_.refs_13_), channel_id=1, source_target_pairs={{0,1},{1,0},{2,3},{3,2},{4,5},{5,4},{6,7},{7,6},{8,9},{9,8},{10,11... | collective-permute-start | bytes 786440 | tf_op jit(solution)/shard_map/ppermute | solution.py:33
  69.9 8.3 %collective-permute-start.19 = (bf16[48,1024]{1,0:T(8,128)(2,1)S(1)}, bf16[48,1024]{1,0:T(8,128)(2,1)S(1)}, u32[]{:S(2)}, u32[]{:S(2)}) collective-permute-start(bf16[48,1024]{1,0:T(8,128)(2,1)S(1)} %fusion.3), channel_id=1, source_target_pairs={{32,18},{33,17},{34,20},{36,22},{38,24},{43,27},{45,29},{47,31},{9... | collective-permute-start | bytes 294920 | tf_op jit(solution)/shard_map/ppermute | solution.py:33
  71.4 7.5 %collective-permute-start.18 = (bf16[128,1024]{1,0:T(8,128)(2,1)S(1)}, bf16[128,1024]{1,0:T(8,128)(2,1)S(1)}, u32[]{:S(2)}, u32[]{:S(2)}) collective-permute-start(bf16[128,1024]{1,0:T(8,128)(2,1)S(1)} %collective-permute-done.8.refs_9_.refs_13_), channel_id=1, source_target_pairs={{0,16},{1,17},{2,18},{3,19},{4,20},{5,21},{6,22},{7,23},{8,24},{9,... | collective-permute-start | bytes 786440 | tf_op jit(solution)/shard_map/ppermute | solution.py:33
  73.2 9.3 %collective-permute-start.20 = (bf16[144,1024]{1,0:T(8,128)(2,1)S(1)}, bf16[144,1024]{1,0:T(8,128)(2,1)S(1)}, u32[]{:S(2)}, u32[]{:S(2)}) collective-permute-start(bf16[144,1024]{1,0:T(8,128)(2,1)S(1)} %slice_select_fusion), channel_id=1, source_target_pairs={{0,2},{1,15},{2,4},{3,1},{4,6},{5,3},{6,8},{7,5},{8,10},{9,7},{10,... | collective-permute-start | bytes 884744 | tf_op jit(solution)/shard_map/ppermute | solution.py:33
  80.0 1.3 %collective-permute-start.23 = (bf16[128,1024]{1,0:T(8,128)(2,1)S(1)}, bf16[128,1024]{1,0:T(8,128)(2,1)S(1)}, u32[]{:S(2)}, u32[]{:S(2)}) collective-permute-start(bf16[128,1024]{1,0:T(8,128)(2,1)S(1)} %add.132), channel_id=1, source_target_pairs={{0,1},{16,17},{64,65},{80,81},{128,129},{144,145},{192,193},{208,2... | collective-permute-start | bytes 786440 | tf_op jit(solution)/shard_map/ppermute | solution.py:33
  80.6 1.8 %collective-permute-start.21 = (bf16[128,1024]{1,0:T(8,128)(2,1)}, bf16[128,1024]{1,0:T(8,128)(2,1)S(1)}, u32[]{:S(2)}, u32[]{:S(2)}) collective-permute-start(bf16[128,1024]{1,0:T(8,128)(2,1)} %collective-permute-done.13.refs_18_), channel_id=1, source_target_pairs={{0,1},{1,0},{2,3},{3,2},{4,5},{5,4},{6,7},{7,6},{8,9},{9,8},{10,11... | collective-permute-start | bytes 786440 | tf_op jit(solution)/shard_map/ppermute | solution.py:33
  80.7 1.9 %collective-permute-start.22 = (bf16[128,1024]{1,0:T(8,128)(2,1)S(1)}, bf16[128,1024]{1,0:T(8,128)(2,1)S(1)}, u32[]{:S(2)}, u32[]{:S(2)}) collective-permute-start(bf16[128,1024]{1,0:T(8,128)(2,1)S(1)} %collective-permute-done.18.refs_21_), channel_id=1, source_target_pairs={{0,1},{1,0},{2,3},{3,2},{4,5},{5,4},{6,7},{7,6},{8,9},{9,8},{10,11... | collective-permute-start | bytes 786440 | tf_op jit(solution)/shard_map/ppermute | solution.py:33
  90.5 1.3 %collective-permute-start.24 = (f32[4,1152]{1,0:T(4,128)S(1)}, f32[4,1152]{1,0:T(4,128)S(1)}, u32[]{:S(2)}, u32[]{:S(2)}) collective-permute-start(f32[4,1152]{1,0:T(4,128)S(1)} %get-tuple-element.62), channel_id=1, source_target_pairs={{0,1},{1,0},{2,3},{3,2},{4,5},{5,4},{6,7},{7,6},{8,9},{9,8},{10,11... | collective-permute-start | bytes 55304 | tf_op jit(solution)/shard_map/ppermute | solution.py:33
  91.8 7.8 %collective-permute-start.25 = (f32[4,512]{1,0:T(4,128)S(1)}, f32[4,512]{1,0:T(4,128)S(1)}, u32[]{:S(2)}, u32[]{:S(2)}) collective-permute-start(f32[4,512]{1,0:T(4,128)S(1)} %slice_add_fusion), channel_id=1, source_target_pairs={{0,16},{1,17},{2,18},{3,19},{4,20},{5,21},{6,22},{7,23},{8,24},{9,... | collective-permute-start | bytes 24584 | tf_op jit(solution)/shard_map/ppermute | solution.py:33
  92.5 7.0 %collective-permute-start.26 = (f32[4,128]{1,0:T(4,128)S(1)}, f32[4,128]{1,0:T(4,128)S(1)}, u32[]{:S(2)}, u32[]{:S(2)}) collective-permute-start(f32[4,128]{1,0:T(4,128)S(1)} %slice_add_fusion.2), channel_id=1, source_target_pairs={{0,32},{64,96},{128,160},{192,224}} | collective-permute-start | bytes 6152 | tf_op jit(solution)/shard_map/ppermute | solution.py:33
  93.8 5.7 %collective-permute-start.27 = (f32[4,128]{1,0:T(4,128)S(1)}, f32[4,128]{1,0:T(4,128)S(1)}, u32[]{:S(2)}, u32[]{:S(2)}) collective-permute-start(f32[4,128]{1,0:T(4,128)S(1)} %slice_add_fusion.2), channel_id=1, source_target_pairs={{16,32},{80,96},{144,160},{208,224}} | collective-permute-start | bytes 6152 | tf_op jit(solution)/shard_map/ppermute | solution.py:33
  99.6 5.2 %collective-permute-start.28 = (f32[4,4,128]{2,1,0:T(4,128)S(1)}, f32[4,4,128]{2,1,0:T(4,128)S(1)}, u32[]{:S(2)}, u32[]{:S(2)}) collective-permute-start(f32[4,4,128]{2,1,0:T(4,128)S(1)} %pad_add_fusion), channel_id=1, source_target_pairs={{0,128},{1,129},{2,130},{3,131},{4,132},{5,133},{6,134},{7,135},{8... | collective-permute-start | bytes 24584 | tf_op jit(solution)/shard_map/ppermute | solution.py:33
  100.2 4.9 %collective-permute-start.29 = (f32[4,4,128]{2,1,0:T(4,128)S(1)}, f32[4,4,128]{2,1,0:T(4,128)S(1)}, u32[]{:S(2)}, u32[]{:S(2)}) collective-permute-start(f32[4,4,128]{2,1,0:T(4,128)S(1)} %pad_add_fusion), channel_id=1, source_target_pairs={{0,64},{1,65},{2,66},{3,67},{4,68},{5,69},{6,70},{7,71},{8,72},{9,... | collective-permute-start | bytes 24584 | tf_op jit(solution)/shard_map/ppermute | solution.py:33
  101.7 3.7 %collective-permute-start.30 = (f32[4,4,128]{2,1,0:T(4,128)S(1)}, f32[4,4,128]{2,1,0:T(4,128)S(1)}, u32[]{:S(2)}, u32[]{:S(2)}) collective-permute-start(f32[4,4,128]{2,1,0:T(4,128)S(1)} %pad_add_fusion), channel_id=1, source_target_pairs={{0,192},{1,193},{2,194},{3,195},{4,196},{5,197},{6,198},{7,199},{8... | collective-permute-start | bytes 24584 | tf_op jit(solution)/shard_map/ppermute | solution.py:33
  (6 other events, 34.4 us)

commit v10 on v9

--- a/solution.py
+++ b/solution.py
@@ -112,52 +112,29 @@
     col_args, refs = refs[:n_cols_args], refs[n_cols_args:]
     held, refs = dict(zip(names, refs)), refs[len(names) :]
     outs, refs = refs[: 4 if late else 2], refs[4 if late else 2 :]
-    rows_at, cols_at, row_tags, col_tags, row_sems, col_sems, tag_sems = refs
+    rows_at, cols_at = refs
     odd_here, core = place[0], place[1]
     tagged = BLOCK + TAG
 
-    def start(source, first, size, target, at, sem):
-        copy = pltpu.make_async_copy(
-            source.at[pl.ds(first, size), :], target.at[pl.ds(at, size), :], sem
-        )
-        copy.start()
-        return copy
-
     starts = [sum(size for _, _, size in col_cuts[:at]) for at in range(n_cols)]
     depth = sum(size for _, _, size in col_cuts)
-    loads = []
     for at, (arg, first, size) in enumerate(col_cuts):
-        source = col_args[arg]
-        loads.append(
-            [
-                start(source, first, size, cols_at, starts[at], col_sems.at[at]),
-                start(source, first - TAG, TAG, col_tags, at * TAG, tag_sems.at[at]),
-            ]
-        )
+        cols_at[pl.ds(starts[at], size), :] = col_args[arg][pl.ds(first, size), :]
     chunks = (0, 2, 1, 3, 4) if late else (0, 2)
-    tags = {
-        chunk: start(
-            held[TAG_OF[chunk]], 0, TAG, row_tags, chunk * TAG, tag_sems.at[n_cols + chunk]
-        )
-        for chunk in chunks
-    }
     turn = jnp.where(core == 0, 3, 1)
     side = [2 * CHUNK * jnp.where(core == b, 0, 1) for b in range(NC)]
-    made = []
 
     def rows(name, first, at):
         at = at if isinstance(at, int) else pl.multiple_of(at, BLOCK)
-        made.append(start(held[name], first, BLOCK, rows_at, at, row_sems.at[len(made)]))
+        rows_at[pl.ds(at, BLOCK), :] = held[name][pl.ds(first, BLOCK), :]
 
     rows("own", TAG, 0)
     rows("y2", 0, 2 * BLOCK)
     for b in range(NC):
         rows("y1", TAG + b * tagged, side[b] + turn * BLOCK)
         rows("y1_t", TAG + b * tagged, side[b] + (NY - turn) * BLOCK)
-    n_near = len(made)
     rows("own_t", TAG, 2 * CHUNK)
     rows("y2_t", 0, 2 * CHUNK + 2 * BLOCK)
-    n_far = len(made)
     if late:
         rows("x1", TAG, CHUNK)
         rows("w2", 0, CHUNK + 2 * BLOCK)
@@ -167,20 +144,16 @@
         rows("x1_t", TAG, 3 * CHUNK)
         rows("w2_t", 0, 3 * CHUNK + 2 * BLOCK)
         rows("odd", 0, 4 * CHUNK)
-    waited = set()
 
     def bin_of(code):
         source = (code >= BINS).astype(jnp.float32)
         return code - BINS * source, source
 
     for chunk in chunks:
-        tags[chunk].wait()
-        for copy in {0: made[:n_near], 2: made[n_near:n_far], 1: made[n_far:]}.get(chunk, []):
-            copy.wait()
         first = chunk * CHUNK
         odd = chunk == 4
         size = BLOCK if odd else CHUNK
-        tag = row_tags[pl.ds(chunk * TAG + 4, 1), pl.ds(0, BLOCK)].astype(jnp.float32) - 1.0
+        tag = held[TAG_OF[chunk]][4:5, pl.ds(0, BLOCK)].astype(jnp.float32) - 1.0
         bins, _ = bin_of(tag)
         if odd:
             bins = jnp.where(odd_here > 0, bins, -2.0)
@@ -192,11 +165,6 @@
         low = EARLY * BLOCK if late and chunk in (0, 2) else 0
         while low < depth:
             high = depth if depth - low < 3 * BLOCK else low + 2 * BLOCK
-            for at in range(n_cols):
-                if low <= starts[at] < high and at not in waited:
-                    waited.add(at)
-                    for copy in loads[at]:
-                        copy.wait()
             products = lax.dot_general(
                 cols_at[pl.ds(low, high - low), :],
                 rows_at[pl.ds(first, size), :],
@@ -215,8 +183,9 @@
                     sub = lax.broadcasted_iota(jnp.int32, block.shape, 0)
                     block = jnp.where(lane == sub + group * PIECE, 0.0, block)
                 part = (block[0:8] + block[8:16]) + (block[16:24] + block[24:32])
-                row = at * TAG + group % 4
-                code = col_tags[pl.ds(row, 1), pl.ds(0, size)].astype(jnp.float32) - 1.0
+                arg, place_of, _ = col_cuts[at]
+                row = place_of - TAG + group % 4
+                code = col_args[arg][pl.ds(row, 1), pl.ds(0, size)].astype(jnp.float32) - 1.0
                 bin_id, source = bin_of(code)
                 match = (bins == bin_id).astype(jnp.float32)
                 is_one = match * source
@@ -247,9 +216,7 @@
     total = 4 * CHUNK + BLOCK if late else 3 * CHUNK
     used, depth = (5 if late else 2) * CHUNK, sum(size for _, _, size in col_cuts)
     feats = col_args[0].shape[1]
-    hbm = pl.BlockSpec(memory_space=pl.ANY)
     vmem = pl.BlockSpec(memory_space=pltpu.VMEM)
-    dma = pltpu.SemaphoreType.DMA
     widths = [CHUNK, CHUNK, 2 * CHUNK + BLOCK, BLOCK] if late else [CHUNK, CHUNK]
     names = NAMES if late else NAMES[:6]
     before = list(before or [])
@@ -258,18 +225,12 @@
             pair_kernel, col_cuts=tuple(col_cuts), n_cols_args=len(col_args), late=late
         ),
         in_specs=[pl.BlockSpec(memory_space=pltpu.SMEM)]
-        + [vmem] * len(before)
-        + [hbm] * (len(col_args) + len(names)),
+        + [vmem] * (len(before) + len(col_args) + len(names)),
         out_specs=[vmem] * len(widths),
         out_shape=[jax.ShapeDtypeStruct((4, width), jnp.float32) for width in widths],
         scratch_shapes=[
             pltpu.VMEM((total, feats), jnp.bfloat16),
             pltpu.VMEM((depth, feats), jnp.bfloat16),
-            pltpu.VMEM((TAG * 5, feats), jnp.bfloat16),
-            pltpu.VMEM((TAG * len(col_cuts), feats), jnp.bfloat16),
-            dma((17,)),
-            dma((len(col_cuts),)),
-            dma((len(col_cuts) + 5,)),
         ],
         compiler_params=pltpu.CompilerParams(vmem_limit_bytes=18 * 2**20),
         cost_estimate=pl.CostEstimate(

time: 106 us -> 104 us (0.981)
  Pallas kernels: 18.4 us -> 14.6 us
  waiting for transfers between devices: 42.3 us -> 43.6 us
    pallas_call x2, Pallas kernels: 12.9 us -> 9.15 us  [pair_sums(): pl.pallas_call(functools.partial(pair_kernel, col_cuts=tuple(col_cuts), n...]
    ppermute x31, waiting for transfers between devices: 42.3 us -> 43.6 us  [permute(): return lax.ppermute(value, AXES, pairs)]
  transfers between devices with their start and end apart: 31 -> 31, of which waited for: 19 -> 19; matrix products, arithmetic and copies ran while one was open for 6% -> 6% of each run, Pallas kernels for 5% -> 4%
where the time goes in v10:
time: 104 us
  waiting for transfers between devices  43.6 us (42%)
  starting transfers between devices  33.5 us (32%)
  Pallas kernels  14.6 us (14%)
  other arithmetic  7.91 us (8%)
  local copies, waits for them, and re-layouts  3.82 us (4%)
    ppermute x31, waiting for transfers between devices, permute(): return lax.ppermute(value, AXES, pairs)  43.6 us
    ppermute x31, starting transfers between devices, permute(): return lax.ppermute(value, AXES, pairs)  33.5 us
    pallas_call x2, Pallas kernels, pair_sums(): pl.pallas_call(functools.partial(pair_kernel, col_cuts=tuple(col_cuts), n...  9.15 us
    pallas_call x1, Pallas kernels, raw_partial(): pl.pallas_call(raw_kernel, grid=(feats // width,), in_specs=[pl.BlockSpec...  5.5 us
    convert_element_type x1, other arithmetic, shards(): tag = tag.astype(jnp.bfloat16)  2.56 us
  transfers between devices with their start and end apart: 31, of which 19 were waited for; matrix products, arithmetic and copies ran while one was open for 6% of the time, Pallas kernels for 4%

profile of v10, /device:TPU:4, one launch (start us, length us, event | category | flops | bytes accessed | tf_op | source)
XLA Modules:
  0.0 103.7 jit_solution(15296607157449402370)
XLA Ops:
  0.0 5.5 %raw.1 = f32[512,1024]{1,0:T(8,128)} custom-call(s32[8,11]{1,0:T(8,128)} %bitcast.41, bf16[1584,512]{1,0:T(8,128)(2,1)} %bitcast.35, bf16[1584,1024]{1,0:T(8,128)(2,1)} %geometry.1), custom_call_target="tpu_custom_call" | custom-call | flops 1660944384 | bytes 8388608 | tf_op jit(solution)/shard_map/raw/pallas_call | solution.py:84
  5.5 1.7 %constant_dynamic-slice_fusion.1 = (f32[4,1,32,1024]{3,2,1,0:T(8,128)S(1)}, f16[4,1,32,1024]{3,2,0,1:T(8,128)(2,1)S(1)}, f16[4,1,32,1024]{3,2,0,1:T(8,128)(2,1)S(1)}, f16[4,1,32,1024]{3,2,0,1:T(8,128)(2,1)S(1)}) fusion(f32[4,4,32,1024]{3,2,1,0:T(8,128)} %bitcast.34, s32[]{:T(128)S(6)} %select_n.180, s32[]{:T(128)S(6)} %select_n.184, s32[]{:T(128)S(6)} %select_n.182, ...), kind=kLoop, calls=%fused_computation.43 | loop fusion | flops 393216 | bytes 3407888 | tf_op jit(solution)/shard_map/jit(dynamic_index_in_dim)/dynamic_slice | solution.py:264
  7.3 3.3 %collective-permute-start = (f16[128,1024]{1,0:T(8,128)(2,1)S(1)}, f16[128,1024]{1,0:T(8,128)(2,1)S(1)}, u32[]{:S(2)}, u32[]{:S(2)}) collective-permute-start(f16[128,1024]{1,0:T(8,128)(2,1)S(1)} %bitcast.38), channel_id=1, source_target_pairs={{0,128},{1,129},{2,130},{3,131},{4,132},{5,133},{6,134},{7,135},{8... | collective-permute-start | bytes 786440 | tf_op jit(solution)/shard_map/ppermute | solution.py:33
  11.2 2.6 %collective-permute-start.2 = (f16[128,1024]{1,0:T(8,128)(2,1)S(1)}, f16[128,1024]{1,0:T(8,128)(2,1)S(1)}, u32[]{:S(2)}, u32[]{:S(2)}) collective-permute-start(f16[128,1024]{1,0:T(8,128)(2,1)S(1)} %bitcast.36), channel_id=1, source_target_pairs={{0,192},{1,193},{2,194},{3,195},{4,196},{5,197},{6,198},{7,199},{8... | collective-permute-start | bytes 786440 | tf_op jit(solution)/shard_map/ppermute | solution.py:33
  14.4 2.6 %select_convert_fusion = bf16[16,1024]{1,0:T(8,128)(2,1)S(1)} fusion(bf16[]{:T(256)} %bitcast.5, bf16[]{:T(256)} %bitcast.4, bf16[]{:T(256)} %bitcast.3, bf16[]{:T(256)} %bitcast.2, s32[1024]{0:T(1024)S(1)} %get-tuple-element.77, s32[1024]{0:T(1024)S(1)} %get-tuple-element.78, pred[16]{0:T(512)(128)(4,1)S(1)} %iota_compare_fusion, pred[1024]{0:T(1024)(128)(4,1)S(1)} %fusion.13), kind=kLoop, calls=%fused_computation.16 | loop fusion | flops 163840 | bytes 42008 | tf_op jit(solution)/shard_map/convert_element_type | solution.py:259
  18.1 4.4 %collective-permute-done.1 = f16[128,1024]{1,0:T(8,128)(2,1)S(1)} collective-permute-done((f16[128,1024]{1,0:T(8,128)(2,1)S(1)}, f16[128,1024]{1,0:T(8,128)(2,1)S(1)}, u32[]{:S(2)}, u32[]{:S(2)}) %collective-permute-start.1) | collective-permute-done | bytes 262176 | tf_op jit(solution)/shard_map/ppermute | solution.py:33
  23.4 1.6 %collective-permute-done.3.refs_6_.refs_10_ = bf16[144,1024]{1,0:T(8,128)(2,1)S(1)} collective-permute-done((bf16[144,1024]{1,0:T(8,128)(2,1)S(1)}, bf16[144,1024]{1,0:T(8,128)(2,1)S(1)}, u32[]{:S(2)}, u32[]{:S(2)}) %collective-permute-start.3) | collective-permute-done | bytes 294944 | tf_op jit(solution)/shard_map/ppermute | solution.py:33
  25.2 2.0 %collective-permute-start.4 = (bf16[288,1024]{1,0:T(8,128)(2,1)S(1)}, bf16[288,1024]{1,0:T(8,128)(2,1)S(1)}, u32[]{:S(2)}, u32[]{:S(2)}) collective-permute-start(bf16[288,1024]{1,0:T(8,128)(2,1)S(1)} %maximum_select_fusion), channel_id=1, source_target_pairs={{0,2},{1,15},{2,4},{3,1},{4,6},{5,3},{6,8},{7,5},{8,10},{9,7},{10,... | collective-permute-start | bytes 1769480 | tf_op jit(solution)/shard_map/ppermute | solution.py:33
  27.2 1.4 %collective-permute-start.5 = (bf16[288,1024]{1,0:T(8,128)(2,1)S(1)}, bf16[288,1024]{1,0:T(8,128)(2,1)S(1)}, u32[]{:S(2)}, u32[]{:S(2)}) collective-permute-start(bf16[288,1024]{1,0:T(8,128)(2,1)S(1)} %maximum_select_fusion), channel_id=1, source_target_pairs={{0,64},{1,193},{2,66},{3,195},{4,68},{5,197},{6,70},{7,199},{8,72}... | collective-permute-start | bytes 1769480 | tf_op jit(solution)/shard_map/ppermute | solution.py:33
  28.5 1.2 %collective-permute-start.6 = (bf16[144,1024]{1,0:T(8,128)(2,1)S(1)}, bf16[144,1024]{1,0:T(8,128)(2,1)S(1)}, u32[]{:S(2)}, u32[]{:S(2)}) collective-permute-start(bf16[144,1024]{1,0:T(8,128)(2,1)S(1)} %pad_maximum_fusion.refs_1_.refs_5_.refs_3_.refs_9_), channel_id=1, source_target_pairs={{0,16},{1,17},{2,18},{3,19},{4,20},{5,21},{6,22},{7,23},{8,24},{9,... | collective-permute-start | bytes 884744 | tf_op jit(solution)/shard_map/ppermute | solution.py:33
  29.7 5.5 %collective-permute-done.6.refs_15_ = bf16[144,1024]{1,0:T(8,128)(2,1)S(1)} collective-permute-done((bf16[144,1024]{1,0:T(8,128)(2,1)S(1)}, bf16[144,1024]{1,0:T(8,128)(2,1)S(1)}, u32[]{:S(2)}, u32[]{:S(2)}) %collective-permute-start.6) | collective-permute-done | bytes 294944 | tf_op jit(solution)/shard_map/ppermute | solution.py:33
  35.3 3.7 %collective-permute-done.4.refs_2_.refs_4_ = bf16[288,1024]{1,0:T(8,128)(2,1)S(1)} collective-permute-done((bf16[288,1024]{1,0:T(8,128)(2,1)S(1)}, bf16[288,1024]{1,0:T(8,128)(2,1)S(1)}, u32[]{:S(2)}, u32[]{:S(2)}) %collective-permute-start.4) | collective-permute-done | bytes 589856 | tf_op jit(solution)/shard_map/ppermute | solution.py:33
  39.0 1.2 %collective-permute-start.10 = (bf16[288,1024]{1,0:T(8,128)(2,1)S(1)}, bf16[288,1024]{1,0:T(8,128)(2,1)S(1)}, u32[]{:S(2)}, u32[]{:S(2)}) collective-permute-start(bf16[288,1024]{1,0:T(8,128)(2,1)S(1)} %collective-permute-done.5.refs_7_.refs_11_), channel_id=1, source_target_pairs={{0,1},{1,0},{2,3},{3,2},{4,5},{5,4},{6,7},{7,6},{8,9},{9,8},{10,11... | collective-permute-start | bytes 1769480 | tf_op jit(solution)/shard_map/ppermute | solution.py:33
  40.2 2.3 %collective-permute-start.11 = (bf16[144,1024]{1,0:T(8,128)(2,1)S(1)}, bf16[144,1024]{1,0:T(8,128)(2,1)S(1)}, u32[]{:S(2)}, u32[]{:S(2)}) collective-permute-start(bf16[144,1024]{1,0:T(8,128)(2,1)S(1)} %collective-permute-done.6.refs_15_), channel_id=1, source_target_pairs={{0,1},{1,0},{2,3},{3,2},{4,5},{5,4},{6,7},{7,6},{8,9},{9,8},{10,11... | collective-permute-start | bytes 884744 | tf_op jit(solution)/shard_map/ppermute | solution.py:33
  43.1 1.2 %collective-permute-start.9 = (bf16[128,1024]{1,0:T(8,128)(2,1)S(1)}, bf16[128,1024]{1,0:T(8,128)(2,1)}, u32[]{:S(2)}, u32[]{:S(2)}) collective-permute-start(bf16[128,1024]{1,0:T(8,128)(2,1)S(1)} %get-tuple-element.69), channel_id=1, source_target_pairs={{0,16},{1,17},{2,18},{3,19},{4,20},{5,21},{6,22},{7,23},{8,24},{9,... | collective-permute-start | bytes 786440 | tf_op jit(solution)/shard_map/ppermute | solution.py:33
  44.3 5.9 %collective-permute-done.8.refs_9_.refs_13_ = bf16[128,1024]{1,0:T(8,128)(2,1)S(1)} collective-permute-done((bf16[128,1024]{1,0:T(8,128)(2,1)S(1)}, bf16[128,1024]{1,0:T(8,128)(2,1)S(1)}, u32[]{:S(2)}, u32[]{:S(2)}) %collective-permute-start.8) | collective-permute-done | bytes 262176 | tf_op jit(solution)/shard_map/ppermute | solution.py:33
  50.2 2.1 %collective-permute-done.9.refs_17_ = bf16[128,1024]{1,0:T(8,128)(2,1)} collective-permute-done((bf16[128,1024]{1,0:T(8,128)(2,1)S(1)}, bf16[128,1024]{1,0:T(8,128)(2,1)}, u32[]{:S(2)}, u32[]{:S(2)}) %collective-permute-start.9) | collective-permute-done | bytes 262176 | tf_op jit(solution)/shard_map/ppermute | solution.py:33
  54.7 3.1 %collective-permute-start.16 = (bf16[128,1024]{1,0:T(8,128)(2,1)}, bf16[128,1024]{1,0:T(8,128)(2,1)}, u32[]{:S(2)}, u32[]{:S(2)}) collective-permute-start(bf16[128,1024]{1,0:T(8,128)(2,1)} %pad_maximum_fusion.1), channel_id=1, source_target_pairs={{32,16},{96,80},{160,144},{224,208}} | collective-permute-start | bytes 786440 | tf_op jit(solution)/shard_map/ppermute | solution.py:33
  57.9 2.0 %collective-permute-start.17 = (bf16[128,1024]{1,0:T(8,128)(2,1)}, bf16[128,1024]{1,0:T(8,128)(2,1)}, u32[]{:S(2)}, u32[]{:S(2)}) collective-permute-start(bf16[128,1024]{1,0:T(8,128)(2,1)} %pad_maximum_fusion.1), channel_id=1, source_target_pairs={{32,0},{96,64},{160,128},{224,192}} | collective-permute-start | bytes 786440 | tf_op jit(solution)/shard_map/ppermute | solution.py:33
  61.4 4.2 %collective-permute-done.17 = bf16[128,1024]{1,0:T(8,128)(2,1)} collective-permute-done((bf16[128,1024]{1,0:T(8,128)(2,1)}, bf16[128,1024]{1,0:T(8,128)(2,1)}, u32[]{:S(2)}, u32[]{:S(2)}) %collective-permute-start.17) | collective-permute-done | bytes 262176 | tf_op jit(solution)/shard_map/ppermute | solution.py:33
  65.6 3.3 %collective-permute-done.13.refs_18_ = bf16[128,1024]{1,0:T(8,128)(2,1)} collective-permute-done((bf16[128,1024]{1,0:T(8,128)(2,1)}, bf16[128,1024]{1,0:T(8,128)(2,1)}, u32[]{:S(2)}, u32[]{:S(2)}) %collective-permute-start.13) | collective-permute-done | bytes 262176 | tf_op jit(solution)/shard_map/ppermute | solution.py:33
  69.9 1.5 %collective-permute-start.19 = (bf16[48,1024]{1,0:T(8,128)(2,1)S(1)}, bf16[48,1024]{1,0:T(8,128)(2,1)S(1)}, u32[]{:S(2)}, u32[]{:S(2)}) collective-permute-start(bf16[48,1024]{1,0:T(8,128)(2,1)S(1)} %fusion.3), channel_id=1, source_target_pairs={{32,18},{33,17},{34,20},{36,22},{38,24},{43,27},{45,29},{47,31},{9... | collective-permute-start | bytes 294920 | tf_op jit(solution)/shard_map/ppermute | solution.py:33
  71.4 1.8 %collective-permute-start.18 = (bf16[128,1024]{1,0:T(8,128)(2,1)S(1)}, bf16[128,1024]{1,0:T(8,128)(2,1)S(1)}, u32[]{:S(2)}, u32[]{:S(2)}) collective-permute-start(bf16[128,1024]{1,0:T(8,128)(2,1)S(1)} %collective-permute-done.8.refs_9_.refs_13_), channel_id=1, source_target_pairs={{0,16},{1,17},{2,18},{3,19},{4,20},{5,21},{6,22},{7,23},{8,24},{9,... | collective-permute-start | bytes 786440 | tf_op jit(solution)/shard_map/ppermute | solution.py:33
  73.2 3.7 %early.1 = (f32[4,512]{1,0:T(4,128)S(1)}, f32[4,512]{1,0:T(4,128)S(1)}) custom-call(s32[2]{0:T(128)S(1)} %pad_add_fusion.1.refs_0_, bf16[144,1024]{1,0:T(8,128)(2,1)S(1)} %pad_maximum_fusion.refs_1_.refs_5_.refs_3_.refs_9_, bf16[288,1024]{1,0:T(8,128)(2,1)S(1)} %collective-permute-done.4.refs_2_.refs_4_, ...), custom_call_target="tpu_custom_call" | custom-call | flops 5637144576 | bytes 11796480 | tf_op jit(solution)/shard_map/early/pallas_call | solution.py:223
  76.9 1.9 %collective-permute-done.18.refs_21_ = bf16[128,1024]{1,0:T(8,128)(2,1)S(1)} collective-permute-done((bf16[128,1024]{1,0:T(8,128)(2,1)S(1)}, bf16[128,1024]{1,0:T(8,128)(2,1)S(1)}, u32[]{:S(2)}, u32[]{:S(2)}) %collective-permute-start.18) | collective-permute-done | bytes 262176 | tf_op jit(solution)/shard_map/ppermute | solution.py:33
  82.6 5.4 %late.1 = (f32[4,512]{1,0:T(4,128)S(1)}, f32[4,512]{1,0:T(4,128)S(1)}, f32[4,1152]{1,0:T(4,128)S(1)}, f32[4,128]{1,0:T(4,128)S(1)}) custom-call(s32[2]{0:T(128)S(1)} %pad_add_fusion.1.refs_0_, f32[4,512]{1,0:T(4,128)S(1)} %get-tuple-element.52.refs_1_, f32[4,512]{1,0:T(4,128)S(1)} %get-tuple-element.53.refs_2_, ...), custom_call_target="tpu_custom_call" | custom-call | flops 16609443840 | bytes 22216704 | tf_op jit(solution)/shard_map/late/pallas_call | solution.py:223
  90.0 1.3 %collective-permute-start.26 = (f32[4,128]{1,0:T(4,128)S(1)}, f32[4,128]{1,0:T(4,128)S(1)}, u32[]{:S(2)}, u32[]{:S(2)}) collective-permute-start(f32[4,128]{1,0:T(4,128)S(1)} %slice_add_fusion.2), channel_id=1, source_target_pairs={{0,32},{64,96},{128,160},{192,224}} | collective-permute-start | bytes 6152 | tf_op jit(solution)/shard_map/ppermute | solution.py:33
  91.3 1.3 %collective-permute-start.27 = (f32[4,128]{1,0:T(4,128)S(1)}, f32[4,128]{1,0:T(4,128)S(1)}, u32[]{:S(2)}, u32[]{:S(2)}) collective-permute-start(f32[4,128]{1,0:T(4,128)S(1)} %slice_add_fusion.2), channel_id=1, source_target_pairs={{16,32},{80,96},{144,160},{208,224}} | collective-permute-start | bytes 6152 | tf_op jit(solution)/shard_map/ppermute | solution.py:33
  92.6 4.4 %collective-permute-done.26 = f32[4,128]{1,0:T(4,128)S(1)} collective-permute-done((f32[4,128]{1,0:T(4,128)S(1)}, f32[4,128]{1,0:T(4,128)S(1)}, u32[]{:S(2)}, u32[]{:S(2)}) %collective-permute-start.26) | collective-permute-done | bytes 2080 | tf_op jit(solution)/shard_map/ppermute | solution.py:33
  97.7 1.5 %collective-permute-start.29 = (f32[4,4,128]{2,1,0:T(4,128)S(1)}, f32[4,4,128]{2,1,0:T(4,128)S(1)}, u32[]{:S(2)}, u32[]{:S(2)}) collective-permute-start(f32[4,4,128]{2,1,0:T(4,128)S(1)} %pad_add_fusion), channel_id=1, source_target_pairs={{0,64},{1,65},{2,66},{3,67},{4,68},{5,69},{6,70},{7,71},{8,72},{9,... | collective-permute-start | bytes 24584 | tf_op jit(solution)/shard_map/ppermute | solution.py:33
  99.3 1.7 %collective-permute-start.30 = (f32[4,4,128]{2,1,0:T(4,128)S(1)}, f32[4,4,128]{2,1,0:T(4,128)S(1)}, u32[]{:S(2)}, u32[]{:S(2)}) collective-permute-start(f32[4,4,128]{2,1,0:T(4,128)S(1)} %pad_add_fusion), channel_id=1, source_target_pairs={{0,192},{1,193},{2,194},{3,195},{4,196},{5,197},{6,198},{7,199},{8... | collective-permute-start | bytes 24584 | tf_op jit(solution)/shard_map/ppermute | solution.py:33
  101.0 1.4 %collective-permute-done.28 = f32[4,4,128]{2,1,0:T(4,128)S(1)} collective-permute-done((f32[4,4,128]{2,1,0:T(4,128)S(1)}, f32[4,4,128]{2,1,0:T(4,128)S(1)}, u32[]{:S(2)}, u32[]{:S(2)}) %collective-permute-start.28) | collective-permute-done | bytes 8224 | tf_op jit(solution)/shard_map/ppermute | solution.py:33
  (89 shorter events, 16.8 us)
Async XLA Ops:
  7.3 10.8 %collective-permute-start = (f16[128,1024]{1,0:T(8,128)(2,1)S(1)}, f16[128,1024]{1,0:T(8,128)(2,1)S(1)}, u32[]{:S(2)}, u32[]{:S(2)}) collective-permute-start(f16[128,1024]{1,0:T(8,128)(2,1)S(1)} %bitcast.38), channel_id=1, source_target_pairs={{0,128},{1,129},{2,130},{3,131},{4,132},{5,133},{6,134},{7,135},{8... | collective-permute-start | bytes 786440 | tf_op jit(solution)/shard_map/ppermute | solution.py:33
  10.5 12.0 %collective-permute-start.1 = (f16[128,1024]{1,0:T(8,128)(2,1)S(1)}, f16[128,1024]{1,0:T(8,128)(2,1)S(1)}, u32[]{:S(2)}, u32[]{:S(2)}) collective-permute-start(f16[128,1024]{1,0:T(8,128)(2,1)S(1)} %bitcast.37), channel_id=1, source_target_pairs={{0,64},{1,65},{2,66},{3,67},{4,68},{5,69},{6,70},{7,71},{8,72},{9,... | collective-permute-start | bytes 786440 | tf_op jit(solution)/shard_map/ppermute | solution.py:33
  11.2 11.7 %collective-permute-start.2 = (f16[128,1024]{1,0:T(8,128)(2,1)S(1)}, f16[128,1024]{1,0:T(8,128)(2,1)S(1)}, u32[]{:S(2)}, u32[]{:S(2)}) collective-permute-start(f16[128,1024]{1,0:T(8,128)(2,1)S(1)} %bitcast.36), channel_id=1, source_target_pairs={{0,192},{1,193},{2,194},{3,195},{4,196},{5,197},{6,198},{7,199},{8... | collective-permute-start | bytes 786440 | tf_op jit(solution)/shard_map/ppermute | solution.py:33
  23.3 1.7 %collective-permute-start.3 = (bf16[144,1024]{1,0:T(8,128)(2,1)S(1)}, bf16[144,1024]{1,0:T(8,128)(2,1)S(1)}, u32[]{:S(2)}, u32[]{:S(2)}) collective-permute-start(bf16[144,1024]{1,0:T(8,128)(2,1)S(1)} %pad_maximum_fusion.refs_1_.refs_5_.refs_3_.refs_9_), channel_id=1, source_target_pairs={{0,1},{1,0},{2,3},{3,2},{4,5},{5,4},{6,7},{7,6},{8,9},{9,8},{10,11... | collective-permute-start | bytes 884744 | tf_op jit(solution)/shard_map/ppermute | solution.py:33
  25.2 13.8 %copy-start.4 = (bf16[288,1024]{1,0:T(8,128)(2,1)}, bf16[288,1024]{1,0:T(8,128)(2,1)S(1)}, u32[]{:S(2)}) copy-start(bf16[288,1024]{1,0:T(8,128)(2,1)S(1)} %maximum_select_fusion) | copy-start | bytes 1769476
  25.2 13.8 %collective-permute-start.4 = (bf16[288,1024]{1,0:T(8,128)(2,1)S(1)}, bf16[288,1024]{1,0:T(8,128)(2,1)S(1)}, u32[]{:S(2)}, u32[]{:S(2)}) collective-permute-start(bf16[288,1024]{1,0:T(8,128)(2,1)S(1)} %maximum_select_fusion), channel_id=1, source_target_pairs={{0,2},{1,15},{2,4},{3,1},{4,6},{5,3},{6,8},{7,5},{8,10},{9,7},{10,... | collective-permute-start | bytes 1769480 | tf_op jit(solution)/shard_map/ppermute | solution.py:33
  27.2 11.8 %collective-permute-start.5 = (bf16[288,1024]{1,0:T(8,128)(2,1)S(1)}, bf16[288,1024]{1,0:T(8,128)(2,1)S(1)}, u32[]{:S(2)}, u32[]{:S(2)}) collective-permute-start(bf16[288,1024]{1,0:T(8,128)(2,1)S(1)} %maximum_select_fusion), channel_id=1, source_target_pairs={{0,64},{1,193},{2,66},{3,195},{4,68},{5,197},{6,70},{7,199},{8,72}... | collective-permute-start | bytes 1769480 | tf_op jit(solution)/shard_map/ppermute | solution.py:33
  28.5 6.7 %collective-permute-start.6 = (bf16[144,1024]{1,0:T(8,128)(2,1)S(1)}, bf16[144,1024]{1,0:T(8,128)(2,1)S(1)}, u32[]{:S(2)}, u32[]{:S(2)}) collective-permute-start(bf16[144,1024]{1,0:T(8,128)(2,1)S(1)} %pad_maximum_fusion.refs_1_.refs_5_.refs_3_.refs_9_), channel_id=1, source_target_pairs={{0,16},{1,17},{2,18},{3,19},{4,20},{5,21},{6,22},{7,23},{8,24},{9,... | collective-permute-start | bytes 884744 | tf_op jit(solution)/shard_map/ppermute | solution.py:33
  39.0 14.0 %collective-permute-start.10 = (bf16[288,1024]{1,0:T(8,128)(2,1)S(1)}, bf16[288,1024]{1,0:T(8,128)(2,1)S(1)}, u32[]{:S(2)}, u32[]{:S(2)}) collective-permute-start(bf16[288,1024]{1,0:T(8,128)(2,1)S(1)} %collective-permute-done.5.refs_7_.refs_11_), channel_id=1, source_target_pairs={{0,1},{1,0},{2,3},{3,2},{4,5},{5,4},{6,7},{7,6},{8,9},{9,8},{10,11... | collective-permute-start | bytes 1769480 | tf_op jit(solution)/shard_map/ppermute | solution.py:33
  40.1 12.9 %collective-permute-start.7 = (bf16[288,1024]{1,0:T(8,128)(2,1)S(1)}, bf16[288,1024]{1,0:T(8,128)(2,1)S(1)}, u32[]{:S(2)}, u32[]{:S(2)}) collective-permute-start(bf16[288,1024]{1,0:T(8,128)(2,1)S(1)} %collective-permute-done.4.refs_2_.refs_4_), channel_id=1, source_target_pairs={{0,2},{1,15},{2,4},{3,1},{4,6},{5,3},{6,8},{7,5},{8,10},{9,7},{10,... | collective-permute-start | bytes 1769480 | tf_op jit(solution)/shard_map/ppermute | solution.py:33
  40.2 12.1 %collective-permute-start.11 = (bf16[144,1024]{1,0:T(8,128)(2,1)S(1)}, bf16[144,1024]{1,0:T(8,128)(2,1)S(1)}, u32[]{:S(2)}, u32[]{:S(2)}) collective-permute-start(bf16[144,1024]{1,0:T(8,128)(2,1)S(1)} %collective-permute-done.6.refs_15_), channel_id=1, source_target_pairs={{0,1},{1,0},{2,3},{3,2},{4,5},{5,4},{6,7},{7,6},{8,9},{9,8},{10,11... | collective-permute-start | bytes 884744 | tf_op jit(solution)/shard_map/ppermute | solution.py:33
  42.6 7.7 %collective-permute-start.8 = (bf16[128,1024]{1,0:T(8,128)(2,1)S(1)}, bf16[128,1024]{1,0:T(8,128)(2,1)S(1)}, u32[]{:S(2)}, u32[]{:S(2)}) collective-permute-start(bf16[128,1024]{1,0:T(8,128)(2,1)S(1)} %get-tuple-element.70), channel_id=1, source_target_pairs={{0,64},{1,193},{2,66},{3,195},{4,68},{5,197},{6,70},{7,199},{8,72}... | collective-permute-start | bytes 786440 | tf_op jit(solution)/shard_map/ppermute | solution.py:33
  43.1 9.2 %collective-permute-start.9 = (bf16[128,1024]{1,0:T(8,128)(2,1)S(1)}, bf16[128,1024]{1,0:T(8,128)(2,1)}, u32[]{:S(2)}, u32[]{:S(2)}) collective-permute-start(bf16[128,1024]{1,0:T(8,128)(2,1)S(1)} %get-tuple-element.69), channel_id=1, source_target_pairs={{0,16},{1,17},{2,18},{3,19},{4,20},{5,21},{6,22},{7,23},{8,24},{9,... | collective-permute-start | bytes 786440 | tf_op jit(solution)/shard_map/ppermute | solution.py:33
  53.9 15.1 %collective-permute-start.12 = (bf16[288,1024]{1,0:T(8,128)(2,1)S(1)}, bf16[288,1024]{1,0:T(8,128)(2,1)S(1)}, u32[]{:S(2)}, u32[]{:S(2)}) collective-permute-start(bf16[288,1024]{1,0:T(8,128)(2,1)S(1)} %collective-permute-done.7.refs_3_.refs_5_), channel_id=1, source_target_pairs={{0,2},{1,15},{2,4},{3,1},{4,6},{5,3},{6,8},{7,5},{8,10},{9,7},{10,... | collective-permute-start | bytes 1769480 | tf_op jit(solution)/shard_map/ppermute | solution.py:33
  54.7 6.6 %collective-permute-start.16 = (bf16[128,1024]{1,0:T(8,128)(2,1)}, bf16[128,1024]{1,0:T(8,128)(2,1)}, u32[]{:S(2)}, u32[]{:S(2)}) collective-permute-start(bf16[128,1024]{1,0:T(8,128)(2,1)} %pad_maximum_fusion.1), channel_id=1, source_target_pairs={{32,16},{96,80},{160,144},{224,208}} | collective-permute-start | bytes 786440 | tf_op jit(solution)/shard_map/ppermute | solution.py:33
  57.9 7.8 %collective-permute-start.17 = (bf16[128,1024]{1,0:T(8,128)(2,1)}, bf16[128,1024]{1,0:T(8,128)(2,1)}, u32[]{:S(2)}, u32[]{:S(2)}) collective-permute-start(bf16[128,1024]{1,0:T(8,128)(2,1)} %pad_maximum_fusion.1), channel_id=1, source_target_pairs={{32,0},{96,64},{160,128},{224,192}} | collective-permute-start | bytes 786440 | tf_op jit(solution)/shard_map/ppermute | solution.py:33
  60.6 8.4 %collective-permute-start.13 = (bf16[128,1024]{1,0:T(8,128)(2,1)}, bf16[128,1024]{1,0:T(8,128)(2,1)}, u32[]{:S(2)}, u32[]{:S(2)}) collective-permute-start(bf16[128,1024]{1,0:T(8,128)(2,1)} %slice.107), channel_id=1, source_target_pairs={{0,16},{1,17},{2,18},{3,19},{4,20},{5,21},{6,22},{7,23},{8,24},{9,... | collective-permute-start | bytes 786440 | tf_op jit(solution)/shard_map/ppermute | solution.py:33
  60.6 8.4 %collective-permute-start.14 = (bf16[128,1024]{1,0:T(8,128)(2,1)}, bf16[128,1024]{1,0:T(8,128)(2,1)}, u32[]{:S(2)}, u32[]{:S(2)}) collective-permute-start(bf16[128,1024]{1,0:T(8,128)(2,1)} %collective-permute-done.9.refs_17_), channel_id=1, source_target_pairs={{0,1},{1,0},{2,3},{3,2},{4,5},{5,4},{6,7},{7,6},{8,9},{9,8},{10,11... | collective-permute-start | bytes 786440 | tf_op jit(solution)/shard_map/ppermute | solution.py:33
  61.3 7.6 %collective-permute-start.15 = (bf16[128,1024]{1,0:T(8,128)(2,1)S(1)}, bf16[128,1024]{1,0:T(8,128)(2,1)}, u32[]{:S(2)}, u32[]{:S(2)}) collective-permute-start(bf16[128,1024]{1,0:T(8,128)(2,1)S(1)} %collective-permute-done.8.refs_9_.refs_13_), channel_id=1, source_target_pairs={{0,1},{1,0},{2,3},{3,2},{4,5},{5,4},{6,7},{7,6},{8,9},{9,8},{10,11... | collective-permute-start | bytes 786440 | tf_op jit(solution)/shard_map/ppermute | solution.py:33
  69.9 7.0 %collective-permute-start.19 = (bf16[48,1024]{1,0:T(8,128)(2,1)S(1)}, bf16[48,1024]{1,0:T(8,128)(2,1)S(1)}, u32[]{:S(2)}, u32[]{:S(2)}) collective-permute-start(bf16[48,1024]{1,0:T(8,128)(2,1)S(1)} %fusion.3), channel_id=1, source_target_pairs={{32,18},{33,17},{34,20},{36,22},{38,24},{43,27},{45,29},{47,31},{9... | collective-permute-start | bytes 294920 | tf_op jit(solution)/shard_map/ppermute | solution.py:33
  71.4 7.5 %collective-permute-start.18 = (bf16[128,1024]{1,0:T(8,128)(2,1)S(1)}, bf16[128,1024]{1,0:T(8,128)(2,1)S(1)}, u32[]{:S(2)}, u32[]{:S(2)}) collective-permute-start(bf16[128,1024]{1,0:T(8,128)(2,1)S(1)} %collective-permute-done.8.refs_9_.refs_13_), channel_id=1, source_target_pairs={{0,16},{1,17},{2,18},{3,19},{4,20},{5,21},{6,22},{7,23},{8,24},{9,... | collective-permute-start | bytes 786440 | tf_op jit(solution)/shard_map/ppermute | solution.py:33
  73.2 9.3 %collective-permute-start.20 = (bf16[144,1024]{1,0:T(8,128)(2,1)S(1)}, bf16[144,1024]{1,0:T(8,128)(2,1)S(1)}, u32[]{:S(2)}, u32[]{:S(2)}) collective-permute-start(bf16[144,1024]{1,0:T(8,128)(2,1)S(1)} %slice_select_fusion), channel_id=1, source_target_pairs={{0,2},{1,15},{2,4},{3,1},{4,6},{5,3},{6,8},{7,5},{8,10},{9,7},{10,... | collective-permute-start | bytes 884744 | tf_op jit(solution)/shard_map/ppermute | solution.py:33
  80.0 1.3 %collective-permute-start.23 = (bf16[128,1024]{1,0:T(8,128)(2,1)S(1)}, bf16[128,1024]{1,0:T(8,128)(2,1)S(1)}, u32[]{:S(2)}, u32[]{:S(2)}) collective-permute-start(bf16[128,1024]{1,0:T(8,128)(2,1)S(1)} %add.132), channel_id=1, source_target_pairs={{0,1},{16,17},{64,65},{80,81},{128,129},{144,145},{192,193},{208,2... | collective-permute-start | bytes 786440 | tf_op jit(solution)/shard_map/ppermute | solution.py:33
  80.6 1.8 %collective-permute-start.21 = (bf16[128,1024]{1,0:T(8,128)(2,1)}, bf16[128,1024]{1,0:T(8,128)(2,1)S(1)}, u32[]{:S(2)}, u32[]{:S(2)}) collective-permute-start(bf16[128,1024]{1,0:T(8,128)(2,1)} %collective-permute-done.13.refs_18_), channel_id=1, source_target_pairs={{0,1},{1,0},{2,3},{3,2},{4,5},{5,4},{6,7},{7,6},{8,9},{9,8},{10,11... | collective-permute-start | bytes 786440 | tf_op jit(solution)/shard_map/ppermute | solution.py:33
  80.7 1.9 %collective-permute-start.22 = (bf16[128,1024]{1,0:T(8,128)(2,1)S(1)}, bf16[128,1024]{1,0:T(8,128)(2,1)S(1)}, u32[]{:S(2)}, u32[]{:S(2)}) collective-permute-start(bf16[128,1024]{1,0:T(8,128)(2,1)S(1)} %collective-permute-done.18.refs_21_), channel_id=1, source_target_pairs={{0,1},{1,0},{2,3},{3,2},{4,5},{5,4},{6,7},{7,6},{8,9},{9,8},{10,11... | collective-permute-start | bytes 786440 | tf_op jit(solution)/shard_map/ppermute | solution.py:33
  88.1 1.3 %collective-permute-start.24 = (f32[4,1152]{1,0:T(4,128)S(1)}, f32[4,1152]{1,0:T(4,128)S(1)}, u32[]{:S(2)}, u32[]{:S(2)}) collective-permute-start(f32[4,1152]{1,0:T(4,128)S(1)} %get-tuple-element.62), channel_id=1, source_target_pairs={{0,1},{1,0},{2,3},{3,2},{4,5},{5,4},{6,7},{7,6},{8,9},{9,8},{10,11... | collective-permute-start | bytes 55304 | tf_op jit(solution)/shard_map/ppermute | solution.py:33
  89.3 7.8 %collective-permute-start.25 = (f32[4,512]{1,0:T(4,128)S(1)}, f32[4,512]{1,0:T(4,128)S(1)}, u32[]{:S(2)}, u32[]{:S(2)}) collective-permute-start(f32[4,512]{1,0:T(4,128)S(1)} %slice_add_fusion), channel_id=1, source_target_pairs={{0,16},{1,17},{2,18},{3,19},{4,20},{5,21},{6,22},{7,23},{8,24},{9,... | collective-permute-start | bytes 24584 | tf_op jit(solution)/shard_map/ppermute | solution.py:33
  90.0 7.0 %collective-permute-start.26 = (f32[4,128]{1,0:T(4,128)S(1)}, f32[4,128]{1,0:T(4,128)S(1)}, u32[]{:S(2)}, u32[]{:S(2)}) collective-permute-start(f32[4,128]{1,0:T(4,128)S(1)} %slice_add_fusion.2), channel_id=1, source_target_pairs={{0,32},{64,96},{128,160},{192,224}} | collective-permute-start | bytes 6152 | tf_op jit(solution)/shard_map/ppermute | solution.py:33
  91.3 5.7 %collective-permute-start.27 = (f32[4,128]{1,0:T(4,128)S(1)}, f32[4,128]{1,0:T(4,128)S(1)}, u32[]{:S(2)}, u32[]{:S(2)}) collective-permute-start(f32[4,128]{1,0:T(4,128)S(1)} %slice_add_fusion.2), channel_id=1, source_target_pairs={{16,32},{80,96},{144,160},{208,224}} | collective-permute-start | bytes 6152 | tf_op jit(solution)/shard_map/ppermute | solution.py:33
  97.1 5.2 %collective-permute-start.28 = (f32[4,4,128]{2,1,0:T(4,128)S(1)}, f32[4,4,128]{2,1,0:T(4,128)S(1)}, u32[]{:S(2)}, u32[]{:S(2)}) collective-permute-start(f32[4,4,128]{2,1,0:T(4,128)S(1)} %pad_add_fusion), channel_id=1, source_target_pairs={{0,128},{1,129},{2,130},{3,131},{4,132},{5,133},{6,134},{7,135},{8... | collective-permute-start | bytes 24584 | tf_op jit(solution)/shard_map/ppermute | solution.py:33
  97.7 4.9 %collective-permute-start.29 = (f32[4,4,128]{2,1,0:T(4,128)S(1)}, f32[4,4,128]{2,1,0:T(4,128)S(1)}, u32[]{:S(2)}, u32[]{:S(2)}) collective-permute-start(f32[4,4,128]{2,1,0:T(4,128)S(1)} %pad_add_fusion), channel_id=1, source_target_pairs={{0,64},{1,65},{2,66},{3,67},{4,68},{5,69},{6,70},{7,71},{8,72},{9,... | collective-permute-start | bytes 24584 | tf_op jit(solution)/shard_map/ppermute | solution.py:33
  99.3 3.7 %collective-permute-start.30 = (f32[4,4,128]{2,1,0:T(4,128)S(1)}, f32[4,4,128]{2,1,0:T(4,128)S(1)}, u32[]{:S(2)}, u32[]{:S(2)}) collective-permute-start(f32[4,4,128]{2,1,0:T(4,128)S(1)} %pad_add_fusion), channel_id=1, source_target_pairs={{0,192},{1,193},{2,194},{3,195},{4,196},{5,197},{6,198},{7,199},{8... | collective-permute-start | bytes 24584 | tf_op jit(solution)/shard_map/ppermute | solution.py:33
  (6 other events, 35.7 us)

commit v11 on v10

--- a/solution.py
+++ b/solution.py
@@ -284,12 +284,12 @@
     z2 = permute(z1, same_core)
     y2 = permute(jnp.where(c == 0, y1[TAG:tagged], y1[tagged + TAG :]), y_way)
     xa = permute(y1[TAG:tagged], swap_x)
-    y1_t = permute(y1, swap_core)
     x1_t = permute(x1, swap_core)
-    z1, z2, y2, xa, y1_t, x1_t, y1 = fence(z1, z2, y2, xa, y1_t, x1_t, y1)
+    z1, z2, y2, xa, y1, x1_t = fence(z1, z2, y2, xa, y1, x1_t)
 
     z3 = permute(z2, same_core)
     xb = permute(y1[tagged + TAG :], swap_x)
+    y1_t = permute(y1, swap_core)
     head = TAG + PIECE
     odd_rows = jnp.concatenate([own[TAG:head], y1_t[TAG:head], y2[:PIECE], y1[TAG:head]], axis=0)
     at_start = lambda y, x, z, c: z == 0 and c == 0
@@ -303,7 +303,9 @@
     ]
     y2_t = permute(y2, swap_core)
     xa_t = permute(xa, swap_core)
-    z2, z3, y2, xb, xa_t, y2_t, *odd_at = fence(z2, z3, y2, xb, xa_t, y2_t, *odd_at)
+    z2, z3, y2, xb, y1_t, y2_t, xa_t, odd_at[0] = fence(
+        z2, z3, y2, xb, y1_t, y2_t, xa_t, odd_at[0]
+    )
 
     z4 = permute(jnp.where(c == 0, z3[:tagged], z3[tagged:]), same_core)
     held = [chip, z1, z2, z3, z3, z3, z2, z1]

time: 104 us -> 103 us (level)
  waiting for transfers between devices: 43.6 us -> 37.6 us
  starting transfers between devices: 33.5 us -> 38.1 us
    ppermute x31, waiting for transfers between devices: 43.6 us -> 37.6 us  [permute(): return lax.ppermute(value, AXES, pairs)]
    ppermute x31, starting transfers between devices: 33.5 us -> 38.1 us  [permute(): return lax.ppermute(value, AXES, pairs)]
  transfers between devices with their start and end apart: 31 -> 31, of which waited for: 19 -> 16; matrix products, arithmetic and copies ran while one was open for 6% -> 7% of each run, Pallas kernels for 4% -> 4%
where the time goes in v11:
time: 103 us; the launch traced here: 102 us
  starting transfers between devices  38.1 us (37%)
  waiting for transfers between devices  37.6 us (37%)
  Pallas kernels  14.6 us (14%)
  other arithmetic  7.85 us (8%)
  local copies, waits for them, and re-layouts  3.84 us (4%)
    ppermute x31, starting transfers between devices, permute(): return lax.ppermute(value, AXES, pairs)  38.1 us
    ppermute x31, waiting for transfers between devices, permute(): return lax.ppermute(value, AXES, pairs)  37.6 us
    pallas_call x2, Pallas kernels, pair_sums(): pl.pallas_call(functools.partial(pair_kernel, col_cuts=tuple(col_cuts), n...  9.16 us
    pallas_call x1, Pallas kernels, raw_partial(): pl.pallas_call(raw_kernel, grid=(feats // width,), in_specs=[pl.BlockSpec...  5.48 us
    convert_element_type x1, other arithmetic, shards(): tag = tag.astype(jnp.bfloat16)  2.59 us
  transfers between devices with their start and end apart: 31, of which 16 were waited for; matrix products, arithmetic and copies ran while one was open for 7% of the time, Pallas kernels for 4%

profile of v11, /device:TPU:4, one launch (start us, length us, event | category | flops | bytes accessed | tf_op | source)
XLA Modules:
  0.0 102.4 jit_solution(16534393074178567872)
XLA Ops:
  0.0 5.5 %raw.1 = f32[512,1024]{1,0:T(8,128)} custom-call(s32[8,11]{1,0:T(8,128)} %bitcast.41, bf16[1584,512]{1,0:T(8,128)(2,1)} %bitcast.35, bf16[1584,1024]{1,0:T(8,128)(2,1)} %geometry.1), custom_call_target="tpu_custom_call" | custom-call | flops 1660944384 | bytes 8388608 | tf_op jit(solution)/shard_map/raw/pallas_call | solution.py:84
  5.5 1.7 %constant_dynamic-slice_fusion.1 = (f32[4,1,32,1024]{3,2,1,0:T(8,128)S(1)}, f16[4,1,32,1024]{3,2,0,1:T(8,128)(2,1)S(1)}, f16[4,1,32,1024]{3,2,0,1:T(8,128)(2,1)S(1)}, f16[4,1,32,1024]{3,2,0,1:T(8,128)(2,1)S(1)}) fusion(f32[4,4,32,1024]{3,2,1,0:T(8,128)} %bitcast.34, s32[]{:T(128)S(6)} %select_n.180, s32[]{:T(128)S(6)} %select_n.184, s32[]{:T(128)S(6)} %select_n.182, ...), kind=kLoop, calls=%fused_computation.43 | loop fusion | flops 393216 | bytes 3407888 | tf_op jit(solution)/shard_map/jit(dynamic_index_in_dim)/dynamic_slice | solution.py:264
  7.2 3.3 %collective-permute-start = (f16[128,1024]{1,0:T(8,128)(2,1)S(1)}, f16[128,1024]{1,0:T(8,128)(2,1)S(1)}, u32[]{:S(2)}, u32[]{:S(2)}) collective-permute-start(f16[128,1024]{1,0:T(8,128)(2,1)S(1)} %bitcast.38), channel_id=1, source_target_pairs={{0,128},{1,129},{2,130},{3,131},{4,132},{5,133},{6,134},{7,135},{8... | collective-permute-start | bytes 786440 | tf_op jit(solution)/shard_map/ppermute | solution.py:33
  11.2 2.6 %collective-permute-start.2 = (f16[128,1024]{1,0:T(8,128)(2,1)S(1)}, f16[128,1024]{1,0:T(8,128)(2,1)S(1)}, u32[]{:S(2)}, u32[]{:S(2)}) collective-permute-start(f16[128,1024]{1,0:T(8,128)(2,1)S(1)} %bitcast.36), channel_id=1, source_target_pairs={{0,192},{1,193},{2,194},{3,195},{4,196},{5,197},{6,198},{7,199},{8... | collective-permute-start | bytes 786440 | tf_op jit(solution)/shard_map/ppermute | solution.py:33
  14.5 2.6 %select_convert_fusion = bf16[16,1024]{1,0:T(8,128)(2,1)S(1)} fusion(bf16[]{:T(256)} %bitcast.5, bf16[]{:T(256)} %bitcast.4, bf16[]{:T(256)} %bitcast.3, bf16[]{:T(256)} %bitcast.2, s32[1024]{0:T(1024)S(1)} %get-tuple-element.75, s32[1024]{0:T(1024)S(1)} %get-tuple-element.76, pred[16]{0:T(512)(128)(4,1)S(1)} %iota_compare_fusion, pred[1024]{0:T(1024)(128)(4,1)S(1)} %fusion.13), kind=kLoop, calls=%fused_computation.16 | loop fusion | flops 163840 | bytes 42008 | tf_op jit(solution)/shard_map/convert_element_type | solution.py:259
  18.1 4.4 %collective-permute-done.1 = f16[128,1024]{1,0:T(8,128)(2,1)S(1)} collective-permute-done((f16[128,1024]{1,0:T(8,128)(2,1)S(1)}, f16[128,1024]{1,0:T(8,128)(2,1)S(1)}, u32[]{:S(2)}, u32[]{:S(2)}) %collective-permute-start.1) | collective-permute-done | bytes 262176 | tf_op jit(solution)/shard_map/ppermute | solution.py:33
  23.4 1.6 %collective-permute-done.3.refs_6_.refs_10_ = bf16[144,1024]{1,0:T(8,128)(2,1)S(1)} collective-permute-done((bf16[144,1024]{1,0:T(8,128)(2,1)S(1)}, bf16[144,1024]{1,0:T(8,128)(2,1)S(1)}, u32[]{:S(2)}, u32[]{:S(2)}) %collective-permute-start.3) | collective-permute-done | bytes 294944 | tf_op jit(solution)/shard_map/ppermute | solution.py:33
  25.2 2.0 %collective-permute-start.4 = (bf16[288,1024]{1,0:T(8,128)(2,1)S(1)}, bf16[288,1024]{1,0:T(8,128)(2,1)S(1)}, u32[]{:S(2)}, u32[]{:S(2)}) collective-permute-start(bf16[288,1024]{1,0:T(8,128)(2,1)S(1)} %maximum_select_fusion), channel_id=1, source_target_pairs={{0,2},{1,15},{2,4},{3,1},{4,6},{5,3},{6,8},{7,5},{8,10},{9,7},{10,... | collective-permute-start | bytes 1769480 | tf_op jit(solution)/shard_map/ppermute | solution.py:33
  27.2 1.4 %collective-permute-start.5 = (bf16[288,1024]{1,0:T(8,128)(2,1)S(1)}, bf16[288,1024]{1,0:T(8,128)(2,1)S(1)}, u32[]{:S(2)}, u32[]{:S(2)}) collective-permute-start(bf16[288,1024]{1,0:T(8,128)(2,1)S(1)} %maximum_select_fusion), channel_id=1, source_target_pairs={{0,64},{1,193},{2,66},{3,195},{4,68},{5,197},{6,70},{7,199},{8,72}... | collective-permute-start | bytes 1769480 | tf_op jit(solution)/shard_map/ppermute | solution.py:33
  28.5 1.2 %collective-permute-start.6 = (bf16[144,1024]{1,0:T(8,128)(2,1)S(1)}, bf16[144,1024]{1,0:T(8,128)(2,1)S(1)}, u32[]{:S(2)}, u32[]{:S(2)}) collective-permute-start(bf16[144,1024]{1,0:T(8,128)(2,1)S(1)} %pad_maximum_fusion.refs_1_.refs_5_.refs_3_.refs_9_), channel_id=1, source_target_pairs={{0,16},{1,17},{2,18},{3,19},{4,20},{5,21},{6,22},{7,23},{8,24},{9,... | collective-permute-start | bytes 884744 | tf_op jit(solution)/shard_map/ppermute | solution.py:33
  29.7 5.5 %collective-permute-done.6.refs_15_ = bf16[144,1024]{1,0:T(8,128)(2,1)S(1)} collective-permute-done((bf16[144,1024]{1,0:T(8,128)(2,1)S(1)}, bf16[144,1024]{1,0:T(8,128)(2,1)S(1)}, u32[]{:S(2)}, u32[]{:S(2)}) %collective-permute-start.6) | collective-permute-done | bytes 294944 | tf_op jit(solution)/shard_map/ppermute | solution.py:33
  35.3 3.7 %collective-permute-done.4.refs_2_.refs_4_ = bf16[288,1024]{1,0:T(8,128)(2,1)S(1)} collective-permute-done((bf16[288,1024]{1,0:T(8,128)(2,1)S(1)}, bf16[288,1024]{1,0:T(8,128)(2,1)S(1)}, u32[]{:S(2)}, u32[]{:S(2)}) %collective-permute-start.4) | collective-permute-done | bytes 589856 | tf_op jit(solution)/shard_map/ppermute | solution.py:33
  39.0 1.2 %collective-permute-start.7 = (bf16[288,1024]{1,0:T(8,128)(2,1)S(1)}, bf16[288,1024]{1,0:T(8,128)(2,1)S(1)}, u32[]{:S(2)}, u32[]{:S(2)}) collective-permute-start(bf16[288,1024]{1,0:T(8,128)(2,1)S(1)} %collective-permute-done.4.refs_2_.refs_4_), channel_id=1, source_target_pairs={{0,2},{1,15},{2,4},{3,1},{4,6},{5,3},{6,8},{7,5},{8,10},{9,7},{10,... | collective-permute-start | bytes 1769480 | tf_op jit(solution)/shard_map/ppermute | solution.py:33
  40.2 2.0 %collective-permute-start.10 = (bf16[144,1024]{1,0:T(8,128)(2,1)S(1)}, bf16[144,1024]{1,0:T(8,128)(2,1)S(1)}, u32[]{:S(2)}, u32[]{:S(2)}) collective-permute-start(bf16[144,1024]{1,0:T(8,128)(2,1)S(1)} %collective-permute-done.6.refs_15_), channel_id=1, source_target_pairs={{0,1},{1,0},{2,3},{3,2},{4,5},{5,4},{6,7},{7,6},{8,9},{9,8},{10,11... | collective-permute-start | bytes 884744 | tf_op jit(solution)/shard_map/ppermute | solution.py:33
  42.4 1.2 %collective-permute-start.9 = (bf16[128,1024]{1,0:T(8,128)(2,1)S(1)}, bf16[128,1024]{1,0:T(8,128)(2,1)}, u32[]{:S(2)}, u32[]{:S(2)}) collective-permute-start(bf16[128,1024]{1,0:T(8,128)(2,1)S(1)} %get-tuple-element.67), channel_id=1, source_target_pairs={{0,16},{1,17},{2,18},{3,19},{4,20},{5,21},{6,22},{7,23},{8,24},{9,... | collective-permute-start | bytes 786440 | tf_op jit(solution)/shard_map/ppermute | solution.py:33
  43.6 6.3 %collective-permute-done.8.refs_9_.refs_13_ = bf16[128,1024]{1,0:T(8,128)(2,1)S(1)} collective-permute-done((bf16[128,1024]{1,0:T(8,128)(2,1)S(1)}, bf16[128,1024]{1,0:T(8,128)(2,1)S(1)}, u32[]{:S(2)}, u32[]{:S(2)}) %collective-permute-start.8) | collective-permute-done | bytes 262176 | tf_op jit(solution)/shard_map/ppermute | solution.py:33
  53.5 1.6 %collective-permute-start.14 = (bf16[128,1024]{1,0:T(8,128)(2,1)S(1)}, bf16[128,1024]{1,0:T(8,128)(2,1)}, u32[]{:S(2)}, u32[]{:S(2)}) collective-permute-start(bf16[128,1024]{1,0:T(8,128)(2,1)S(1)} %collective-permute-done.8.refs_9_.refs_13_), channel_id=1, source_target_pairs={{0,1},{1,0},{2,3},{3,2},{4,5},{5,4},{6,7},{7,6},{8,9},{9,8},{10,11... | collective-permute-start | bytes 786440 | tf_op jit(solution)/shard_map/ppermute | solution.py:33
  55.1 1.2 %collective-permute-start.12 = (bf16[128,1024]{1,0:T(8,128)(2,1)}, bf16[128,1024]{1,0:T(8,128)(2,1)}, u32[]{:S(2)}, u32[]{:S(2)}) collective-permute-start(bf16[128,1024]{1,0:T(8,128)(2,1)} %slice.107), channel_id=1, source_target_pairs={{0,16},{1,17},{2,18},{3,19},{4,20},{5,21},{6,22},{7,23},{8,24},{9,... | collective-permute-start | bytes 786440 | tf_op jit(solution)/shard_map/ppermute | solution.py:33
  57.9 2.5 %collective-permute-start.16 = (bf16[128,1024]{1,0:T(8,128)(2,1)}, bf16[128,1024]{1,0:T(8,128)(2,1)}, u32[]{:S(2)}, u32[]{:S(2)}) collective-permute-start(bf16[128,1024]{1,0:T(8,128)(2,1)} %pad_maximum_fusion.1), channel_id=1, source_target_pairs={{32,16},{96,80},{160,144},{224,208}} | collective-permute-start | bytes 786440 | tf_op jit(solution)/shard_map/ppermute | solution.py:33
  60.4 3.3 %collective-permute-done.12.refs_18_ = bf16[128,1024]{1,0:T(8,128)(2,1)} collective-permute-done((bf16[128,1024]{1,0:T(8,128)(2,1)}, bf16[128,1024]{1,0:T(8,128)(2,1)}, u32[]{:S(2)}, u32[]{:S(2)}) %collective-permute-start.12) | collective-permute-done | bytes 262176 | tf_op jit(solution)/shard_map/ppermute | solution.py:33
  63.7 2.4 %collective-permute-start.18 = (bf16[128,1024]{1,0:T(8,128)(2,1)}, bf16[128,1024]{1,0:T(8,128)(2,1)S(1)}, u32[]{:S(2)}, u32[]{:S(2)}) collective-permute-start(bf16[128,1024]{1,0:T(8,128)(2,1)} %pad_maximum_fusion.1), channel_id=1, source_target_pairs={{32,0},{96,64},{160,128},{224,192}} | collective-permute-start | bytes 786440 | tf_op jit(solution)/shard_map/ppermute | solution.py:33
  67.2 1.5 %collective-permute-start.19 = (bf16[48,1024]{1,0:T(8,128)(2,1)S(1)}, bf16[48,1024]{1,0:T(8,128)(2,1)S(1)}, u32[]{:S(2)}, u32[]{:S(2)}) collective-permute-start(bf16[48,1024]{1,0:T(8,128)(2,1)S(1)} %fusion.3), channel_id=1, source_target_pairs={{32,18},{33,17},{34,20},{36,22},{38,24},{43,27},{45,29},{47,31},{9... | collective-permute-start | bytes 294920 | tf_op jit(solution)/shard_map/ppermute | solution.py:33
  68.8 1.3 %collective-permute-start.20 = (bf16[144,1024]{1,0:T(8,128)(2,1)S(1)}, bf16[144,1024]{1,0:T(8,128)(2,1)S(1)}, u32[]{:S(2)}, u32[]{:S(2)}) collective-permute-start(bf16[144,1024]{1,0:T(8,128)(2,1)S(1)} %slice_select_fusion), channel_id=1, source_target_pairs={{0,2},{1,15},{2,4},{3,1},{4,6},{5,3},{6,8},{7,5},{8,10},{9,7},{10,... | collective-permute-start | bytes 884744 | tf_op jit(solution)/shard_map/ppermute | solution.py:33
  70.1 3.7 %early.1 = (f32[4,512]{1,0:T(4,128)S(1)}, f32[4,512]{1,0:T(4,128)S(1)}) custom-call(s32[2]{0:T(128)S(1)} %pad_add_fusion.1.refs_0_, bf16[144,1024]{1,0:T(8,128)(2,1)S(1)} %pad_maximum_fusion.refs_1_.refs_5_.refs_3_.refs_9_, bf16[288,1024]{1,0:T(8,128)(2,1)S(1)} %collective-permute-done.4.refs_2_.refs_4_, ...), custom_call_target="tpu_custom_call" | custom-call | flops 5637144576 | bytes 11796480 | tf_op jit(solution)/shard_map/early/pallas_call | solution.py:223
  73.8 1.9 %collective-permute-done.17.refs_21_ = bf16[128,1024]{1,0:T(8,128)(2,1)S(1)} collective-permute-done((bf16[128,1024]{1,0:T(8,128)(2,1)S(1)}, bf16[128,1024]{1,0:T(8,128)(2,1)S(1)}, u32[]{:S(2)}, u32[]{:S(2)}) %collective-permute-start.17) | collective-permute-done | bytes 262176 | tf_op jit(solution)/shard_map/ppermute | solution.py:33
  78.1 1.2 %collective-permute-done.21.refs_20_ = bf16[128,1024]{1,0:T(8,128)(2,1)S(1)} collective-permute-done((bf16[128,1024]{1,0:T(8,128)(2,1)}, bf16[128,1024]{1,0:T(8,128)(2,1)S(1)}, u32[]{:S(2)}, u32[]{:S(2)}) %collective-permute-start.21) | collective-permute-done | bytes 262176 | tf_op jit(solution)/shard_map/ppermute | solution.py:33
  79.5 5.4 %late.1 = (f32[4,512]{1,0:T(4,128)S(1)}, f32[4,512]{1,0:T(4,128)S(1)}, f32[4,1152]{1,0:T(4,128)S(1)}, f32[4,128]{1,0:T(4,128)S(1)}) custom-call(s32[2]{0:T(128)S(1)} %pad_add_fusion.1.refs_0_, f32[4,512]{1,0:T(4,128)S(1)} %get-tuple-element.50.refs_1_, f32[4,512]{1,0:T(4,128)S(1)} %get-tuple-element.51.refs_2_, ...), custom_call_target="tpu_custom_call" | custom-call | flops 16609443840 | bytes 22216704 | tf_op jit(solution)/shard_map/late/pallas_call | solution.py:223
  86.2 2.5 %collective-permute-start.25 = (f32[4,512]{1,0:T(4,128)S(1)}, f32[4,512]{1,0:T(4,128)S(1)}, u32[]{:S(2)}, u32[]{:S(2)}) collective-permute-start(f32[4,512]{1,0:T(4,128)S(1)} %slice_add_fusion), channel_id=1, source_target_pairs={{0,16},{1,17},{2,18},{3,19},{4,20},{5,21},{6,22},{7,23},{8,24},{9,... | collective-permute-start | bytes 24584 | tf_op jit(solution)/shard_map/ppermute | solution.py:33
  88.6 1.3 %collective-permute-start.26 = (f32[4,128]{1,0:T(4,128)S(1)}, f32[4,128]{1,0:T(4,128)S(1)}, u32[]{:S(2)}, u32[]{:S(2)}) collective-permute-start(f32[4,128]{1,0:T(4,128)S(1)} %slice_add_fusion.2), channel_id=1, source_target_pairs={{0,32},{64,96},{128,160},{192,224}} | collective-permute-start | bytes 6152 | tf_op jit(solution)/shard_map/ppermute | solution.py:33
  89.9 1.3 %collective-permute-start.27 = (f32[4,128]{1,0:T(4,128)S(1)}, f32[4,128]{1,0:T(4,128)S(1)}, u32[]{:S(2)}, u32[]{:S(2)}) collective-permute-start(f32[4,128]{1,0:T(4,128)S(1)} %slice_add_fusion.2), channel_id=1, source_target_pairs={{16,32},{80,96},{144,160},{208,224}} | collective-permute-start | bytes 6152 | tf_op jit(solution)/shard_map/ppermute | solution.py:33
  91.2 4.4 %collective-permute-done.26 = f32[4,128]{1,0:T(4,128)S(1)} collective-permute-done((f32[4,128]{1,0:T(4,128)S(1)}, f32[4,128]{1,0:T(4,128)S(1)}, u32[]{:S(2)}, u32[]{:S(2)}) %collective-permute-start.26) | collective-permute-done | bytes 2080 | tf_op jit(solution)/shard_map/ppermute | solution.py:33
  97.4 2.6 %collective-permute-start.30 = (f32[4,4,128]{2,1,0:T(4,128)S(1)}, f32[4,4,128]{2,1,0:T(4,128)S(1)}, u32[]{:S(2)}, u32[]{:S(2)}) collective-permute-start(f32[4,4,128]{2,1,0:T(4,128)S(1)} %pad_add_fusion), channel_id=1, source_target_pairs={{0,192},{1,193},{2,194},{3,195},{4,196},{5,197},{6,198},{7,199},{8... | collective-permute-start | bytes 24584 | tf_op jit(solution)/shard_map/ppermute | solution.py:33
  (92 shorter events, 18.0 us)
Async XLA Ops:
  7.2 10.8 %collective-permute-start = (f16[128,1024]{1,0:T(8,128)(2,1)S(1)}, f16[128,1024]{1,0:T(8,128)(2,1)S(1)}, u32[]{:S(2)}, u32[]{:S(2)}) collective-permute-start(f16[128,1024]{1,0:T(8,128)(2,1)S(1)} %bitcast.38), channel_id=1, source_target_pairs={{0,128},{1,129},{2,130},{3,131},{4,132},{5,133},{6,134},{7,135},{8... | collective-permute-start | bytes 786440 | tf_op jit(solution)/shard_map/ppermute | solution.py:33
  10.5 12.0 %collective-permute-start.1 = (f16[128,1024]{1,0:T(8,128)(2,1)S(1)}, f16[128,1024]{1,0:T(8,128)(2,1)S(1)}, u32[]{:S(2)}, u32[]{:S(2)}) collective-permute-start(f16[128,1024]{1,0:T(8,128)(2,1)S(1)} %bitcast.37), channel_id=1, source_target_pairs={{0,64},{1,65},{2,66},{3,67},{4,68},{5,69},{6,70},{7,71},{8,72},{9,... | collective-permute-start | bytes 786440 | tf_op jit(solution)/shard_map/ppermute | solution.py:33
  11.2 11.7 %collective-permute-start.2 = (f16[128,1024]{1,0:T(8,128)(2,1)S(1)}, f16[128,1024]{1,0:T(8,128)(2,1)S(1)}, u32[]{:S(2)}, u32[]{:S(2)}) collective-permute-start(f16[128,1024]{1,0:T(8,128)(2,1)S(1)} %bitcast.36), channel_id=1, source_target_pairs={{0,192},{1,193},{2,194},{3,195},{4,196},{5,197},{6,198},{7,199},{8... | collective-permute-start | bytes 786440 | tf_op jit(solution)/shard_map/ppermute | solution.py:33
  23.3 1.7 %collective-permute-start.3 = (bf16[144,1024]{1,0:T(8,128)(2,1)S(1)}, bf16[144,1024]{1,0:T(8,128)(2,1)S(1)}, u32[]{:S(2)}, u32[]{:S(2)}) collective-permute-start(bf16[144,1024]{1,0:T(8,128)(2,1)S(1)} %pad_maximum_fusion.refs_1_.refs_5_.refs_3_.refs_9_), channel_id=1, source_target_pairs={{0,1},{1,0},{2,3},{3,2},{4,5},{5,4},{6,7},{7,6},{8,9},{9,8},{10,11... | collective-permute-start | bytes 884744 | tf_op jit(solution)/shard_map/ppermute | solution.py:33
  25.2 32.7 %copy-start.5 = (bf16[288,1024]{1,0:T(8,128)(2,1)}, bf16[288,1024]{1,0:T(8,128)(2,1)S(1)}, u32[]{:S(2)}) copy-start(bf16[288,1024]{1,0:T(8,128)(2,1)S(1)} %maximum_select_fusion) | copy-start | bytes 1769476
  25.2 13.8 %collective-permute-start.4 = (bf16[288,1024]{1,0:T(8,128)(2,1)S(1)}, bf16[288,1024]{1,0:T(8,128)(2,1)S(1)}, u32[]{:S(2)}, u32[]{:S(2)}) collective-permute-start(bf16[288,1024]{1,0:T(8,128)(2,1)S(1)} %maximum_select_fusion), channel_id=1, source_target_pairs={{0,2},{1,15},{2,4},{3,1},{4,6},{5,3},{6,8},{7,5},{8,10},{9,7},{10,... | collective-permute-start | bytes 1769480 | tf_op jit(solution)/shard_map/ppermute | solution.py:33
  27.2 11.8 %collective-permute-start.5 = (bf16[288,1024]{1,0:T(8,128)(2,1)S(1)}, bf16[288,1024]{1,0:T(8,128)(2,1)S(1)}, u32[]{:S(2)}, u32[]{:S(2)}) collective-permute-start(bf16[288,1024]{1,0:T(8,128)(2,1)S(1)} %maximum_select_fusion), channel_id=1, source_target_pairs={{0,64},{1,193},{2,66},{3,195},{4,68},{5,197},{6,70},{7,199},{8,72}... | collective-permute-start | bytes 1769480 | tf_op jit(solution)/shard_map/ppermute | solution.py:33
  28.5 6.7 %collective-permute-start.6 = (bf16[144,1024]{1,0:T(8,128)(2,1)S(1)}, bf16[144,1024]{1,0:T(8,128)(2,1)S(1)}, u32[]{:S(2)}, u32[]{:S(2)}) collective-permute-start(bf16[144,1024]{1,0:T(8,128)(2,1)S(1)} %pad_maximum_fusion.refs_1_.refs_5_.refs_3_.refs_9_), channel_id=1, source_target_pairs={{0,16},{1,17},{2,18},{3,19},{4,20},{5,21},{6,22},{7,23},{8,24},{9,... | collective-permute-start | bytes 884744 | tf_op jit(solution)/shard_map/ppermute | solution.py:33
  39.0 12.7 %collective-permute-start.7 = (bf16[288,1024]{1,0:T(8,128)(2,1)S(1)}, bf16[288,1024]{1,0:T(8,128)(2,1)S(1)}, u32[]{:S(2)}, u32[]{:S(2)}) collective-permute-start(bf16[288,1024]{1,0:T(8,128)(2,1)S(1)} %collective-permute-done.4.refs_2_.refs_4_), channel_id=1, source_target_pairs={{0,2},{1,15},{2,4},{3,1},{4,6},{5,3},{6,8},{7,5},{8,10},{9,7},{10,... | collective-permute-start | bytes 1769480 | tf_op jit(solution)/shard_map/ppermute | solution.py:33
  40.2 10.8 %collective-permute-start.10 = (bf16[144,1024]{1,0:T(8,128)(2,1)S(1)}, bf16[144,1024]{1,0:T(8,128)(2,1)S(1)}, u32[]{:S(2)}, u32[]{:S(2)}) collective-permute-start(bf16[144,1024]{1,0:T(8,128)(2,1)S(1)} %collective-permute-done.6.refs_15_), channel_id=1, source_target_pairs={{0,1},{1,0},{2,3},{3,2},{4,5},{5,4},{6,7},{7,6},{8,9},{9,8},{10,11... | collective-permute-start | bytes 884744 | tf_op jit(solution)/shard_map/ppermute | solution.py:33
  42.2 7.7 %collective-permute-start.8 = (bf16[128,1024]{1,0:T(8,128)(2,1)S(1)}, bf16[128,1024]{1,0:T(8,128)(2,1)S(1)}, u32[]{:S(2)}, u32[]{:S(2)}) collective-permute-start(bf16[128,1024]{1,0:T(8,128)(2,1)S(1)} %get-tuple-element.68), channel_id=1, source_target_pairs={{0,64},{1,193},{2,66},{3,195},{4,68},{5,197},{6,70},{7,199},{8,72}... | collective-permute-start | bytes 786440 | tf_op jit(solution)/shard_map/ppermute | solution.py:33
  42.4 8.6 %collective-permute-start.9 = (bf16[128,1024]{1,0:T(8,128)(2,1)S(1)}, bf16[128,1024]{1,0:T(8,128)(2,1)}, u32[]{:S(2)}, u32[]{:S(2)}) collective-permute-start(bf16[128,1024]{1,0:T(8,128)(2,1)S(1)} %get-tuple-element.67), channel_id=1, source_target_pairs={{0,16},{1,17},{2,18},{3,19},{4,20},{5,21},{6,22},{7,23},{8,24},{9,... | collective-permute-start | bytes 786440 | tf_op jit(solution)/shard_map/ppermute | solution.py:33
  51.7 4.6 %collective-permute-start.13 = (bf16[288,1024]{1,0:T(8,128)(2,1)S(1)}, bf16[288,1024]{1,0:T(8,128)(2,1)S(1)}, u32[]{:S(2)}, u32[]{:S(2)}) collective-permute-start(bf16[288,1024]{1,0:T(8,128)(2,1)S(1)} %collective-permute-done.5.refs_7_.refs_11_), channel_id=1, source_target_pairs={{0,1},{1,0},{2,3},{3,2},{4,5},{5,4},{6,7},{7,6},{8,9},{9,8},{10,11... | collective-permute-start | bytes 1769480 | tf_op jit(solution)/shard_map/ppermute | solution.py:33
  52.2 14.0 %collective-permute-start.11 = (bf16[288,1024]{1,0:T(8,128)(2,1)S(1)}, bf16[288,1024]{1,0:T(8,128)(2,1)S(1)}, u32[]{:S(2)}, u32[]{:S(2)}) collective-permute-start(bf16[288,1024]{1,0:T(8,128)(2,1)S(1)} %collective-permute-done.7.refs_3_.refs_5_), channel_id=1, source_target_pairs={{0,2},{1,15},{2,4},{3,1},{4,6},{5,3},{6,8},{7,5},{8,10},{9,7},{10,... | collective-permute-start | bytes 1769480 | tf_op jit(solution)/shard_map/ppermute | solution.py:33
  53.5 12.7 %collective-permute-start.14 = (bf16[128,1024]{1,0:T(8,128)(2,1)S(1)}, bf16[128,1024]{1,0:T(8,128)(2,1)}, u32[]{:S(2)}, u32[]{:S(2)}) collective-permute-start(bf16[128,1024]{1,0:T(8,128)(2,1)S(1)} %collective-permute-done.8.refs_9_.refs_13_), channel_id=1, source_target_pairs={{0,1},{1,0},{2,3},{3,2},{4,5},{5,4},{6,7},{7,6},{8,9},{9,8},{10,11... | collective-permute-start | bytes 786440 | tf_op jit(solution)/shard_map/ppermute | solution.py:33
  55.1 8.6 %collective-permute-start.12 = (bf16[128,1024]{1,0:T(8,128)(2,1)}, bf16[128,1024]{1,0:T(8,128)(2,1)}, u32[]{:S(2)}, u32[]{:S(2)}) collective-permute-start(bf16[128,1024]{1,0:T(8,128)(2,1)} %slice.107), channel_id=1, source_target_pairs={{0,16},{1,17},{2,18},{3,19},{4,20},{5,21},{6,22},{7,23},{8,24},{9,... | collective-permute-start | bytes 786440 | tf_op jit(solution)/shard_map/ppermute | solution.py:33
  56.3 9.9 %collective-permute-start.15 = (bf16[128,1024]{1,0:T(8,128)(2,1)}, bf16[128,1024]{1,0:T(8,128)(2,1)}, u32[]{:S(2)}, u32[]{:S(2)}) collective-permute-start(bf16[128,1024]{1,0:T(8,128)(2,1)} %collective-permute-done.9.refs_17_), channel_id=1, source_target_pairs={{0,1},{1,0},{2,3},{3,2},{4,5},{5,4},{6,7},{7,6},{8,9},{9,8},{10,11... | collective-permute-start | bytes 786440 | tf_op jit(solution)/shard_map/ppermute | solution.py:33
  57.9 8.3 %collective-permute-start.16 = (bf16[128,1024]{1,0:T(8,128)(2,1)}, bf16[128,1024]{1,0:T(8,128)(2,1)}, u32[]{:S(2)}, u32[]{:S(2)}) collective-permute-start(bf16[128,1024]{1,0:T(8,128)(2,1)} %pad_maximum_fusion.1), channel_id=1, source_target_pairs={{32,16},{96,80},{160,144},{224,208}} | collective-permute-start | bytes 786440 | tf_op jit(solution)/shard_map/ppermute | solution.py:33
  63.7 10.1 %collective-permute-start.18 = (bf16[128,1024]{1,0:T(8,128)(2,1)}, bf16[128,1024]{1,0:T(8,128)(2,1)S(1)}, u32[]{:S(2)}, u32[]{:S(2)}) collective-permute-start(bf16[128,1024]{1,0:T(8,128)(2,1)} %pad_maximum_fusion.1), channel_id=1, source_target_pairs={{32,0},{96,64},{160,128},{224,192}} | collective-permute-start | bytes 786440 | tf_op jit(solution)/shard_map/ppermute | solution.py:33
  67.2 6.7 %collective-permute-start.19 = (bf16[48,1024]{1,0:T(8,128)(2,1)S(1)}, bf16[48,1024]{1,0:T(8,128)(2,1)S(1)}, u32[]{:S(2)}, u32[]{:S(2)}) collective-permute-start(bf16[48,1024]{1,0:T(8,128)(2,1)S(1)} %fusion.3), channel_id=1, source_target_pairs={{32,18},{33,17},{34,20},{36,22},{38,24},{43,27},{45,29},{47,31},{9... | collective-permute-start | bytes 294920 | tf_op jit(solution)/shard_map/ppermute | solution.py:33
  68.7 7.1 %collective-permute-start.17 = (bf16[128,1024]{1,0:T(8,128)(2,1)S(1)}, bf16[128,1024]{1,0:T(8,128)(2,1)S(1)}, u32[]{:S(2)}, u32[]{:S(2)}) collective-permute-start(bf16[128,1024]{1,0:T(8,128)(2,1)S(1)} %collective-permute-done.8.refs_9_.refs_13_), channel_id=1, source_target_pairs={{0,16},{1,17},{2,18},{3,19},{4,20},{5,21},{6,22},{7,23},{8,24},{9,... | collective-permute-start | bytes 786440 | tf_op jit(solution)/shard_map/ppermute | solution.py:33
  68.8 10.5 %collective-permute-start.20 = (bf16[144,1024]{1,0:T(8,128)(2,1)S(1)}, bf16[144,1024]{1,0:T(8,128)(2,1)S(1)}, u32[]{:S(2)}, u32[]{:S(2)}) collective-permute-start(bf16[144,1024]{1,0:T(8,128)(2,1)S(1)} %slice_select_fusion), channel_id=1, source_target_pairs={{0,2},{1,15},{2,4},{3,1},{4,6},{5,3},{6,8},{7,5},{8,10},{9,7},{10,... | collective-permute-start | bytes 884744 | tf_op jit(solution)/shard_map/ppermute | solution.py:33
  76.8 1.3 %collective-permute-start.23 = (bf16[128,1024]{1,0:T(8,128)(2,1)S(1)}, bf16[128,1024]{1,0:T(8,128)(2,1)S(1)}, u32[]{:S(2)}, u32[]{:S(2)}) collective-permute-start(bf16[128,1024]{1,0:T(8,128)(2,1)S(1)} %add.132), channel_id=1, source_target_pairs={{0,1},{16,17},{64,65},{80,81},{128,129},{144,145},{192,193},{208,2... | collective-permute-start | bytes 786440 | tf_op jit(solution)/shard_map/ppermute | solution.py:33
  77.5 1.8 %collective-permute-start.21 = (bf16[128,1024]{1,0:T(8,128)(2,1)}, bf16[128,1024]{1,0:T(8,128)(2,1)S(1)}, u32[]{:S(2)}, u32[]{:S(2)}) collective-permute-start(bf16[128,1024]{1,0:T(8,128)(2,1)} %collective-permute-done.12.refs_18_), channel_id=1, source_target_pairs={{0,1},{1,0},{2,3},{3,2},{4,5},{5,4},{6,7},{7,6},{8,9},{9,8},{10,11... | collective-permute-start | bytes 786440 | tf_op jit(solution)/shard_map/ppermute | solution.py:33
  77.6 1.9 %collective-permute-start.22 = (bf16[128,1024]{1,0:T(8,128)(2,1)S(1)}, bf16[128,1024]{1,0:T(8,128)(2,1)S(1)}, u32[]{:S(2)}, u32[]{:S(2)}) collective-permute-start(bf16[128,1024]{1,0:T(8,128)(2,1)S(1)} %collective-permute-done.17.refs_21_), channel_id=1, source_target_pairs={{0,1},{1,0},{2,3},{3,2},{4,5},{5,4},{6,7},{7,6},{8,9},{9,8},{10,11... | collective-permute-start | bytes 786440 | tf_op jit(solution)/shard_map/ppermute | solution.py:33
  84.9 1.3 %collective-permute-start.24 = (f32[4,1152]{1,0:T(4,128)S(1)}, f32[4,1152]{1,0:T(4,128)S(1)}, u32[]{:S(2)}, u32[]{:S(2)}) collective-permute-start(f32[4,1152]{1,0:T(4,128)S(1)} %get-tuple-element.60), channel_id=1, source_target_pairs={{0,1},{1,0},{2,3},{3,2},{4,5},{5,4},{6,7},{7,6},{8,9},{9,8},{10,11... | collective-permute-start | bytes 55304 | tf_op jit(solution)/shard_map/ppermute | solution.py:33
  86.2 9.5 %collective-permute-start.25 = (f32[4,512]{1,0:T(4,128)S(1)}, f32[4,512]{1,0:T(4,128)S(1)}, u32[]{:S(2)}, u32[]{:S(2)}) collective-permute-start(f32[4,512]{1,0:T(4,128)S(1)} %slice_add_fusion), channel_id=1, source_target_pairs={{0,16},{1,17},{2,18},{3,19},{4,20},{5,21},{6,22},{7,23},{8,24},{9,... | collective-permute-start | bytes 24584 | tf_op jit(solution)/shard_map/ppermute | solution.py:33
  88.6 7.0 %collective-permute-start.26 = (f32[4,128]{1,0:T(4,128)S(1)}, f32[4,128]{1,0:T(4,128)S(1)}, u32[]{:S(2)}, u32[]{:S(2)}) collective-permute-start(f32[4,128]{1,0:T(4,128)S(1)} %slice_add_fusion.2), channel_id=1, source_target_pairs={{0,32},{64,96},{128,160},{192,224}} | collective-permute-start | bytes 6152 | tf_op jit(solution)/shard_map/ppermute | solution.py:33
  89.9 5.7 %collective-permute-start.27 = (f32[4,128]{1,0:T(4,128)S(1)}, f32[4,128]{1,0:T(4,128)S(1)}, u32[]{:S(2)}, u32[]{:S(2)}) collective-permute-start(f32[4,128]{1,0:T(4,128)S(1)} %slice_add_fusion.2), channel_id=1, source_target_pairs={{16,32},{80,96},{144,160},{208,224}} | collective-permute-start | bytes 6152 | tf_op jit(solution)/shard_map/ppermute | solution.py:33
  95.7 5.2 %collective-permute-start.28 = (f32[4,4,128]{2,1,0:T(4,128)S(1)}, f32[4,4,128]{2,1,0:T(4,128)S(1)}, u32[]{:S(2)}, u32[]{:S(2)}) collective-permute-start(f32[4,4,128]{2,1,0:T(4,128)S(1)} %pad_add_fusion), channel_id=1, source_target_pairs={{0,128},{1,129},{2,130},{3,131},{4,132},{5,133},{6,134},{7,135},{8... | collective-permute-start | bytes 24584 | tf_op jit(solution)/shard_map/ppermute | solution.py:33
  96.7 4.9 %collective-permute-start.29 = (f32[4,4,128]{2,1,0:T(4,128)S(1)}, f32[4,4,128]{2,1,0:T(4,128)S(1)}, u32[]{:S(2)}, u32[]{:S(2)}) collective-permute-start(f32[4,4,128]{2,1,0:T(4,128)S(1)} %pad_add_fusion), channel_id=1, source_target_pairs={{0,64},{1,65},{2,66},{3,67},{4,68},{5,69},{6,70},{7,71},{8,72},{9,... | collective-permute-start | bytes 24584 | tf_op jit(solution)/shard_map/ppermute | solution.py:33
  97.4 4.2 %collective-permute-start.30 = (f32[4,4,128]{2,1,0:T(4,128)S(1)}, f32[4,4,128]{2,1,0:T(4,128)S(1)}, u32[]{:S(2)}, u32[]{:S(2)}) collective-permute-start(f32[4,4,128]{2,1,0:T(4,128)S(1)} %pad_add_fusion), channel_id=1, source_target_pairs={{0,192},{1,193},{2,194},{3,195},{4,196},{5,197},{6,198},{7,199},{8... | collective-permute-start | bytes 24584 | tf_op jit(solution)/shard_map/ppermute | solution.py:33
  (8 other events, 67.2 us)

commit v12 on v11

--- a/solution.py
+++ b/solution.py
@@ -260,12 +260,16 @@
 
     partial_sums = raw_partial(showers, geometry, pattern).reshape(blocks, NY, PIECE, feats)
 
-    def share(turn):
-        part = lax.dynamic_index_in_dim(partial_sums, (y + turn) % NY, 1, keepdims=False)
+    def share(sums, turn):
+        part = lax.dynamic_index_in_dim(sums, (y + turn) % NY, 1, keepdims=False)
         return part.reshape(BLOCK, feats)
 
-    raw = share(0)
-    arrived = [permute(share(turn).astype(jnp.float16), along_y(turn)) for turn in (2, 1, 3)]
+    arrived = []
+    for turn in (2, 1, 3):
+        part = share(partial_sums, turn).astype(jnp.float16)
+        partial_sums, part = lax.optimization_barrier((partial_sums, part))
+        arrived.append(permute(part, along_y(turn)))
+    raw = share(partial_sums, 0)
     for part in arrived:
         raw = raw + part.astype(jnp.float32)
     scale = lax.rsqrt(jnp.mean(raw * raw, axis=1, keepdims=True) + 1e-05)
@@ -285,10 +289,11 @@
     y2 = permute(jnp.where(c == 0, y1[TAG:tagged], y1[tagged + TAG :]), y_way)
     xa = permute(y1[TAG:tagged], swap_x)
     x1_t = permute(x1, swap_core)
-    z1, z2, y2, xa, y1, x1_t = fence(z1, z2, y2, xa, y1, x1_t)
+    xb_from = y1[tagged + TAG :]
+    z1, z2, y2, xa, y1, x1_t, xb_from = fence(z1, z2, y2, xa, y1, x1_t, xb_from)
 
     z3 = permute(z2, same_core)
-    xb = permute(y1[tagged + TAG :], swap_x)
+    xb = permute(xb_from, swap_x)
     y1_t = permute(y1, swap_core)
     head = TAG + PIECE
     odd_rows = jnp.concatenate([own[TAG:head], y1_t[TAG:head], y2[:PIECE], y1[TAG:head]], axis=0)

time: 103 us -> 106 us (1.029)
  starting transfers between devices: 38.1 us -> 35.1 us
  waiting for transfers between devices: 37.6 us -> 40 us
  other arithmetic: 7.85 us -> 10 us
  local copies, waits for them, and re-layouts: 3.84 us -> 5.4 us
    convert_element_type x0 -> x3, other arithmetic: none -> 3.26 us  [shards(): part = share(partial_sums, turn).astype(jnp.float16)]
    ppermute x31, starting transfers between devices: 38.1 us -> 35.1 us  [permute(): return lax.ppermute(value, AXES, pairs)]
    ppermute x31, waiting for transfers between devices: 37.6 us -> 40 us  [permute(): return lax.ppermute(value, AXES, pairs)]
    dynamic_slice x1 -> x0, other arithmetic: 1.74 us -> none  [share(): lax.dynamic_index_in_dim(partial_sums, (y + turn) % NY, 1, keepdims=False)]
    dynamic_slice x0 -> x1, local copies, waits for them, and re-layouts: none -> 1.09 us  [share(): part = lax.dynamic_index_in_dim(sums, (y + turn) % NY, 1, keepdims=False)]
  transfers between devices with their start and end apart: 31 -> 31, of which waited for: 16 -> 15; matrix products, arithmetic and copies ran while one was open for 7% -> 8% of each run, Pallas kernels for 4% -> 4%
where the time goes in v12:
time: 106 us
  waiting for transfers between devices  40 us (38%)
  starting transfers between devices  35.1 us (33%)
  Pallas kernels  14.7 us (14%)
  other arithmetic  10 us (9%)
  local copies, waits for them, and re-layouts  5.4 us (5%)
    ppermute x31, waiting for transfers between devices, permute(): return lax.ppermute(value, AXES, pairs)  40 us
    ppermute x31, starting transfers between devices, permute(): return lax.ppermute(value, AXES, pairs)  35.1 us
    pallas_call x2, Pallas kernels, pair_sums(): pl.pallas_call(functools.partial(pair_kernel, col_cuts=tuple(col_cuts), n...  9.15 us
    pallas_call x1, Pallas kernels, raw_partial(): pl.pallas_call(raw_kernel, grid=(feats // width,), in_specs=[pl.BlockSpec...  5.5 us
    convert_element_type x3, other arithmetic, shards(): part = share(partial_sums, turn).astype(jnp.float16)  3.26 us
    convert_element_type x1, other arithmetic, shards(): tag = tag.astype(jnp.bfloat16)  2.51 us
  transfers between devices with their start and end apart: 31, of which 15 were waited for; matrix products, arithmetic and copies ran while one was open for 8% of the time, Pallas kernels for 4%

profile of v12, /device:TPU:4, one launch (start us, length us, event | category | flops | bytes accessed | tf_op | source)
XLA Modules:
  0.0 105.6 jit_solution(1035504611899576566)
XLA Ops:
  0.0 5.5 %raw.1 = f32[512,1024]{1,0:T(8,128)} custom-call(s32[8,11]{1,0:T(8,128)} %bitcast.38, bf16[1584,512]{1,0:T(8,128)(2,1)} %bitcast.32, bf16[1584,1024]{1,0:T(8,128)(2,1)} %geometry.1), custom_call_target="tpu_custom_call" | custom-call | flops 1660944384 | bytes 8388608 | tf_op jit(solution)/shard_map/raw/pallas_call | solution.py:84
  5.5 1.1 %bitcast_convert_fusion = f16[4,1,32,1024]{3,2,0,1:T(8,128)(2,1)S(1)} fusion(f32[4,4,32,1024]{3,2,1,0:T(8,128)} %bitcast.28, s32[]{:T(128)S(6)} %select_n.180), kind=kLoop, calls=%fused_computation.1 | loop fusion | flops 131072 | bytes 786436 | tf_op jit(solution)/shard_map/convert_element_type | solution.py:269
  8.8 3.1 %collective-permute-start.2 = (f16[128,1024]{1,0:T(8,128)(2,1)S(1)}, f16[128,1024]{1,0:T(8,128)(2,1)S(1)}, u32[]{:S(2)}, u32[]{:S(2)}) collective-permute-start(f16[128,1024]{1,0:T(8,128)(2,1)S(1)} %bitcast.35), channel_id=1, source_target_pairs={{0,192},{1,193},{2,194},{3,195},{4,196},{5,197},{6,198},{7,199},{8... | collective-permute-start | bytes 786440 | tf_op jit(solution)/shard_map/ppermute | solution.py:33
  11.9 2.2 %collective-permute-start = (f16[128,1024]{1,0:T(8,128)(2,1)S(1)}, f16[128,1024]{1,0:T(8,128)(2,1)S(1)}, u32[]{:S(2)}, u32[]{:S(2)}) collective-permute-start(f16[128,1024]{1,0:T(8,128)(2,1)S(1)} %bitcast.33), channel_id=1, source_target_pairs={{0,128},{1,129},{2,130},{3,131},{4,132},{5,133},{6,134},{7,135},{8... | collective-permute-start | bytes 786440 | tf_op jit(solution)/shard_map/ppermute | solution.py:33
  14.8 2.5 %select_convert_fusion = bf16[16,1024]{1,0:T(8,128)(2,1)S(1)} fusion(bf16[]{:T(256)} %bitcast.5, bf16[]{:T(256)} %bitcast.4, bf16[]{:T(256)} %bitcast.3, bf16[]{:T(256)} %bitcast.2, s32[1024]{0:T(1024)S(1)} %get-tuple-element.86, s32[1024]{0:T(1024)S(1)} %get-tuple-element.87, pred[16]{0:T(512)(128)(4,1)S(1)} %iota_compare_fusion, pred[1024]{0:T(1024)(128)(4,1)S(1)} %fusion.13), kind=kLoop, calls=%fused_computation.16 | loop fusion | flops 163840 | bytes 42008 | tf_op jit(solution)/shard_map/convert_element_type | solution.py:259
  18.4 4.7 %collective-permute-done.2 = f16[128,1024]{1,0:T(8,128)(2,1)S(1)} collective-permute-done((f16[128,1024]{1,0:T(8,128)(2,1)S(1)}, f16[128,1024]{1,0:T(8,128)(2,1)S(1)}, u32[]{:S(2)}, u32[]{:S(2)}) %collective-permute-start.2) | collective-permute-done | bytes 262176 | tf_op jit(solution)/shard_map/ppermute | solution.py:33
  23.1 3.4 %collective-permute-done.1 = f16[128,1024]{1,0:T(8,128)(2,1)S(1)} collective-permute-done((f16[128,1024]{1,0:T(8,128)(2,1)S(1)}, f16[128,1024]{1,0:T(8,128)(2,1)S(1)}, u32[]{:S(2)}, u32[]{:S(2)}) %collective-permute-start.1) | collective-permute-done | bytes 262176 | tf_op jit(solution)/shard_map/ppermute | solution.py:33
  27.0 1.6 %collective-permute-done.3.refs_6_.refs_10_ = bf16[144,1024]{1,0:T(8,128)(2,1)S(1)} collective-permute-done((bf16[144,1024]{1,0:T(8,128)(2,1)S(1)}, bf16[144,1024]{1,0:T(8,128)(2,1)S(1)}, u32[]{:S(2)}, u32[]{:S(2)}) %collective-permute-start.3) | collective-permute-done | bytes 294944 | tf_op jit(solution)/shard_map/ppermute | solution.py:33
  28.8 2.0 %collective-permute-start.4 = (bf16[288,1024]{1,0:T(8,128)(2,1)S(1)}, bf16[288,1024]{1,0:T(8,128)(2,1)S(1)}, u32[]{:S(2)}, u32[]{:S(2)}) collective-permute-start(bf16[288,1024]{1,0:T(8,128)(2,1)S(1)} %maximum_select_fusion), channel_id=1, source_target_pairs={{0,2},{1,15},{2,4},{3,1},{4,6},{5,3},{6,8},{7,5},{8,10},{9,7},{10,... | collective-permute-start | bytes 1769480 | tf_op jit(solution)/shard_map/ppermute | solution.py:33
  30.8 1.2 %collective-permute-start.6 = (bf16[144,1024]{1,0:T(8,128)(2,1)S(1)}, bf16[144,1024]{1,0:T(8,128)(2,1)S(1)}, u32[]{:S(2)}, u32[]{:S(2)}) collective-permute-start(bf16[144,1024]{1,0:T(8,128)(2,1)S(1)} %pad_maximum_fusion.refs_1_.refs_5_.refs_3_.refs_9_), channel_id=1, source_target_pairs={{0,16},{1,17},{2,18},{3,19},{4,20},{5,21},{6,22},{7,23},{8,24},{9,... | collective-permute-start | bytes 884744 | tf_op jit(solution)/shard_map/ppermute | solution.py:33
  32.0 5.8 %collective-permute-done.6.refs_15_ = bf16[144,1024]{1,0:T(8,128)(2,1)S(1)} collective-permute-done((bf16[144,1024]{1,0:T(8,128)(2,1)S(1)}, bf16[144,1024]{1,0:T(8,128)(2,1)S(1)}, u32[]{:S(2)}, u32[]{:S(2)}) %collective-permute-start.6) | collective-permute-done | bytes 294944 | tf_op jit(solution)/shard_map/ppermute | solution.py:33
  37.8 4.8 %collective-permute-done.4.refs_2_.refs_4_ = bf16[288,1024]{1,0:T(8,128)(2,1)S(1)} collective-permute-done((bf16[288,1024]{1,0:T(8,128)(2,1)S(1)}, bf16[288,1024]{1,0:T(8,128)(2,1)S(1)}, u32[]{:S(2)}, u32[]{:S(2)}) %collective-permute-start.4) | collective-permute-done | bytes 589856 | tf_op jit(solution)/shard_map/ppermute | solution.py:33
  42.6 1.2 %collective-permute-start.7 = (bf16[288,1024]{1,0:T(8,128)(2,1)S(1)}, bf16[288,1024]{1,0:T(8,128)(2,1)S(1)}, u32[]{:S(2)}, u32[]{:S(2)}) collective-permute-start(bf16[288,1024]{1,0:T(8,128)(2,1)S(1)} %collective-permute-done.4.refs_2_.refs_4_), channel_id=1, source_target_pairs={{0,2},{1,15},{2,4},{3,1},{4,6},{5,3},{6,8},{7,5},{8,10},{9,7},{10,... | collective-permute-start | bytes 1769480 | tf_op jit(solution)/shard_map/ppermute | solution.py:33
  45.6 1.2 %collective-permute-start.9 = (bf16[128,1024]{1,0:T(8,128)(2,1)S(1)}, bf16[128,1024]{1,0:T(8,128)(2,1)}, u32[]{:S(2)}, u32[]{:S(2)}) collective-permute-start(bf16[128,1024]{1,0:T(8,128)(2,1)S(1)} %get-tuple-element.79), channel_id=1, source_target_pairs={{0,16},{1,17},{2,18},{3,19},{4,20},{5,21},{6,22},{7,23},{8,24},{9,... | collective-permute-start | bytes 786440 | tf_op jit(solution)/shard_map/ppermute | solution.py:33
  46.8 6.4 %collective-permute-done.8.refs_9_.refs_13_ = bf16[128,1024]{1,0:T(8,128)(2,1)S(1)} collective-permute-done((bf16[128,1024]{1,0:T(8,128)(2,1)S(1)}, bf16[128,1024]{1,0:T(8,128)(2,1)S(1)}, u32[]{:S(2)}, u32[]{:S(2)}) %collective-permute-start.8) | collective-permute-done | bytes 262176 | tf_op jit(solution)/shard_map/ppermute | solution.py:33
  53.1 1.2 %collective-permute-done.9.refs_17_ = bf16[128,1024]{1,0:T(8,128)(2,1)} collective-permute-done((bf16[128,1024]{1,0:T(8,128)(2,1)S(1)}, bf16[128,1024]{1,0:T(8,128)(2,1)}, u32[]{:S(2)}, u32[]{:S(2)}) %collective-permute-start.9) | collective-permute-done | bytes 262176 | tf_op jit(solution)/shard_map/ppermute | solution.py:33
  57.3 1.2 %collective-permute-start.12 = (bf16[128,1024]{1,0:T(8,128)(2,1)}, bf16[128,1024]{1,0:T(8,128)(2,1)}, u32[]{:S(2)}, u32[]{:S(2)}) collective-permute-start(bf16[128,1024]{1,0:T(8,128)(2,1)} %get-tuple-element.52), channel_id=1, source_target_pairs={{0,16},{1,17},{2,18},{3,19},{4,20},{5,21},{6,22},{7,23},{8,24},{9,... | collective-permute-start | bytes 786440 | tf_op jit(solution)/shard_map/ppermute | solution.py:33
  60.1 2.5 %collective-permute-start.16 = (bf16[128,1024]{1,0:T(8,128)(2,1)}, bf16[128,1024]{1,0:T(8,128)(2,1)}, u32[]{:S(2)}, u32[]{:S(2)}) collective-permute-start(bf16[128,1024]{1,0:T(8,128)(2,1)} %pad_maximum_fusion.1), channel_id=1, source_target_pairs={{32,16},{96,80},{160,144},{224,208}} | collective-permute-start | bytes 786440 | tf_op jit(solution)/shard_map/ppermute | solution.py:33
  62.7 3.3 %collective-permute-done.12.refs_18_ = bf16[128,1024]{1,0:T(8,128)(2,1)} collective-permute-done((bf16[128,1024]{1,0:T(8,128)(2,1)}, bf16[128,1024]{1,0:T(8,128)(2,1)}, u32[]{:S(2)}, u32[]{:S(2)}) %collective-permute-start.12) | collective-permute-done | bytes 262176 | tf_op jit(solution)/shard_map/ppermute | solution.py:33
  66.0 2.4 %collective-permute-start.18 = (bf16[128,1024]{1,0:T(8,128)(2,1)}, bf16[128,1024]{1,0:T(8,128)(2,1)S(1)}, u32[]{:S(2)}, u32[]{:S(2)}) collective-permute-start(bf16[128,1024]{1,0:T(8,128)(2,1)} %pad_maximum_fusion.1), channel_id=1, source_target_pairs={{32,0},{96,64},{160,128},{224,192}} | collective-permute-start | bytes 786440 | tf_op jit(solution)/shard_map/ppermute | solution.py:33
  69.5 2.8 %collective-permute-start.19 = (bf16[48,1024]{1,0:T(8,128)(2,1)S(1)}, bf16[48,1024]{1,0:T(8,128)(2,1)S(1)}, u32[]{:S(2)}, u32[]{:S(2)}) collective-permute-start(bf16[48,1024]{1,0:T(8,128)(2,1)S(1)} %fusion.3), channel_id=1, source_target_pairs={{32,18},{33,17},{34,20},{36,22},{38,24},{43,27},{45,29},{47,31},{9... | collective-permute-start | bytes 294920 | tf_op jit(solution)/shard_map/ppermute | solution.py:33
  72.3 1.1 %collective-permute-start.20 = (bf16[144,1024]{1,0:T(8,128)(2,1)S(1)}, bf16[144,1024]{1,0:T(8,128)(2,1)S(1)}, u32[]{:S(2)}, u32[]{:S(2)}) collective-permute-start(bf16[144,1024]{1,0:T(8,128)(2,1)S(1)} %slice_select_fusion), channel_id=1, source_target_pairs={{0,2},{1,15},{2,4},{3,1},{4,6},{5,3},{6,8},{7,5},{8,10},{9,7},{10,... | collective-permute-start | bytes 884744 | tf_op jit(solution)/shard_map/ppermute | solution.py:33
  74.5 3.7 %early.1 = (f32[4,512]{1,0:T(4,128)S(1)}, f32[4,512]{1,0:T(4,128)S(1)}) custom-call(s32[2]{0:T(128)S(1)} %pad_add_fusion.1.refs_0_, bf16[144,1024]{1,0:T(8,128)(2,1)S(1)} %pad_maximum_fusion.refs_1_.refs_5_.refs_3_.refs_9_, bf16[288,1024]{1,0:T(8,128)(2,1)S(1)} %collective-permute-done.4.refs_2_.refs_4_, ...), custom_call_target="tpu_custom_call" | custom-call | flops 5637144576 | bytes 11796480 | tf_op jit(solution)/shard_map/early/pallas_call | solution.py:223
  81.1 1.2 %collective-permute-done.21.refs_20_ = bf16[128,1024]{1,0:T(8,128)(2,1)S(1)} collective-permute-done((bf16[128,1024]{1,0:T(8,128)(2,1)}, bf16[128,1024]{1,0:T(8,128)(2,1)S(1)}, u32[]{:S(2)}, u32[]{:S(2)}) %collective-permute-start.21) | collective-permute-done | bytes 262176 | tf_op jit(solution)/shard_map/ppermute | solution.py:33
  82.4 5.4 %late.1 = (f32[4,512]{1,0:T(4,128)S(1)}, f32[4,512]{1,0:T(4,128)S(1)}, f32[4,1152]{1,0:T(4,128)S(1)}, f32[4,128]{1,0:T(4,128)S(1)}) custom-call(s32[2]{0:T(128)S(1)} %pad_add_fusion.1.refs_0_, f32[4,512]{1,0:T(4,128)S(1)} %get-tuple-element.64.refs_1_, f32[4,512]{1,0:T(4,128)S(1)} %get-tuple-element.65.refs_2_, ...), custom_call_target="tpu_custom_call" | custom-call | flops 16609443840 | bytes 22216704 | tf_op jit(solution)/shard_map/late/pallas_call | solution.py:223
  89.1 1.9 %collective-permute-start.25 = (f32[4,512]{1,0:T(4,128)S(1)}, f32[4,512]{1,0:T(4,128)S(1)}, u32[]{:S(2)}, u32[]{:S(2)}) collective-permute-start(f32[4,512]{1,0:T(4,128)S(1)} %slice_add_fusion), channel_id=1, source_target_pairs={{0,16},{1,17},{2,18},{3,19},{4,20},{5,21},{6,22},{7,23},{8,24},{9,... | collective-permute-start | bytes 24584 | tf_op jit(solution)/shard_map/ppermute | solution.py:33
  91.0 1.3 %collective-permute-start.26 = (f32[4,128]{1,0:T(4,128)S(1)}, f32[4,128]{1,0:T(4,128)S(1)}, u32[]{:S(2)}, u32[]{:S(2)}) collective-permute-start(f32[4,128]{1,0:T(4,128)S(1)} %slice_add_fusion.2), channel_id=1, source_target_pairs={{0,32},{64,96},{128,160},{192,224}} | collective-permute-start | bytes 6152 | tf_op jit(solution)/shard_map/ppermute | solution.py:33
  92.2 1.3 %collective-permute-start.27 = (f32[4,128]{1,0:T(4,128)S(1)}, f32[4,128]{1,0:T(4,128)S(1)}, u32[]{:S(2)}, u32[]{:S(2)}) collective-permute-start(f32[4,128]{1,0:T(4,128)S(1)} %slice_add_fusion.2), channel_id=1, source_target_pairs={{16,32},{80,96},{144,160},{208,224}} | collective-permute-start | bytes 6152 | tf_op jit(solution)/shard_map/ppermute | solution.py:33
  93.5 4.4 %collective-permute-done.26 = f32[4,128]{1,0:T(4,128)S(1)} collective-permute-done((f32[4,128]{1,0:T(4,128)S(1)}, f32[4,128]{1,0:T(4,128)S(1)}, u32[]{:S(2)}, u32[]{:S(2)}) %collective-permute-start.26) | collective-permute-done | bytes 2080 | tf_op jit(solution)/shard_map/ppermute | solution.py:33
  98.1 1.8 %collective-permute-start.28 = (f32[4,4,128]{2,1,0:T(4,128)S(1)}, f32[4,4,128]{2,1,0:T(4,128)S(1)}, u32[]{:S(2)}, u32[]{:S(2)}) collective-permute-start(f32[4,4,128]{2,1,0:T(4,128)S(1)} %pad_add_fusion), channel_id=1, source_target_pairs={{0,128},{1,129},{2,130},{3,131},{4,132},{5,133},{6,134},{7,135},{8... | collective-permute-start | bytes 24584 | tf_op jit(solution)/shard_map/ppermute | solution.py:33
  99.8 3.2 %collective-permute-start.30 = (f32[4,4,128]{2,1,0:T(4,128)S(1)}, f32[4,4,128]{2,1,0:T(4,128)S(1)}, u32[]{:S(2)}, u32[]{:S(2)}) collective-permute-start(f32[4,4,128]{2,1,0:T(4,128)S(1)} %pad_add_fusion), channel_id=1, source_target_pairs={{0,192},{1,193},{2,194},{3,195},{4,196},{5,197},{6,198},{7,199},{8... | collective-permute-start | bytes 24584 | tf_op jit(solution)/shard_map/ppermute | solution.py:33
  103.3 1.4 %collective-permute-done.29 = f32[4,4,128]{2,1,0:T(4,128)S(1)} collective-permute-done((f32[4,4,128]{2,1,0:T(4,128)S(1)}, f32[4,4,128]{2,1,0:T(4,128)S(1)}, u32[]{:S(2)}, u32[]{:S(2)}) %collective-permute-start.29) | collective-permute-done | bytes 8224 | tf_op jit(solution)/shard_map/ppermute | solution.py:33
  (93 shorter events, 18.6 us)
Async XLA Ops:
  8.8 14.3 %collective-permute-start.2 = (f16[128,1024]{1,0:T(8,128)(2,1)S(1)}, f16[128,1024]{1,0:T(8,128)(2,1)S(1)}, u32[]{:S(2)}, u32[]{:S(2)}) collective-permute-start(f16[128,1024]{1,0:T(8,128)(2,1)S(1)} %bitcast.35), channel_id=1, source_target_pairs={{0,192},{1,193},{2,194},{3,195},{4,196},{5,197},{6,198},{7,199},{8... | collective-permute-start | bytes 786440 | tf_op jit(solution)/shard_map/ppermute | solution.py:33
  11.9 14.6 %collective-permute-start.1 = (f16[128,1024]{1,0:T(8,128)(2,1)S(1)}, f16[128,1024]{1,0:T(8,128)(2,1)S(1)}, u32[]{:S(2)}, u32[]{:S(2)}) collective-permute-start(f16[128,1024]{1,0:T(8,128)(2,1)S(1)} %bitcast.34), channel_id=1, source_target_pairs={{0,64},{1,65},{2,66},{3,67},{4,68},{5,69},{6,70},{7,71},{8,72},{9,... | collective-permute-start | bytes 786440 | tf_op jit(solution)/shard_map/ppermute | solution.py:33
  11.9 14.6 %collective-permute-start = (f16[128,1024]{1,0:T(8,128)(2,1)S(1)}, f16[128,1024]{1,0:T(8,128)(2,1)S(1)}, u32[]{:S(2)}, u32[]{:S(2)}) collective-permute-start(f16[128,1024]{1,0:T(8,128)(2,1)S(1)} %bitcast.33), channel_id=1, source_target_pairs={{0,128},{1,129},{2,130},{3,131},{4,132},{5,133},{6,134},{7,135},{8... | collective-permute-start | bytes 786440 | tf_op jit(solution)/shard_map/ppermute | solution.py:33
  26.9 1.7 %collective-permute-start.3 = (bf16[144,1024]{1,0:T(8,128)(2,1)S(1)}, bf16[144,1024]{1,0:T(8,128)(2,1)S(1)}, u32[]{:S(2)}, u32[]{:S(2)}) collective-permute-start(bf16[144,1024]{1,0:T(8,128)(2,1)S(1)} %pad_maximum_fusion.refs_1_.refs_5_.refs_3_.refs_9_), channel_id=1, source_target_pairs={{0,1},{1,0},{2,3},{3,2},{4,5},{5,4},{6,7},{7,6},{8,9},{9,8},{10,11... | collective-permute-start | bytes 884744 | tf_op jit(solution)/shard_map/ppermute | solution.py:33
  28.8 31.4 %copy-start.5 = (bf16[288,1024]{1,0:T(8,128)(2,1)}, bf16[288,1024]{1,0:T(8,128)(2,1)S(1)}, u32[]{:S(2)}) copy-start(bf16[288,1024]{1,0:T(8,128)(2,1)S(1)} %maximum_select_fusion) | copy-start | bytes 1769476
  28.8 13.8 %collective-permute-start.4 = (bf16[288,1024]{1,0:T(8,128)(2,1)S(1)}, bf16[288,1024]{1,0:T(8,128)(2,1)S(1)}, u32[]{:S(2)}, u32[]{:S(2)}) collective-permute-start(bf16[288,1024]{1,0:T(8,128)(2,1)S(1)} %maximum_select_fusion), channel_id=1, source_target_pairs={{0,2},{1,15},{2,4},{3,1},{4,6},{5,3},{6,8},{7,5},{8,10},{9,7},{10,... | collective-permute-start | bytes 1769480 | tf_op jit(solution)/shard_map/ppermute | solution.py:33
  30.8 11.8 %collective-permute-start.5 = (bf16[288,1024]{1,0:T(8,128)(2,1)S(1)}, bf16[288,1024]{1,0:T(8,128)(2,1)S(1)}, u32[]{:S(2)}, u32[]{:S(2)}) collective-permute-start(bf16[288,1024]{1,0:T(8,128)(2,1)S(1)} %maximum_select_fusion), channel_id=1, source_target_pairs={{0,64},{1,193},{2,66},{3,195},{4,68},{5,197},{6,70},{7,199},{8,72}... | collective-permute-start | bytes 1769480 | tf_op jit(solution)/shard_map/ppermute | solution.py:33
  30.8 7.0 %collective-permute-start.6 = (bf16[144,1024]{1,0:T(8,128)(2,1)S(1)}, bf16[144,1024]{1,0:T(8,128)(2,1)S(1)}, u32[]{:S(2)}, u32[]{:S(2)}) collective-permute-start(bf16[144,1024]{1,0:T(8,128)(2,1)S(1)} %pad_maximum_fusion.refs_1_.refs_5_.refs_3_.refs_9_), channel_id=1, source_target_pairs={{0,16},{1,17},{2,18},{3,19},{4,20},{5,21},{6,22},{7,23},{8,24},{9,... | collective-permute-start | bytes 884744 | tf_op jit(solution)/shard_map/ppermute | solution.py:33
  42.6 11.8 %collective-permute-start.7 = (bf16[288,1024]{1,0:T(8,128)(2,1)S(1)}, bf16[288,1024]{1,0:T(8,128)(2,1)S(1)}, u32[]{:S(2)}, u32[]{:S(2)}) collective-permute-start(bf16[288,1024]{1,0:T(8,128)(2,1)S(1)} %collective-permute-done.4.refs_2_.refs_4_), channel_id=1, source_target_pairs={{0,2},{1,15},{2,4},{3,1},{4,6},{5,3},{6,8},{7,5},{8,10},{9,7},{10,... | collective-permute-start | bytes 1769480 | tf_op jit(solution)/shard_map/ppermute | solution.py:33
  43.8 10.5 %collective-permute-start.10 = (bf16[144,1024]{1,0:T(8,128)(2,1)S(1)}, bf16[144,1024]{1,0:T(8,128)(2,1)S(1)}, u32[]{:S(2)}, u32[]{:S(2)}) collective-permute-start(bf16[144,1024]{1,0:T(8,128)(2,1)S(1)} %collective-permute-done.6.refs_15_), channel_id=1, source_target_pairs={{0,1},{1,0},{2,3},{3,2},{4,5},{5,4},{6,7},{7,6},{8,9},{9,8},{10,11... | collective-permute-start | bytes 884744 | tf_op jit(solution)/shard_map/ppermute | solution.py:33
  45.5 7.6 %collective-permute-start.8 = (bf16[128,1024]{1,0:T(8,128)(2,1)S(1)}, bf16[128,1024]{1,0:T(8,128)(2,1)S(1)}, u32[]{:S(2)}, u32[]{:S(2)}) collective-permute-start(bf16[128,1024]{1,0:T(8,128)(2,1)S(1)} %get-tuple-element.78), channel_id=1, source_target_pairs={{0,64},{1,193},{2,66},{3,195},{4,68},{5,197},{6,70},{7,199},{8,72}... | collective-permute-start | bytes 786440 | tf_op jit(solution)/shard_map/ppermute | solution.py:33
  45.6 8.8 %collective-permute-start.9 = (bf16[128,1024]{1,0:T(8,128)(2,1)S(1)}, bf16[128,1024]{1,0:T(8,128)(2,1)}, u32[]{:S(2)}, u32[]{:S(2)}) collective-permute-start(bf16[128,1024]{1,0:T(8,128)(2,1)S(1)} %get-tuple-element.79), channel_id=1, source_target_pairs={{0,16},{1,17},{2,18},{3,19},{4,20},{5,21},{6,22},{7,23},{8,24},{9,... | collective-permute-start | bytes 786440 | tf_op jit(solution)/shard_map/ppermute | solution.py:33
  54.3 4.2 %collective-permute-start.13 = (bf16[288,1024]{1,0:T(8,128)(2,1)S(1)}, bf16[288,1024]{1,0:T(8,128)(2,1)S(1)}, u32[]{:S(2)}, u32[]{:S(2)}) collective-permute-start(bf16[288,1024]{1,0:T(8,128)(2,1)S(1)} %collective-permute-done.5.refs_7_.refs_11_), channel_id=1, source_target_pairs={{0,1},{1,0},{2,3},{3,2},{4,5},{5,4},{6,7},{7,6},{8,9},{9,8},{10,11... | collective-permute-start | bytes 1769480 | tf_op jit(solution)/shard_map/ppermute | solution.py:33
  54.4 14.0 %collective-permute-start.11 = (bf16[288,1024]{1,0:T(8,128)(2,1)S(1)}, bf16[288,1024]{1,0:T(8,128)(2,1)S(1)}, u32[]{:S(2)}, u32[]{:S(2)}) collective-permute-start(bf16[288,1024]{1,0:T(8,128)(2,1)S(1)} %collective-permute-done.7.refs_3_.refs_5_), channel_id=1, source_target_pairs={{0,2},{1,15},{2,4},{3,1},{4,6},{5,3},{6,8},{7,5},{8,10},{9,7},{10,... | collective-permute-start | bytes 1769480 | tf_op jit(solution)/shard_map/ppermute | solution.py:33
  56.4 12.0 %collective-permute-start.14 = (bf16[128,1024]{1,0:T(8,128)(2,1)S(1)}, bf16[128,1024]{1,0:T(8,128)(2,1)}, u32[]{:S(2)}, u32[]{:S(2)}) collective-permute-start(bf16[128,1024]{1,0:T(8,128)(2,1)S(1)} %collective-permute-done.8.refs_9_.refs_13_), channel_id=1, source_target_pairs={{0,1},{1,0},{2,3},{3,2},{4,5},{5,4},{6,7},{7,6},{8,9},{9,8},{10,11... | collective-permute-start | bytes 786440 | tf_op jit(solution)/shard_map/ppermute | solution.py:33
  57.3 8.6 %collective-permute-start.12 = (bf16[128,1024]{1,0:T(8,128)(2,1)}, bf16[128,1024]{1,0:T(8,128)(2,1)}, u32[]{:S(2)}, u32[]{:S(2)}) collective-permute-start(bf16[128,1024]{1,0:T(8,128)(2,1)} %get-tuple-element.52), channel_id=1, source_target_pairs={{0,16},{1,17},{2,18},{3,19},{4,20},{5,21},{6,22},{7,23},{8,24},{9,... | collective-permute-start | bytes 786440 | tf_op jit(solution)/shard_map/ppermute | solution.py:33
  58.5 9.9 %collective-permute-start.15 = (bf16[128,1024]{1,0:T(8,128)(2,1)}, bf16[128,1024]{1,0:T(8,128)(2,1)}, u32[]{:S(2)}, u32[]{:S(2)}) collective-permute-start(bf16[128,1024]{1,0:T(8,128)(2,1)} %collective-permute-done.9.refs_17_), channel_id=1, source_target_pairs={{0,1},{1,0},{2,3},{3,2},{4,5},{5,4},{6,7},{7,6},{8,9},{9,8},{10,11... | collective-permute-start | bytes 786440 | tf_op jit(solution)/shard_map/ppermute | solution.py:33
  60.1 8.3 %collective-permute-start.16 = (bf16[128,1024]{1,0:T(8,128)(2,1)}, bf16[128,1024]{1,0:T(8,128)(2,1)}, u32[]{:S(2)}, u32[]{:S(2)}) collective-permute-start(bf16[128,1024]{1,0:T(8,128)(2,1)} %pad_maximum_fusion.1), channel_id=1, source_target_pairs={{32,16},{96,80},{160,144},{224,208}} | collective-permute-start | bytes 786440 | tf_op jit(solution)/shard_map/ppermute | solution.py:33
  66.0 12.2 %collective-permute-start.18 = (bf16[128,1024]{1,0:T(8,128)(2,1)}, bf16[128,1024]{1,0:T(8,128)(2,1)S(1)}, u32[]{:S(2)}, u32[]{:S(2)}) collective-permute-start(bf16[128,1024]{1,0:T(8,128)(2,1)} %pad_maximum_fusion.1), channel_id=1, source_target_pairs={{32,0},{96,64},{160,128},{224,192}} | collective-permute-start | bytes 786440 | tf_op jit(solution)/shard_map/ppermute | solution.py:33
  69.5 8.8 %collective-permute-start.19 = (bf16[48,1024]{1,0:T(8,128)(2,1)S(1)}, bf16[48,1024]{1,0:T(8,128)(2,1)S(1)}, u32[]{:S(2)}, u32[]{:S(2)}) collective-permute-start(bf16[48,1024]{1,0:T(8,128)(2,1)S(1)} %fusion.3), channel_id=1, source_target_pairs={{32,18},{33,17},{34,20},{36,22},{38,24},{43,27},{45,29},{47,31},{9... | collective-permute-start | bytes 294920 | tf_op jit(solution)/shard_map/ppermute | solution.py:33
  72.2 6.5 %collective-permute-start.17 = (bf16[128,1024]{1,0:T(8,128)(2,1)S(1)}, bf16[128,1024]{1,0:T(8,128)(2,1)S(1)}, u32[]{:S(2)}, u32[]{:S(2)}) collective-permute-start(bf16[128,1024]{1,0:T(8,128)(2,1)S(1)} %collective-permute-done.8.refs_9_.refs_13_), channel_id=1, source_target_pairs={{0,16},{1,17},{2,18},{3,19},{4,20},{5,21},{6,22},{7,23},{8,24},{9,... | collective-permute-start | bytes 786440 | tf_op jit(solution)/shard_map/ppermute | solution.py:33
  72.3 9.9 %collective-permute-start.20 = (bf16[144,1024]{1,0:T(8,128)(2,1)S(1)}, bf16[144,1024]{1,0:T(8,128)(2,1)S(1)}, u32[]{:S(2)}, u32[]{:S(2)}) collective-permute-start(bf16[144,1024]{1,0:T(8,128)(2,1)S(1)} %slice_select_fusion), channel_id=1, source_target_pairs={{0,2},{1,15},{2,4},{3,1},{4,6},{5,3},{6,8},{7,5},{8,10},{9,7},{10,... | collective-permute-start | bytes 884744 | tf_op jit(solution)/shard_map/ppermute | solution.py:33
  79.7 1.3 %collective-permute-start.23 = (bf16[128,1024]{1,0:T(8,128)(2,1)S(1)}, bf16[128,1024]{1,0:T(8,128)(2,1)S(1)}, u32[]{:S(2)}, u32[]{:S(2)}) collective-permute-start(bf16[128,1024]{1,0:T(8,128)(2,1)S(1)} %add.132), channel_id=1, source_target_pairs={{0,1},{16,17},{64,65},{80,81},{128,129},{144,145},{192,193},{208,2... | collective-permute-start | bytes 786440 | tf_op jit(solution)/shard_map/ppermute | solution.py:33
  80.4 1.8 %collective-permute-start.21 = (bf16[128,1024]{1,0:T(8,128)(2,1)}, bf16[128,1024]{1,0:T(8,128)(2,1)S(1)}, u32[]{:S(2)}, u32[]{:S(2)}) collective-permute-start(bf16[128,1024]{1,0:T(8,128)(2,1)} %collective-permute-done.12.refs_18_), channel_id=1, source_target_pairs={{0,1},{1,0},{2,3},{3,2},{4,5},{5,4},{6,7},{7,6},{8,9},{9,8},{10,11... | collective-permute-start | bytes 786440 | tf_op jit(solution)/shard_map/ppermute | solution.py:33
  80.5 1.9 %collective-permute-start.22 = (bf16[128,1024]{1,0:T(8,128)(2,1)S(1)}, bf16[128,1024]{1,0:T(8,128)(2,1)S(1)}, u32[]{:S(2)}, u32[]{:S(2)}) collective-permute-start(bf16[128,1024]{1,0:T(8,128)(2,1)S(1)} %collective-permute-done.17.refs_21_), channel_id=1, source_target_pairs={{0,1},{1,0},{2,3},{3,2},{4,5},{5,4},{6,7},{7,6},{8,9},{9,8},{10,11... | collective-permute-start | bytes 786440 | tf_op jit(solution)/shard_map/ppermute | solution.py:33
  87.8 1.3 %collective-permute-start.24 = (f32[4,1152]{1,0:T(4,128)S(1)}, f32[4,1152]{1,0:T(4,128)S(1)}, u32[]{:S(2)}, u32[]{:S(2)}) collective-permute-start(f32[4,1152]{1,0:T(4,128)S(1)} %get-tuple-element.74), channel_id=1, source_target_pairs={{0,1},{1,0},{2,3},{3,2},{4,5},{5,4},{6,7},{7,6},{8,9},{9,8},{10,11... | collective-permute-start | bytes 55304 | tf_op jit(solution)/shard_map/ppermute | solution.py:33
  89.1 8.9 %collective-permute-start.25 = (f32[4,512]{1,0:T(4,128)S(1)}, f32[4,512]{1,0:T(4,128)S(1)}, u32[]{:S(2)}, u32[]{:S(2)}) collective-permute-start(f32[4,512]{1,0:T(4,128)S(1)} %slice_add_fusion), channel_id=1, source_target_pairs={{0,16},{1,17},{2,18},{3,19},{4,20},{5,21},{6,22},{7,23},{8,24},{9,... | collective-permute-start | bytes 24584 | tf_op jit(solution)/shard_map/ppermute | solution.py:33
  91.0 7.0 %collective-permute-start.26 = (f32[4,128]{1,0:T(4,128)S(1)}, f32[4,128]{1,0:T(4,128)S(1)}, u32[]{:S(2)}, u32[]{:S(2)}) collective-permute-start(f32[4,128]{1,0:T(4,128)S(1)} %slice_add_fusion.2), channel_id=1, source_target_pairs={{0,32},{64,96},{128,160},{192,224}} | collective-permute-start | bytes 6152 | tf_op jit(solution)/shard_map/ppermute | solution.py:33
  92.2 5.7 %collective-permute-start.27 = (f32[4,128]{1,0:T(4,128)S(1)}, f32[4,128]{1,0:T(4,128)S(1)}, u32[]{:S(2)}, u32[]{:S(2)}) collective-permute-start(f32[4,128]{1,0:T(4,128)S(1)} %slice_add_fusion.2), channel_id=1, source_target_pairs={{16,32},{80,96},{144,160},{208,224}} | collective-permute-start | bytes 6152 | tf_op jit(solution)/shard_map/ppermute | solution.py:33
  98.1 5.2 %collective-permute-start.28 = (f32[4,4,128]{2,1,0:T(4,128)S(1)}, f32[4,4,128]{2,1,0:T(4,128)S(1)}, u32[]{:S(2)}, u32[]{:S(2)}) collective-permute-start(f32[4,4,128]{2,1,0:T(4,128)S(1)} %pad_add_fusion), channel_id=1, source_target_pairs={{0,128},{1,129},{2,130},{3,131},{4,132},{5,133},{6,134},{7,135},{8... | collective-permute-start | bytes 24584 | tf_op jit(solution)/shard_map/ppermute | solution.py:33
  99.8 4.9 %collective-permute-start.29 = (f32[4,4,128]{2,1,0:T(4,128)S(1)}, f32[4,4,128]{2,1,0:T(4,128)S(1)}, u32[]{:S(2)}, u32[]{:S(2)}) collective-permute-start(f32[4,4,128]{2,1,0:T(4,128)S(1)} %pad_add_fusion), channel_id=1, source_target_pairs={{0,64},{1,65},{2,66},{3,67},{4,68},{5,69},{6,70},{7,71},{8,72},{9,... | collective-permute-start | bytes 24584 | tf_op jit(solution)/shard_map/ppermute | solution.py:33
  99.8 4.9 %collective-permute-start.30 = (f32[4,4,128]{2,1,0:T(4,128)S(1)}, f32[4,4,128]{2,1,0:T(4,128)S(1)}, u32[]{:S(2)}, u32[]{:S(2)}) collective-permute-start(f32[4,4,128]{2,1,0:T(4,128)S(1)} %pad_add_fusion), channel_id=1, source_target_pairs={{0,192},{1,193},{2,194},{3,195},{4,196},{5,197},{6,198},{7,199},{8... | collective-permute-start | bytes 24584 | tf_op jit(solution)/shard_map/ppermute | solution.py:33
  (7 other events, 39.0 us)

commit v13 on v11

--- a/solution.py
+++ b/solution.py
@@ -138,9 +138,10 @@
     if late:
         rows("x1", TAG, CHUNK)
         rows("w2", 0, CHUNK + 2 * BLOCK)
-        for b in range(NC):
-            rows(("xa", "xb")[b], 0, CHUNK + side[b] + turn * BLOCK)
-            rows(("xa_t", "xb_t")[b], 0, CHUNK + side[b] + (NY - turn) * BLOCK)
+        rows("xa", 0, CHUNK + turn * BLOCK)
+        rows("xb", 0, 3 * CHUNK + turn * BLOCK)
+        rows("xa_t", 0, 3 * CHUNK + (NY - turn) * BLOCK)
+        rows("xb_t", 0, CHUNK + (NY - turn) * BLOCK)
         rows("x1_t", TAG, 3 * CHUNK)
         rows("w2_t", 0, 3 * CHUNK + 2 * BLOCK)
         rows("odd", 0, 4 * CHUNK)
@@ -282,13 +283,17 @@
     z1, y1, x1 = fence(z1, y1, x1)
 
     z2 = permute(z1, same_core)
-    y2 = permute(jnp.where(c == 0, y1[TAG:tagged], y1[tagged + TAG :]), y_way)
-    xa = permute(y1[TAG:tagged], swap_x)
+    near_one, far_one = y1[TAG:tagged], y1[tagged + TAG :]
+    y1_mine = jnp.where(c == 0, near_one, far_one)
+    y1_other = jnp.where(c == 0, far_one, near_one)
+    y1_mine, y1_other = fence(y1_mine, y1_other)
+    y2 = permute(y1_mine, y_way)
+    xa = permute(y1_mine, swap_x)
     x1_t = permute(x1, swap_core)
     z1, z2, y2, xa, y1, x1_t = fence(z1, z2, y2, xa, y1, x1_t)
 
     z3 = permute(z2, same_core)
-    xb = permute(y1[tagged + TAG :], swap_x)
+    xb = permute(y1_other, swap_x)
     y1_t = permute(y1, swap_core)
     head = TAG + PIECE
     odd_rows = jnp.concatenate([own[TAG:head], y1_t[TAG:head], y2[:PIECE], y1[TAG:head]], axis=0)

time: 103 us -> 103 us (level)
  transfers between devices with their start and end apart: 31 -> 31, of which waited for: 16 -> 16; matrix products, arithmetic and copies ran while one was open for 7% -> 8% of each run, Pallas kernels for 4% -> 4%
where the time goes in v13:
time: 103 us; the launch traced here: 102 us
  starting transfers between devices  37.9 us (37%)
  waiting for transfers between devices  37.5 us (36%)
  Pallas kernels  14.6 us (14%)
  other arithmetic  8.62 us (8%)
  local copies, waits for them, and re-layouts  3.26 us (3%)
    ppermute x31, starting transfers between devices, permute(): return lax.ppermute(value, AXES, pairs)  37.9 us
    ppermute x31, waiting for transfers between devices, permute(): return lax.ppermute(value, AXES, pairs)  37.5 us
    pallas_call x2, Pallas kernels, pair_sums(): pl.pallas_call(functools.partial(pair_kernel, col_cuts=tuple(col_cuts), n...  9.16 us
    pallas_call x1, Pallas kernels, raw_partial(): pl.pallas_call(raw_kernel, grid=(feats // width,), in_specs=[pl.BlockSpec...  5.49 us
    convert_element_type x1, other arithmetic, shards(): tag = tag.astype(jnp.bfloat16)  2.66 us
  transfers between devices with their start and end apart: 31, of which 16 were waited for; matrix products, arithmetic and copies ran while one was open for 8% of the time, Pallas kernels for 4%

profile of v13, /device:TPU:4, one launch (start us, length us, event | category | flops | bytes accessed | tf_op | source)
XLA Modules:
  0.0 102.3 jit_solution(2091814144224415836)
XLA Ops:
  0.0 5.5 %raw.1 = f32[512,1024]{1,0:T(8,128)} custom-call(s32[8,11]{1,0:T(8,128)} %bitcast.41, bf16[1584,512]{1,0:T(8,128)(2,1)} %bitcast.35, bf16[1584,1024]{1,0:T(8,128)(2,1)} %geometry.1), custom_call_target="tpu_custom_call" | custom-call | flops 1660944384 | bytes 8388608 | tf_op jit(solution)/shard_map/raw/pallas_call | solution.py:84
  5.5 1.7 %constant_dynamic-slice_fusion.1 = (f32[4,1,32,1024]{3,2,1,0:T(8,128)S(1)}, f16[4,1,32,1024]{3,2,0,1:T(8,128)(2,1)S(1)}, f16[4,1,32,1024]{3,2,0,1:T(8,128)(2,1)S(1)}, f16[4,1,32,1024]{3,2,0,1:T(8,128)(2,1)S(1)}) fusion(f32[4,4,32,1024]{3,2,1,0:T(8,128)} %bitcast.34, s32[]{:T(128)S(6)} %select_n.184, s32[]{:T(128)S(6)} %select_n.188, s32[]{:T(128)S(6)} %select_n.186, ...), kind=kLoop, calls=%fused_computation.44 | loop fusion | flops 393216 | bytes 3407888 | tf_op jit(solution)/shard_map/jit(dynamic_index_in_dim)/dynamic_slice | solution.py:265
  7.2 3.3 %collective-permute-start = (f16[128,1024]{1,0:T(8,128)(2,1)S(1)}, f16[128,1024]{1,0:T(8,128)(2,1)S(1)}, u32[]{:S(2)}, u32[]{:S(2)}) collective-permute-start(f16[128,1024]{1,0:T(8,128)(2,1)S(1)} %bitcast.38), channel_id=1, source_target_pairs={{0,128},{1,129},{2,130},{3,131},{4,132},{5,133},{6,134},{7,135},{8... | collective-permute-start | bytes 786440 | tf_op jit(solution)/shard_map/ppermute | solution.py:33
  11.2 2.6 %collective-permute-start.2 = (f16[128,1024]{1,0:T(8,128)(2,1)S(1)}, f16[128,1024]{1,0:T(8,128)(2,1)S(1)}, u32[]{:S(2)}, u32[]{:S(2)}) collective-permute-start(f16[128,1024]{1,0:T(8,128)(2,1)S(1)} %bitcast.36), channel_id=1, source_target_pairs={{0,192},{1,193},{2,194},{3,195},{4,196},{5,197},{6,198},{7,199},{8... | collective-permute-start | bytes 786440 | tf_op jit(solution)/shard_map/ppermute | solution.py:33
  14.5 2.7 %select_convert_fusion = bf16[16,1024]{1,0:T(8,128)(2,1)S(1)} fusion(bf16[]{:T(256)} %bitcast.5, bf16[]{:T(256)} %bitcast.4, bf16[]{:T(256)} %bitcast.3, bf16[]{:T(256)} %bitcast.2, s32[1024]{0:T(1024)S(1)} %get-tuple-element.79, s32[1024]{0:T(1024)S(1)} %get-tuple-element.80, pred[16]{0:T(512)(128)(4,1)S(1)} %iota_compare_fusion, pred[1024]{0:T(1024)(128)(4,1)S(1)} %fusion.13), kind=kLoop, calls=%fused_computation.17 | loop fusion | flops 163840 | bytes 42008 | tf_op jit(solution)/shard_map/convert_element_type | solution.py:260
  18.1 4.4 %collective-permute-done.1 = f16[128,1024]{1,0:T(8,128)(2,1)S(1)} collective-permute-done((f16[128,1024]{1,0:T(8,128)(2,1)S(1)}, f16[128,1024]{1,0:T(8,128)(2,1)S(1)}, u32[]{:S(2)}, u32[]{:S(2)}) %collective-permute-start.1) | collective-permute-done | bytes 262176 | tf_op jit(solution)/shard_map/ppermute | solution.py:33
  23.4 1.6 %collective-permute-done.3.refs_6_.refs_10_ = bf16[144,1024]{1,0:T(8,128)(2,1)S(1)} collective-permute-done((bf16[144,1024]{1,0:T(8,128)(2,1)S(1)}, bf16[144,1024]{1,0:T(8,128)(2,1)S(1)}, u32[]{:S(2)}, u32[]{:S(2)}) %collective-permute-start.3) | collective-permute-done | bytes 294944 | tf_op jit(solution)/shard_map/ppermute | solution.py:33
  25.2 2.0 %collective-permute-start.4 = (bf16[288,1024]{1,0:T(8,128)(2,1)S(1)}, bf16[288,1024]{1,0:T(8,128)(2,1)S(1)}, u32[]{:S(2)}, u32[]{:S(2)}) collective-permute-start(bf16[288,1024]{1,0:T(8,128)(2,1)S(1)} %maximum_select_fusion), channel_id=1, source_target_pairs={{0,2},{1,15},{2,4},{3,1},{4,6},{5,3},{6,8},{7,5},{8,10},{9,7},{10,... | collective-permute-start | bytes 1769480 | tf_op jit(solution)/shard_map/ppermute | solution.py:33
  27.2 1.4 %collective-permute-start.5 = (bf16[288,1024]{1,0:T(8,128)(2,1)S(1)}, bf16[288,1024]{1,0:T(8,128)(2,1)S(1)}, u32[]{:S(2)}, u32[]{:S(2)}) collective-permute-start(bf16[288,1024]{1,0:T(8,128)(2,1)S(1)} %maximum_select_fusion), channel_id=1, source_target_pairs={{0,64},{1,193},{2,66},{3,195},{4,68},{5,197},{6,70},{7,199},{8,72}... | collective-permute-start | bytes 1769480 | tf_op jit(solution)/shard_map/ppermute | solution.py:33
  28.5 1.2 %collective-permute-start.6 = (bf16[144,1024]{1,0:T(8,128)(2,1)S(1)}, bf16[144,1024]{1,0:T(8,128)(2,1)S(1)}, u32[]{:S(2)}, u32[]{:S(2)}) collective-permute-start(bf16[144,1024]{1,0:T(8,128)(2,1)S(1)} %pad_maximum_fusion.refs_1_.refs_5_.refs_3_.refs_9_), channel_id=1, source_target_pairs={{0,16},{1,17},{2,18},{3,19},{4,20},{5,21},{6,22},{7,23},{8,24},{9,... | collective-permute-start | bytes 884744 | tf_op jit(solution)/shard_map/ppermute | solution.py:33
  29.7 5.5 %collective-permute-done.6.refs_15_ = bf16[144,1024]{1,0:T(8,128)(2,1)S(1)} collective-permute-done((bf16[144,1024]{1,0:T(8,128)(2,1)S(1)}, bf16[144,1024]{1,0:T(8,128)(2,1)S(1)}, u32[]{:S(2)}, u32[]{:S(2)}) %collective-permute-start.6) | collective-permute-done | bytes 294944 | tf_op jit(solution)/shard_map/ppermute | solution.py:33
  35.3 3.7 %collective-permute-done.4.refs_2_.refs_4_ = bf16[288,1024]{1,0:T(8,128)(2,1)S(1)} collective-permute-done((bf16[288,1024]{1,0:T(8,128)(2,1)S(1)}, bf16[288,1024]{1,0:T(8,128)(2,1)S(1)}, u32[]{:S(2)}, u32[]{:S(2)}) %collective-permute-start.4) | collective-permute-done | bytes 589856 | tf_op jit(solution)/shard_map/ppermute | solution.py:33
  39.0 1.2 %collective-permute-start.7 = (bf16[288,1024]{1,0:T(8,128)(2,1)S(1)}, bf16[288,1024]{1,0:T(8,128)(2,1)S(1)}, u32[]{:S(2)}, u32[]{:S(2)}) collective-permute-start(bf16[288,1024]{1,0:T(8,128)(2,1)S(1)} %collective-permute-done.4.refs_2_.refs_4_), channel_id=1, source_target_pairs={{0,2},{1,15},{2,4},{3,1},{4,6},{5,3},{6,8},{7,5},{8,10},{9,7},{10,... | collective-permute-start | bytes 1769480 | tf_op jit(solution)/shard_map/ppermute | solution.py:33
  40.2 2.0 %collective-permute-start.10 = (bf16[144,1024]{1,0:T(8,128)(2,1)S(1)}, bf16[144,1024]{1,0:T(8,128)(2,1)S(1)}, u32[]{:S(2)}, u32[]{:S(2)}) collective-permute-start(bf16[144,1024]{1,0:T(8,128)(2,1)S(1)} %collective-permute-done.6.refs_15_), channel_id=1, source_target_pairs={{0,1},{1,0},{2,3},{3,2},{4,5},{5,4},{6,7},{7,6},{8,9},{9,8},{10,11... | collective-permute-start | bytes 884744 | tf_op jit(solution)/shard_map/ppermute | solution.py:33
  43.0 1.2 %collective-permute-start.9 = (bf16[128,1024]{1,0:T(8,128)(2,1)S(1)}, bf16[128,1024]{1,0:T(8,128)(2,1)}, u32[]{:S(2)}, u32[]{:S(2)}) collective-permute-start(bf16[128,1024]{1,0:T(8,128)(2,1)S(1)} %get-tuple-element.38), channel_id=1, source_target_pairs={{0,16},{1,17},{2,18},{3,19},{4,20},{5,21},{6,22},{7,23},{8,24},{9,... | collective-permute-start | bytes 786440 | tf_op jit(solution)/shard_map/ppermute | solution.py:33
  44.2 6.3 %collective-permute-done.8.refs_9_.refs_13_ = bf16[128,1024]{1,0:T(8,128)(2,1)S(1)} collective-permute-done((bf16[128,1024]{1,0:T(8,128)(2,1)S(1)}, bf16[128,1024]{1,0:T(8,128)(2,1)S(1)}, u32[]{:S(2)}, u32[]{:S(2)}) %collective-permute-start.8) | collective-permute-done | bytes 262176 | tf_op jit(solution)/shard_map/ppermute | solution.py:33
  53.6 1.2 %collective-permute-start.12 = (bf16[128,1024]{1,0:T(8,128)(2,1)}, bf16[128,1024]{1,0:T(8,128)(2,1)}, u32[]{:S(2)}, u32[]{:S(2)}) collective-permute-start(bf16[128,1024]{1,0:T(8,128)(2,1)} %get-tuple-element.42), channel_id=1, source_target_pairs={{0,16},{1,17},{2,18},{3,19},{4,20},{5,21},{6,22},{7,23},{8,24},{9,... | collective-permute-start | bytes 786440 | tf_op jit(solution)/shard_map/ppermute | solution.py:33
  54.8 1.2 %collective-permute-start.14 = (bf16[128,1024]{1,0:T(8,128)(2,1)S(1)}, bf16[128,1024]{1,0:T(8,128)(2,1)}, u32[]{:S(2)}, u32[]{:S(2)}) collective-permute-start(bf16[128,1024]{1,0:T(8,128)(2,1)S(1)} %collective-permute-done.8.refs_9_.refs_13_), channel_id=1, source_target_pairs={{0,1},{1,0},{2,3},{3,2},{4,5},{5,4},{6,7},{7,6},{8,9},{9,8},{10,11... | collective-permute-start | bytes 786440 | tf_op jit(solution)/shard_map/ppermute | solution.py:33
  57.9 2.5 %collective-permute-start.16 = (bf16[128,1024]{1,0:T(8,128)(2,1)}, bf16[128,1024]{1,0:T(8,128)(2,1)}, u32[]{:S(2)}, u32[]{:S(2)}) collective-permute-start(bf16[128,1024]{1,0:T(8,128)(2,1)} %pad_maximum_fusion.1), channel_id=1, source_target_pairs={{32,16},{96,80},{160,144},{224,208}} | collective-permute-start | bytes 786440 | tf_op jit(solution)/shard_map/ppermute | solution.py:33
  60.4 2.3 %collective-permute-done.12.refs_18_ = bf16[128,1024]{1,0:T(8,128)(2,1)} collective-permute-done((bf16[128,1024]{1,0:T(8,128)(2,1)}, bf16[128,1024]{1,0:T(8,128)(2,1)}, u32[]{:S(2)}, u32[]{:S(2)}) %collective-permute-start.12) | collective-permute-done | bytes 262176 | tf_op jit(solution)/shard_map/ppermute | solution.py:33
  62.7 2.4 %collective-permute-start.18 = (bf16[128,1024]{1,0:T(8,128)(2,1)}, bf16[128,1024]{1,0:T(8,128)(2,1)S(1)}, u32[]{:S(2)}, u32[]{:S(2)}) collective-permute-start(bf16[128,1024]{1,0:T(8,128)(2,1)} %pad_maximum_fusion.1), channel_id=1, source_target_pairs={{32,0},{96,64},{160,128},{224,192}} | collective-permute-start | bytes 786440 | tf_op jit(solution)/shard_map/ppermute | solution.py:33
  66.1 1.3 %collective-permute-start.19 = (bf16[48,1024]{1,0:T(8,128)(2,1)S(1)}, bf16[48,1024]{1,0:T(8,128)(2,1)S(1)}, u32[]{:S(2)}, u32[]{:S(2)}) collective-permute-start(bf16[48,1024]{1,0:T(8,128)(2,1)S(1)} %fusion.3), channel_id=1, source_target_pairs={{32,18},{33,17},{34,20},{36,22},{38,24},{43,27},{45,29},{47,31},{9... | collective-permute-start | bytes 294920 | tf_op jit(solution)/shard_map/ppermute | solution.py:33
  68.7 3.7 %early.1 = (f32[4,512]{1,0:T(4,128)S(1)}, f32[4,512]{1,0:T(4,128)S(1)}) custom-call(s32[2]{0:T(128)S(1)} %pad_add_fusion.1.refs_0_, bf16[144,1024]{1,0:T(8,128)(2,1)S(1)} %pad_maximum_fusion.refs_1_.refs_5_.refs_3_.refs_9_, bf16[288,1024]{1,0:T(8,128)(2,1)S(1)} %collective-permute-done.4.refs_2_.refs_4_, ...), custom_call_target="tpu_custom_call" | custom-call | flops 5637144576 | bytes 11796480 | tf_op jit(solution)/shard_map/early/pallas_call | solution.py:224
  72.4 2.9 %collective-permute-done.17.refs_21_ = bf16[128,1024]{1,0:T(8,128)(2,1)S(1)} collective-permute-done((bf16[128,1024]{1,0:T(8,128)(2,1)S(1)}, bf16[128,1024]{1,0:T(8,128)(2,1)S(1)}, u32[]{:S(2)}, u32[]{:S(2)}) %collective-permute-start.17) | collective-permute-done | bytes 262176 | tf_op jit(solution)/shard_map/ppermute | solution.py:33
  79.1 5.4 %late.1 = (f32[4,512]{1,0:T(4,128)S(1)}, f32[4,512]{1,0:T(4,128)S(1)}, f32[4,1152]{1,0:T(4,128)S(1)}, f32[4,128]{1,0:T(4,128)S(1)}) custom-call(s32[2]{0:T(128)S(1)} %pad_add_fusion.1.refs_0_, f32[4,512]{1,0:T(4,128)S(1)} %get-tuple-element.54.refs_1_, f32[4,512]{1,0:T(4,128)S(1)} %get-tuple-element.55.refs_2_, ...), custom_call_target="tpu_custom_call" | custom-call | flops 16609443840 | bytes 22216704 | tf_op jit(solution)/shard_map/late/pallas_call | solution.py:224
  85.8 1.9 %collective-permute-start.25 = (f32[4,512]{1,0:T(4,128)S(1)}, f32[4,512]{1,0:T(4,128)S(1)}, u32[]{:S(2)}, u32[]{:S(2)}) collective-permute-start(f32[4,512]{1,0:T(4,128)S(1)} %slice_add_fusion), channel_id=1, source_target_pairs={{0,16},{1,17},{2,18},{3,19},{4,20},{5,21},{6,22},{7,23},{8,24},{9,... | collective-permute-start | bytes 24584 | tf_op jit(solution)/shard_map/ppermute | solution.py:33
  87.7 1.3 %collective-permute-start.26 = (f32[4,128]{1,0:T(4,128)S(1)}, f32[4,128]{1,0:T(4,128)S(1)}, u32[]{:S(2)}, u32[]{:S(2)}) collective-permute-start(f32[4,128]{1,0:T(4,128)S(1)} %slice_add_fusion.2), channel_id=1, source_target_pairs={{0,32},{64,96},{128,160},{192,224}} | collective-permute-start | bytes 6152 | tf_op jit(solution)/shard_map/ppermute | solution.py:33
  89.0 1.3 %collective-permute-start.27 = (f32[4,128]{1,0:T(4,128)S(1)}, f32[4,128]{1,0:T(4,128)S(1)}, u32[]{:S(2)}, u32[]{:S(2)}) collective-permute-start(f32[4,128]{1,0:T(4,128)S(1)} %slice_add_fusion.2), channel_id=1, source_target_pairs={{16,32},{80,96},{144,160},{208,224}} | collective-permute-start | bytes 6152 | tf_op jit(solution)/shard_map/ppermute | solution.py:33
  90.3 4.4 %collective-permute-done.26 = f32[4,128]{1,0:T(4,128)S(1)} collective-permute-done((f32[4,128]{1,0:T(4,128)S(1)}, f32[4,128]{1,0:T(4,128)S(1)}, u32[]{:S(2)}, u32[]{:S(2)}) %collective-permute-start.26) | collective-permute-done | bytes 2080 | tf_op jit(solution)/shard_map/ppermute | solution.py:33
  94.8 1.8 %collective-permute-start.28 = (f32[4,4,128]{2,1,0:T(4,128)S(1)}, f32[4,4,128]{2,1,0:T(4,128)S(1)}, u32[]{:S(2)}, u32[]{:S(2)}) collective-permute-start(f32[4,4,128]{2,1,0:T(4,128)S(1)} %pad_add_fusion), channel_id=1, source_target_pairs={{0,128},{1,129},{2,130},{3,131},{4,132},{5,133},{6,134},{7,135},{8... | collective-permute-start | bytes 24584 | tf_op jit(solution)/shard_map/ppermute | solution.py:33
  97.2 2.6 %collective-permute-start.30 = (f32[4,4,128]{2,1,0:T(4,128)S(1)}, f32[4,4,128]{2,1,0:T(4,128)S(1)}, u32[]{:S(2)}, u32[]{:S(2)}) collective-permute-start(f32[4,4,128]{2,1,0:T(4,128)S(1)} %pad_add_fusion), channel_id=1, source_target_pairs={{0,192},{1,193},{2,194},{3,195},{4,196},{5,197},{6,198},{7,199},{8... | collective-permute-start | bytes 24584 | tf_op jit(solution)/shard_map/ppermute | solution.py:33
  100.1 1.4 %collective-permute-done.29 = f32[4,4,128]{2,1,0:T(4,128)S(1)} collective-permute-done((f32[4,4,128]{2,1,0:T(4,128)S(1)}, f32[4,4,128]{2,1,0:T(4,128)S(1)}, u32[]{:S(2)}, u32[]{:S(2)}) %collective-permute-start.29) | collective-permute-done | bytes 8224 | tf_op jit(solution)/shard_map/ppermute | solution.py:33
  (90 shorter events, 18.2 us)
Async XLA Ops:
  7.2 10.8 %collective-permute-start = (f16[128,1024]{1,0:T(8,128)(2,1)S(1)}, f16[128,1024]{1,0:T(8,128)(2,1)S(1)}, u32[]{:S(2)}, u32[]{:S(2)}) collective-permute-start(f16[128,1024]{1,0:T(8,128)(2,1)S(1)} %bitcast.38), channel_id=1, source_target_pairs={{0,128},{1,129},{2,130},{3,131},{4,132},{5,133},{6,134},{7,135},{8... | collective-permute-start | bytes 786440 | tf_op jit(solution)/shard_map/ppermute | solution.py:33
  10.5 12.0 %collective-permute-start.1 = (f16[128,1024]{1,0:T(8,128)(2,1)S(1)}, f16[128,1024]{1,0:T(8,128)(2,1)S(1)}, u32[]{:S(2)}, u32[]{:S(2)}) collective-permute-start(f16[128,1024]{1,0:T(8,128)(2,1)S(1)} %bitcast.37), channel_id=1, source_target_pairs={{0,64},{1,65},{2,66},{3,67},{4,68},{5,69},{6,70},{7,71},{8,72},{9,... | collective-permute-start | bytes 786440 | tf_op jit(solution)/shard_map/ppermute | solution.py:33
  11.2 11.7 %collective-permute-start.2 = (f16[128,1024]{1,0:T(8,128)(2,1)S(1)}, f16[128,1024]{1,0:T(8,128)(2,1)S(1)}, u32[]{:S(2)}, u32[]{:S(2)}) collective-permute-start(f16[128,1024]{1,0:T(8,128)(2,1)S(1)} %bitcast.36), channel_id=1, source_target_pairs={{0,192},{1,193},{2,194},{3,195},{4,196},{5,197},{6,198},{7,199},{8... | collective-permute-start | bytes 786440 | tf_op jit(solution)/shard_map/ppermute | solution.py:33
  23.3 1.7 %collective-permute-start.3 = (bf16[144,1024]{1,0:T(8,128)(2,1)S(1)}, bf16[144,1024]{1,0:T(8,128)(2,1)S(1)}, u32[]{:S(2)}, u32[]{:S(2)}) collective-permute-start(bf16[144,1024]{1,0:T(8,128)(2,1)S(1)} %pad_maximum_fusion.refs_1_.refs_5_.refs_3_.refs_9_), channel_id=1, source_target_pairs={{0,1},{1,0},{2,3},{3,2},{4,5},{5,4},{6,7},{7,6},{8,9},{9,8},{10,11... | collective-permute-start | bytes 884744 | tf_op jit(solution)/shard_map/ppermute | solution.py:33
  25.2 32.7 %copy-start.5 = (bf16[288,1024]{1,0:T(8,128)(2,1)}, bf16[288,1024]{1,0:T(8,128)(2,1)S(1)}, u32[]{:S(2)}) copy-start(bf16[288,1024]{1,0:T(8,128)(2,1)S(1)} %maximum_select_fusion) | copy-start | bytes 1769476
  25.2 13.8 %collective-permute-start.4 = (bf16[288,1024]{1,0:T(8,128)(2,1)S(1)}, bf16[288,1024]{1,0:T(8,128)(2,1)S(1)}, u32[]{:S(2)}, u32[]{:S(2)}) collective-permute-start(bf16[288,1024]{1,0:T(8,128)(2,1)S(1)} %maximum_select_fusion), channel_id=1, source_target_pairs={{0,2},{1,15},{2,4},{3,1},{4,6},{5,3},{6,8},{7,5},{8,10},{9,7},{10,... | collective-permute-start | bytes 1769480 | tf_op jit(solution)/shard_map/ppermute | solution.py:33
  27.2 11.8 %collective-permute-start.5 = (bf16[288,1024]{1,0:T(8,128)(2,1)S(1)}, bf16[288,1024]{1,0:T(8,128)(2,1)S(1)}, u32[]{:S(2)}, u32[]{:S(2)}) collective-permute-start(bf16[288,1024]{1,0:T(8,128)(2,1)S(1)} %maximum_select_fusion), channel_id=1, source_target_pairs={{0,64},{1,193},{2,66},{3,195},{4,68},{5,197},{6,70},{7,199},{8,72}... | collective-permute-start | bytes 1769480 | tf_op jit(solution)/shard_map/ppermute | solution.py:33
  28.5 6.7 %collective-permute-start.6 = (bf16[144,1024]{1,0:T(8,128)(2,1)S(1)}, bf16[144,1024]{1,0:T(8,128)(2,1)S(1)}, u32[]{:S(2)}, u32[]{:S(2)}) collective-permute-start(bf16[144,1024]{1,0:T(8,128)(2,1)S(1)} %pad_maximum_fusion.refs_1_.refs_5_.refs_3_.refs_9_), channel_id=1, source_target_pairs={{0,16},{1,17},{2,18},{3,19},{4,20},{5,21},{6,22},{7,23},{8,24},{9,... | collective-permute-start | bytes 884744 | tf_op jit(solution)/shard_map/ppermute | solution.py:33
  39.0 12.6 %collective-permute-start.7 = (bf16[288,1024]{1,0:T(8,128)(2,1)S(1)}, bf16[288,1024]{1,0:T(8,128)(2,1)S(1)}, u32[]{:S(2)}, u32[]{:S(2)}) collective-permute-start(bf16[288,1024]{1,0:T(8,128)(2,1)S(1)} %collective-permute-done.4.refs_2_.refs_4_), channel_id=1, source_target_pairs={{0,2},{1,15},{2,4},{3,1},{4,6},{5,3},{6,8},{7,5},{8,10},{9,7},{10,... | collective-permute-start | bytes 1769480 | tf_op jit(solution)/shard_map/ppermute | solution.py:33
  40.2 11.4 %collective-permute-start.10 = (bf16[144,1024]{1,0:T(8,128)(2,1)S(1)}, bf16[144,1024]{1,0:T(8,128)(2,1)S(1)}, u32[]{:S(2)}, u32[]{:S(2)}) collective-permute-start(bf16[144,1024]{1,0:T(8,128)(2,1)S(1)} %collective-permute-done.6.refs_15_), channel_id=1, source_target_pairs={{0,1},{1,0},{2,3},{3,2},{4,5},{5,4},{6,7},{7,6},{8,9},{9,8},{10,11... | collective-permute-start | bytes 884744 | tf_op jit(solution)/shard_map/ppermute | solution.py:33
  42.9 7.6 %collective-permute-start.8 = (bf16[128,1024]{1,0:T(8,128)(2,1)S(1)}, bf16[128,1024]{1,0:T(8,128)(2,1)S(1)}, u32[]{:S(2)}, u32[]{:S(2)}) collective-permute-start(bf16[128,1024]{1,0:T(8,128)(2,1)S(1)} %get-tuple-element.38), channel_id=1, source_target_pairs={{0,64},{1,193},{2,66},{3,195},{4,68},{5,197},{6,70},{7,199},{8,72}... | collective-permute-start | bytes 786440 | tf_op jit(solution)/shard_map/ppermute | solution.py:33
  43.0 8.6 %collective-permute-start.9 = (bf16[128,1024]{1,0:T(8,128)(2,1)S(1)}, bf16[128,1024]{1,0:T(8,128)(2,1)}, u32[]{:S(2)}, u32[]{:S(2)}) collective-permute-start(bf16[128,1024]{1,0:T(8,128)(2,1)S(1)} %get-tuple-element.38), channel_id=1, source_target_pairs={{0,16},{1,17},{2,18},{3,19},{4,20},{5,21},{6,22},{7,23},{8,24},{9,... | collective-permute-start | bytes 786440 | tf_op jit(solution)/shard_map/ppermute | solution.py:33
  51.6 4.7 %collective-permute-start.13 = (bf16[288,1024]{1,0:T(8,128)(2,1)S(1)}, bf16[288,1024]{1,0:T(8,128)(2,1)S(1)}, u32[]{:S(2)}, u32[]{:S(2)}) collective-permute-start(bf16[288,1024]{1,0:T(8,128)(2,1)S(1)} %collective-permute-done.5.refs_7_.refs_11_), channel_id=1, source_target_pairs={{0,1},{1,0},{2,3},{3,2},{4,5},{5,4},{6,7},{7,6},{8,9},{9,8},{10,11... | collective-permute-start | bytes 1769480 | tf_op jit(solution)/shard_map/ppermute | solution.py:33
  52.2 12.9 %collective-permute-start.11 = (bf16[288,1024]{1,0:T(8,128)(2,1)S(1)}, bf16[288,1024]{1,0:T(8,128)(2,1)S(1)}, u32[]{:S(2)}, u32[]{:S(2)}) collective-permute-start(bf16[288,1024]{1,0:T(8,128)(2,1)S(1)} %collective-permute-done.7.refs_3_.refs_5_), channel_id=1, source_target_pairs={{0,2},{1,15},{2,4},{3,1},{4,6},{5,3},{6,8},{7,5},{8,10},{9,7},{10,... | collective-permute-start | bytes 1769480 | tf_op jit(solution)/shard_map/ppermute | solution.py:33
  53.6 9.1 %collective-permute-start.12 = (bf16[128,1024]{1,0:T(8,128)(2,1)}, bf16[128,1024]{1,0:T(8,128)(2,1)}, u32[]{:S(2)}, u32[]{:S(2)}) collective-permute-start(bf16[128,1024]{1,0:T(8,128)(2,1)} %get-tuple-element.42), channel_id=1, source_target_pairs={{0,16},{1,17},{2,18},{3,19},{4,20},{5,21},{6,22},{7,23},{8,24},{9,... | collective-permute-start | bytes 786440 | tf_op jit(solution)/shard_map/ppermute | solution.py:33
  54.8 10.3 %collective-permute-start.14 = (bf16[128,1024]{1,0:T(8,128)(2,1)S(1)}, bf16[128,1024]{1,0:T(8,128)(2,1)}, u32[]{:S(2)}, u32[]{:S(2)}) collective-permute-start(bf16[128,1024]{1,0:T(8,128)(2,1)S(1)} %collective-permute-done.8.refs_9_.refs_13_), channel_id=1, source_target_pairs={{0,1},{1,0},{2,3},{3,2},{4,5},{5,4},{6,7},{7,6},{8,9},{9,8},{10,11... | collective-permute-start | bytes 786440 | tf_op jit(solution)/shard_map/ppermute | solution.py:33
  56.0 9.1 %collective-permute-start.15 = (bf16[128,1024]{1,0:T(8,128)(2,1)}, bf16[128,1024]{1,0:T(8,128)(2,1)}, u32[]{:S(2)}, u32[]{:S(2)}) collective-permute-start(bf16[128,1024]{1,0:T(8,128)(2,1)} %collective-permute-done.9.refs_17_), channel_id=1, source_target_pairs={{0,1},{1,0},{2,3},{3,2},{4,5},{5,4},{6,7},{7,6},{8,9},{9,8},{10,11... | collective-permute-start | bytes 786440 | tf_op jit(solution)/shard_map/ppermute | solution.py:33
  57.9 7.3 %collective-permute-start.16 = (bf16[128,1024]{1,0:T(8,128)(2,1)}, bf16[128,1024]{1,0:T(8,128)(2,1)}, u32[]{:S(2)}, u32[]{:S(2)}) collective-permute-start(bf16[128,1024]{1,0:T(8,128)(2,1)} %pad_maximum_fusion.1), channel_id=1, source_target_pairs={{32,16},{96,80},{160,144},{224,208}} | collective-permute-start | bytes 786440 | tf_op jit(solution)/shard_map/ppermute | solution.py:33
  62.7 9.7 %collective-permute-start.18 = (bf16[128,1024]{1,0:T(8,128)(2,1)}, bf16[128,1024]{1,0:T(8,128)(2,1)S(1)}, u32[]{:S(2)}, u32[]{:S(2)}) collective-permute-start(bf16[128,1024]{1,0:T(8,128)(2,1)} %pad_maximum_fusion.1), channel_id=1, source_target_pairs={{32,0},{96,64},{160,128},{224,192}} | collective-permute-start | bytes 786440 | tf_op jit(solution)/shard_map/ppermute | solution.py:33
  66.1 6.3 %collective-permute-start.19 = (bf16[48,1024]{1,0:T(8,128)(2,1)S(1)}, bf16[48,1024]{1,0:T(8,128)(2,1)S(1)}, u32[]{:S(2)}, u32[]{:S(2)}) collective-permute-start(bf16[48,1024]{1,0:T(8,128)(2,1)S(1)} %fusion.3), channel_id=1, source_target_pairs={{32,18},{33,17},{34,20},{36,22},{38,24},{43,27},{45,29},{47,31},{9... | collective-permute-start | bytes 294920 | tf_op jit(solution)/shard_map/ppermute | solution.py:33
  67.4 7.9 %collective-permute-start.17 = (bf16[128,1024]{1,0:T(8,128)(2,1)S(1)}, bf16[128,1024]{1,0:T(8,128)(2,1)S(1)}, u32[]{:S(2)}, u32[]{:S(2)}) collective-permute-start(bf16[128,1024]{1,0:T(8,128)(2,1)S(1)} %collective-permute-done.8.refs_9_.refs_13_), channel_id=1, source_target_pairs={{0,16},{1,17},{2,18},{3,19},{4,20},{5,21},{6,22},{7,23},{8,24},{9,... | collective-permute-start | bytes 786440 | tf_op jit(solution)/shard_map/ppermute | solution.py:33
  67.5 11.4 %collective-permute-start.20 = (bf16[144,1024]{1,0:T(8,128)(2,1)S(1)}, bf16[144,1024]{1,0:T(8,128)(2,1)S(1)}, u32[]{:S(2)}, u32[]{:S(2)}) collective-permute-start(bf16[144,1024]{1,0:T(8,128)(2,1)S(1)} %slice_select_fusion), channel_id=1, source_target_pairs={{0,2},{1,15},{2,4},{3,1},{4,6},{5,3},{6,8},{7,5},{8,10},{9,7},{10,... | collective-permute-start | bytes 884744 | tf_op jit(solution)/shard_map/ppermute | solution.py:33
  76.4 1.3 %collective-permute-start.23 = (bf16[128,1024]{1,0:T(8,128)(2,1)S(1)}, bf16[128,1024]{1,0:T(8,128)(2,1)S(1)}, u32[]{:S(2)}, u32[]{:S(2)}) collective-permute-start(bf16[128,1024]{1,0:T(8,128)(2,1)S(1)} %add.132), channel_id=1, source_target_pairs={{0,1},{16,17},{64,65},{80,81},{128,129},{144,145},{192,193},{208,2... | collective-permute-start | bytes 786440 | tf_op jit(solution)/shard_map/ppermute | solution.py:33
  77.1 1.8 %collective-permute-start.21 = (bf16[128,1024]{1,0:T(8,128)(2,1)}, bf16[128,1024]{1,0:T(8,128)(2,1)S(1)}, u32[]{:S(2)}, u32[]{:S(2)}) collective-permute-start(bf16[128,1024]{1,0:T(8,128)(2,1)} %collective-permute-done.12.refs_18_), channel_id=1, source_target_pairs={{0,1},{1,0},{2,3},{3,2},{4,5},{5,4},{6,7},{7,6},{8,9},{9,8},{10,11... | collective-permute-start | bytes 786440 | tf_op jit(solution)/shard_map/ppermute | solution.py:33
  77.2 1.9 %collective-permute-start.22 = (bf16[128,1024]{1,0:T(8,128)(2,1)S(1)}, bf16[128,1024]{1,0:T(8,128)(2,1)S(1)}, u32[]{:S(2)}, u32[]{:S(2)}) collective-permute-start(bf16[128,1024]{1,0:T(8,128)(2,1)S(1)} %collective-permute-done.17.refs_21_), channel_id=1, source_target_pairs={{0,1},{1,0},{2,3},{3,2},{4,5},{5,4},{6,7},{7,6},{8,9},{9,8},{10,11... | collective-permute-start | bytes 786440 | tf_op jit(solution)/shard_map/ppermute | solution.py:33
  84.5 1.3 %collective-permute-start.24 = (f32[4,1152]{1,0:T(4,128)S(1)}, f32[4,1152]{1,0:T(4,128)S(1)}, u32[]{:S(2)}, u32[]{:S(2)}) collective-permute-start(f32[4,1152]{1,0:T(4,128)S(1)} %get-tuple-element.64), channel_id=1, source_target_pairs={{0,1},{1,0},{2,3},{3,2},{4,5},{5,4},{6,7},{7,6},{8,9},{9,8},{10,11... | collective-permute-start | bytes 55304 | tf_op jit(solution)/shard_map/ppermute | solution.py:33
  85.8 9.0 %collective-permute-start.25 = (f32[4,512]{1,0:T(4,128)S(1)}, f32[4,512]{1,0:T(4,128)S(1)}, u32[]{:S(2)}, u32[]{:S(2)}) collective-permute-start(f32[4,512]{1,0:T(4,128)S(1)} %slice_add_fusion), channel_id=1, source_target_pairs={{0,16},{1,17},{2,18},{3,19},{4,20},{5,21},{6,22},{7,23},{8,24},{9,... | collective-permute-start | bytes 24584 | tf_op jit(solution)/shard_map/ppermute | solution.py:33
  87.7 7.0 %collective-permute-start.26 = (f32[4,128]{1,0:T(4,128)S(1)}, f32[4,128]{1,0:T(4,128)S(1)}, u32[]{:S(2)}, u32[]{:S(2)}) collective-permute-start(f32[4,128]{1,0:T(4,128)S(1)} %slice_add_fusion.2), channel_id=1, source_target_pairs={{0,32},{64,96},{128,160},{192,224}} | collective-permute-start | bytes 6152 | tf_op jit(solution)/shard_map/ppermute | solution.py:33
  89.0 5.7 %collective-permute-start.27 = (f32[4,128]{1,0:T(4,128)S(1)}, f32[4,128]{1,0:T(4,128)S(1)}, u32[]{:S(2)}, u32[]{:S(2)}) collective-permute-start(f32[4,128]{1,0:T(4,128)S(1)} %slice_add_fusion.2), channel_id=1, source_target_pairs={{16,32},{80,96},{144,160},{208,224}} | collective-permute-start | bytes 6152 | tf_op jit(solution)/shard_map/ppermute | solution.py:33
  94.8 5.2 %collective-permute-start.28 = (f32[4,4,128]{2,1,0:T(4,128)S(1)}, f32[4,4,128]{2,1,0:T(4,128)S(1)}, u32[]{:S(2)}, u32[]{:S(2)}) collective-permute-start(f32[4,4,128]{2,1,0:T(4,128)S(1)} %pad_add_fusion), channel_id=1, source_target_pairs={{0,128},{1,129},{2,130},{3,131},{4,132},{5,133},{6,134},{7,135},{8... | collective-permute-start | bytes 24584 | tf_op jit(solution)/shard_map/ppermute | solution.py:33
  96.6 4.9 %collective-permute-start.29 = (f32[4,4,128]{2,1,0:T(4,128)S(1)}, f32[4,4,128]{2,1,0:T(4,128)S(1)}, u32[]{:S(2)}, u32[]{:S(2)}) collective-permute-start(f32[4,4,128]{2,1,0:T(4,128)S(1)} %pad_add_fusion), channel_id=1, source_target_pairs={{0,64},{1,65},{2,66},{3,67},{4,68},{5,69},{6,70},{7,71},{8,72},{9,... | collective-permute-start | bytes 24584 | tf_op jit(solution)/shard_map/ppermute | solution.py:33
  97.2 4.3 %collective-permute-start.30 = (f32[4,4,128]{2,1,0:T(4,128)S(1)}, f32[4,4,128]{2,1,0:T(4,128)S(1)}, u32[]{:S(2)}, u32[]{:S(2)}) collective-permute-start(f32[4,4,128]{2,1,0:T(4,128)S(1)} %pad_add_fusion), channel_id=1, source_target_pairs={{0,192},{1,193},{2,194},{3,195},{4,196},{5,197},{6,198},{7,199},{8... | collective-permute-start | bytes 24584 | tf_op jit(solution)/shard_map/ppermute | solution.py:33
  (7 other events, 38.8 us)

commit v14 on v13

--- a/solution.py
+++ b/solution.py
@@ -280,7 +280,7 @@
     z1 = permute(chip, same_core)
     y1 = permute(chip, y_way)
     x1 = permute(own, swap_x)
-    z1, y1, x1 = fence(z1, y1, x1)
+    z1, x1 = fence(z1, x1)
 
     z2 = permute(z1, same_core)
     near_one, far_one = y1[TAG:tagged], y1[tagged + TAG :]

time: 103 us -> 101 us (0.981)
  starting transfers between devices: 37.9 us -> 35.8 us
    ppermute x31, starting transfers between devices: 37.9 us -> 35.8 us  [permute(): return lax.ppermute(value, AXES, pairs)]
where the time goes in v14:
time: 101 us
  waiting for transfers between devices  38.1 us (38%)
  starting transfers between devices  35.8 us (35%)
  Pallas kernels  14.6 us (14%)
  other arithmetic  8.62 us (9%)
  local copies, waits for them, and re-layouts  3.26 us (3%)
    ppermute x31, waiting for transfers between devices, permute(): return lax.ppermute(value, AXES, pairs)  38.1 us
    ppermute x31, starting transfers between devices, permute(): return lax.ppermute(value, AXES, pairs)  35.8 us
    pallas_call x2, Pallas kernels, pair_sums(): pl.pallas_call(functools.partial(pair_kernel, col_cuts=tuple(col_cuts), n...  9.15 us
    pallas_call x1, Pallas kernels, raw_partial(): pl.pallas_call(raw_kernel, grid=(feats // width,), in_specs=[pl.BlockSpec...  5.49 us
    convert_element_type x1, other arithmetic, shards(): tag = tag.astype(jnp.bfloat16)  2.66 us
  transfers between devices with their start and end apart: 31, of which 16 were waited for; matrix products, arithmetic and copies ran while one was open for 8% of the time, Pallas kernels for 4%

profile of v14, /device:TPU:4, one launch (start us, length us, event | category | flops | bytes accessed | tf_op | source)
XLA Modules:
  0.0 100.8 jit_solution(17630861946330857590)
XLA Ops:
  0.0 5.5 %raw.1 = f32[512,1024]{1,0:T(8,128)} custom-call(s32[8,11]{1,0:T(8,128)} %bitcast.41, bf16[1584,512]{1,0:T(8,128)(2,1)} %bitcast.35, bf16[1584,1024]{1,0:T(8,128)(2,1)} %geometry.1), custom_call_target="tpu_custom_call" | custom-call | flops 1660944384 | bytes 8388608 | tf_op jit(solution)/shard_map/raw/pallas_call | solution.py:84
  5.5 1.7 %constant_dynamic-slice_fusion.1 = (f32[4,1,32,1024]{3,2,1,0:T(8,128)S(1)}, f16[4,1,32,1024]{3,2,0,1:T(8,128)(2,1)S(1)}, f16[4,1,32,1024]{3,2,0,1:T(8,128)(2,1)S(1)}, f16[4,1,32,1024]{3,2,0,1:T(8,128)(2,1)S(1)}) fusion(f32[4,4,32,1024]{3,2,1,0:T(8,128)} %bitcast.34, s32[]{:T(128)S(6)} %select_n.184, s32[]{:T(128)S(6)} %select_n.188, s32[]{:T(128)S(6)} %select_n.186, ...), kind=kLoop, calls=%fused_computation.44 | loop fusion | flops 393216 | bytes 3407888 | tf_op jit(solution)/shard_map/jit(dynamic_index_in_dim)/dynamic_slice | solution.py:265
  7.2 3.3 %collective-permute-start = (f16[128,1024]{1,0:T(8,128)(2,1)S(1)}, f16[128,1024]{1,0:T(8,128)(2,1)S(1)}, u32[]{:S(2)}, u32[]{:S(2)}) collective-permute-start(f16[128,1024]{1,0:T(8,128)(2,1)S(1)} %bitcast.38), channel_id=1, source_target_pairs={{0,128},{1,129},{2,130},{3,131},{4,132},{5,133},{6,134},{7,135},{8... | collective-permute-start | bytes 786440 | tf_op jit(solution)/shard_map/ppermute | solution.py:33
  11.2 2.6 %collective-permute-start.2 = (f16[128,1024]{1,0:T(8,128)(2,1)S(1)}, f16[128,1024]{1,0:T(8,128)(2,1)S(1)}, u32[]{:S(2)}, u32[]{:S(2)}) collective-permute-start(f16[128,1024]{1,0:T(8,128)(2,1)S(1)} %bitcast.36), channel_id=1, source_target_pairs={{0,192},{1,193},{2,194},{3,195},{4,196},{5,197},{6,198},{7,199},{8... | collective-permute-start | bytes 786440 | tf_op jit(solution)/shard_map/ppermute | solution.py:33
  14.5 2.7 %select_convert_fusion = bf16[16,1024]{1,0:T(8,128)(2,1)S(1)} fusion(bf16[]{:T(256)} %bitcast.5, bf16[]{:T(256)} %bitcast.4, bf16[]{:T(256)} %bitcast.3, bf16[]{:T(256)} %bitcast.2, s32[1024]{0:T(1024)S(1)} %get-tuple-element.77, s32[1024]{0:T(1024)S(1)} %get-tuple-element.78, pred[16]{0:T(512)(128)(4,1)S(1)} %iota_compare_fusion, pred[1024]{0:T(1024)(128)(4,1)S(1)} %fusion.13), kind=kLoop, calls=%fused_computation.17 | loop fusion | flops 163840 | bytes 42008 | tf_op jit(solution)/shard_map/convert_element_type | solution.py:260
  18.1 4.4 %collective-permute-done.1 = f16[128,1024]{1,0:T(8,128)(2,1)S(1)} collective-permute-done((f16[128,1024]{1,0:T(8,128)(2,1)S(1)}, f16[128,1024]{1,0:T(8,128)(2,1)S(1)}, u32[]{:S(2)}, u32[]{:S(2)}) %collective-permute-start.1) | collective-permute-done | bytes 262176 | tf_op jit(solution)/shard_map/ppermute | solution.py:33
  23.4 1.6 %collective-permute-done.3.refs_6_.refs_10_ = bf16[144,1024]{1,0:T(8,128)(2,1)S(1)} collective-permute-done((bf16[144,1024]{1,0:T(8,128)(2,1)S(1)}, bf16[144,1024]{1,0:T(8,128)(2,1)S(1)}, u32[]{:S(2)}, u32[]{:S(2)}) %collective-permute-start.3) | collective-permute-done | bytes 294944 | tf_op jit(solution)/shard_map/ppermute | solution.py:33
  25.2 2.0 %collective-permute-start.4 = (bf16[288,1024]{1,0:T(8,128)(2,1)S(1)}, bf16[288,1024]{1,0:T(8,128)(2,1)S(1)}, u32[]{:S(2)}, u32[]{:S(2)}) collective-permute-start(bf16[288,1024]{1,0:T(8,128)(2,1)S(1)} %maximum_select_fusion), channel_id=1, source_target_pairs={{0,2},{1,15},{2,4},{3,1},{4,6},{5,3},{6,8},{7,5},{8,10},{9,7},{10,... | collective-permute-start | bytes 1769480 | tf_op jit(solution)/shard_map/ppermute | solution.py:33
  27.2 1.4 %collective-permute-start.7 = (bf16[288,1024]{1,0:T(8,128)(2,1)S(1)}, bf16[288,1024]{1,0:T(8,128)(2,1)S(1)}, u32[]{:S(2)}, u32[]{:S(2)}) collective-permute-start(bf16[288,1024]{1,0:T(8,128)(2,1)S(1)} %maximum_select_fusion), channel_id=1, source_target_pairs={{0,64},{1,193},{2,66},{3,195},{4,68},{5,197},{6,70},{7,199},{8,72}... | collective-permute-start | bytes 1769480 | tf_op jit(solution)/shard_map/ppermute | solution.py:33
  28.5 1.2 %collective-permute-start.5 = (bf16[144,1024]{1,0:T(8,128)(2,1)S(1)}, bf16[144,1024]{1,0:T(8,128)(2,1)S(1)}, u32[]{:S(2)}, u32[]{:S(2)}) collective-permute-start(bf16[144,1024]{1,0:T(8,128)(2,1)S(1)} %pad_maximum_fusion.refs_1_.refs_5_.refs_3_.refs_9_), channel_id=1, source_target_pairs={{0,16},{1,17},{2,18},{3,19},{4,20},{5,21},{6,22},{7,23},{8,24},{9,... | collective-permute-start | bytes 884744 | tf_op jit(solution)/shard_map/ppermute | solution.py:33
  29.7 5.5 %collective-permute-done.5.refs_15_ = bf16[144,1024]{1,0:T(8,128)(2,1)S(1)} collective-permute-done((bf16[144,1024]{1,0:T(8,128)(2,1)S(1)}, bf16[144,1024]{1,0:T(8,128)(2,1)S(1)}, u32[]{:S(2)}, u32[]{:S(2)}) %collective-permute-start.5) | collective-permute-done | bytes 294944 | tf_op jit(solution)/shard_map/ppermute | solution.py:33
  35.3 3.7 %collective-permute-done.4.refs_2_.refs_4_ = bf16[288,1024]{1,0:T(8,128)(2,1)S(1)} collective-permute-done((bf16[288,1024]{1,0:T(8,128)(2,1)S(1)}, bf16[288,1024]{1,0:T(8,128)(2,1)S(1)}, u32[]{:S(2)}, u32[]{:S(2)}) %collective-permute-start.4) | collective-permute-done | bytes 589856 | tf_op jit(solution)/shard_map/ppermute | solution.py:33
  39.0 3.2 %collective-permute-start.10 = (bf16[144,1024]{1,0:T(8,128)(2,1)S(1)}, bf16[144,1024]{1,0:T(8,128)(2,1)S(1)}, u32[]{:S(2)}, u32[]{:S(2)}) collective-permute-start(bf16[144,1024]{1,0:T(8,128)(2,1)S(1)} %collective-permute-done.5.refs_15_), channel_id=1, source_target_pairs={{0,1},{1,0},{2,3},{3,2},{4,5},{5,4},{6,7},{7,6},{8,9},{9,8},{10,11... | collective-permute-start | bytes 884744 | tf_op jit(solution)/shard_map/ppermute | solution.py:33
  43.0 1.2 %collective-permute-start.9 = (bf16[128,1024]{1,0:T(8,128)(2,1)S(1)}, bf16[128,1024]{1,0:T(8,128)(2,1)}, u32[]{:S(2)}, u32[]{:S(2)}) collective-permute-start(bf16[128,1024]{1,0:T(8,128)(2,1)S(1)} %get-tuple-element.36), channel_id=1, source_target_pairs={{0,16},{1,17},{2,18},{3,19},{4,20},{5,21},{6,22},{7,23},{8,24},{9,... | collective-permute-start | bytes 786440 | tf_op jit(solution)/shard_map/ppermute | solution.py:33
  44.2 6.3 %collective-permute-done.8.refs_9_.refs_13_ = bf16[128,1024]{1,0:T(8,128)(2,1)S(1)} collective-permute-done((bf16[128,1024]{1,0:T(8,128)(2,1)S(1)}, bf16[128,1024]{1,0:T(8,128)(2,1)S(1)}, u32[]{:S(2)}, u32[]{:S(2)}) %collective-permute-start.8) | collective-permute-done | bytes 262176 | tf_op jit(solution)/shard_map/ppermute | solution.py:33
  50.5 1.8 %collective-permute-done.9.refs_17_ = bf16[128,1024]{1,0:T(8,128)(2,1)} collective-permute-done((bf16[128,1024]{1,0:T(8,128)(2,1)S(1)}, bf16[128,1024]{1,0:T(8,128)(2,1)}, u32[]{:S(2)}, u32[]{:S(2)}) %collective-permute-start.9) | collective-permute-done | bytes 262176 | tf_op jit(solution)/shard_map/ppermute | solution.py:33
  53.3 1.2 %collective-permute-start.12 = (bf16[128,1024]{1,0:T(8,128)(2,1)}, bf16[128,1024]{1,0:T(8,128)(2,1)}, u32[]{:S(2)}, u32[]{:S(2)}) collective-permute-start(bf16[128,1024]{1,0:T(8,128)(2,1)} %get-tuple-element.40), channel_id=1, source_target_pairs={{0,16},{1,17},{2,18},{3,19},{4,20},{5,21},{6,22},{7,23},{8,24},{9,... | collective-permute-start | bytes 786440 | tf_op jit(solution)/shard_map/ppermute | solution.py:33
  54.5 1.5 %collective-permute-start.14 = (bf16[128,1024]{1,0:T(8,128)(2,1)S(1)}, bf16[128,1024]{1,0:T(8,128)(2,1)}, u32[]{:S(2)}, u32[]{:S(2)}) collective-permute-start(bf16[128,1024]{1,0:T(8,128)(2,1)S(1)} %collective-permute-done.8.refs_9_.refs_13_), channel_id=1, source_target_pairs={{0,1},{1,0},{2,3},{3,2},{4,5},{5,4},{6,7},{7,6},{8,9},{9,8},{10,11... | collective-permute-start | bytes 786440 | tf_op jit(solution)/shard_map/ppermute | solution.py:33
  57.9 2.5 %collective-permute-start.16 = (bf16[128,1024]{1,0:T(8,128)(2,1)}, bf16[128,1024]{1,0:T(8,128)(2,1)}, u32[]{:S(2)}, u32[]{:S(2)}) collective-permute-start(bf16[128,1024]{1,0:T(8,128)(2,1)} %pad_maximum_fusion.1), channel_id=1, source_target_pairs={{32,16},{96,80},{160,144},{224,208}} | collective-permute-start | bytes 786440 | tf_op jit(solution)/shard_map/ppermute | solution.py:33
  60.4 1.7 %collective-permute-done.12.refs_18_ = bf16[128,1024]{1,0:T(8,128)(2,1)} collective-permute-done((bf16[128,1024]{1,0:T(8,128)(2,1)}, bf16[128,1024]{1,0:T(8,128)(2,1)}, u32[]{:S(2)}, u32[]{:S(2)}) %collective-permute-start.12) | collective-permute-done | bytes 262176 | tf_op jit(solution)/shard_map/ppermute | solution.py:33
  62.1 2.4 %collective-permute-start.18 = (bf16[128,1024]{1,0:T(8,128)(2,1)}, bf16[128,1024]{1,0:T(8,128)(2,1)S(1)}, u32[]{:S(2)}, u32[]{:S(2)}) collective-permute-start(bf16[128,1024]{1,0:T(8,128)(2,1)} %pad_maximum_fusion.1), channel_id=1, source_target_pairs={{32,0},{96,64},{160,128},{224,192}} | collective-permute-start | bytes 786440 | tf_op jit(solution)/shard_map/ppermute | solution.py:33
  65.6 1.3 %collective-permute-start.19 = (bf16[48,1024]{1,0:T(8,128)(2,1)S(1)}, bf16[48,1024]{1,0:T(8,128)(2,1)S(1)}, u32[]{:S(2)}, u32[]{:S(2)}) collective-permute-start(bf16[48,1024]{1,0:T(8,128)(2,1)S(1)} %fusion.3), channel_id=1, source_target_pairs={{32,18},{33,17},{34,20},{36,22},{38,24},{43,27},{45,29},{47,31},{9... | collective-permute-start | bytes 294920 | tf_op jit(solution)/shard_map/ppermute | solution.py:33
  67.8 3.7 %early.1 = (f32[4,512]{1,0:T(4,128)S(1)}, f32[4,512]{1,0:T(4,128)S(1)}) custom-call(s32[2]{0:T(128)S(1)} %pad_add_fusion.1.refs_0_, bf16[144,1024]{1,0:T(8,128)(2,1)S(1)} %pad_maximum_fusion.refs_1_.refs_5_.refs_3_.refs_9_, bf16[288,1024]{1,0:T(8,128)(2,1)S(1)} %collective-permute-done.4.refs_2_.refs_4_, ...), custom_call_target="tpu_custom_call" | custom-call | flops 5637144576 | bytes 11796480 | tf_op jit(solution)/shard_map/early/pallas_call | solution.py:224
  71.6 3.4 %collective-permute-done.17.refs_21_ = bf16[128,1024]{1,0:T(8,128)(2,1)S(1)} collective-permute-done((bf16[128,1024]{1,0:T(8,128)(2,1)S(1)}, bf16[128,1024]{1,0:T(8,128)(2,1)S(1)}, u32[]{:S(2)}, u32[]{:S(2)}) %collective-permute-start.17) | collective-permute-done | bytes 262176 | tf_op jit(solution)/shard_map/ppermute | solution.py:33
  77.4 1.2 %collective-permute-done.21.refs_20_ = bf16[128,1024]{1,0:T(8,128)(2,1)S(1)} collective-permute-done((bf16[128,1024]{1,0:T(8,128)(2,1)}, bf16[128,1024]{1,0:T(8,128)(2,1)S(1)}, u32[]{:S(2)}, u32[]{:S(2)}) %collective-permute-start.21) | collective-permute-done | bytes 262176 | tf_op jit(solution)/shard_map/ppermute | solution.py:33
  78.7 5.4 %late.1 = (f32[4,512]{1,0:T(4,128)S(1)}, f32[4,512]{1,0:T(4,128)S(1)}, f32[4,1152]{1,0:T(4,128)S(1)}, f32[4,128]{1,0:T(4,128)S(1)}) custom-call(s32[2]{0:T(128)S(1)} %pad_add_fusion.1.refs_0_, f32[4,512]{1,0:T(4,128)S(1)} %get-tuple-element.52.refs_1_, f32[4,512]{1,0:T(4,128)S(1)} %get-tuple-element.53.refs_2_, ...), custom_call_target="tpu_custom_call" | custom-call | flops 16609443840 | bytes 22216704 | tf_op jit(solution)/shard_map/late/pallas_call | solution.py:224
  85.4 1.7 %collective-permute-start.25 = (f32[4,512]{1,0:T(4,128)S(1)}, f32[4,512]{1,0:T(4,128)S(1)}, u32[]{:S(2)}, u32[]{:S(2)}) collective-permute-start(f32[4,512]{1,0:T(4,128)S(1)} %slice_add_fusion), channel_id=1, source_target_pairs={{0,16},{1,17},{2,18},{3,19},{4,20},{5,21},{6,22},{7,23},{8,24},{9,... | collective-permute-start | bytes 24584 | tf_op jit(solution)/shard_map/ppermute | solution.py:33
  87.1 1.3 %collective-permute-start.26 = (f32[4,128]{1,0:T(4,128)S(1)}, f32[4,128]{1,0:T(4,128)S(1)}, u32[]{:S(2)}, u32[]{:S(2)}) collective-permute-start(f32[4,128]{1,0:T(4,128)S(1)} %slice_add_fusion.2), channel_id=1, source_target_pairs={{0,32},{64,96},{128,160},{192,224}} | collective-permute-start | bytes 6152 | tf_op jit(solution)/shard_map/ppermute | solution.py:33
  88.4 1.3 %collective-permute-start.27 = (f32[4,128]{1,0:T(4,128)S(1)}, f32[4,128]{1,0:T(4,128)S(1)}, u32[]{:S(2)}, u32[]{:S(2)}) collective-permute-start(f32[4,128]{1,0:T(4,128)S(1)} %slice_add_fusion.2), channel_id=1, source_target_pairs={{16,32},{80,96},{144,160},{208,224}} | collective-permute-start | bytes 6152 | tf_op jit(solution)/shard_map/ppermute | solution.py:33
  89.7 4.4 %collective-permute-done.26 = f32[4,128]{1,0:T(4,128)S(1)} collective-permute-done((f32[4,128]{1,0:T(4,128)S(1)}, f32[4,128]{1,0:T(4,128)S(1)}, u32[]{:S(2)}, u32[]{:S(2)}) %collective-permute-start.26) | collective-permute-done | bytes 2080 | tf_op jit(solution)/shard_map/ppermute | solution.py:33
  95.8 2.6 %collective-permute-start.30 = (f32[4,4,128]{2,1,0:T(4,128)S(1)}, f32[4,4,128]{2,1,0:T(4,128)S(1)}, u32[]{:S(2)}, u32[]{:S(2)}) collective-permute-start(f32[4,4,128]{2,1,0:T(4,128)S(1)} %pad_add_fusion), channel_id=1, source_target_pairs={{0,192},{1,193},{2,194},{3,195},{4,196},{5,197},{6,198},{7,199},{8... | collective-permute-start | bytes 24584 | tf_op jit(solution)/shard_map/ppermute | solution.py:33
  98.3 1.1 %collective-permute-done.28 = f32[4,4,128]{2,1,0:T(4,128)S(1)} collective-permute-done((f32[4,4,128]{2,1,0:T(4,128)S(1)}, f32[4,4,128]{2,1,0:T(4,128)S(1)}, u32[]{:S(2)}, u32[]{:S(2)}) %collective-permute-start.28) | collective-permute-done | bytes 8224 | tf_op jit(solution)/shard_map/ppermute | solution.py:33
  (90 shorter events, 15.9 us)
Async XLA Ops:
  7.2 10.8 %collective-permute-start = (f16[128,1024]{1,0:T(8,128)(2,1)S(1)}, f16[128,1024]{1,0:T(8,128)(2,1)S(1)}, u32[]{:S(2)}, u32[]{:S(2)}) collective-permute-start(f16[128,1024]{1,0:T(8,128)(2,1)S(1)} %bitcast.38), channel_id=1, source_target_pairs={{0,128},{1,129},{2,130},{3,131},{4,132},{5,133},{6,134},{7,135},{8... | collective-permute-start | bytes 786440 | tf_op jit(solution)/shard_map/ppermute | solution.py:33
  10.5 12.0 %collective-permute-start.1 = (f16[128,1024]{1,0:T(8,128)(2,1)S(1)}, f16[128,1024]{1,0:T(8,128)(2,1)S(1)}, u32[]{:S(2)}, u32[]{:S(2)}) collective-permute-start(f16[128,1024]{1,0:T(8,128)(2,1)S(1)} %bitcast.37), channel_id=1, source_target_pairs={{0,64},{1,65},{2,66},{3,67},{4,68},{5,69},{6,70},{7,71},{8,72},{9,... | collective-permute-start | bytes 786440 | tf_op jit(solution)/shard_map/ppermute | solution.py:33
  11.2 11.7 %collective-permute-start.2 = (f16[128,1024]{1,0:T(8,128)(2,1)S(1)}, f16[128,1024]{1,0:T(8,128)(2,1)S(1)}, u32[]{:S(2)}, u32[]{:S(2)}) collective-permute-start(f16[128,1024]{1,0:T(8,128)(2,1)S(1)} %bitcast.36), channel_id=1, source_target_pairs={{0,192},{1,193},{2,194},{3,195},{4,196},{5,197},{6,198},{7,199},{8... | collective-permute-start | bytes 786440 | tf_op jit(solution)/shard_map/ppermute | solution.py:33
  23.3 1.7 %collective-permute-start.3 = (bf16[144,1024]{1,0:T(8,128)(2,1)S(1)}, bf16[144,1024]{1,0:T(8,128)(2,1)S(1)}, u32[]{:S(2)}, u32[]{:S(2)}) collective-permute-start(bf16[144,1024]{1,0:T(8,128)(2,1)S(1)} %pad_maximum_fusion.refs_1_.refs_5_.refs_3_.refs_9_), channel_id=1, source_target_pairs={{0,1},{1,0},{2,3},{3,2},{4,5},{5,4},{6,7},{7,6},{8,9},{9,8},{10,11... | collective-permute-start | bytes 884744 | tf_op jit(solution)/shard_map/ppermute | solution.py:33
  25.2 32.7 %copy-start.5 = (bf16[288,1024]{1,0:T(8,128)(2,1)}, bf16[288,1024]{1,0:T(8,128)(2,1)S(1)}, u32[]{:S(2)}) copy-start(bf16[288,1024]{1,0:T(8,128)(2,1)S(1)} %maximum_select_fusion) | copy-start | bytes 1769476
  25.2 13.8 %collective-permute-start.4 = (bf16[288,1024]{1,0:T(8,128)(2,1)S(1)}, bf16[288,1024]{1,0:T(8,128)(2,1)S(1)}, u32[]{:S(2)}, u32[]{:S(2)}) collective-permute-start(bf16[288,1024]{1,0:T(8,128)(2,1)S(1)} %maximum_select_fusion), channel_id=1, source_target_pairs={{0,2},{1,15},{2,4},{3,1},{4,6},{5,3},{6,8},{7,5},{8,10},{9,7},{10,... | collective-permute-start | bytes 1769480 | tf_op jit(solution)/shard_map/ppermute | solution.py:33
  27.2 15.0 %collective-permute-start.7 = (bf16[288,1024]{1,0:T(8,128)(2,1)S(1)}, bf16[288,1024]{1,0:T(8,128)(2,1)S(1)}, u32[]{:S(2)}, u32[]{:S(2)}) collective-permute-start(bf16[288,1024]{1,0:T(8,128)(2,1)S(1)} %maximum_select_fusion), channel_id=1, source_target_pairs={{0,64},{1,193},{2,66},{3,195},{4,68},{5,197},{6,70},{7,199},{8,72}... | collective-permute-start | bytes 1769480 | tf_op jit(solution)/shard_map/ppermute | solution.py:33
  28.5 6.7 %collective-permute-start.5 = (bf16[144,1024]{1,0:T(8,128)(2,1)S(1)}, bf16[144,1024]{1,0:T(8,128)(2,1)S(1)}, u32[]{:S(2)}, u32[]{:S(2)}) collective-permute-start(bf16[144,1024]{1,0:T(8,128)(2,1)S(1)} %pad_maximum_fusion.refs_1_.refs_5_.refs_3_.refs_9_), channel_id=1, source_target_pairs={{0,16},{1,17},{2,18},{3,19},{4,20},{5,21},{6,22},{7,23},{8,24},{9,... | collective-permute-start | bytes 884744 | tf_op jit(solution)/shard_map/ppermute | solution.py:33
  39.0 13.3 %collective-permute-start.6 = (bf16[288,1024]{1,0:T(8,128)(2,1)S(1)}, bf16[288,1024]{1,0:T(8,128)(2,1)S(1)}, u32[]{:S(2)}, u32[]{:S(2)}) collective-permute-start(bf16[288,1024]{1,0:T(8,128)(2,1)S(1)} %collective-permute-done.4.refs_2_.refs_4_), channel_id=1, source_target_pairs={{0,2},{1,15},{2,4},{3,1},{4,6},{5,3},{6,8},{7,5},{8,10},{9,7},{10,... | collective-permute-start | bytes 1769480 | tf_op jit(solution)/shard_map/ppermute | solution.py:33
  39.0 13.3 %collective-permute-start.10 = (bf16[144,1024]{1,0:T(8,128)(2,1)S(1)}, bf16[144,1024]{1,0:T(8,128)(2,1)S(1)}, u32[]{:S(2)}, u32[]{:S(2)}) collective-permute-start(bf16[144,1024]{1,0:T(8,128)(2,1)S(1)} %collective-permute-done.5.refs_15_), channel_id=1, source_target_pairs={{0,1},{1,0},{2,3},{3,2},{4,5},{5,4},{6,7},{7,6},{8,9},{9,8},{10,11... | collective-permute-start | bytes 884744 | tf_op jit(solution)/shard_map/ppermute | solution.py:33
  42.9 7.6 %collective-permute-start.8 = (bf16[128,1024]{1,0:T(8,128)(2,1)S(1)}, bf16[128,1024]{1,0:T(8,128)(2,1)S(1)}, u32[]{:S(2)}, u32[]{:S(2)}) collective-permute-start(bf16[128,1024]{1,0:T(8,128)(2,1)S(1)} %get-tuple-element.36), channel_id=1, source_target_pairs={{0,64},{1,193},{2,66},{3,195},{4,68},{5,197},{6,70},{7,199},{8,72}... | collective-permute-start | bytes 786440 | tf_op jit(solution)/shard_map/ppermute | solution.py:33
  43.0 9.3 %collective-permute-start.9 = (bf16[128,1024]{1,0:T(8,128)(2,1)S(1)}, bf16[128,1024]{1,0:T(8,128)(2,1)}, u32[]{:S(2)}, u32[]{:S(2)}) collective-permute-start(bf16[128,1024]{1,0:T(8,128)(2,1)S(1)} %get-tuple-element.36), channel_id=1, source_target_pairs={{0,16},{1,17},{2,18},{3,19},{4,20},{5,21},{6,22},{7,23},{8,24},{9,... | collective-permute-start | bytes 786440 | tf_op jit(solution)/shard_map/ppermute | solution.py:33
  52.3 4.0 %collective-permute-start.13 = (bf16[288,1024]{1,0:T(8,128)(2,1)S(1)}, bf16[288,1024]{1,0:T(8,128)(2,1)S(1)}, u32[]{:S(2)}, u32[]{:S(2)}) collective-permute-start(bf16[288,1024]{1,0:T(8,128)(2,1)S(1)} %collective-permute-done.7.refs_7_.refs_11_), channel_id=1, source_target_pairs={{0,1},{1,0},{2,3},{3,2},{4,5},{5,4},{6,7},{7,6},{8,9},{9,8},{10,11... | collective-permute-start | bytes 1769480 | tf_op jit(solution)/shard_map/ppermute | solution.py:33
  52.5 12.1 %collective-permute-start.11 = (bf16[288,1024]{1,0:T(8,128)(2,1)S(1)}, bf16[288,1024]{1,0:T(8,128)(2,1)S(1)}, u32[]{:S(2)}, u32[]{:S(2)}) collective-permute-start(bf16[288,1024]{1,0:T(8,128)(2,1)S(1)} %collective-permute-done.6.refs_3_.refs_5_), channel_id=1, source_target_pairs={{0,2},{1,15},{2,4},{3,1},{4,6},{5,3},{6,8},{7,5},{8,10},{9,7},{10,... | collective-permute-start | bytes 1769480 | tf_op jit(solution)/shard_map/ppermute | solution.py:33
  53.3 8.8 %collective-permute-start.12 = (bf16[128,1024]{1,0:T(8,128)(2,1)}, bf16[128,1024]{1,0:T(8,128)(2,1)}, u32[]{:S(2)}, u32[]{:S(2)}) collective-permute-start(bf16[128,1024]{1,0:T(8,128)(2,1)} %get-tuple-element.40), channel_id=1, source_target_pairs={{0,16},{1,17},{2,18},{3,19},{4,20},{5,21},{6,22},{7,23},{8,24},{9,... | collective-permute-start | bytes 786440 | tf_op jit(solution)/shard_map/ppermute | solution.py:33
  54.5 10.0 %collective-permute-start.14 = (bf16[128,1024]{1,0:T(8,128)(2,1)S(1)}, bf16[128,1024]{1,0:T(8,128)(2,1)}, u32[]{:S(2)}, u32[]{:S(2)}) collective-permute-start(bf16[128,1024]{1,0:T(8,128)(2,1)S(1)} %collective-permute-done.8.refs_9_.refs_13_), channel_id=1, source_target_pairs={{0,1},{1,0},{2,3},{3,2},{4,5},{5,4},{6,7},{7,6},{8,9},{9,8},{10,11... | collective-permute-start | bytes 786440 | tf_op jit(solution)/shard_map/ppermute | solution.py:33
  56.0 8.5 %collective-permute-start.15 = (bf16[128,1024]{1,0:T(8,128)(2,1)}, bf16[128,1024]{1,0:T(8,128)(2,1)}, u32[]{:S(2)}, u32[]{:S(2)}) collective-permute-start(bf16[128,1024]{1,0:T(8,128)(2,1)} %collective-permute-done.9.refs_17_), channel_id=1, source_target_pairs={{0,1},{1,0},{2,3},{3,2},{4,5},{5,4},{6,7},{7,6},{8,9},{9,8},{10,11... | collective-permute-start | bytes 786440 | tf_op jit(solution)/shard_map/ppermute | solution.py:33
  57.9 6.7 %collective-permute-start.16 = (bf16[128,1024]{1,0:T(8,128)(2,1)}, bf16[128,1024]{1,0:T(8,128)(2,1)}, u32[]{:S(2)}, u32[]{:S(2)}) collective-permute-start(bf16[128,1024]{1,0:T(8,128)(2,1)} %pad_maximum_fusion.1), channel_id=1, source_target_pairs={{32,16},{96,80},{160,144},{224,208}} | collective-permute-start | bytes 786440 | tf_op jit(solution)/shard_map/ppermute | solution.py:33
  62.1 9.4 %collective-permute-start.18 = (bf16[128,1024]{1,0:T(8,128)(2,1)}, bf16[128,1024]{1,0:T(8,128)(2,1)S(1)}, u32[]{:S(2)}, u32[]{:S(2)}) collective-permute-start(bf16[128,1024]{1,0:T(8,128)(2,1)} %pad_maximum_fusion.1), channel_id=1, source_target_pairs={{32,0},{96,64},{160,128},{224,192}} | collective-permute-start | bytes 786440 | tf_op jit(solution)/shard_map/ppermute | solution.py:33
  65.6 6.0 %collective-permute-start.19 = (bf16[48,1024]{1,0:T(8,128)(2,1)S(1)}, bf16[48,1024]{1,0:T(8,128)(2,1)S(1)}, u32[]{:S(2)}, u32[]{:S(2)}) collective-permute-start(bf16[48,1024]{1,0:T(8,128)(2,1)S(1)} %fusion.3), channel_id=1, source_target_pairs={{32,18},{33,17},{34,20},{36,22},{38,24},{43,27},{45,29},{47,31},{9... | collective-permute-start | bytes 294920 | tf_op jit(solution)/shard_map/ppermute | solution.py:33
  66.9 8.1 %collective-permute-start.17 = (bf16[128,1024]{1,0:T(8,128)(2,1)S(1)}, bf16[128,1024]{1,0:T(8,128)(2,1)S(1)}, u32[]{:S(2)}, u32[]{:S(2)}) collective-permute-start(bf16[128,1024]{1,0:T(8,128)(2,1)S(1)} %collective-permute-done.8.refs_9_.refs_13_), channel_id=1, source_target_pairs={{0,16},{1,17},{2,18},{3,19},{4,20},{5,21},{6,22},{7,23},{8,24},{9,... | collective-permute-start | bytes 786440 | tf_op jit(solution)/shard_map/ppermute | solution.py:33
  67.0 11.6 %collective-permute-start.20 = (bf16[144,1024]{1,0:T(8,128)(2,1)S(1)}, bf16[144,1024]{1,0:T(8,128)(2,1)S(1)}, u32[]{:S(2)}, u32[]{:S(2)}) collective-permute-start(bf16[144,1024]{1,0:T(8,128)(2,1)S(1)} %slice_select_fusion), channel_id=1, source_target_pairs={{0,2},{1,15},{2,4},{3,1},{4,6},{5,3},{6,8},{7,5},{8,10},{9,7},{10,... | collective-permute-start | bytes 884744 | tf_op jit(solution)/shard_map/ppermute | solution.py:33
  76.0 1.3 %collective-permute-start.23 = (bf16[128,1024]{1,0:T(8,128)(2,1)S(1)}, bf16[128,1024]{1,0:T(8,128)(2,1)S(1)}, u32[]{:S(2)}, u32[]{:S(2)}) collective-permute-start(bf16[128,1024]{1,0:T(8,128)(2,1)S(1)} %add.132), channel_id=1, source_target_pairs={{0,1},{16,17},{64,65},{80,81},{128,129},{144,145},{192,193},{208,2... | collective-permute-start | bytes 786440 | tf_op jit(solution)/shard_map/ppermute | solution.py:33
  76.7 1.8 %collective-permute-start.21 = (bf16[128,1024]{1,0:T(8,128)(2,1)}, bf16[128,1024]{1,0:T(8,128)(2,1)S(1)}, u32[]{:S(2)}, u32[]{:S(2)}) collective-permute-start(bf16[128,1024]{1,0:T(8,128)(2,1)} %collective-permute-done.12.refs_18_), channel_id=1, source_target_pairs={{0,1},{1,0},{2,3},{3,2},{4,5},{5,4},{6,7},{7,6},{8,9},{9,8},{10,11... | collective-permute-start | bytes 786440 | tf_op jit(solution)/shard_map/ppermute | solution.py:33
  76.8 1.9 %collective-permute-start.22 = (bf16[128,1024]{1,0:T(8,128)(2,1)S(1)}, bf16[128,1024]{1,0:T(8,128)(2,1)S(1)}, u32[]{:S(2)}, u32[]{:S(2)}) collective-permute-start(bf16[128,1024]{1,0:T(8,128)(2,1)S(1)} %collective-permute-done.17.refs_21_), channel_id=1, source_target_pairs={{0,1},{1,0},{2,3},{3,2},{4,5},{5,4},{6,7},{7,6},{8,9},{9,8},{10,11... | collective-permute-start | bytes 786440 | tf_op jit(solution)/shard_map/ppermute | solution.py:33
  84.1 1.3 %collective-permute-start.24 = (f32[4,1152]{1,0:T(4,128)S(1)}, f32[4,1152]{1,0:T(4,128)S(1)}, u32[]{:S(2)}, u32[]{:S(2)}) collective-permute-start(f32[4,1152]{1,0:T(4,128)S(1)} %get-tuple-element.62), channel_id=1, source_target_pairs={{0,1},{1,0},{2,3},{3,2},{4,5},{5,4},{6,7},{7,6},{8,9},{9,8},{10,11... | collective-permute-start | bytes 55304 | tf_op jit(solution)/shard_map/ppermute | solution.py:33
  85.4 8.8 %collective-permute-start.25 = (f32[4,512]{1,0:T(4,128)S(1)}, f32[4,512]{1,0:T(4,128)S(1)}, u32[]{:S(2)}, u32[]{:S(2)}) collective-permute-start(f32[4,512]{1,0:T(4,128)S(1)} %slice_add_fusion), channel_id=1, source_target_pairs={{0,16},{1,17},{2,18},{3,19},{4,20},{5,21},{6,22},{7,23},{8,24},{9,... | collective-permute-start | bytes 24584 | tf_op jit(solution)/shard_map/ppermute | solution.py:33
  87.1 7.0 %collective-permute-start.26 = (f32[4,128]{1,0:T(4,128)S(1)}, f32[4,128]{1,0:T(4,128)S(1)}, u32[]{:S(2)}, u32[]{:S(2)}) collective-permute-start(f32[4,128]{1,0:T(4,128)S(1)} %slice_add_fusion.2), channel_id=1, source_target_pairs={{0,32},{64,96},{128,160},{192,224}} | collective-permute-start | bytes 6152 | tf_op jit(solution)/shard_map/ppermute | solution.py:33
  88.4 5.7 %collective-permute-start.27 = (f32[4,128]{1,0:T(4,128)S(1)}, f32[4,128]{1,0:T(4,128)S(1)}, u32[]{:S(2)}, u32[]{:S(2)}) collective-permute-start(f32[4,128]{1,0:T(4,128)S(1)} %slice_add_fusion.2), channel_id=1, source_target_pairs={{16,32},{80,96},{144,160},{208,224}} | collective-permute-start | bytes 6152 | tf_op jit(solution)/shard_map/ppermute | solution.py:33
  94.2 5.2 %collective-permute-start.28 = (f32[4,4,128]{2,1,0:T(4,128)S(1)}, f32[4,4,128]{2,1,0:T(4,128)S(1)}, u32[]{:S(2)}, u32[]{:S(2)}) collective-permute-start(f32[4,4,128]{2,1,0:T(4,128)S(1)} %pad_add_fusion), channel_id=1, source_target_pairs={{0,128},{1,129},{2,130},{3,131},{4,132},{5,133},{6,134},{7,135},{8... | collective-permute-start | bytes 24584 | tf_op jit(solution)/shard_map/ppermute | solution.py:33
  94.9 5.1 %collective-permute-start.29 = (f32[4,4,128]{2,1,0:T(4,128)S(1)}, f32[4,4,128]{2,1,0:T(4,128)S(1)}, u32[]{:S(2)}, u32[]{:S(2)}) collective-permute-start(f32[4,4,128]{2,1,0:T(4,128)S(1)} %pad_add_fusion), channel_id=1, source_target_pairs={{0,64},{1,65},{2,66},{3,67},{4,68},{5,69},{6,70},{7,71},{8,72},{9,... | collective-permute-start | bytes 24584 | tf_op jit(solution)/shard_map/ppermute | solution.py:33
  95.8 4.2 %collective-permute-start.30 = (f32[4,4,128]{2,1,0:T(4,128)S(1)}, f32[4,4,128]{2,1,0:T(4,128)S(1)}, u32[]{:S(2)}, u32[]{:S(2)}) collective-permute-start(f32[4,4,128]{2,1,0:T(4,128)S(1)} %pad_add_fusion), channel_id=1, source_target_pairs={{0,192},{1,193},{2,194},{3,195},{4,196},{5,197},{6,198},{7,199},{8... | collective-permute-start | bytes 24584 | tf_op jit(solution)/shard_map/ppermute | solution.py:33
  (7 other events, 37.8 us)

commit v15 on v14

--- a/solution.py
+++ b/solution.py
@@ -308,8 +308,8 @@
     ]
     y2_t = permute(y2, swap_core)
     xa_t = permute(xa, swap_core)
-    z2, z3, y2, xb, y1_t, y2_t, xa_t, odd_at[0] = fence(
-        z2, z3, y2, xb, y1_t, y2_t, xa_t, odd_at[0]
+    z2, z3, y2, y1_t, y2_t, xa_t, odd_at[0] = fence(
+        z2, z3, y2, y1_t, y2_t, xa_t, odd_at[0]
     )
 
     z4 = permute(jnp.where(c == 0, z3[:tagged], z3[tagged:]), same_core)

time: 101 us -> 102 us (level)
  transfers between devices with their start and end apart: 31 -> 31, of which waited for: 16 -> 17; matrix products, arithmetic and copies ran while one was open for 8% -> 8% of each run, Pallas kernels for 4% -> 4%
where the time goes in v15:
time: 102 us; the launch traced here: 101 us
  waiting for transfers between devices  37.9 us (37%)
  starting transfers between devices  36.5 us (36%)
  Pallas kernels  14.6 us (14%)
  other arithmetic  8.63 us (8%)
  local copies, waits for them, and re-layouts  3.26 us (3%)
    ppermute x31, waiting for transfers between devices, permute(): return lax.ppermute(value, AXES, pairs)  37.9 us
    ppermute x31, starting transfers between devices, permute(): return lax.ppermute(value, AXES, pairs)  36.5 us
    pallas_call x2, Pallas kernels, pair_sums(): pl.pallas_call(functools.partial(pair_kernel, col_cuts=tuple(col_cuts), n...  9.08 us
    pallas_call x1, Pallas kernels, raw_partial(): pl.pallas_call(raw_kernel, grid=(feats // width,), in_specs=[pl.BlockSpec...  5.49 us
    convert_element_type x1, other arithmetic, shards(): tag = tag.astype(jnp.bfloat16)  2.66 us
  transfers between devices with their start and end apart: 31, of which 17 were waited for; matrix products, arithmetic and copies ran while one was open for 8% of the time, Pallas kernels for 4%

profile of v15, /device:TPU:4, one launch (start us, length us, event | category | flops | bytes accessed | tf_op | source)
XLA Modules:
  0.0 101.3 jit_solution(15936606138465139652)
XLA Ops:
  0.0 5.5 %raw.1 = f32[512,1024]{1,0:T(8,128)} custom-call(s32[8,11]{1,0:T(8,128)} %bitcast.41, bf16[1584,512]{1,0:T(8,128)(2,1)} %bitcast.35, bf16[1584,1024]{1,0:T(8,128)(2,1)} %geometry.1), custom_call_target="tpu_custom_call" | custom-call | flops 1660944384 | bytes 8388608 | tf_op jit(solution)/shard_map/raw/pallas_call | solution.py:84
  5.5 1.7 %constant_dynamic-slice_fusion.1 = (f32[4,1,32,1024]{3,2,1,0:T(8,128)S(1)}, f16[4,1,32,1024]{3,2,0,1:T(8,128)(2,1)S(1)}, f16[4,1,32,1024]{3,2,0,1:T(8,128)(2,1)S(1)}, f16[4,1,32,1024]{3,2,0,1:T(8,128)(2,1)S(1)}) fusion(f32[4,4,32,1024]{3,2,1,0:T(8,128)} %bitcast.34, s32[]{:T(128)S(6)} %select_n.184, s32[]{:T(128)S(6)} %select_n.188, s32[]{:T(128)S(6)} %select_n.186, ...), kind=kLoop, calls=%fused_computation.44 | loop fusion | flops 393216 | bytes 3407888 | tf_op jit(solution)/shard_map/jit(dynamic_index_in_dim)/dynamic_slice | solution.py:265
  7.2 3.3 %collective-permute-start = (f16[128,1024]{1,0:T(8,128)(2,1)S(1)}, f16[128,1024]{1,0:T(8,128)(2,1)S(1)}, u32[]{:S(2)}, u32[]{:S(2)}) collective-permute-start(f16[128,1024]{1,0:T(8,128)(2,1)S(1)} %bitcast.38), channel_id=1, source_target_pairs={{0,128},{1,129},{2,130},{3,131},{4,132},{5,133},{6,134},{7,135},{8... | collective-permute-start | bytes 786440 | tf_op jit(solution)/shard_map/ppermute | solution.py:33
  11.2 2.6 %collective-permute-start.2 = (f16[128,1024]{1,0:T(8,128)(2,1)S(1)}, f16[128,1024]{1,0:T(8,128)(2,1)S(1)}, u32[]{:S(2)}, u32[]{:S(2)}) collective-permute-start(f16[128,1024]{1,0:T(8,128)(2,1)S(1)} %bitcast.36), channel_id=1, source_target_pairs={{0,192},{1,193},{2,194},{3,195},{4,196},{5,197},{6,198},{7,199},{8... | collective-permute-start | bytes 786440 | tf_op jit(solution)/shard_map/ppermute | solution.py:33
  14.5 2.7 %select_convert_fusion = bf16[16,1024]{1,0:T(8,128)(2,1)S(1)} fusion(bf16[]{:T(256)} %bitcast.5, bf16[]{:T(256)} %bitcast.4, bf16[]{:T(256)} %bitcast.3, bf16[]{:T(256)} %bitcast.2, s32[1024]{0:T(1024)S(1)} %get-tuple-element.75, s32[1024]{0:T(1024)S(1)} %get-tuple-element.76, pred[16]{0:T(512)(128)(4,1)S(1)} %iota_compare_fusion, pred[1024]{0:T(1024)(128)(4,1)S(1)} %fusion.13), kind=kLoop, calls=%fused_computation.17 | loop fusion | flops 163840 | bytes 42008 | tf_op jit(solution)/shard_map/convert_element_type | solution.py:260
  18.1 4.4 %collective-permute-done.1 = f16[128,1024]{1,0:T(8,128)(2,1)S(1)} collective-permute-done((f16[128,1024]{1,0:T(8,128)(2,1)S(1)}, f16[128,1024]{1,0:T(8,128)(2,1)S(1)}, u32[]{:S(2)}, u32[]{:S(2)}) %collective-permute-start.1) | collective-permute-done | bytes 262176 | tf_op jit(solution)/shard_map/ppermute | solution.py:33
  23.4 1.6 %collective-permute-done.3.refs_6_.refs_10_ = bf16[144,1024]{1,0:T(8,128)(2,1)S(1)} collective-permute-done((bf16[144,1024]{1,0:T(8,128)(2,1)S(1)}, bf16[144,1024]{1,0:T(8,128)(2,1)S(1)}, u32[]{:S(2)}, u32[]{:S(2)}) %collective-permute-start.3) | collective-permute-done | bytes 294944 | tf_op jit(solution)/shard_map/ppermute | solution.py:33
  25.2 2.0 %collective-permute-start.4 = (bf16[288,1024]{1,0:T(8,128)(2,1)S(1)}, bf16[288,1024]{1,0:T(8,128)(2,1)S(1)}, u32[]{:S(2)}, u32[]{:S(2)}) collective-permute-start(bf16[288,1024]{1,0:T(8,128)(2,1)S(1)} %maximum_select_fusion), channel_id=1, source_target_pairs={{0,2},{1,15},{2,4},{3,1},{4,6},{5,3},{6,8},{7,5},{8,10},{9,7},{10,... | collective-permute-start | bytes 1769480 | tf_op jit(solution)/shard_map/ppermute | solution.py:33
  27.2 1.4 %collective-permute-start.7 = (bf16[288,1024]{1,0:T(8,128)(2,1)S(1)}, bf16[288,1024]{1,0:T(8,128)(2,1)S(1)}, u32[]{:S(2)}, u32[]{:S(2)}) collective-permute-start(bf16[288,1024]{1,0:T(8,128)(2,1)S(1)} %maximum_select_fusion), channel_id=1, source_target_pairs={{0,64},{1,193},{2,66},{3,195},{4,68},{5,197},{6,70},{7,199},{8,72}... | collective-permute-start | bytes 1769480 | tf_op jit(solution)/shard_map/ppermute | solution.py:33
  28.5 1.2 %collective-permute-start.5 = (bf16[144,1024]{1,0:T(8,128)(2,1)S(1)}, bf16[144,1024]{1,0:T(8,128)(2,1)S(1)}, u32[]{:S(2)}, u32[]{:S(2)}) collective-permute-start(bf16[144,1024]{1,0:T(8,128)(2,1)S(1)} %pad_maximum_fusion.refs_1_.refs_5_.refs_3_.refs_9_), channel_id=1, source_target_pairs={{0,16},{1,17},{2,18},{3,19},{4,20},{5,21},{6,22},{7,23},{8,24},{9,... | collective-permute-start | bytes 884744 | tf_op jit(solution)/shard_map/ppermute | solution.py:33
  29.7 5.5 %collective-permute-done.5.refs_15_ = bf16[144,1024]{1,0:T(8,128)(2,1)S(1)} collective-permute-done((bf16[144,1024]{1,0:T(8,128)(2,1)S(1)}, bf16[144,1024]{1,0:T(8,128)(2,1)S(1)}, u32[]{:S(2)}, u32[]{:S(2)}) %collective-permute-start.5) | collective-permute-done | bytes 294944 | tf_op jit(solution)/shard_map/ppermute | solution.py:33
  35.3 3.7 %collective-permute-done.4.refs_2_.refs_4_ = bf16[288,1024]{1,0:T(8,128)(2,1)S(1)} collective-permute-done((bf16[288,1024]{1,0:T(8,128)(2,1)S(1)}, bf16[288,1024]{1,0:T(8,128)(2,1)S(1)}, u32[]{:S(2)}, u32[]{:S(2)}) %collective-permute-start.4) | collective-permute-done | bytes 589856 | tf_op jit(solution)/shard_map/ppermute | solution.py:33
  39.0 3.2 %collective-permute-start.10 = (bf16[144,1024]{1,0:T(8,128)(2,1)S(1)}, bf16[144,1024]{1,0:T(8,128)(2,1)S(1)}, u32[]{:S(2)}, u32[]{:S(2)}) collective-permute-start(bf16[144,1024]{1,0:T(8,128)(2,1)S(1)} %collective-permute-done.5.refs_15_), channel_id=1, source_target_pairs={{0,1},{1,0},{2,3},{3,2},{4,5},{5,4},{6,7},{7,6},{8,9},{9,8},{10,11... | collective-permute-start | bytes 884744 | tf_op jit(solution)/shard_map/ppermute | solution.py:33
  43.0 1.2 %collective-permute-start.9 = (bf16[128,1024]{1,0:T(8,128)(2,1)S(1)}, bf16[128,1024]{1,0:T(8,128)(2,1)}, u32[]{:S(2)}, u32[]{:S(2)}) collective-permute-start(bf16[128,1024]{1,0:T(8,128)(2,1)S(1)} %get-tuple-element.35), channel_id=1, source_target_pairs={{0,16},{1,17},{2,18},{3,19},{4,20},{5,21},{6,22},{7,23},{8,24},{9,... | collective-permute-start | bytes 786440 | tf_op jit(solution)/shard_map/ppermute | solution.py:33
  44.2 6.3 %collective-permute-done.8.refs_9_.refs_13_ = bf16[128,1024]{1,0:T(8,128)(2,1)S(1)} collective-permute-done((bf16[128,1024]{1,0:T(8,128)(2,1)S(1)}, bf16[128,1024]{1,0:T(8,128)(2,1)S(1)}, u32[]{:S(2)}, u32[]{:S(2)}) %collective-permute-start.8) | collective-permute-done | bytes 262176 | tf_op jit(solution)/shard_map/ppermute | solution.py:33
  50.5 1.8 %collective-permute-done.9.refs_17_ = bf16[128,1024]{1,0:T(8,128)(2,1)} collective-permute-done((bf16[128,1024]{1,0:T(8,128)(2,1)S(1)}, bf16[128,1024]{1,0:T(8,128)(2,1)}, u32[]{:S(2)}, u32[]{:S(2)}) %collective-permute-start.9) | collective-permute-done | bytes 262176 | tf_op jit(solution)/shard_map/ppermute | solution.py:33
  53.4 1.8 %collective-permute-start.13 = (bf16[128,1024]{1,0:T(8,128)(2,1)S(1)}, bf16[128,1024]{1,0:T(8,128)(2,1)}, u32[]{:S(2)}, u32[]{:S(2)}) collective-permute-start(bf16[128,1024]{1,0:T(8,128)(2,1)S(1)} %collective-permute-done.8.refs_9_.refs_13_), channel_id=1, source_target_pairs={{0,1},{1,0},{2,3},{3,2},{4,5},{5,4},{6,7},{7,6},{8,9},{9,8},{10,11... | collective-permute-start | bytes 786440 | tf_op jit(solution)/shard_map/ppermute | solution.py:33
  56.8 3.1 %collective-permute-start.15 = (bf16[128,1024]{1,0:T(8,128)(2,1)}, bf16[128,1024]{1,0:T(8,128)(2,1)}, u32[]{:S(2)}, u32[]{:S(2)}) collective-permute-start(bf16[128,1024]{1,0:T(8,128)(2,1)} %pad_maximum_fusion.1), channel_id=1, source_target_pairs={{32,16},{96,80},{160,144},{224,208}} | collective-permute-start | bytes 786440 | tf_op jit(solution)/shard_map/ppermute | solution.py:33
  60.2 2.1 %collective-permute-start.17 = (bf16[128,1024]{1,0:T(8,128)(2,1)}, bf16[128,1024]{1,0:T(8,128)(2,1)S(1)}, u32[]{:S(2)}, u32[]{:S(2)}) collective-permute-start(bf16[128,1024]{1,0:T(8,128)(2,1)} %pad_maximum_fusion.1), channel_id=1, source_target_pairs={{32,0},{96,64},{160,128},{224,192}} | collective-permute-start | bytes 786440 | tf_op jit(solution)/shard_map/ppermute | solution.py:33
  62.4 1.2 %collective-permute-done.11.refs_4_.refs_6_ = bf16[288,1024]{1,0:T(8,128)(2,1)S(1)} collective-permute-done((bf16[288,1024]{1,0:T(8,128)(2,1)S(1)}, bf16[288,1024]{1,0:T(8,128)(2,1)S(1)}, u32[]{:S(2)}, u32[]{:S(2)}) %collective-permute-start.11) | collective-permute-done | bytes 589856 | tf_op jit(solution)/shard_map/ppermute | solution.py:33
  64.5 1.3 %collective-permute-start.18 = (bf16[48,1024]{1,0:T(8,128)(2,1)S(1)}, bf16[48,1024]{1,0:T(8,128)(2,1)S(1)}, u32[]{:S(2)}, u32[]{:S(2)}) collective-permute-start(bf16[48,1024]{1,0:T(8,128)(2,1)S(1)} %fusion.3), channel_id=1, source_target_pairs={{32,18},{33,17},{34,20},{36,22},{38,24},{43,27},{45,29},{47,31},{9... | collective-permute-start | bytes 294920 | tf_op jit(solution)/shard_map/ppermute | solution.py:33
  67.0 3.7 %early.1 = (f32[4,512]{1,0:T(4,128)S(1)}, f32[4,512]{1,0:T(4,128)S(1)}) custom-call(s32[2]{0:T(128)S(1)} %pad_add_fusion.1.refs_0_, bf16[144,1024]{1,0:T(8,128)(2,1)S(1)} %pad_maximum_fusion.refs_1_.refs_5_.refs_3_.refs_9_, bf16[288,1024]{1,0:T(8,128)(2,1)S(1)} %collective-permute-done.4.refs_2_.refs_4_, ...), custom_call_target="tpu_custom_call" | custom-call | flops 5637144576 | bytes 11796480 | tf_op jit(solution)/shard_map/early/pallas_call | solution.py:224
  71.7 2.7 %collective-permute-done.16.refs_21_ = bf16[128,1024]{1,0:T(8,128)(2,1)S(1)} collective-permute-done((bf16[128,1024]{1,0:T(8,128)(2,1)S(1)}, bf16[128,1024]{1,0:T(8,128)(2,1)S(1)}, u32[]{:S(2)}, u32[]{:S(2)}) %collective-permute-start.16) | collective-permute-done | bytes 262176 | tf_op jit(solution)/shard_map/ppermute | solution.py:33
  74.4 1.0 %add.132 = bf16[128,1024]{1,0:T(8,128)(2,1)S(1)} add(bf16[128,1024]{1,0:T(8,128)(2,1)} %collective-permute-done.15, bf16[128,1024]{1,0:T(8,128)(2,1)S(1)} %collective-permute-done.17) | non-fusion elementwise | flops 131072 | bytes 786432 | tf_op jit(solution)/shard_map/add | solution.py:333
  78.1 5.3 %late.1 = (f32[4,512]{1,0:T(4,128)S(1)}, f32[4,512]{1,0:T(4,128)S(1)}, f32[4,1152]{1,0:T(4,128)S(1)}, f32[4,128]{1,0:T(4,128)S(1)}) custom-call(s32[2]{0:T(128)S(1)} %pad_add_fusion.1.refs_0_, f32[4,512]{1,0:T(4,128)S(1)} %get-tuple-element.50.refs_1_, f32[4,512]{1,0:T(4,128)S(1)} %get-tuple-element.51.refs_2_, ...), custom_call_target="tpu_custom_call" | custom-call | flops 16609443840 | bytes 22216704 | tf_op jit(solution)/shard_map/late/pallas_call | solution.py:224
  83.7 1.1 %collective-permute-done.24 = f32[4,1152]{1,0:T(4,128)S(1)} collective-permute-done((f32[4,1152]{1,0:T(4,128)S(1)}, f32[4,1152]{1,0:T(4,128)S(1)}, u32[]{:S(2)}, u32[]{:S(2)}) %collective-permute-start.24) | collective-permute-done | bytes 18464 | tf_op jit(solution)/shard_map/ppermute | solution.py:33
  84.8 2.5 %collective-permute-start.25 = (f32[4,512]{1,0:T(4,128)S(1)}, f32[4,512]{1,0:T(4,128)S(1)}, u32[]{:S(2)}, u32[]{:S(2)}) collective-permute-start(f32[4,512]{1,0:T(4,128)S(1)} %slice_add_fusion), channel_id=1, source_target_pairs={{0,16},{1,17},{2,18},{3,19},{4,20},{5,21},{6,22},{7,23},{8,24},{9,... | collective-permute-start | bytes 24584 | tf_op jit(solution)/shard_map/ppermute | solution.py:33
  87.3 1.3 %collective-permute-start.26 = (f32[4,128]{1,0:T(4,128)S(1)}, f32[4,128]{1,0:T(4,128)S(1)}, u32[]{:S(2)}, u32[]{:S(2)}) collective-permute-start(f32[4,128]{1,0:T(4,128)S(1)} %slice_add_fusion.2), channel_id=1, source_target_pairs={{0,32},{64,96},{128,160},{192,224}} | collective-permute-start | bytes 6152 | tf_op jit(solution)/shard_map/ppermute | solution.py:33
  88.5 1.3 %collective-permute-start.27 = (f32[4,128]{1,0:T(4,128)S(1)}, f32[4,128]{1,0:T(4,128)S(1)}, u32[]{:S(2)}, u32[]{:S(2)}) collective-permute-start(f32[4,128]{1,0:T(4,128)S(1)} %slice_add_fusion.2), channel_id=1, source_target_pairs={{16,32},{80,96},{144,160},{208,224}} | collective-permute-start | bytes 6152 | tf_op jit(solution)/shard_map/ppermute | solution.py:33
  89.8 4.4 %collective-permute-done.26 = f32[4,128]{1,0:T(4,128)S(1)} collective-permute-done((f32[4,128]{1,0:T(4,128)S(1)}, f32[4,128]{1,0:T(4,128)S(1)}, u32[]{:S(2)}, u32[]{:S(2)}) %collective-permute-start.26) | collective-permute-done | bytes 2080 | tf_op jit(solution)/shard_map/ppermute | solution.py:33
  94.4 1.2 %collective-permute-start.28 = (f32[4,4,128]{2,1,0:T(4,128)S(1)}, f32[4,4,128]{2,1,0:T(4,128)S(1)}, u32[]{:S(2)}, u32[]{:S(2)}) collective-permute-start(f32[4,4,128]{2,1,0:T(4,128)S(1)} %pad_add_fusion), channel_id=1, source_target_pairs={{0,128},{1,129},{2,130},{3,131},{4,132},{5,133},{6,134},{7,135},{8... | collective-permute-start | bytes 24584 | tf_op jit(solution)/shard_map/ppermute | solution.py:33
  95.9 2.9 %collective-permute-start.30 = (f32[4,4,128]{2,1,0:T(4,128)S(1)}, f32[4,4,128]{2,1,0:T(4,128)S(1)}, u32[]{:S(2)}, u32[]{:S(2)}) collective-permute-start(f32[4,4,128]{2,1,0:T(4,128)S(1)} %pad_add_fusion), channel_id=1, source_target_pairs={{0,192},{1,193},{2,194},{3,195},{4,196},{5,197},{6,198},{7,199},{8... | collective-permute-start | bytes 24584 | tf_op jit(solution)/shard_map/ppermute | solution.py:33
  (90 shorter events, 16.2 us)
Async XLA Ops:
  7.2 10.8 %collective-permute-start = (f16[128,1024]{1,0:T(8,128)(2,1)S(1)}, f16[128,1024]{1,0:T(8,128)(2,1)S(1)}, u32[]{:S(2)}, u32[]{:S(2)}) collective-permute-start(f16[128,1024]{1,0:T(8,128)(2,1)S(1)} %bitcast.38), channel_id=1, source_target_pairs={{0,128},{1,129},{2,130},{3,131},{4,132},{5,133},{6,134},{7,135},{8... | collective-permute-start | bytes 786440 | tf_op jit(solution)/shard_map/ppermute | solution.py:33
  10.5 12.0 %collective-permute-start.1 = (f16[128,1024]{1,0:T(8,128)(2,1)S(1)}, f16[128,1024]{1,0:T(8,128)(2,1)S(1)}, u32[]{:S(2)}, u32[]{:S(2)}) collective-permute-start(f16[128,1024]{1,0:T(8,128)(2,1)S(1)} %bitcast.37), channel_id=1, source_target_pairs={{0,64},{1,65},{2,66},{3,67},{4,68},{5,69},{6,70},{7,71},{8,72},{9,... | collective-permute-start | bytes 786440 | tf_op jit(solution)/shard_map/ppermute | solution.py:33
  11.2 11.7 %collective-permute-start.2 = (f16[128,1024]{1,0:T(8,128)(2,1)S(1)}, f16[128,1024]{1,0:T(8,128)(2,1)S(1)}, u32[]{:S(2)}, u32[]{:S(2)}) collective-permute-start(f16[128,1024]{1,0:T(8,128)(2,1)S(1)} %bitcast.36), channel_id=1, source_target_pairs={{0,192},{1,193},{2,194},{3,195},{4,196},{5,197},{6,198},{7,199},{8... | collective-permute-start | bytes 786440 | tf_op jit(solution)/shard_map/ppermute | solution.py:33
  23.3 1.7 %collective-permute-start.3 = (bf16[144,1024]{1,0:T(8,128)(2,1)S(1)}, bf16[144,1024]{1,0:T(8,128)(2,1)S(1)}, u32[]{:S(2)}, u32[]{:S(2)}) collective-permute-start(bf16[144,1024]{1,0:T(8,128)(2,1)S(1)} %pad_maximum_fusion.refs_1_.refs_5_.refs_3_.refs_9_), channel_id=1, source_target_pairs={{0,1},{1,0},{2,3},{3,2},{4,5},{5,4},{6,7},{7,6},{8,9},{9,8},{10,11... | collective-permute-start | bytes 884744 | tf_op jit(solution)/shard_map/ppermute | solution.py:33
  25.2 31.6 %copy-start.5 = (bf16[288,1024]{1,0:T(8,128)(2,1)}, bf16[288,1024]{1,0:T(8,128)(2,1)S(1)}, u32[]{:S(2)}) copy-start(bf16[288,1024]{1,0:T(8,128)(2,1)S(1)} %maximum_select_fusion) | copy-start | bytes 1769476
  25.2 13.8 %collective-permute-start.4 = (bf16[288,1024]{1,0:T(8,128)(2,1)S(1)}, bf16[288,1024]{1,0:T(8,128)(2,1)S(1)}, u32[]{:S(2)}, u32[]{:S(2)}) collective-permute-start(bf16[288,1024]{1,0:T(8,128)(2,1)S(1)} %maximum_select_fusion), channel_id=1, source_target_pairs={{0,2},{1,15},{2,4},{3,1},{4,6},{5,3},{6,8},{7,5},{8,10},{9,7},{10,... | collective-permute-start | bytes 1769480 | tf_op jit(solution)/shard_map/ppermute | solution.py:33
  27.2 15.0 %collective-permute-start.7 = (bf16[288,1024]{1,0:T(8,128)(2,1)S(1)}, bf16[288,1024]{1,0:T(8,128)(2,1)S(1)}, u32[]{:S(2)}, u32[]{:S(2)}) collective-permute-start(bf16[288,1024]{1,0:T(8,128)(2,1)S(1)} %maximum_select_fusion), channel_id=1, source_target_pairs={{0,64},{1,193},{2,66},{3,195},{4,68},{5,197},{6,70},{7,199},{8,72}... | collective-permute-start | bytes 1769480 | tf_op jit(solution)/shard_map/ppermute | solution.py:33
  28.5 6.7 %collective-permute-start.5 = (bf16[144,1024]{1,0:T(8,128)(2,1)S(1)}, bf16[144,1024]{1,0:T(8,128)(2,1)S(1)}, u32[]{:S(2)}, u32[]{:S(2)}) collective-permute-start(bf16[144,1024]{1,0:T(8,128)(2,1)S(1)} %pad_maximum_fusion.refs_1_.refs_5_.refs_3_.refs_9_), channel_id=1, source_target_pairs={{0,16},{1,17},{2,18},{3,19},{4,20},{5,21},{6,22},{7,23},{8,24},{9,... | collective-permute-start | bytes 884744 | tf_op jit(solution)/shard_map/ppermute | solution.py:33
  39.0 13.3 %collective-permute-start.6 = (bf16[288,1024]{1,0:T(8,128)(2,1)S(1)}, bf16[288,1024]{1,0:T(8,128)(2,1)S(1)}, u32[]{:S(2)}, u32[]{:S(2)}) collective-permute-start(bf16[288,1024]{1,0:T(8,128)(2,1)S(1)} %collective-permute-done.4.refs_2_.refs_4_), channel_id=1, source_target_pairs={{0,2},{1,15},{2,4},{3,1},{4,6},{5,3},{6,8},{7,5},{8,10},{9,7},{10,... | collective-permute-start | bytes 1769480 | tf_op jit(solution)/shard_map/ppermute | solution.py:33
  39.0 13.3 %collective-permute-start.10 = (bf16[144,1024]{1,0:T(8,128)(2,1)S(1)}, bf16[144,1024]{1,0:T(8,128)(2,1)S(1)}, u32[]{:S(2)}, u32[]{:S(2)}) collective-permute-start(bf16[144,1024]{1,0:T(8,128)(2,1)S(1)} %collective-permute-done.5.refs_15_), channel_id=1, source_target_pairs={{0,1},{1,0},{2,3},{3,2},{4,5},{5,4},{6,7},{7,6},{8,9},{9,8},{10,11... | collective-permute-start | bytes 884744 | tf_op jit(solution)/shard_map/ppermute | solution.py:33
  42.9 7.6 %collective-permute-start.8 = (bf16[128,1024]{1,0:T(8,128)(2,1)S(1)}, bf16[128,1024]{1,0:T(8,128)(2,1)S(1)}, u32[]{:S(2)}, u32[]{:S(2)}) collective-permute-start(bf16[128,1024]{1,0:T(8,128)(2,1)S(1)} %get-tuple-element.35), channel_id=1, source_target_pairs={{0,64},{1,193},{2,66},{3,195},{4,68},{5,197},{6,70},{7,199},{8,72}... | collective-permute-start | bytes 786440 | tf_op jit(solution)/shard_map/ppermute | solution.py:33
  43.0 9.3 %collective-permute-start.9 = (bf16[128,1024]{1,0:T(8,128)(2,1)S(1)}, bf16[128,1024]{1,0:T(8,128)(2,1)}, u32[]{:S(2)}, u32[]{:S(2)}) collective-permute-start(bf16[128,1024]{1,0:T(8,128)(2,1)S(1)} %get-tuple-element.35), channel_id=1, source_target_pairs={{0,16},{1,17},{2,18},{3,19},{4,20},{5,21},{6,22},{7,23},{8,24},{9,... | collective-permute-start | bytes 786440 | tf_op jit(solution)/shard_map/ppermute | solution.py:33
  52.3 3.0 %collective-permute-start.12 = (bf16[288,1024]{1,0:T(8,128)(2,1)S(1)}, bf16[288,1024]{1,0:T(8,128)(2,1)S(1)}, u32[]{:S(2)}, u32[]{:S(2)}) collective-permute-start(bf16[288,1024]{1,0:T(8,128)(2,1)S(1)} %collective-permute-done.7.refs_7_.refs_11_), channel_id=1, source_target_pairs={{0,1},{1,0},{2,3},{3,2},{4,5},{5,4},{6,7},{7,6},{8,9},{9,8},{10,11... | collective-permute-start | bytes 1769480 | tf_op jit(solution)/shard_map/ppermute | solution.py:33
  52.5 11.1 %collective-permute-start.11 = (bf16[288,1024]{1,0:T(8,128)(2,1)S(1)}, bf16[288,1024]{1,0:T(8,128)(2,1)S(1)}, u32[]{:S(2)}, u32[]{:S(2)}) collective-permute-start(bf16[288,1024]{1,0:T(8,128)(2,1)S(1)} %collective-permute-done.6.refs_3_.refs_5_), channel_id=1, source_target_pairs={{0,2},{1,15},{2,4},{3,1},{4,6},{5,3},{6,8},{7,5},{8,10},{9,7},{10,... | collective-permute-start | bytes 1769480 | tf_op jit(solution)/shard_map/ppermute | solution.py:33
  53.4 6.9 %collective-permute-start.13 = (bf16[128,1024]{1,0:T(8,128)(2,1)S(1)}, bf16[128,1024]{1,0:T(8,128)(2,1)}, u32[]{:S(2)}, u32[]{:S(2)}) collective-permute-start(bf16[128,1024]{1,0:T(8,128)(2,1)S(1)} %collective-permute-done.8.refs_9_.refs_13_), channel_id=1, source_target_pairs={{0,1},{1,0},{2,3},{3,2},{4,5},{5,4},{6,7},{7,6},{8,9},{9,8},{10,11... | collective-permute-start | bytes 786440 | tf_op jit(solution)/shard_map/ppermute | solution.py:33
  55.1 7.2 %collective-permute-start.14 = (bf16[128,1024]{1,0:T(8,128)(2,1)}, bf16[128,1024]{1,0:T(8,128)(2,1)}, u32[]{:S(2)}, u32[]{:S(2)}) collective-permute-start(bf16[128,1024]{1,0:T(8,128)(2,1)} %collective-permute-done.9.refs_17_), channel_id=1, source_target_pairs={{0,1},{1,0},{2,3},{3,2},{4,5},{5,4},{6,7},{7,6},{8,9},{9,8},{10,11... | collective-permute-start | bytes 786440 | tf_op jit(solution)/shard_map/ppermute | solution.py:33
  56.8 6.8 %collective-permute-start.15 = (bf16[128,1024]{1,0:T(8,128)(2,1)}, bf16[128,1024]{1,0:T(8,128)(2,1)}, u32[]{:S(2)}, u32[]{:S(2)}) collective-permute-start(bf16[128,1024]{1,0:T(8,128)(2,1)} %pad_maximum_fusion.1), channel_id=1, source_target_pairs={{32,16},{96,80},{160,144},{224,208}} | collective-permute-start | bytes 786440 | tf_op jit(solution)/shard_map/ppermute | solution.py:33
  60.0 16.1 %collective-permute-start.20 = (bf16[128,1024]{1,0:T(8,128)(2,1)}, bf16[128,1024]{1,0:T(8,128)(2,1)S(1)}, u32[]{:S(2)}, u32[]{:S(2)}) collective-permute-start(bf16[128,1024]{1,0:T(8,128)(2,1)} %get-tuple-element.54), channel_id=1, source_target_pairs={{0,16},{1,17},{2,18},{3,19},{4,20},{5,21},{6,22},{7,23},{8,24},{9,... | collective-permute-start | bytes 786440 | tf_op jit(solution)/shard_map/ppermute | solution.py:33
  60.2 11.5 %collective-permute-start.17 = (bf16[128,1024]{1,0:T(8,128)(2,1)}, bf16[128,1024]{1,0:T(8,128)(2,1)S(1)}, u32[]{:S(2)}, u32[]{:S(2)}) collective-permute-start(bf16[128,1024]{1,0:T(8,128)(2,1)} %pad_maximum_fusion.1), channel_id=1, source_target_pairs={{32,0},{96,64},{160,128},{224,192}} | collective-permute-start | bytes 786440 | tf_op jit(solution)/shard_map/ppermute | solution.py:33
  64.5 7.2 %collective-permute-start.18 = (bf16[48,1024]{1,0:T(8,128)(2,1)S(1)}, bf16[48,1024]{1,0:T(8,128)(2,1)S(1)}, u32[]{:S(2)}, u32[]{:S(2)}) collective-permute-start(bf16[48,1024]{1,0:T(8,128)(2,1)S(1)} %fusion.3), channel_id=1, source_target_pairs={{32,18},{33,17},{34,20},{36,22},{38,24},{43,27},{45,29},{47,31},{9... | collective-permute-start | bytes 294920 | tf_op jit(solution)/shard_map/ppermute | solution.py:33
  65.8 8.6 %collective-permute-start.16 = (bf16[128,1024]{1,0:T(8,128)(2,1)S(1)}, bf16[128,1024]{1,0:T(8,128)(2,1)S(1)}, u32[]{:S(2)}, u32[]{:S(2)}) collective-permute-start(bf16[128,1024]{1,0:T(8,128)(2,1)S(1)} %collective-permute-done.8.refs_9_.refs_13_), channel_id=1, source_target_pairs={{0,16},{1,17},{2,18},{3,19},{4,20},{5,21},{6,22},{7,23},{8,24},{9,... | collective-permute-start | bytes 786440 | tf_op jit(solution)/shard_map/ppermute | solution.py:33
  66.5 11.3 %collective-permute-start.19 = (bf16[144,1024]{1,0:T(8,128)(2,1)S(1)}, bf16[144,1024]{1,0:T(8,128)(2,1)S(1)}, u32[]{:S(2)}, u32[]{:S(2)}) collective-permute-start(bf16[144,1024]{1,0:T(8,128)(2,1)S(1)} %slice_select_fusion), channel_id=1, source_target_pairs={{0,2},{1,15},{2,4},{3,1},{4,6},{5,3},{6,8},{7,5},{8,10},{9,7},{10,... | collective-permute-start | bytes 884744 | tf_op jit(solution)/shard_map/ppermute | solution.py:33
  75.5 1.3 %collective-permute-start.23 = (bf16[128,1024]{1,0:T(8,128)(2,1)S(1)}, bf16[128,1024]{1,0:T(8,128)(2,1)S(1)}, u32[]{:S(2)}, u32[]{:S(2)}) collective-permute-start(bf16[128,1024]{1,0:T(8,128)(2,1)S(1)} %add.132), channel_id=1, source_target_pairs={{0,1},{16,17},{64,65},{80,81},{128,129},{144,145},{192,193},{208,2... | collective-permute-start | bytes 786440 | tf_op jit(solution)/shard_map/ppermute | solution.py:33
  76.1 1.6 %collective-permute-start.21 = (bf16[128,1024]{1,0:T(8,128)(2,1)S(1)}, bf16[128,1024]{1,0:T(8,128)(2,1)S(1)}, u32[]{:S(2)}, u32[]{:S(2)}) collective-permute-start(bf16[128,1024]{1,0:T(8,128)(2,1)S(1)} %collective-permute-done.20.refs_18_), channel_id=1, source_target_pairs={{0,1},{1,0},{2,3},{3,2},{4,5},{5,4},{6,7},{7,6},{8,9},{9,8},{10,11... | collective-permute-start | bytes 786440 | tf_op jit(solution)/shard_map/ppermute | solution.py:33
  76.2 1.9 %collective-permute-start.22 = (bf16[128,1024]{1,0:T(8,128)(2,1)S(1)}, bf16[128,1024]{1,0:T(8,128)(2,1)S(1)}, u32[]{:S(2)}, u32[]{:S(2)}) collective-permute-start(bf16[128,1024]{1,0:T(8,128)(2,1)S(1)} %collective-permute-done.16.refs_21_), channel_id=1, source_target_pairs={{0,1},{1,0},{2,3},{3,2},{4,5},{5,4},{6,7},{7,6},{8,9},{9,8},{10,11... | collective-permute-start | bytes 786440 | tf_op jit(solution)/shard_map/ppermute | solution.py:33
  83.5 1.3 %collective-permute-start.24 = (f32[4,1152]{1,0:T(4,128)S(1)}, f32[4,1152]{1,0:T(4,128)S(1)}, u32[]{:S(2)}, u32[]{:S(2)}) collective-permute-start(f32[4,1152]{1,0:T(4,128)S(1)} %get-tuple-element.60), channel_id=1, source_target_pairs={{0,1},{1,0},{2,3},{3,2},{4,5},{5,4},{6,7},{7,6},{8,9},{9,8},{10,11... | collective-permute-start | bytes 55304 | tf_op jit(solution)/shard_map/ppermute | solution.py:33
  84.8 9.5 %collective-permute-start.25 = (f32[4,512]{1,0:T(4,128)S(1)}, f32[4,512]{1,0:T(4,128)S(1)}, u32[]{:S(2)}, u32[]{:S(2)}) collective-permute-start(f32[4,512]{1,0:T(4,128)S(1)} %slice_add_fusion), channel_id=1, source_target_pairs={{0,16},{1,17},{2,18},{3,19},{4,20},{5,21},{6,22},{7,23},{8,24},{9,... | collective-permute-start | bytes 24584 | tf_op jit(solution)/shard_map/ppermute | solution.py:33
  87.3 7.0 %collective-permute-start.26 = (f32[4,128]{1,0:T(4,128)S(1)}, f32[4,128]{1,0:T(4,128)S(1)}, u32[]{:S(2)}, u32[]{:S(2)}) collective-permute-start(f32[4,128]{1,0:T(4,128)S(1)} %slice_add_fusion.2), channel_id=1, source_target_pairs={{0,32},{64,96},{128,160},{192,224}} | collective-permute-start | bytes 6152 | tf_op jit(solution)/shard_map/ppermute | solution.py:33
  88.5 5.7 %collective-permute-start.27 = (f32[4,128]{1,0:T(4,128)S(1)}, f32[4,128]{1,0:T(4,128)S(1)}, u32[]{:S(2)}, u32[]{:S(2)}) collective-permute-start(f32[4,128]{1,0:T(4,128)S(1)} %slice_add_fusion.2), channel_id=1, source_target_pairs={{16,32},{80,96},{144,160},{208,224}} | collective-permute-start | bytes 6152 | tf_op jit(solution)/shard_map/ppermute | solution.py:33
  94.4 5.2 %collective-permute-start.28 = (f32[4,4,128]{2,1,0:T(4,128)S(1)}, f32[4,4,128]{2,1,0:T(4,128)S(1)}, u32[]{:S(2)}, u32[]{:S(2)}) collective-permute-start(f32[4,4,128]{2,1,0:T(4,128)S(1)} %pad_add_fusion), channel_id=1, source_target_pairs={{0,128},{1,129},{2,130},{3,131},{4,132},{5,133},{6,134},{7,135},{8... | collective-permute-start | bytes 24584 | tf_op jit(solution)/shard_map/ppermute | solution.py:33
  95.5 4.9 %collective-permute-start.29 = (f32[4,4,128]{2,1,0:T(4,128)S(1)}, f32[4,4,128]{2,1,0:T(4,128)S(1)}, u32[]{:S(2)}, u32[]{:S(2)}) collective-permute-start(f32[4,4,128]{2,1,0:T(4,128)S(1)} %pad_add_fusion), channel_id=1, source_target_pairs={{0,64},{1,65},{2,66},{3,67},{4,68},{5,69},{6,70},{7,71},{8,72},{9,... | collective-permute-start | bytes 24584 | tf_op jit(solution)/shard_map/ppermute | solution.py:33
  95.9 4.5 %collective-permute-start.30 = (f32[4,4,128]{2,1,0:T(4,128)S(1)}, f32[4,4,128]{2,1,0:T(4,128)S(1)}, u32[]{:S(2)}, u32[]{:S(2)}) collective-permute-start(f32[4,4,128]{2,1,0:T(4,128)S(1)} %pad_add_fusion), channel_id=1, source_target_pairs={{0,192},{1,193},{2,194},{3,195},{4,196},{5,197},{6,198},{7,199},{8... | collective-permute-start | bytes 24584 | tf_op jit(solution)/shard_map/ppermute | solution.py:33
  (7 other events, 36.6 us)
